TPU v7x, 256 devices: a whole 4x4x8 slice. The times are simulated.
256 devices in a mesh: pipe: 4 (over z_lo, core), vocab: 64 (over x, y, z_hi).
Axes of the slice: x: 4, y: 4, z: 8 (z_hi: 4, z_lo: 2; z = z_hi * 2 + z_lo), core: 2. Of those that a mesh axis runs over, the one named last changes fastest.
Arguments:
- student_hidden: bfloat16 [512, 5120], P('pipe', 'vocab'), may hold values from -30 to 30
- teacher_hidden: bfloat16 [512, 4096], P('pipe', 'vocab'), may hold values from -30 to 30
- student_head: bfloat16 [98304, 5120], P(('pipe', 'vocab')), may hold values from -3 to 3
- teacher_head: bfloat16 [98304, 4096], P(('pipe', 'vocab')), may hold values from -3 to 3
- row_weight: float32 [512], replicated, may hold values from 2 to 16
Outputs:
- kl_rows: float32 [512], P('pipe')
- hidden_grad: float32 [512, 5120], P('pipe', 'vocab')
- head_grad: bfloat16 [98304, 5120], P(('pipe', 'vocab'))
All inputs are finite; a program needn't handle non-finite values.
Results may differ from a plain program's by a relative error of at most 0.017.
Values may be sent and summed in bfloat16 or wider, within the bound.
No kernel may reach another device: no remote copies, remote signals or barrier semaphores. Data moves between devices by JAX's collectives and lax.ppermute only.
A program may use at most 128 MiB of HBM per device.

v0:
```python
import jax
import jax.numpy as jnp
from jax import lax
from jax.sharding import PartitionSpec as P


def dot_rows(left, right):
    return lax.dot_general(
        left, right, (((1,), (1,)), ((), ())), preferred_element_type=jnp.float32
    )


def per_device(student_hidden, teacher_hidden, student_head, teacher_head, row_weight):
    tok_dev = student_hidden.shape[0]
    wide_student, wide_teacher = (
        lax.all_gather(student_hidden, "vocab", axis=1, tiled=True),
        lax.all_gather(teacher_hidden, "vocab", axis=1, tiled=True),
    )
    full_student, full_teacher = (
        lax.all_gather(wide_student, "pipe", axis=0, tiled=True),
        lax.all_gather(wide_teacher, "pipe", axis=0, tiled=True),
    )
    student_logits = dot_rows(full_student, student_head)
    teacher_logits = dot_rows(full_teacher, teacher_head)
    local_smax = jnp.max(student_logits, axis=1)
    local_tmax = jnp.max(teacher_logits, axis=1)
    student_max, teacher_max = lax.pmax((local_smax, local_tmax), ("pipe", "vocab"))
    student_exp = jnp.exp(student_logits - student_max[:, None])
    teacher_exp = jnp.exp(teacher_logits - teacher_max[:, None])
    student_total, teacher_total, cross = lax.psum(
        (
            jnp.sum(student_exp, axis=1),
            jnp.sum(teacher_exp, axis=1),
            jnp.sum(teacher_exp * (teacher_logits - student_logits), axis=1),
        ),
        ("pipe", "vocab"),
    )
    kl_all = (
        cross / teacher_total
        - teacher_max
        - jnp.log(teacher_total)
        + student_max
        + jnp.log(student_total)
    )
    kl_rows = lax.dynamic_slice_in_dim(kl_all, lax.axis_index("pipe") * tok_dev, tok_dev, 0)
    logit_grad = (
        row_weight[:, None]
        * (student_exp / student_total[:, None] - teacher_exp / teacher_total[:, None])
    ).astype(jnp.bfloat16)
    head_grad = lax.dot_general(
        logit_grad, full_student, (((0,), (0,)), ((), ())), preferred_element_type=jnp.float32
    ).astype(jnp.bfloat16)
    whole_term = jnp.dot(logit_grad, student_head, preferred_element_type=jnp.float32)
    feature_part = lax.psum_scatter(whole_term, "vocab", scatter_dimension=1, tiled=True)
    hidden_grad = lax.psum_scatter(feature_part, "pipe", scatter_dimension=0, tiled=True)
    return (kl_rows, hidden_grad, head_grad)


def solution(mesh):
    placed = (
        P("pipe", "vocab"),
        P("pipe", "vocab"),
        P(("pipe", "vocab"), None),
        P(("pipe", "vocab"), None),
        P(),
    )
    return jax.shard_map(
        per_device,
        mesh=mesh,
        in_specs=placed,
        out_specs=(P("pipe"), P("pipe", "vocab"), P(("pipe", "vocab"), None)),
        check_vma=False,
    )
```

profile of v0, /device:TPU:2, one launch (start us, length us, event | category | flops | bytes accessed | tf_op | source)
XLA Modules:
  0.0 878.4 jit_solution(4081750375414610562)
XLA Ops:
  7.2 0.0 all-gather.5.cloned.1.call-start
  7.2 0.7 all-gather.5.cloned.1.call-update
  7.9 0.0 all-gather.9.cloned.1.call-start
  8.0 0.7 all-gather.9.cloned.1.call-update
  8.7 0.0 all-gather.7.cloned.1.call-start
  8.7 81.2 %all-gather.5.cloned.1.call-done = bf16[128,4096]{0,1:T(8,128)(2,1)} async-done(((bf16[128,64]{0,1:T(8,128)(2,1)}), bf16[128,4096]{0,1:T(8,128)(2,1)}) %all-gather.5.cloned.1.call-update) | async-done | bytes 1048592 | tf_op jit(solution)/shard_map/all_gather | solution.py:17
  89.9 0.0 all-gather.7.cloned.1.call-update
  89.9 0.0 all-gather.11.cloned.1.call-start
  89.9 76.3 %all-gather.9.cloned.1.call-done = bf16[128,5120]{0,1:T(8,128)(2,1)} async-done(((bf16[128,80]{0,1:T(8,128)(2,1)}), bf16[128,5120]{0,1:T(8,128)(2,1)}) %all-gather.9.cloned.1.call-update) | async-done | bytes 1310736 | tf_op jit(solution)/shard_map/all_gather | solution.py:16
  166.3 0.0 all-gather.11.cloned.1.call-update
  166.3 0.0 reduce-scatter.3.cloned.1.call-start
  166.3 47.2 %all-gather.7.cloned.1.call-done = bf16[512,4096]{0,1:T(8,128)(2,1)} async-done(((bf16[128,4096]{0,1:T(8,128)(2,1)}), bf16[512,4096]{0,1:T(8,128)(2,1)}) %all-gather.7.cloned.1.call-update) | async-done | bytes 4194320 | tf_op jit(solution)/shard_map/all_gather | solution.py:21
  213.6 4.9 fusion.3
  218.4 55.1 %all-gather.11.cloned.1.call-done = bf16[512,5120]{0,1:T(8,128)(2,1)} async-done(((bf16[128,5120]{0,1:T(8,128)(2,1)}), bf16[512,5120]{0,1:T(8,128)(2,1)}) %all-gather.11.cloned.1.call-update) | async-done | bytes 5242896 | tf_op jit(solution)/shard_map/all_gather | solution.py:20
  273.5 6.8 fusion.4
  280.3 76.8 %all-reduce.1 = (f32[512]{0:T(512)S(1)}, f32[512]{0:T(512)S(1)}) all-reduce(f32[512]{0:T(512)S(1)} %get-tuple-element.11, f32[512]{0:T(512)S(1)} %get-tuple-element.13), channel_id=1, replica_groups=mesh['pipe'=4,'vocab'=64] {'pipe','vocab'}, use_global_device_ids=true, to_apply=%region_1.0 | all-reduce | flops 1024 | bytes 8192 | tf_op jit(solution)/shard_map/pmax | solution.py:27
  357.1 1.7 multiply_reduce_fusion
  358.8 73.7 %all-reduce = (f32[512]{0:T(512)S(1)}, f32[512]{0:T(512)S(1)}, f32[512]{0:T(512)S(1)}) all-reduce(f32[512]{0:T(512)S(1)} %get-tuple-element.5, f32[512]{0:T(512)S(1)} %get-tuple-element.4, f32[512]{0:T(512)S(1)} %get-tuple-element.3), channel_id=1, replica_groups=mesh['pipe'=4,'vocab'=64] {'pipe','vocab'}, use_global_device_ids=true, to_apply=%region_9.0 | all-reduce | flops 1536 | bytes 12288 | tf_op jit(solution)/shard_map/psum | solution.py:30
  432.5 9.6 %fusion.2 = f32[512,5120]{0,1:T(8,128)} fusion(bf16[384,5120]{1,0:T(8,128)(2,1)} %param.7, f32[512,384]{0,1:T(8,128)} %get-tuple-element.12, f32[512,384]{0,1:T(8,128)} %get-tuple-element.14, f32[512]{0:T(512)S(1)} %get-tuple-element.7, f32[512]{0:T(512)S(1)} %get-tuple-element.6, f32[512]{0:T(512)S(1)} %copy-done.1, f32[512]{0:T(512)S(1)} %get-tuple-element.10, ...), kind=kOutput, calls=%fused_computation.8 | convolution fusion | flops 2014642176 | bytes 16001024 | tf_op jit(solution)/shard_map/dot_general | solution.py:53
  442.2 0.0 reduce-scatter.5.cloned.1.call-start
  442.2 375.3 %reduce-scatter.3.cloned.1.call-done = f32[512,80]{0,1:T(8,128)} async-done(((f32[512,5120]{0,1:T(8,128)}), f32[512,80]{0,1:T(8,128)}) %reduce-scatter.3.cloned.1.call-update) | async-done | bytes 163856 | tf_op jit(solution)/shard_map/reduce_scatter | solution.py:54
  817.6 7.2 convolution_convert_fusion
  824.8 0.6 dynamic_slice.3
  825.4 46.2 %reduce-scatter.5.cloned.1.call-done = f32[128,80]{0,1:T(8,128)} async-done(((f32[512,80]{0,1:T(8,128)}), f32[128,80]{0,1:T(8,128)}) %reduce-scatter.5.cloned.1.call-update) | async-done | bytes 40976 | tf_op jit(solution)/shard_map/reduce_scatter | solution.py:55
  (7 shorter events, 0.1 us)
Async XLA Ops:
  7.2 206.4 %copy-start = (bf16[384,4096]{1,0:T(8,128)(2,1)S(1)}, bf16[384,4096]{1,0:T(8,128)(2,1)}, u32[]{:S(2)}) copy-start(bf16[384,4096]{1,0:T(8,128)(2,1)} %param.8) | copy-start | bytes 9437188
  7.2 82.7 %all-gather.5.cloned.1.call-start = ((), (), s32[]{:S(2)}) async-start(), calls=%async_computation.2 | async-start | bytes 1064960 | tf_op jit(solution)/shard_map/all_gather | solution.py:17
  7.9 158.3 %all-gather.9.cloned.1.call-start = ((), (), s32[]{:S(2)}) async-start(), calls=%async_computation.4 | async-start | bytes 1331200 | tf_op jit(solution)/shard_map/all_gather | solution.py:16
  8.7 204.9 %all-gather.7.cloned.1.call-start = ((), (), s32[]{:S(2)}) async-start(), calls=%async_computation.3 | async-start | bytes 5242880 | tf_op jit(solution)/shard_map/all_gather | solution.py:21
  89.9 183.6 %all-gather.11.cloned.1.call-start = ((), (), s32[]{:S(2)}) async-start(), calls=%async_computation.5 | async-start | bytes 6553600 | tf_op jit(solution)/shard_map/all_gather | solution.py:20
  166.3 651.3 %reduce-scatter.3.cloned.1.call-start = ((), (), s32[]{:S(2)}) async-start(), calls=%async_computation.6 | async-start | bytes 10649600 | tf_op jit(solution)/shard_map/reduce_scatter | solution.py:54
  218.4 214.1 %copy-start.1 = (f32[512]{0:T(512)S(1)}, f32[512]{0:T(512)}, u32[]{:S(2)}) copy-start(f32[512]{0:T(512)} %param.9) | copy-start | bytes 6148
  442.2 429.4 %reduce-scatter.5.cloned.1.call-start = ((), (), s32[]{:S(2)}) async-start(), calls=%async_computation.7 | async-start | bytes 204800 | tf_op jit(solution)/shard_map/reduce_scatter | solution.py:55
Sparse Core Ops, SparseCore 0:
  11.3 78.5 all-gather.4
  93.2 73.0 all-gather.8
  168.1 45.4 all-gather.6
  215.2 58.2 all-gather.10
  442.3 375.2 reduce-scatter.2
  820.5 51.0 reduce-scatter.4
where the time goes:
time: 880 us; the launch traced here: 878 us
  waiting for transfers between devices  683 us (78%)
  blocking collectives  151 us (17%)
  matrix products  28.5 us (3%)
  between operations  14.1 us (2%)
    reduce_scatter x1, waiting for transfers between devices, per_device(): lax.psum_scatter(whole_term, 'vocab', scatter_dimension=1, tiled=True)  375 us
    all_gather x1, waiting for transfers between devices, per_device(): lax.all_gather(teacher_hidden, 'vocab', axis=1, tiled=True)  81.2 us
    pmax x1, blocking collectives, per_device(): lax.pmax((local_smax, local_tmax), ('pipe', 'vocab'))  76.8 us
    all_gather x1, waiting for transfers between devices, per_device(): lax.all_gather(student_hidden, 'vocab', axis=1, tiled=True)  76.3 us
    psum x1, blocking collectives, per_device(): lax.psum((jnp.sum(student_exp, axis=1), jnp.sum(teacher_exp, axis=1), jnp...  73.7 us
    all_gather x1, waiting for transfers between devices, per_device(): lax.all_gather(wide_student, 'pipe', axis=0, tiled=True)  55.1 us
    all_gather x1, waiting for transfers between devices, per_device(): lax.all_gather(wide_teacher, 'pipe', axis=0, tiled=True)  47.2 us
    reduce_scatter x1, waiting for transfers between devices, per_device(): lax.psum_scatter(feature_part, 'pipe', scatter_dimension=0, tiled=True)  46.2 us
  transfers between devices with their start and end apart: 6, of which 6 were waited for; matrix products, arithmetic and copies ran while one was open for 1% of the time, Pallas kernels for 0%

commit v1 on v0

v1 whole, which is shorter than its diff:
```python
import jax
import jax.numpy as jnp
from jax import lax
from jax.experimental import pallas as pl
from jax.experimental.pallas import tpu as pltpu
from jax.sharding import PartitionSpec as P

DS, DT = 5120, 4096
ROWS = 384
TOK = 256
NS, NT = 320, 256
AXES = ("pipe", "vocab")
F32, BF16 = jnp.float32, jnp.bfloat16
VMEM_LIMIT = 48 * 1024 * 1024


def coords(i):
    p, v = divmod(i, 64)
    return p >> 1, p & 1, v >> 4, (v >> 2) & 3, v & 3


def index(zl, c, x, y, zh):
    return (zl * 2 + c) * 64 + x * 16 + y * 4 + zh


def perm(move):
    return [(i, index(*move(*coords(i)))) for i in range(256)]


PAIR = perm(lambda zl, c, x, y, zh: (1 - zl, c, x, y, zh))
CORE = perm(lambda zl, c, x, y, zh: (zl, 1 - c, x, y, zh))
ZH = {k: perm(lambda zl, c, x, y, zh, k=k: (zl, c, x, y, (zh + k) % 4)) for k in (1, 2, 3)}
FIRST = {
    k: perm(lambda zl, c, x, y, zh, k=k: (zl, c, (x + k * (1 - c)) % 4, (y + k * c) % 4, zh))
    for k in (1, 2, 3)
}
SECOND = {
    k: perm(lambda zl, c, x, y, zh, k=k: (zl, c, (x + k * c) % 4, (y + k * (1 - c)) % 4, zh))
    for k in (1, 2, 3)
}


def send(value, pairs):
    return lax.ppermute(value, AXES, pairs)


def ring(value, perms):
    got = {k: send(value, perms[k]) for k in (1, 3, 2)}
    return got[1], got[2], got[3]


def place():
    p, v = lax.axis_index("pipe"), lax.axis_index("vocab")
    return p >> 1, p & 1, v >> 4, (v >> 2) & 3, v & 3


def block_at(c, x, y, first, second):
    in_x = jnp.where(c == 0, first, second)
    in_y = jnp.where(c == 0, second, first)
    return ((x + in_x) & 3) * 4 + ((y + in_y) & 3)


def dot(a, b, dims):
    return lax.dot_general(a, b, (dims, ((), ())), preferred_element_type=F32)


def logits_kernel(
    t0, t1, t2, t3, ws, wso, wt, wto, es_ref, et_ref, st_ref, hs_out, hs, ht, wsb, wtb, hsem, wsem, osem
):
    _, c, x, y, _ = place()
    copies_t, copies_s = [], []
    for j, t in enumerate((t0, t1, t2, t3)):
        for i in range(4):
            at = block_at(c, x, y, (4 - i) & 3, (4 - j) & 3)
            n = (j * 4 + i) * 2
            copies_t.append(
                pltpu.make_async_copy(
                    t.at[i, pl.ds(NS, NT)],
                    ht.at[pl.ds(pl.multiple_of(at * NT, NT), NT)],
                    hsem.at[n],
                )
            )
            copies_s.append(
                pltpu.make_async_copy(
                    t.at[i, pl.ds(0, NS)],
                    hs.at[pl.ds(pl.multiple_of(at * NS, NS), NS)],
                    hsem.at[n + 1],
                )
            )
    weights = [
        pltpu.make_async_copy(src, dst.at[pl.ds(half * ROWS, ROWS)], wsem.at[n])
        for n, (src, dst, half) in enumerate(
            ((wt, wtb, 0), (wto, wtb, 1), (ws, wsb, 0), (wso, wsb, 1))
        )
    ]
    for copy in copies_t + weights[:2] + copies_s + weights[2:]:
        copy.start()
    for copy in copies_t:
        copy.wait()
    for half in range(2):
        weights[half].wait()
        rows = pl.ds(half * ROWS, ROWS)
        et_ref[rows] = dot(wtb[rows], ht[...], ((1,), (0,)))
    for copy in copies_s:
        copy.wait()
    out = pltpu.make_async_copy(hs, hs_out, osem)
    out.start()
    for half in range(2):
        weights[2 + half].wait()
        rows = pl.ds(half * ROWS, ROWS)
        es_ref[rows] = dot(wsb[rows], hs[...], ((1,), (0,)))
    s, t = es_ref[...], et_ref[...]
    sm = jnp.max(s, axis=0, keepdims=True)
    tm = jnp.max(t, axis=0, keepdims=True)
    es, et = jnp.exp(s - sm), jnp.exp(t - tm)
    st_ref[0:1] = sm
    st_ref[1:2] = tm
    st_ref[2:3] = jnp.sum(es, axis=0, keepdims=True)
    st_ref[3:4] = jnp.sum(et, axis=0, keepdims=True)
    st_ref[4:5] = jnp.sum(et * (t - s), axis=0, keepdims=True)
    st_ref[5:8] = jnp.zeros((3, TOK), F32)
    es_ref[...] = es
    et_ref[...] = et
    out.wait()


def logits_call(parts, ws, wso, wt, wto):
    hbm = pl.BlockSpec(memory_space=pl.ANY)
    vmem = pl.BlockSpec(memory_space=pltpu.VMEM)
    return pl.pallas_call(
        logits_kernel,
        out_shape=(
            jax.ShapeDtypeStruct((2 * ROWS, TOK), F32),
            jax.ShapeDtypeStruct((2 * ROWS, TOK), F32),
            jax.ShapeDtypeStruct((8, TOK), F32),
            jax.ShapeDtypeStruct((DS, TOK), BF16),
        ),
        in_specs=[hbm] * 8,
        out_specs=(vmem, vmem, vmem, hbm),
        scratch_shapes=[
            pltpu.VMEM((DS, TOK), BF16),
            pltpu.VMEM((DT, TOK), BF16),
            pltpu.VMEM((2 * ROWS, DS), BF16),
            pltpu.VMEM((2 * ROWS, DT), BF16),
            pltpu.SemaphoreType.DMA((32,)),
            pltpu.SemaphoreType.DMA((4,)),
            pltpu.SemaphoreType.DMA,
        ],
        compiler_params=pltpu.CompilerParams(vmem_limit_bytes=VMEM_LIMIT),
        cost_estimate=pl.CostEstimate(
            flops=2 * 2 * ROWS * TOK * (DS + DT), bytes_accessed=22_000_000, transcendentals=4 * ROWS * TOK
        ),
        name="logits",
    )(*parts, ws, wso, wt, wto)


CHUNK = 1280


def grads_kernel(
    es_ref, et_ref, coef_ref, ws, wso, g_own, g_oth, o0, o1, o2, o3, wsb, acc, accb, wsem, osem
):
    _, c, x, y, _ = place()
    weights = []
    for n in range(DS // CHUNK):
        for half, src in enumerate((ws, wso)):
            cols = pl.ds(n * CHUNK, CHUNK)
            weights.append(
                pltpu.make_async_copy(
                    src.at[:, cols], wsb.at[pl.ds(half * ROWS, ROWS), cols], wsem.at[2 * n + half]
                )
            )
    for copy in weights:
        copy.start()
    g = (es_ref[...] * coef_ref[0:1] - et_ref[...] * coef_ref[1:2]).astype(BF16)
    g_own[...] = g[:ROWS]
    g_oth[...] = g[ROWS:]
    for n in range(DS // CHUNK):
        weights[2 * n].wait()
        weights[2 * n + 1].wait()
        part = dot(wsb[:, n * CHUNK : (n + 1) * CHUNK], g, ((0,), (0,)))
        acc[n * CHUNK : (n + 1) * CHUNK] = part
        accb[n * CHUNK : (n + 1) * CHUNK] = part.astype(BF16)
    outs = []
    for k, o in ((1, o1), (3, o3), (2, o2), (0, o0)):
        for r in range(4):
            at = block_at(c, x, y, r, k)
            src = acc if k == 0 else accb
            outs.append(
                pltpu.make_async_copy(
                    src.at[pl.ds(pl.multiple_of(at * NS, NS), NS)], o.at[r], osem.at[k * 4 + r]
                )
            )
    for copy in outs:
        copy.start()
    for copy in outs:
        copy.wait()


def grads_call(es, et, coef, ws, wso):
    hbm = pl.BlockSpec(memory_space=pl.ANY)
    vmem = pl.BlockSpec(memory_space=pltpu.VMEM)
    piece = (4, NS, TOK)
    return pl.pallas_call(
        grads_kernel,
        out_shape=(
            jax.ShapeDtypeStruct((ROWS, TOK), BF16),
            jax.ShapeDtypeStruct((ROWS, TOK), BF16),
            jax.ShapeDtypeStruct(piece, F32),
            jax.ShapeDtypeStruct(piece, BF16),
            jax.ShapeDtypeStruct(piece, BF16),
            jax.ShapeDtypeStruct(piece, BF16),
        ),
        in_specs=[vmem, vmem, vmem, hbm, hbm],
        out_specs=(vmem, vmem, hbm, hbm, hbm, hbm),
        scratch_shapes=[
            pltpu.VMEM((2 * ROWS, DS), BF16),
            pltpu.VMEM((DS, TOK), F32),
            pltpu.VMEM((DS, TOK), BF16),
            pltpu.SemaphoreType.DMA((8,)),
            pltpu.SemaphoreType.DMA((16,)),
        ],
        compiler_params=pltpu.CompilerParams(vmem_limit_bytes=VMEM_LIMIT),
        cost_estimate=pl.CostEstimate(
            flops=2 * 2 * ROWS * TOK * DS, bytes_accessed=14_000_000, transcendentals=0
        ),
        name="grads",
    )(es, et, coef, ws, wso)


def head_kernel(g_own, g_got, h_own, h_got, out):
    out[...] = (
        dot(g_own[...], h_own[...], ((1,), (1,))) + dot(g_got[...], h_got[...], ((1,), (1,)))
    ).astype(BF16)


def head_call(g_own, g_got, h_own, h_got):
    step = 640
    whole = pl.BlockSpec((ROWS, TOK), lambda i: (0, 0))
    some = pl.BlockSpec((step, TOK), lambda i: (i, 0))
    return pl.pallas_call(
        head_kernel,
        out_shape=jax.ShapeDtypeStruct((ROWS, DS), BF16),
        grid=(DS // step,),
        in_specs=[whole, whole, some, some],
        out_specs=pl.BlockSpec((ROWS, step), lambda i: (0, i)),
        compiler_params=pltpu.CompilerParams(vmem_limit_bytes=VMEM_LIMIT),
        cost_estimate=pl.CostEstimate(
            flops=2 * 2 * ROWS * TOK * DS, bytes_accessed=10_000_000, transcendentals=0
        ),
        name="head",
    )(g_own, g_got, h_own, h_got)


def merge(stats):
    top = stats[0][0:2]
    for s in stats[1:]:
        top = jnp.maximum(top, s[0:2])
    total = jnp.zeros_like(stats[0][2:5])
    for s in stats:
        scale = jnp.exp(s[0:2] - top)
        total = total + s[2:5] * jnp.concatenate([scale, scale[1:2]], axis=0)
    return jnp.concatenate([top, total, stats[0][5:8]], axis=0)


def per_device(student_hidden, teacher_hidden, student_head, teacher_head, row_weight):
    zl, c, x, y, zh = place()

    teacher_other = send(teacher_head, CORE)
    student_other = send(student_head, CORE)

    mine = jnp.concatenate([student_hidden.T, teacher_hidden.T], axis=0)
    pair = send(mine, PAIR)
    both = jnp.concatenate(
        [jnp.where(zl == 0, mine, pair), jnp.where(zl == 0, pair, mine)], axis=1
    )
    around = (both,) + ring(both, ZH)
    ordered = [lax.select_n((zh - q) & 3, *around) for q in range(4)]
    block = jnp.concatenate([o[:80] for o in ordered] + [o[80:] for o in ordered], axis=0)
    line = jnp.stack((block,) + ring(block, FIRST))
    parts = (line,) + ring(line, SECOND)

    es, et, local, hidden_own = logits_call(
        parts, student_head, student_other, teacher_head, teacher_other
    )
    hidden_got = send(hidden_own, CORE)

    stats = merge((local, send(local, PAIR)))
    for perms in (ZH, FIRST, SECOND):
        stats = merge((stats,) + ring(stats, perms))
    student_max, teacher_max, student_total, teacher_total, cross = (stats[i] for i in range(5))
    kl_both = (
        cross / teacher_total
        - teacher_max
        - jnp.log(teacher_total)
        + student_max
        + jnp.log(student_total)
    )
    kl_rows = lax.dynamic_slice_in_dim(kl_both, zl * 128, 128, 0)
    weight = lax.dynamic_index_in_dim(row_weight.reshape(2, 2, 128), c, 1, False).reshape(TOK)
    coef = jnp.stack(
        [
            weight * (jnp.exp(local[0] - student_max) / student_total),
            weight * (jnp.exp(local[1] - teacher_max) / teacher_total),
        ]
    )
    coef = jnp.concatenate([coef, jnp.zeros((6, TOK), F32)], axis=0)

    g_own, g_oth, o0, o1, o2, o3 = grads_call(es, et, coef, student_head, student_other)
    g_got = send(g_oth, CORE)
    r1, r3, r2 = send(o1, SECOND[1]), send(o3, SECOND[3]), send(o2, SECOND[2])
    head_grad = head_call(g_own, g_got, hidden_own, hidden_got)

    sums = o0 + (r1.astype(F32) + r3.astype(F32)) + r2.astype(F32)
    r1, r3, r2 = (send(sums[k].astype(BF16), FIRST[k]) for k in (1, 3, 2))
    sums = (sums[0] + (r1.astype(F32) + r3.astype(F32)) + r2.astype(F32)).reshape(4, 80, TOK)
    narrow = sums.astype(BF16)
    r1, r3, r2 = (
        send(lax.dynamic_index_in_dim(narrow, (zh + k) & 3, 0, False), ZH[k]) for k in (1, 3, 2)
    )
    sums = lax.dynamic_index_in_dim(sums, zh, 0, False) + (r1.astype(F32) + r3.astype(F32)) + r2.astype(F32)
    low, high = sums[:, :128], sums[:, 128:]
    got = send(jnp.where(zl == 0, high, low), PAIR)
    hidden_grad = (jnp.where(zl == 0, low, high) + got).T
    return (kl_rows, hidden_grad, head_grad)


def solution(mesh):
    placed = (
        P("pipe", "vocab"),
        P("pipe", "vocab"),
        P(("pipe", "vocab"), None),
        P(("pipe", "vocab"), None),
        P(),
    )
    return jax.shard_map(
        per_device,
        mesh=mesh,
        in_specs=placed,
        out_specs=(P("pipe"), P("pipe", "vocab"), P(("pipe", "vocab"), None)),
        check_vma=False,
    )
```

time: 880 us -> 200 us (0.23)
  waiting for transfers between devices: 683 us -> 85.2 us
  blocking collectives: 151 us -> 0 us
  starting transfers between devices: 0.23 us -> 68.2 us
  Pallas kernels: 0 us -> 31.1 us
  matrix products: 28.5 us -> 0 us
  between operations: 14.1 us -> 1.08 us
    reduce_scatter x2 -> x0, waiting for transfers between devices: 422 us -> none  [the longest x1 375 us: per_device(): lax.psum_scatter(whole_term, 'vocab', scatter_dimension=1, tiled=True)]
    all_gather x4 -> x0, waiting for transfers between devices: 260 us -> none  [the longest x1 81.2 us: per_device(): lax.all_gather(teacher_hidden, 'vocab', axis=1, tiled=True)]
    ppermute x0 -> x34, waiting for transfers between devices: none -> 85.2 us  [send(): return lax.ppermute(value, AXES, pairs)]
    pmax x1 -> x0, blocking collectives: 76.8 us -> none  [per_device(): lax.pmax((local_smax, local_tmax), ('pipe', 'vocab'))]
    psum x1 -> x0, blocking collectives: 73.7 us -> none  [per_device(): lax.psum((jnp.sum(student_exp, axis=1), jnp.sum(teacher_exp, axis=1), jnp...]
    ppermute x0 -> x34, starting transfers between devices: none -> 68.2 us  [send(): return lax.ppermute(value, AXES, pairs)]
    pallas_call x0 -> x3, Pallas kernels: none -> 31.1 us  [the longest x1 13.4 us: logits_call(): pl.pallas_call(logits_kernel, out_shape=(jax.ShapeDtypeStruct((2 * ROWS,...]
    dot_general x4 -> x0, matrix products: 28.5 us -> none  [the longest x2 11.7 us: dot_rows(): lax.dot_general(left, right, (((1,), (1,)), ((), ())), preferred_element_...]
  transfers between devices with their start and end apart: 6 -> 34, of which waited for: 6 -> 22; matrix products, arithmetic and copies ran while one was open for 1% -> 3% of each run, Pallas kernels for 0% -> 0%
where the time goes in v1:
time: 200 us; the launch traced here: 198 us
  waiting for transfers between devices  85.2 us (43%)
  starting transfers between devices  68.2 us (34%)
  Pallas kernels  31.1 us (16%)
  other arithmetic  6.76 us (3%)
  local copies, waits for them, and re-layouts  5.78 us (3%)
    ppermute x34, waiting for transfers between devices, send(): return lax.ppermute(value, AXES, pairs)  85.2 us
    ppermute x34, starting transfers between devices, send(): return lax.ppermute(value, AXES, pairs)  68.2 us
    pallas_call x1, Pallas kernels, logits_call(): pl.pallas_call(logits_kernel, out_shape=(jax.ShapeDtypeStruct((2 * ROWS,...  13.4 us
    pallas_call x1, Pallas kernels, grads_call(): pl.pallas_call(grads_kernel, out_shape=(jax.ShapeDtypeStruct((ROWS, TOK),...  9.87 us
    pallas_call x1, Pallas kernels, head_call(): pl.pallas_call(head_kernel, out_shape=jax.ShapeDtypeStruct((ROWS, DS), BF...  7.87 us
    unnamed x33, local copies, waits for them, and re-layouts  4.13 us
  transfers between devices with their start and end apart: 34, of which 22 were waited for; matrix products, arithmetic and copies ran while one was open for 3% of the time, Pallas kernels for 0%

profile of v1, /device:TPU:2, one launch (start us, length us, event | category | flops | bytes accessed | tf_op | source)
XLA Modules:
  0.0 198.2 jit_solution(9707802796496393303)
XLA Ops:
  6.1 3.3 %collective-permute-start.1 = (bf16[144,256]{1,0:T(8,128)(2,1)S(1)}, bf16[144,256]{1,0:T(8,128)(2,1)S(1)}, u32[]{:S(2)}, u32[]{:S(2)}) collective-permute-start(bf16[144,256]{1,0:T(8,128)(2,1)S(1)} %pad_maximum_fusion.1), channel_id=1, source_target_pairs={{0,1},{1,2},{2,3},{3,0},{4,5},{5,6},{6,7},{7,4},{8,9},{9,10},{10,1... | collective-permute-start | bytes 221192 | tf_op jit(solution)/shard_map/ppermute | solution.py:44
  9.5 5.4 %collective-permute-start.2 = (bf16[144,256]{1,0:T(8,128)(2,1)S(1)}, bf16[144,256]{1,0:T(8,128)(2,1)S(1)}, u32[]{:S(2)}, u32[]{:S(2)}) collective-permute-start(bf16[144,256]{1,0:T(8,128)(2,1)S(1)} %pad_maximum_fusion.1), channel_id=1, source_target_pairs={{0,2},{1,3},{2,0},{3,1},{4,6},{5,7},{6,4},{7,5},{8,10},{9,11},{10,... | collective-permute-start | bytes 221192 | tf_op jit(solution)/shard_map/ppermute | solution.py:44
  14.9 2.7 %collective-permute-start.3 = (bf16[144,256]{1,0:T(8,128)(2,1)S(1)}, bf16[144,256]{1,0:T(8,128)(2,1)S(1)}, u32[]{:S(2)}, u32[]{:S(2)}) collective-permute-start(bf16[144,256]{1,0:T(8,128)(2,1)S(1)} %pad_maximum_fusion.1), channel_id=1, source_target_pairs={{0,3},{1,0},{2,1},{3,2},{4,7},{5,4},{6,5},{7,6},{8,11},{9,8},{10,9... | collective-permute-start | bytes 221192 | tf_op jit(solution)/shard_map/ppermute | solution.py:44
  28.7 3.1 %collective-permute-done.5 = bf16[576,256]{1,0:T(8,128)(2,1)S(1)} collective-permute-done((bf16[576,256]{1,0:T(8,128)(2,1)S(1)}, bf16[576,256]{1,0:T(8,128)(2,1)S(1)}, u32[]{:S(2)}, u32[]{:S(2)}) %collective-permute-start.5) | collective-permute-done | bytes 294944 | tf_op jit(solution)/shard_map/ppermute | solution.py:44
  31.8 2.7 %collective-permute-done.6 = bf16[576,256]{1,0:T(8,128)(2,1)S(1)} collective-permute-done((bf16[576,256]{1,0:T(8,128)(2,1)S(1)}, bf16[576,256]{1,0:T(8,128)(2,1)S(1)}, u32[]{:S(2)}, u32[]{:S(2)}) %collective-permute-start.6) | collective-permute-done | bytes 294944 | tf_op jit(solution)/shard_map/ppermute | solution.py:44
  36.3 3.8 %collective-permute-start.8 = (bf16[4,576,256]{2,1,0:T(8,128)(2,1)S(1)}, bf16[4,576,256]{2,1,0:T(8,128)(2,1)S(1)}, u32[]{:S(2)}, u32[]{:S(2)}) collective-permute-start(bf16[4,576,256]{2,1,0:T(8,128)(2,1)S(1)} %pad_maximum_fusion.t0), channel_id=1, source_target_pairs={{0,8},{1,9},{2,10},{3,11},{4,12},{5,13},{6,14},{7,15},{8,0},{9,1},... | collective-permute-start | bytes 3538952 | tf_op jit(solution)/shard_map/ppermute | solution.py:44
  40.8 12.0 %collective-permute-done.7.t1 = bf16[4,576,256]{2,1,0:T(8,128)(2,1)S(1)} collective-permute-done((bf16[4,576,256]{2,1,0:T(8,128)(2,1)S(1)}, bf16[4,576,256]{2,1,0:T(8,128)(2,1)S(1)}, u32[]{:S(2)}, u32[]{:S(2)}) %collective-permute-start.7) | collective-permute-done | bytes 1179680 | tf_op jit(solution)/shard_map/ppermute | solution.py:44
  52.8 14.1 %collective-permute-done.8.t2 = bf16[4,576,256]{2,1,0:T(8,128)(2,1)S(1)} collective-permute-done((bf16[4,576,256]{2,1,0:T(8,128)(2,1)S(1)}, bf16[4,576,256]{2,1,0:T(8,128)(2,1)S(1)}, u32[]{:S(2)}, u32[]{:S(2)}) %collective-permute-start.8) | collective-permute-done | bytes 1179680 | tf_op jit(solution)/shard_map/ppermute | solution.py:44
  69.0 13.4 %logits.1 = (f32[768,256]{1,0:T(8,128)S(1)}, f32[768,256]{1,0:T(8,128)S(1)}, f32[8,256]{1,0:T(8,128)S(1)}, bf16[5120,256]{1,0:T(8,128)(2,1)}) custom-call(bf16[4,576,256]{2,1,0:T(8,128)(2,1)S(1)} %pad_maximum_fusion.t0, bf16[4,576,256]{2,1,0:T(8,128)(2,1)S(1)} %collective-permute-done.7.t1, bf16[4,576,256]{2,1,0:T(8,128)(2,1)S(1)} %collective-permute-done.8.t2, ...), custom_call_target="tpu_custom_call" | custom-call | flops 3623878656 | bytes 22000000 | tf_op jit(solution)/shard_map/logits/pallas_call | solution.py:130
  83.3 3.6 %collective-permute-done.12 = f32[8,256]{1,0:T(8,128)S(1)} collective-permute-done((f32[8,256]{1,0:T(8,128)S(1)}, f32[8,256]{1,0:T(8,128)S(1)}, u32[]{:S(2)}, u32[]{:S(2)}) %collective-permute-start.12) | collective-permute-done | bytes 8224 | tf_op jit(solution)/shard_map/ppermute | solution.py:44
  87.0 15.1 %collective-permute-start.13 = (f32[8,256]{1,0:T(8,128)S(1)}, f32[8,256]{1,0:T(8,128)S(1)}, u32[]{:S(2)}, u32[]{:S(2)}) collective-permute-start(f32[8,256]{1,0:T(8,128)S(1)} %pad_maximum_fusion.5), channel_id=1, source_target_pairs={{0,1},{1,2},{2,3},{3,0},{4,5},{5,6},{6,7},{7,4},{8,9},{9,10},{10,1... | collective-permute-start | bytes 24584 | tf_op jit(solution)/shard_map/ppermute | solution.py:44
  102.1 3.9 %collective-permute-start.15 = (f32[8,256]{1,0:T(8,128)S(1)}, f32[8,256]{1,0:T(8,128)S(1)}, u32[]{:S(2)}, u32[]{:S(2)}) collective-permute-start(f32[8,256]{1,0:T(8,128)S(1)} %pad_maximum_fusion.5), channel_id=1, source_target_pairs={{0,3},{1,0},{2,1},{3,2},{4,7},{5,4},{6,5},{7,6},{8,11},{9,8},{10,9... | collective-permute-start | bytes 24584 | tf_op jit(solution)/shard_map/ppermute | solution.py:44
  106.1 3.6 %collective-permute-done.14 = f32[8,256]{1,0:T(8,128)S(1)} collective-permute-done((f32[8,256]{1,0:T(8,128)S(1)}, f32[8,256]{1,0:T(8,128)S(1)}, u32[]{:S(2)}, u32[]{:S(2)}) %collective-permute-start.14) | collective-permute-done | bytes 8224 | tf_op jit(solution)/shard_map/ppermute | solution.py:44
  124.0 9.9 %grads.1 = (bf16[384,256]{1,0:T(8,128)(2,1)S(1)}, bf16[384,256]{1,0:T(8,128)(2,1)S(1)}, f32[4,320,256]{2,1,0:T(8,128)S(1)}, bf16[4,320,256]{2,1,0:T(8,128)(2,1)S...) custom-call(f32[768,256]{1,0:T(8,128)S(1)} %get-tuple-element.14.es_ref, ...), custom_call_target="tpu_custom_call" | custom-call | flops 2013265920 | bytes 14000000 | tf_op jit(solution)/shard_map/grads/pallas_call | solution.py:204
  134.5 2.7 %collective-permute-start.23 = (bf16[4,320,256]{2,1,0:T(8,128)(2,1)S(1)}, bf16[4,320,256]{2,1,0:T(8,128)(2,1)S(1)}, u32[]{:S(2)}, u32[]{:S(2)}) collective-permute-start(bf16[4,320,256]{2,1,0:T(8,128)(2,1)S(1)} %get-tuple-element.18), channel_id=1, source_target_pairs={{0,12},{1,13},{2,14},{3,15},{4,0},{5,1},{6,2},{7,3},{8,4},{9,5},{1... | collective-permute-start | bytes 1966088 | tf_op jit(solution)/shard_map/ppermute | solution.py:44
  138.4 8.0 %collective-permute-done.22 = bf16[4,320,256]{2,1,0:T(8,128)(2,1)S(1)} collective-permute-done((bf16[4,320,256]{2,1,0:T(8,128)(2,1)S(1)}, bf16[4,320,256]{2,1,0:T(8,128)(2,1)S(1)}, u32[]{:S(2)}, u32[]{:S(2)}) %collective-permute-start.22) | collective-permute-done | bytes 655392 | tf_op jit(solution)/shard_map/ppermute | solution.py:44
  147.9 9.6 %collective-permute-done.24 = bf16[4,320,256]{2,1,0:T(8,128)(2,1)S(1)} collective-permute-done((bf16[4,320,256]{2,1,0:T(8,128)(2,1)S(1)}, bf16[4,320,256]{2,1,0:T(8,128)(2,1)S(1)}, u32[]{:S(2)}, u32[]{:S(2)}) %collective-permute-start.24) | collective-permute-done | bytes 655392 | tf_op jit(solution)/shard_map/ppermute | solution.py:44
  161.6 3.2 %collective-permute-start.27 = (bf16[320,256]{1,0:T(8,128)(2,1)}, bf16[320,256]{1,0:T(8,128)(2,1)}, u32[]{:S(2)}, u32[]{:S(2)}) collective-permute-start(bf16[320,256]{1,0:T(8,128)(2,1)} %get-tuple-element.34), channel_id=1, source_target_pairs={{0,32},{1,33},{2,34},{3,35},{4,36},{5,37},{6,38},{7,39},{8,40},{9,... | collective-permute-start | bytes 491528 | tf_op jit(solution)/shard_map/ppermute | solution.py:44
  166.9 3.2 %collective-permute-done.27 = bf16[320,256]{1,0:T(8,128)(2,1)} collective-permute-done((bf16[320,256]{1,0:T(8,128)(2,1)}, bf16[320,256]{1,0:T(8,128)(2,1)}, u32[]{:S(2)}, u32[]{:S(2)}) %collective-permute-start.27) | collective-permute-done | bytes 163872 | tf_op jit(solution)/shard_map/ppermute | solution.py:44
  172.7 3.6 %collective-permute-start.29 = (bf16[80,256]{1,0:T(8,128)(2,1)}, bf16[80,256]{1,0:T(8,128)(2,1)S(1)}, u32[]{:S(2)}, u32[]{:S(2)}) collective-permute-start(bf16[80,256]{1,0:T(8,128)(2,1)} %get-tuple-element.41), channel_id=1, source_target_pairs={{0,3},{1,0},{2,1},{3,2},{4,7},{5,4},{6,5},{7,6},{8,11},{9,8},{10,9... | collective-permute-start | bytes 122888 | tf_op jit(solution)/shard_map/ppermute | solution.py:44
  176.3 2.9 %collective-permute-start.30 = (bf16[80,256]{1,0:T(8,128)(2,1)S(1)}, bf16[80,256]{1,0:T(8,128)(2,1)S(1)}, u32[]{:S(2)}, u32[]{:S(2)}) collective-permute-start(bf16[80,256]{1,0:T(8,128)(2,1)S(1)} %get-tuple-element.40), channel_id=1, source_target_pairs={{0,2},{1,3},{2,0},{3,1},{4,6},{5,7},{6,4},{7,5},{8,10},{9,11},{10,... | collective-permute-start | bytes 122888 | tf_op jit(solution)/shard_map/ppermute | solution.py:44
  179.2 5.5 %collective-permute-done.30 = bf16[80,256]{1,0:T(8,128)(2,1)S(1)} collective-permute-done((bf16[80,256]{1,0:T(8,128)(2,1)S(1)}, bf16[80,256]{1,0:T(8,128)(2,1)S(1)}, u32[]{:S(2)}, u32[]{:S(2)}) %collective-permute-start.30) | collective-permute-done | bytes 40992 | tf_op jit(solution)/shard_map/ppermute | solution.py:44
  186.3 3.5 %collective-permute-done.31 = f32[80,128]{1,0:T(8,128)S(1)} collective-permute-done((f32[80,128]{1,0:T(8,128)S(1)}, f32[80,128]{1,0:T(8,128)S(1)}, u32[]{:S(2)}, u32[]{:S(2)}) %collective-permute-start.31) | collective-permute-done | bytes 40992 | tf_op jit(solution)/shard_map/ppermute | solution.py:44
  190.3 7.9 %head.1 = bf16[384,5120]{1,0:T(8,128)(2,1)} custom-call(bf16[384,256]{1,0:T(8,128)(2,1)S(1)} %copy-done.4, bf16[384,256]{1,0:T(8,128)(2,1)S(1)} %collective-permute-done.32.g_got, bf16[5120,256]{1,0:T(8,128)(2,1)S(1)} %copy-done, bf16[5120,256]{1,0:T(8,128)(2,1)} %collective-permute-done.33.h_got), custom_call_target="tpu_custom_call" | custom-call | flops 2013265920 | bytes 10000000 | tf_op jit(solution)/shard_map/head/pallas_call | solution.py:241
  (129 shorter events, 50.5 us)
Async XLA Ops:
  6.1 11.9 %collective-permute-start.1 = (bf16[144,256]{1,0:T(8,128)(2,1)S(1)}, bf16[144,256]{1,0:T(8,128)(2,1)S(1)}, u32[]{:S(2)}, u32[]{:S(2)}) collective-permute-start(bf16[144,256]{1,0:T(8,128)(2,1)S(1)} %pad_maximum_fusion.1), channel_id=1, source_target_pairs={{0,1},{1,2},{2,3},{3,0},{4,5},{5,6},{6,7},{7,4},{8,9},{9,10},{10,1... | collective-permute-start | bytes 221192 | tf_op jit(solution)/shard_map/ppermute | solution.py:44
  9.5 9.9 %collective-permute-start.2 = (bf16[144,256]{1,0:T(8,128)(2,1)S(1)}, bf16[144,256]{1,0:T(8,128)(2,1)S(1)}, u32[]{:S(2)}, u32[]{:S(2)}) collective-permute-start(bf16[144,256]{1,0:T(8,128)(2,1)S(1)} %pad_maximum_fusion.1), channel_id=1, source_target_pairs={{0,2},{1,3},{2,0},{3,1},{4,6},{5,7},{6,4},{7,5},{8,10},{9,11},{10,... | collective-permute-start | bytes 221192 | tf_op jit(solution)/shard_map/ppermute | solution.py:44
  14.9 6.8 %collective-permute-start.3 = (bf16[144,256]{1,0:T(8,128)(2,1)S(1)}, bf16[144,256]{1,0:T(8,128)(2,1)S(1)}, u32[]{:S(2)}, u32[]{:S(2)}) collective-permute-start(bf16[144,256]{1,0:T(8,128)(2,1)S(1)} %pad_maximum_fusion.1), channel_id=1, source_target_pairs={{0,3},{1,0},{2,1},{3,2},{4,7},{5,4},{6,5},{7,6},{8,11},{9,8},{10,9... | collective-permute-start | bytes 221192 | tf_op jit(solution)/shard_map/ppermute | solution.py:44
  17.5 51.1 %collective-permute-start.10 = (bf16[384,5120]{1,0:T(8,128)(2,1)}, bf16[384,5120]{1,0:T(8,128)(2,1)}, u32[]{:S(2)}, u32[]{:S(2)}) collective-permute-start(bf16[384,5120]{1,0:T(8,128)(2,1)} %ws.3), channel_id=1, source_target_pairs={{0,64},{1,65},{2,66},{3,67},{4,68},{5,69},{6,70},{7,71},{8,72},{9,... | collective-permute-start | bytes 11796488 | tf_op jit(solution)/shard_map/ppermute | solution.py:44
  17.5 49.4 %collective-permute-start.11 = (bf16[384,4096]{1,0:T(8,128)(2,1)}, bf16[384,4096]{1,0:T(8,128)(2,1)S(1)}, u32[]{:S(2)}, u32[]{:S(2)}) collective-permute-start(bf16[384,4096]{1,0:T(8,128)(2,1)} %wt.1), channel_id=1, source_target_pairs={{0,64},{1,65},{2,66},{3,67},{4,68},{5,69},{6,70},{7,71},{8,72},{9,... | collective-permute-start | bytes 9437192 | tf_op jit(solution)/shard_map/ppermute | solution.py:44
  21.9 6.8 %collective-permute-start.4 = (bf16[576,256]{1,0:T(8,128)(2,1)S(1)}, bf16[576,256]{1,0:T(8,128)(2,1)S(1)}, u32[]{:S(2)}, u32[]{:S(2)}) collective-permute-start(bf16[576,256]{1,0:T(8,128)(2,1)S(1)} %slice_dynamic-update-slice_fusion.4), channel_id=1, source_target_pairs={{0,16},{1,17},{2,18},{3,19},{4,20},{5,21},{6,22},{7,23},{8,24},{9,... | collective-permute-start | bytes 884744 | tf_op jit(solution)/shard_map/ppermute | solution.py:44
  23.5 8.3 %collective-permute-start.5 = (bf16[576,256]{1,0:T(8,128)(2,1)S(1)}, bf16[576,256]{1,0:T(8,128)(2,1)S(1)}, u32[]{:S(2)}, u32[]{:S(2)}) collective-permute-start(bf16[576,256]{1,0:T(8,128)(2,1)S(1)} %slice_dynamic-update-slice_fusion.4), channel_id=1, source_target_pairs={{0,32},{1,33},{2,34},{3,35},{4,36},{5,37},{6,38},{7,39},{8,40},{9,... | collective-permute-start | bytes 884744 | tf_op jit(solution)/shard_map/ppermute | solution.py:44
  24.6 9.9 %collective-permute-start.6 = (bf16[576,256]{1,0:T(8,128)(2,1)S(1)}, bf16[576,256]{1,0:T(8,128)(2,1)S(1)}, u32[]{:S(2)}, u32[]{:S(2)}) collective-permute-start(bf16[576,256]{1,0:T(8,128)(2,1)S(1)} %slice_dynamic-update-slice_fusion.4), channel_id=1, source_target_pairs={{0,48},{1,49},{2,50},{3,51},{4,52},{5,53},{6,54},{7,55},{8,56},{9,... | collective-permute-start | bytes 884744 | tf_op jit(solution)/shard_map/ppermute | solution.py:44
  34.6 18.2 %collective-permute-start.7 = (bf16[4,576,256]{2,1,0:T(8,128)(2,1)S(1)}, bf16[4,576,256]{2,1,0:T(8,128)(2,1)S(1)}, u32[]{:S(2)}, u32[]{:S(2)}) collective-permute-start(bf16[4,576,256]{2,1,0:T(8,128)(2,1)S(1)} %pad_maximum_fusion.t0), channel_id=1, source_target_pairs={{0,4},{1,5},{2,6},{3,7},{4,8},{5,9},{6,10},{7,11},{8,12},{9,13},{1... | collective-permute-start | bytes 3538952 | tf_op jit(solution)/shard_map/ppermute | solution.py:44
  36.3 30.6 %collective-permute-start.8 = (bf16[4,576,256]{2,1,0:T(8,128)(2,1)S(1)}, bf16[4,576,256]{2,1,0:T(8,128)(2,1)S(1)}, u32[]{:S(2)}, u32[]{:S(2)}) collective-permute-start(bf16[4,576,256]{2,1,0:T(8,128)(2,1)S(1)} %pad_maximum_fusion.t0), channel_id=1, source_target_pairs={{0,8},{1,9},{2,10},{3,11},{4,12},{5,13},{6,14},{7,15},{8,0},{9,1},... | collective-permute-start | bytes 3538952 | tf_op jit(solution)/shard_map/ppermute | solution.py:44
  40.1 26.8 %collective-permute-start.9 = (bf16[4,576,256]{2,1,0:T(8,128)(2,1)S(1)}, bf16[4,576,256]{2,1,0:T(8,128)(2,1)S(1)}, u32[]{:S(2)}, u32[]{:S(2)}) collective-permute-start(bf16[4,576,256]{2,1,0:T(8,128)(2,1)S(1)} %pad_maximum_fusion.t0), channel_id=1, source_target_pairs={{0,12},{1,13},{2,14},{3,15},{4,0},{5,1},{6,2},{7,3},{8,4},{9,5},{1... | collective-permute-start | bytes 3538952 | tf_op jit(solution)/shard_map/ppermute | solution.py:44
  87.0 19.1 %collective-permute-start.13 = (f32[8,256]{1,0:T(8,128)S(1)}, f32[8,256]{1,0:T(8,128)S(1)}, u32[]{:S(2)}, u32[]{:S(2)}) collective-permute-start(f32[8,256]{1,0:T(8,128)S(1)} %pad_maximum_fusion.5), channel_id=1, source_target_pairs={{0,1},{1,2},{2,3},{3,0},{4,5},{5,6},{6,7},{7,4},{8,9},{9,10},{10,1... | collective-permute-start | bytes 24584 | tf_op jit(solution)/shard_map/ppermute | solution.py:44
  102.1 7.6 %collective-permute-start.14 = (f32[8,256]{1,0:T(8,128)S(1)}, f32[8,256]{1,0:T(8,128)S(1)}, u32[]{:S(2)}, u32[]{:S(2)}) collective-permute-start(f32[8,256]{1,0:T(8,128)S(1)} %pad_maximum_fusion.5), channel_id=1, source_target_pairs={{0,2},{1,3},{2,0},{3,1},{4,6},{5,7},{6,4},{7,5},{8,10},{9,11},{10,... | collective-permute-start | bytes 24584 | tf_op jit(solution)/shard_map/ppermute | solution.py:44
  102.1 7.6 %collective-permute-start.15 = (f32[8,256]{1,0:T(8,128)S(1)}, f32[8,256]{1,0:T(8,128)S(1)}, u32[]{:S(2)}, u32[]{:S(2)}) collective-permute-start(f32[8,256]{1,0:T(8,128)S(1)} %pad_maximum_fusion.5), channel_id=1, source_target_pairs={{0,3},{1,0},{2,1},{3,2},{4,7},{5,4},{6,5},{7,6},{8,11},{9,8},{10,9... | collective-permute-start | bytes 24584 | tf_op jit(solution)/shard_map/ppermute | solution.py:44
  133.9 12.5 %collective-permute-start.22 = (bf16[4,320,256]{2,1,0:T(8,128)(2,1)S(1)}, bf16[4,320,256]{2,1,0:T(8,128)(2,1)S(1)}, u32[]{:S(2)}, u32[]{:S(2)}) collective-permute-start(bf16[4,320,256]{2,1,0:T(8,128)(2,1)S(1)} %get-tuple-element.17), channel_id=1, source_target_pairs={{0,4},{1,5},{2,6},{3,7},{4,8},{5,9},{6,10},{7,11},{8,12},{9,13},{1... | collective-permute-start | bytes 1966088 | tf_op jit(solution)/shard_map/ppermute | solution.py:44
  134.5 13.3 %collective-permute-start.23 = (bf16[4,320,256]{2,1,0:T(8,128)(2,1)S(1)}, bf16[4,320,256]{2,1,0:T(8,128)(2,1)S(1)}, u32[]{:S(2)}, u32[]{:S(2)}) collective-permute-start(bf16[4,320,256]{2,1,0:T(8,128)(2,1)S(1)} %get-tuple-element.18), channel_id=1, source_target_pairs={{0,12},{1,13},{2,14},{3,15},{4,0},{5,1},{6,2},{7,3},{8,4},{9,5},{1... | collective-permute-start | bytes 1966088 | tf_op jit(solution)/shard_map/ppermute | solution.py:44
  137.2 20.3 %collective-permute-start.24 = (bf16[4,320,256]{2,1,0:T(8,128)(2,1)S(1)}, bf16[4,320,256]{2,1,0:T(8,128)(2,1)S(1)}, u32[]{:S(2)}, u32[]{:S(2)}) collective-permute-start(bf16[4,320,256]{2,1,0:T(8,128)(2,1)S(1)} %get-tuple-element.19), channel_id=1, source_target_pairs={{0,8},{1,9},{2,10},{3,11},{4,12},{5,13},{6,14},{7,15},{8,0},{9,1},... | collective-permute-start | bytes 1966088 | tf_op jit(solution)/shard_map/ppermute | solution.py:44
  138.4 52.0 %collective-permute-start.33 = (bf16[5120,256]{1,0:T(8,128)(2,1)S(1)}, bf16[5120,256]{1,0:T(8,128)(2,1)}, u32[]{:S(2)}, u32[]{:S(2)}) collective-permute-start(bf16[5120,256]{1,0:T(8,128)(2,1)S(1)} %copy-done), channel_id=1, source_target_pairs={{0,64},{1,65},{2,66},{3,67},{4,68},{5,69},{6,70},{7,71},{8,72},{9,... | collective-permute-start | bytes 7864328 | tf_op jit(solution)/shard_map/ppermute | solution.py:44
  159.6 5.5 %collective-permute-start.25 = (bf16[320,256]{1,0:T(8,128)(2,1)}, bf16[320,256]{1,0:T(8,128)(2,1)S(1)}, u32[]{:S(2)}, u32[]{:S(2)}) collective-permute-start(bf16[320,256]{1,0:T(8,128)(2,1)} %get-tuple-element.33), channel_id=1, source_target_pairs={{0,16},{1,17},{2,18},{3,19},{4,20},{5,21},{6,22},{7,23},{8,24},{9,... | collective-permute-start | bytes 491528 | tf_op jit(solution)/shard_map/ppermute | solution.py:44
  161.6 8.6 %collective-permute-start.27 = (bf16[320,256]{1,0:T(8,128)(2,1)}, bf16[320,256]{1,0:T(8,128)(2,1)}, u32[]{:S(2)}, u32[]{:S(2)}) collective-permute-start(bf16[320,256]{1,0:T(8,128)(2,1)} %get-tuple-element.34), channel_id=1, source_target_pairs={{0,32},{1,33},{2,34},{3,35},{4,36},{5,37},{6,38},{7,39},{8,40},{9,... | collective-permute-start | bytes 491528 | tf_op jit(solution)/shard_map/ppermute | solution.py:44
  172.2 7.0 %collective-permute-start.28 = (bf16[80,256]{1,0:T(8,128)(2,1)}, bf16[80,256]{1,0:T(8,128)(2,1)S(1)}, u32[]{:S(2)}, u32[]{:S(2)}) collective-permute-start(bf16[80,256]{1,0:T(8,128)(2,1)} %get-tuple-element.39), channel_id=1, source_target_pairs={{0,1},{1,2},{2,3},{3,0},{4,5},{5,6},{6,7},{7,4},{8,9},{9,10},{10,1... | collective-permute-start | bytes 122888 | tf_op jit(solution)/shard_map/ppermute | solution.py:44
  172.7 6.5 %collective-permute-start.29 = (bf16[80,256]{1,0:T(8,128)(2,1)}, bf16[80,256]{1,0:T(8,128)(2,1)S(1)}, u32[]{:S(2)}, u32[]{:S(2)}) collective-permute-start(bf16[80,256]{1,0:T(8,128)(2,1)} %get-tuple-element.41), channel_id=1, source_target_pairs={{0,3},{1,0},{2,1},{3,2},{4,7},{5,4},{6,5},{7,6},{8,11},{9,8},{10,9... | collective-permute-start | bytes 122888 | tf_op jit(solution)/shard_map/ppermute | solution.py:44
  176.3 8.4 %collective-permute-start.30 = (bf16[80,256]{1,0:T(8,128)(2,1)S(1)}, bf16[80,256]{1,0:T(8,128)(2,1)S(1)}, u32[]{:S(2)}, u32[]{:S(2)}) collective-permute-start(bf16[80,256]{1,0:T(8,128)(2,1)S(1)} %get-tuple-element.40), channel_id=1, source_target_pairs={{0,2},{1,3},{2,0},{3,1},{4,6},{5,7},{6,4},{7,5},{8,10},{9,11},{10,... | collective-permute-start | bytes 122888 | tf_op jit(solution)/shard_map/ppermute | solution.py:44
  179.2 11.2 %collective-permute-start.32 = (bf16[384,256]{1,0:T(8,128)(2,1)S(1)}, bf16[384,256]{1,0:T(8,128)(2,1)S(1)}, u32[]{:S(2)}, u32[]{:S(2)}) collective-permute-start(bf16[384,256]{1,0:T(8,128)(2,1)S(1)} %copy-done.6), channel_id=1, source_target_pairs={{0,64},{1,65},{2,66},{3,67},{4,68},{5,69},{6,70},{7,71},{8,72},{9,... | collective-permute-start | bytes 589832 | tf_op jit(solution)/shard_map/ppermute | solution.py:44
  (23 other events, 271.0 us)

commit v2 on v1

--- a/solution.py
+++ b/solution.py
@@ -11,7 +11,7 @@
 NS, NT = 320, 256
 AXES = ("pipe", "vocab")
 F32, BF16 = jnp.float32, jnp.bfloat16
-VMEM_LIMIT = 48 * 1024 * 1024
+VMEM_LIMIT = 20 * 1024 * 1024
 
 
 def coords(i):
@@ -64,51 +64,19 @@
     return lax.dot_general(a, b, (dims, ((), ())), preferred_element_type=F32)
 
 
-def logits_kernel(
-    t0, t1, t2, t3, ws, wso, wt, wto, es_ref, et_ref, st_ref, hs_out, hs, ht, wsb, wtb, hsem, wsem, osem
-):
+def logits_kernel(t0, t1, t3, t2a, t2b, ws, wso, wt, wto, es_ref, et_ref, st_ref, hs, ht):
     _, c, x, y, _ = place()
-    copies_t, copies_s = [], []
-    for j, t in enumerate((t0, t1, t2, t3)):
-        for i in range(4):
+    parts = [(0, t0, 0, range(4)), (1, t1, 0, range(4)), (3, t3, 0, range(4))]
+    parts += [(2, t2a, 0, range(2)), (2, t2b, 2, range(2, 4))]
+    for j, t, base, lines in parts:
+        for i in lines:
             at = block_at(c, x, y, (4 - i) & 3, (4 - j) & 3)
-            n = (j * 4 + i) * 2
-            copies_t.append(
-                pltpu.make_async_copy(
-                    t.at[i, pl.ds(NS, NT)],
-                    ht.at[pl.ds(pl.multiple_of(at * NT, NT), NT)],
-                    hsem.at[n],
-                )
-            )
-            copies_s.append(
-                pltpu.make_async_copy(
-                    t.at[i, pl.ds(0, NS)],
-                    hs.at[pl.ds(pl.multiple_of(at * NS, NS), NS)],
-                    hsem.at[n + 1],
-                )
-            )
-    weights = [
-        pltpu.make_async_copy(src, dst.at[pl.ds(half * ROWS, ROWS)], wsem.at[n])
-        for n, (src, dst, half) in enumerate(
-            ((wt, wtb, 0), (wto, wtb, 1), (ws, wsb, 0), (wso, wsb, 1))
-        )
-    ]
-    for copy in copies_t + weights[:2] + copies_s + weights[2:]:
-        copy.start()
-    for copy in copies_t:
-        copy.wait()
-    for half in range(2):
-        weights[half].wait()
-        rows = pl.ds(half * ROWS, ROWS)
-        et_ref[rows] = dot(wtb[rows], ht[...], ((1,), (0,)))
-    for copy in copies_s:
-        copy.wait()
-    out = pltpu.make_async_copy(hs, hs_out, osem)
-    out.start()
-    for half in range(2):
-        weights[2 + half].wait()
-        rows = pl.ds(half * ROWS, ROWS)
-        es_ref[rows] = dot(wsb[rows], hs[...], ((1,), (0,)))
+            ht[pl.ds(pl.multiple_of(at * NT, NT), NT)] = t[i - base, NS : NS + NT]
+            hs[pl.ds(pl.multiple_of(at * NS, NS), NS)] = t[i - base, 0:NS]
+    et_ref[:ROWS] = dot(wt[...], ht[...], ((1,), (0,)))
+    et_ref[ROWS:] = dot(wto[...], ht[...], ((1,), (0,)))
+    es_ref[:ROWS] = dot(ws[...], hs[...], ((1,), (0,)))
+    es_ref[ROWS:] = dot(wso[...], hs[...], ((1,), (0,)))
     s, t = es_ref[...], et_ref[...]
     sm = jnp.max(s, axis=0, keepdims=True)
     tm = jnp.max(t, axis=0, keepdims=True)
@@ -121,11 +89,9 @@
     st_ref[5:8] = jnp.zeros((3, TOK), F32)
     es_ref[...] = es
     et_ref[...] = et
-    out.wait()
 
 
 def logits_call(parts, ws, wso, wt, wto):
-    hbm = pl.BlockSpec(memory_space=pl.ANY)
     vmem = pl.BlockSpec(memory_space=pltpu.VMEM)
     return pl.pallas_call(
         logits_kernel,
@@ -135,17 +101,9 @@
             jax.ShapeDtypeStruct((8, TOK), F32),
             jax.ShapeDtypeStruct((DS, TOK), BF16),
         ),
-        in_specs=[hbm] * 8,
-        out_specs=(vmem, vmem, vmem, hbm),
-        scratch_shapes=[
-            pltpu.VMEM((DS, TOK), BF16),
-            pltpu.VMEM((DT, TOK), BF16),
-            pltpu.VMEM((2 * ROWS, DS), BF16),
-            pltpu.VMEM((2 * ROWS, DT), BF16),
-            pltpu.SemaphoreType.DMA((32,)),
-            pltpu.SemaphoreType.DMA((4,)),
-            pltpu.SemaphoreType.DMA,
-        ],
+        in_specs=[vmem] * 9,
+        out_specs=(vmem,) * 4,
+        scratch_shapes=[pltpu.VMEM((DT, TOK), BF16)],
         compiler_params=pltpu.CompilerParams(vmem_limit_bytes=VMEM_LIMIT),
         cost_estimate=pl.CostEstimate(
             flops=2 * 2 * ROWS * TOK * (DS + DT), bytes_accessed=22_000_000, transcendentals=4 * ROWS * TOK
@@ -157,69 +115,34 @@
 CHUNK = 1280
 
 
-def grads_kernel(
-    es_ref, et_ref, coef_ref, ws, wso, g_own, g_oth, o0, o1, o2, o3, wsb, acc, accb, wsem, osem
-):
+def grads_kernel(es_ref, et_ref, coef_ref, ws, wso, g_own, g_oth, o0, o1, o3, o2a, o2b, acc):
     _, c, x, y, _ = place()
-    weights = []
-    for n in range(DS // CHUNK):
-        for half, src in enumerate((ws, wso)):
-            cols = pl.ds(n * CHUNK, CHUNK)
-            weights.append(
-                pltpu.make_async_copy(
-                    src.at[:, cols], wsb.at[pl.ds(half * ROWS, ROWS), cols], wsem.at[2 * n + half]
-                )
-            )
-    for copy in weights:
-        copy.start()
     g = (es_ref[...] * coef_ref[0:1] - et_ref[...] * coef_ref[1:2]).astype(BF16)
     g_own[...] = g[:ROWS]
     g_oth[...] = g[ROWS:]
     for n in range(DS // CHUNK):
-        weights[2 * n].wait()
-        weights[2 * n + 1].wait()
-        part = dot(wsb[:, n * CHUNK : (n + 1) * CHUNK], g, ((0,), (0,)))
-        acc[n * CHUNK : (n + 1) * CHUNK] = part
-        accb[n * CHUNK : (n + 1) * CHUNK] = part.astype(BF16)
-    outs = []
-    for k, o in ((1, o1), (3, o3), (2, o2), (0, o0)):
-        for r in range(4):
+        cols = slice(n * CHUNK, (n + 1) * CHUNK)
+        part = dot(g[:ROWS], ws[:, cols], ((0,), (0,))) + dot(g[ROWS:], wso[:, cols], ((0,), (0,)))
+        acc[cols] = part.astype(BF16).T
+    outs = [(0, o0, 0, range(4)), (1, o1, 0, range(4)), (3, o3, 0, range(4))]
+    outs += [(2, o2a, 0, range(2)), (2, o2b, 2, range(2, 4))]
+    for k, o, base, lines in outs:
+        for r in lines:
             at = block_at(c, x, y, r, k)
-            src = acc if k == 0 else accb
-            outs.append(
-                pltpu.make_async_copy(
-                    src.at[pl.ds(pl.multiple_of(at * NS, NS), NS)], o.at[r], osem.at[k * 4 + r]
-                )
-            )
-    for copy in outs:
-        copy.start()
-    for copy in outs:
-        copy.wait()
+            o[r - base] = acc[pl.ds(pl.multiple_of(at * NS, NS), NS)]
 
 
 def grads_call(es, et, coef, ws, wso):
-    hbm = pl.BlockSpec(memory_space=pl.ANY)
     vmem = pl.BlockSpec(memory_space=pltpu.VMEM)
-    piece = (4, NS, TOK)
+    whole = jax.ShapeDtypeStruct((4, NS, TOK), BF16)
+    half = jax.ShapeDtypeStruct((2, NS, TOK), BF16)
+    rows = jax.ShapeDtypeStruct((ROWS, TOK), BF16)
     return pl.pallas_call(
         grads_kernel,
-        out_shape=(
-            jax.ShapeDtypeStruct((ROWS, TOK), BF16),
-            jax.ShapeDtypeStruct((ROWS, TOK), BF16),
-            jax.ShapeDtypeStruct(piece, F32),
-            jax.ShapeDtypeStruct(piece, BF16),
-            jax.ShapeDtypeStruct(piece, BF16),
-            jax.ShapeDtypeStruct(piece, BF16),
-        ),
-        in_specs=[vmem, vmem, vmem, hbm, hbm],
-        out_specs=(vmem, vmem, hbm, hbm, hbm, hbm),
-        scratch_shapes=[
-            pltpu.VMEM((2 * ROWS, DS), BF16),
-            pltpu.VMEM((DS, TOK), F32),
-            pltpu.VMEM((DS, TOK), BF16),
-            pltpu.SemaphoreType.DMA((8,)),
-            pltpu.SemaphoreType.DMA((16,)),
-        ],
+        out_shape=(rows, rows, whole, whole, whole, half, half),
+        in_specs=[vmem] * 5,
+        out_specs=(vmem,) * 7,
+        scratch_shapes=[pltpu.VMEM((DS, TOK), BF16)],
         compiler_params=pltpu.CompilerParams(vmem_limit_bytes=VMEM_LIMIT),
         cost_estimate=pl.CostEstimate(
             flops=2 * 2 * ROWS * TOK * DS, bytes_accessed=14_000_000, transcendentals=0
@@ -278,7 +201,9 @@
     ordered = [lax.select_n((zh - q) & 3, *around) for q in range(4)]
     block = jnp.concatenate([o[:80] for o in ordered] + [o[80:] for o in ordered], axis=0)
     line = jnp.stack((block,) + ring(block, FIRST))
-    parts = (line,) + ring(line, SECOND)
+    before, after = send(line, SECOND[1]), send(line, SECOND[3])
+    far_low, far_high = send(before[:2], SECOND[1]), send(after[2:], SECOND[3])
+    parts = (line, before, after, far_low, far_high)
 
     es, et, local, hidden_own = logits_call(
         parts, student_head, student_other, teacher_head, teacher_other
@@ -306,12 +231,15 @@
     )
     coef = jnp.concatenate([coef, jnp.zeros((6, TOK), F32)], axis=0)
 
-    g_own, g_oth, o0, o1, o2, o3 = grads_call(es, et, coef, student_head, student_other)
+    g_own, g_oth, o0, o1, o3, o2a, o2b = grads_call(es, et, coef, student_head, student_other)
+    low, high = send(o2a, SECOND[1]), send(o2b, SECOND[3])
     g_got = send(g_oth, CORE)
-    r1, r3, r2 = send(o1, SECOND[1]), send(o3, SECOND[3]), send(o2, SECOND[2])
+    r1 = send(jnp.concatenate([(o1[:2].astype(F32) + low.astype(F32)).astype(BF16), o1[2:]]), SECOND[1])
+    r3 = send(jnp.concatenate([o3[:2], (o3[2:].astype(F32) + high.astype(F32)).astype(BF16)]), SECOND[3])
     head_grad = head_call(g_own, g_got, hidden_own, hidden_got)
-
-    sums = o0 + (r1.astype(F32) + r3.astype(F32)) + r2.astype(F32)
+    r1, r3, head_grad = lax.optimization_barrier((r1, r3, head_grad))
+
+    sums = o0.astype(F32) + (r1.astype(F32) + r3.astype(F32))
     r1, r3, r2 = (send(sums[k].astype(BF16), FIRST[k]) for k in (1, 3, 2))
     sums = (sums[0] + (r1.astype(F32) + r3.astype(F32)) + r2.astype(F32)).reshape(4, 80, TOK)
     narrow = sums.astype(BF16)

time: 200 us -> 169 us (0.84)
  Pallas kernels: 31.1 us -> 17.4 us
  waiting for transfers between devices: 85.2 us -> 76.1 us
  starting transfers between devices: 68.2 us -> 59.7 us
  local copies, waits for them, and re-layouts: 5.78 us -> 9.9 us
  other arithmetic: 6.76 us -> 3.87 us
    ppermute x34 -> x36, waiting for transfers between devices: 85.2 us -> 76.1 us  [send(): return lax.ppermute(value, AXES, pairs)]
    ppermute x34 -> x36, starting transfers between devices: 68.2 us -> 59.7 us  [send(): return lax.ppermute(value, AXES, pairs)]
    pallas_call x1, Pallas kernels: 13.4 us -> 6.52 us  [logits_call(): pl.pallas_call(logits_kernel, out_shape=(jax.ShapeDtypeStruct((2 * ROWS,...]
    unnamed x33 -> x27, local copies, waits for them, and re-layouts: 4.13 us -> 9.58 us
    pallas_call x1, Pallas kernels: 9.87 us -> 5.27 us  [grads_call(): pl.pallas_call(grads_kernel, out_shape=(rows, rows, whole, whole, whole,...]
    pallas_call x1, Pallas kernels: 7.87 us -> 5.62 us  [head_call(): pl.pallas_call(head_kernel, out_shape=jax.ShapeDtypeStruct((ROWS, DS), BF...]
  transfers between devices with their start and end apart: 34 -> 36, of which waited for: 22 -> 25; matrix products, arithmetic and copies ran while one was open for 3% -> 1% of each run, Pallas kernels for 0% -> 6%
where the time goes in v2:
time: 169 us; the launch traced here: 168 us
  waiting for transfers between devices  76.1 us (45%)
  starting transfers between devices  59.7 us (35%)
  Pallas kernels  17.4 us (10%)
  local copies, waits for them, and re-layouts  9.9 us (6%)
  other arithmetic  3.87 us (2%)
    ppermute x36, waiting for transfers between devices, send(): return lax.ppermute(value, AXES, pairs)  76.1 us
    ppermute x36, starting transfers between devices, send(): return lax.ppermute(value, AXES, pairs)  59.7 us
    unnamed x27, local copies, waits for them, and re-layouts  9.58 us
    pallas_call x1, Pallas kernels, logits_call(): pl.pallas_call(logits_kernel, out_shape=(jax.ShapeDtypeStruct((2 * ROWS,...  6.52 us
    pallas_call x1, Pallas kernels, head_call(): pl.pallas_call(head_kernel, out_shape=jax.ShapeDtypeStruct((ROWS, DS), BF...  5.62 us
    pallas_call x1, Pallas kernels, grads_call(): pl.pallas_call(grads_kernel, out_shape=(rows, rows, whole, whole, whole,...  5.27 us
  transfers between devices with their start and end apart: 36, of which 25 were waited for; matrix products, arithmetic and copies ran while one was open for 1% of the time, Pallas kernels for 6%

profile of v2, /device:TPU:2, one launch (start us, length us, event | category | flops | bytes accessed | tf_op | source)
XLA Modules:
  0.0 168.1 jit_solution(9961923465982535911)
XLA Ops:
  6.1 3.3 %collective-permute-start.1 = (bf16[144,256]{1,0:T(8,128)(2,1)S(1)}, bf16[144,256]{1,0:T(8,128)(2,1)S(1)}, u32[]{:S(2)}, u32[]{:S(2)}) collective-permute-start(bf16[144,256]{1,0:T(8,128)(2,1)S(1)} %pad_maximum_fusion.3), channel_id=1, source_target_pairs={{0,1},{1,2},{2,3},{3,0},{4,5},{5,6},{6,7},{7,4},{8,9},{9,10},{10,1... | collective-permute-start | bytes 221192 | tf_op jit(solution)/shard_map/ppermute | solution.py:44
  9.5 5.4 %collective-permute-start.2 = (bf16[144,256]{1,0:T(8,128)(2,1)S(1)}, bf16[144,256]{1,0:T(8,128)(2,1)S(1)}, u32[]{:S(2)}, u32[]{:S(2)}) collective-permute-start(bf16[144,256]{1,0:T(8,128)(2,1)S(1)} %pad_maximum_fusion.3), channel_id=1, source_target_pairs={{0,2},{1,3},{2,0},{3,1},{4,6},{5,7},{6,4},{7,5},{8,10},{9,11},{10,... | collective-permute-start | bytes 221192 | tf_op jit(solution)/shard_map/ppermute | solution.py:44
  28.7 3.1 %collective-permute-done.5 = bf16[576,256]{1,0:T(8,128)(2,1)S(1)} collective-permute-done((bf16[576,256]{1,0:T(8,128)(2,1)S(1)}, bf16[576,256]{1,0:T(8,128)(2,1)S(1)}, u32[]{:S(2)}, u32[]{:S(2)}) %collective-permute-start.5) | collective-permute-done | bytes 294944 | tf_op jit(solution)/shard_map/ppermute | solution.py:44
  31.8 4.6 %collective-permute-done.6 = bf16[576,256]{1,0:T(8,128)(2,1)S(1)} collective-permute-done((bf16[576,256]{1,0:T(8,128)(2,1)S(1)}, bf16[576,256]{1,0:T(8,128)(2,1)S(1)}, u32[]{:S(2)}, u32[]{:S(2)}) %collective-permute-start.6) | collective-permute-done | bytes 294944 | tf_op jit(solution)/shard_map/ppermute | solution.py:44
  36.6 3.7 %collective-permute-start.8 = (bf16[4,576,256]{2,1,0:T(8,128)(2,1)S(1)}, bf16[4,576,256]{2,1,0:T(8,128)(2,1)S(1)}, u32[]{:S(2)}, u32[]{:S(2)}) collective-permute-start(bf16[4,576,256]{2,1,0:T(8,128)(2,1)S(1)} %pad_maximum_fusion.t0), channel_id=1, source_target_pairs={{0,12},{1,13},{2,14},{3,15},{4,0},{5,1},{6,2},{7,3},{8,4},{9,5},{1... | collective-permute-start | bytes 3538952 | tf_op jit(solution)/shard_map/ppermute | solution.py:44
  40.3 13.7 %collective-permute-done.8.t3 = bf16[4,576,256]{2,1,0:T(8,128)(2,1)S(1)} collective-permute-done((bf16[4,576,256]{2,1,0:T(8,128)(2,1)S(1)}, bf16[4,576,256]{2,1,0:T(8,128)(2,1)S(1)}, u32[]{:S(2)}, u32[]{:S(2)}) %collective-permute-start.8) | collective-permute-done | bytes 1179680 | tf_op jit(solution)/shard_map/ppermute | solution.py:44
  54.1 3.8 %collective-permute-start.10 = (bf16[2,576,256]{2,1,0:T(8,128)(2,1)S(1)}, bf16[2,576,256]{2,1,0:T(8,128)(2,1)S(1)}, u32[]{:S(2)}, u32[]{:S(2)}) collective-permute-start(bf16[2,576,256]{2,1,0:T(8,128)(2,1)S(1)} %slice.279), channel_id=1, source_target_pairs={{0,12},{1,13},{2,14},{3,15},{4,0},{5,1},{6,2},{7,3},{8,4},{9,5},{1... | collective-permute-start | bytes 1769480 | tf_op jit(solution)/shard_map/ppermute | solution.py:44
  58.2 7.1 %collective-permute-done.10.t2b = bf16[2,576,256]{2,1,0:T(8,128)(2,1)S(1)} collective-permute-done((bf16[2,576,256]{2,1,0:T(8,128)(2,1)S(1)}, bf16[2,576,256]{2,1,0:T(8,128)(2,1)S(1)}, u32[]{:S(2)}, u32[]{:S(2)}) %collective-permute-start.10) | collective-permute-done | bytes 589856 | tf_op jit(solution)/shard_map/ppermute | solution.py:44
  65.3 4.0 %collective-permute-done.9.t2a = bf16[2,576,256]{2,1,0:T(8,128)(2,1)S(1)} collective-permute-done((bf16[2,576,256]{2,1,0:T(8,128)(2,1)S(1)}, bf16[2,576,256]{2,1,0:T(8,128)(2,1)S(1)}, u32[]{:S(2)}, u32[]{:S(2)}) %collective-permute-start.9) | collective-permute-done | bytes 589856 | tf_op jit(solution)/shard_map/ppermute | solution.py:44
  71.2 6.5 %logits.1 = (f32[768,256]{1,0:T(8,128)S(1)}, f32[768,256]{1,0:T(8,128)S(1)}, f32[8,256]{1,0:T(8,128)S(1)}, bf16[5120,256]{1,0:T(8,128)(2,1)S(1)}) custom-call(bf16[4,576,256]{2,1,0:T(8,128)(2,1)S(1)} %pad_maximum_fusion.t0, bf16[4,576,256]{2,1,0:T(8,128)(2,1)S(1)} %collective-permute-done.7.t1, bf16[4,576,256]{2,1,0:T(8,128)(2,1)S(1)} %collective-permute-done.8.t3, ...), custom_call_target="tpu_custom_call" | custom-call | flops 3623878656 | bytes 22000000 | tf_op jit(solution)/shard_map/logits/pallas_call | solution.py:96
  81.0 3.6 %collective-permute-done.13 = f32[8,256]{1,0:T(8,128)S(1)} collective-permute-done((f32[8,256]{1,0:T(8,128)S(1)}, f32[8,256]{1,0:T(8,128)S(1)}, u32[]{:S(2)}, u32[]{:S(2)}) %collective-permute-start.13) | collective-permute-done | bytes 8224 | tf_op jit(solution)/shard_map/ppermute | solution.py:44
  86.9 2.7 %collective-permute-start.15 = (f32[8,256]{1,0:T(8,128)S(1)}, f32[8,256]{1,0:T(8,128)S(1)}, u32[]{:S(2)}, u32[]{:S(2)}) collective-permute-start(f32[8,256]{1,0:T(8,128)S(1)} %pad_maximum_fusion.7), channel_id=1, source_target_pairs={{0,2},{1,3},{2,0},{3,1},{4,6},{5,7},{6,4},{7,5},{8,10},{9,11},{10,... | collective-permute-start | bytes 24584 | tf_op jit(solution)/shard_map/ppermute | solution.py:44
  91.4 3.1 %collective-permute-done.15 = f32[8,256]{1,0:T(8,128)S(1)} collective-permute-done((f32[8,256]{1,0:T(8,128)S(1)}, f32[8,256]{1,0:T(8,128)S(1)}, u32[]{:S(2)}, u32[]{:S(2)}) %collective-permute-start.15) | collective-permute-done | bytes 8224 | tf_op jit(solution)/shard_map/ppermute | solution.py:44
  98.3 2.9 %collective-permute-done.18 = f32[8,256]{1,0:T(8,128)S(1)} collective-permute-done((f32[8,256]{1,0:T(8,128)S(1)}, f32[8,256]{1,0:T(8,128)S(1)}, u32[]{:S(2)}, u32[]{:S(2)}) %collective-permute-start.18) | collective-permute-done | bytes 8224 | tf_op jit(solution)/shard_map/ppermute | solution.py:44
  111.9 5.3 %grads.1 = (bf16[384,256]{1,0:T(8,128)(2,1)S(1)}, bf16[384,256]{1,0:T(8,128)(2,1)S(1)}, bf16[4,320,256]{2,1,0:T(8,128)(2,1)S(1)}, bf16[4,320,256]{2,1,0:T(8,128)...) custom-call(f32[768,256]{1,0:T(8,128)S(1)} %copy-done.6, ...), custom_call_target="tpu_custom_call" | custom-call | flops 2013265920 | bytes 14000000 | tf_op jit(solution)/shard_map/grads/pallas_call | solution.py:140
  120.0 4.4 %collective-permute-done.25 = bf16[2,320,256]{2,1,0:T(8,128)(2,1)S(1)} collective-permute-done((bf16[2,320,256]{2,1,0:T(8,128)(2,1)S(1)}, bf16[2,320,256]{2,1,0:T(8,128)(2,1)S(1)}, u32[]{:S(2)}, u32[]{:S(2)}) %collective-permute-start.25) | collective-permute-done | bytes 327712 | tf_op jit(solution)/shard_map/ppermute | solution.py:44
  124.6 3.8 %collective-permute-start.26 = (bf16[4,320,256]{2,1,0:T(8,128)(2,1)S(1)}, bf16[4,320,256]{2,1,0:T(8,128)(2,1)S(1)}, u32[]{:S(2)}, u32[]{:S(2)}) collective-permute-start(bf16[4,320,256]{2,1,0:T(8,128)(2,1)S(1)} %pad_maximum_fusion.2), channel_id=1, source_target_pairs={{0,12},{1,13},{2,14},{3,15},{4,0},{5,1},{6,2},{7,3},{8,4},{9,5},{1... | collective-permute-start | bytes 1966088 | tf_op jit(solution)/shard_map/ppermute | solution.py:44
  130.1 5.6 %head.1 = bf16[384,5120]{1,0:T(8,128)(2,1)} custom-call(bf16[384,256]{1,0:T(8,128)(2,1)S(1)} %get-tuple-element.25.g_own, bf16[384,256]{1,0:T(8,128)(2,1)S(1)} %collective-permute-done.27.g_got, bf16[5120,256]{1,0:T(8,128)(2,1)S(1)} %copy-done.4, bf16[5120,256]{1,0:T(8,128)(2,1)S(1)} %collective-permute-done.28.h_got), custom_call_target="tpu_custom_call" | custom-call | flops 2013265920 | bytes 10000000 | tf_op jit(solution)/shard_map/head/pallas_call | solution.py:164
  136.5 4.0 %collective-permute-done.24 = bf16[4,320,256]{2,1,0:T(8,128)(2,1)S(1)} collective-permute-done((bf16[4,320,256]{2,1,0:T(8,128)(2,1)S(1)}, bf16[4,320,256]{2,1,0:T(8,128)(2,1)S(1)}, u32[]{:S(2)}, u32[]{:S(2)}) %collective-permute-start.24) | collective-permute-done | bytes 655392 | tf_op jit(solution)/shard_map/ppermute | solution.py:44
  142.8 3.2 %collective-permute-start.31 = (bf16[320,256]{1,0:T(8,128)(2,1)S(1)}, bf16[320,256]{1,0:T(8,128)(2,1)S(1)}, u32[]{:S(2)}, u32[]{:S(2)}) collective-permute-start(bf16[320,256]{1,0:T(8,128)(2,1)S(1)} %get-tuple-element.42), channel_id=1, source_target_pairs={{0,32},{1,33},{2,34},{3,35},{4,36},{5,37},{6,38},{7,39},{8,40},{9,... | collective-permute-start | bytes 491528 | tf_op jit(solution)/shard_map/ppermute | solution.py:44
  147.9 3.2 %collective-permute-done.31 = bf16[320,256]{1,0:T(8,128)(2,1)S(1)} collective-permute-done((bf16[320,256]{1,0:T(8,128)(2,1)S(1)}, bf16[320,256]{1,0:T(8,128)(2,1)S(1)}, u32[]{:S(2)}, u32[]{:S(2)}) %collective-permute-start.31) | collective-permute-done | bytes 163872 | tf_op jit(solution)/shard_map/ppermute | solution.py:44
  155.4 2.9 %collective-permute-start.34 = (bf16[80,256]{1,0:T(8,128)(2,1)S(1)}, bf16[80,256]{1,0:T(8,128)(2,1)S(1)}, u32[]{:S(2)}, u32[]{:S(2)}) collective-permute-start(bf16[80,256]{1,0:T(8,128)(2,1)S(1)} %get-tuple-element.48), channel_id=1, source_target_pairs={{0,2},{1,3},{2,0},{3,1},{4,6},{5,7},{6,4},{7,5},{8,10},{9,11},{10,... | collective-permute-start | bytes 122888 | tf_op jit(solution)/shard_map/ppermute | solution.py:44
  158.4 5.0 %collective-permute-done.34 = bf16[80,256]{1,0:T(8,128)(2,1)S(1)} collective-permute-done((bf16[80,256]{1,0:T(8,128)(2,1)S(1)}, bf16[80,256]{1,0:T(8,128)(2,1)S(1)}, u32[]{:S(2)}, u32[]{:S(2)}) %collective-permute-start.34) | collective-permute-done | bytes 40992 | tf_op jit(solution)/shard_map/ppermute | solution.py:44
  164.1 3.4 %collective-permute-done.35 = f32[80,128]{1,0:T(8,128)S(1)} collective-permute-done((f32[80,128]{1,0:T(8,128)S(1)}, f32[80,128]{1,0:T(8,128)S(1)}, u32[]{:S(2)}, u32[]{:S(2)}) %collective-permute-start.35) | collective-permute-done | bytes 40992 | tf_op jit(solution)/shard_map/ppermute | solution.py:44
  (135 shorter events, 58.6 us)
Async XLA Ops:
  6.1 11.9 %collective-permute-start.1 = (bf16[144,256]{1,0:T(8,128)(2,1)S(1)}, bf16[144,256]{1,0:T(8,128)(2,1)S(1)}, u32[]{:S(2)}, u32[]{:S(2)}) collective-permute-start(bf16[144,256]{1,0:T(8,128)(2,1)S(1)} %pad_maximum_fusion.3), channel_id=1, source_target_pairs={{0,1},{1,2},{2,3},{3,0},{4,5},{5,6},{6,7},{7,4},{8,9},{9,10},{10,1... | collective-permute-start | bytes 221192 | tf_op jit(solution)/shard_map/ppermute | solution.py:44
  9.5 9.9 %collective-permute-start.2 = (bf16[144,256]{1,0:T(8,128)(2,1)S(1)}, bf16[144,256]{1,0:T(8,128)(2,1)S(1)}, u32[]{:S(2)}, u32[]{:S(2)}) collective-permute-start(bf16[144,256]{1,0:T(8,128)(2,1)S(1)} %pad_maximum_fusion.3), channel_id=1, source_target_pairs={{0,2},{1,3},{2,0},{3,1},{4,6},{5,7},{6,4},{7,5},{8,10},{9,11},{10,... | collective-permute-start | bytes 221192 | tf_op jit(solution)/shard_map/ppermute | solution.py:44
  14.9 6.8 %collective-permute-start.3 = (bf16[144,256]{1,0:T(8,128)(2,1)S(1)}, bf16[144,256]{1,0:T(8,128)(2,1)S(1)}, u32[]{:S(2)}, u32[]{:S(2)}) collective-permute-start(bf16[144,256]{1,0:T(8,128)(2,1)S(1)} %pad_maximum_fusion.3), channel_id=1, source_target_pairs={{0,3},{1,0},{2,1},{3,2},{4,7},{5,4},{6,5},{7,6},{8,11},{9,8},{10,9... | collective-permute-start | bytes 221192 | tf_op jit(solution)/shard_map/ppermute | solution.py:44
  17.5 51.7 %collective-permute-start.11 = (bf16[384,5120]{1,0:T(8,128)(2,1)}, bf16[384,5120]{1,0:T(8,128)(2,1)}, u32[]{:S(2)}, u32[]{:S(2)}) collective-permute-start(bf16[384,5120]{1,0:T(8,128)(2,1)} %ws.3), channel_id=1, source_target_pairs={{0,64},{1,65},{2,66},{3,67},{4,68},{5,69},{6,70},{7,71},{8,72},{9,... | collective-permute-start | bytes 11796488 | tf_op jit(solution)/shard_map/ppermute | solution.py:44
  17.5 51.7 %collective-permute-start.12 = (bf16[384,4096]{1,0:T(8,128)(2,1)}, bf16[384,4096]{1,0:T(8,128)(2,1)S(1)}, u32[]{:S(2)}, u32[]{:S(2)}) collective-permute-start(bf16[384,4096]{1,0:T(8,128)(2,1)} %wt.1), channel_id=1, source_target_pairs={{0,64},{1,65},{2,66},{3,67},{4,68},{5,69},{6,70},{7,71},{8,72},{9,... | collective-permute-start | bytes 9437192 | tf_op jit(solution)/shard_map/ppermute | solution.py:44
  21.9 6.8 %collective-permute-start.4 = (bf16[576,256]{1,0:T(8,128)(2,1)S(1)}, bf16[576,256]{1,0:T(8,128)(2,1)S(1)}, u32[]{:S(2)}, u32[]{:S(2)}) collective-permute-start(bf16[576,256]{1,0:T(8,128)(2,1)S(1)} %slice_dynamic-update-slice_fusion.4), channel_id=1, source_target_pairs={{0,16},{1,17},{2,18},{3,19},{4,20},{5,21},{6,22},{7,23},{8,24},{9,... | collective-permute-start | bytes 884744 | tf_op jit(solution)/shard_map/ppermute | solution.py:44
  23.5 8.3 %collective-permute-start.5 = (bf16[576,256]{1,0:T(8,128)(2,1)S(1)}, bf16[576,256]{1,0:T(8,128)(2,1)S(1)}, u32[]{:S(2)}, u32[]{:S(2)}) collective-permute-start(bf16[576,256]{1,0:T(8,128)(2,1)S(1)} %slice_dynamic-update-slice_fusion.4), channel_id=1, source_target_pairs={{0,32},{1,33},{2,34},{3,35},{4,36},{5,37},{6,38},{7,39},{8,40},{9,... | collective-permute-start | bytes 884744 | tf_op jit(solution)/shard_map/ppermute | solution.py:44
  24.6 11.9 %collective-permute-start.6 = (bf16[576,256]{1,0:T(8,128)(2,1)S(1)}, bf16[576,256]{1,0:T(8,128)(2,1)S(1)}, u32[]{:S(2)}, u32[]{:S(2)}) collective-permute-start(bf16[576,256]{1,0:T(8,128)(2,1)S(1)} %slice_dynamic-update-slice_fusion.4), channel_id=1, source_target_pairs={{0,48},{1,49},{2,50},{3,51},{4,52},{5,53},{6,54},{7,55},{8,56},{9,... | collective-permute-start | bytes 884744 | tf_op jit(solution)/shard_map/ppermute | solution.py:44
  36.6 17.4 %collective-permute-start.8 = (bf16[4,576,256]{2,1,0:T(8,128)(2,1)S(1)}, bf16[4,576,256]{2,1,0:T(8,128)(2,1)S(1)}, u32[]{:S(2)}, u32[]{:S(2)}) collective-permute-start(bf16[4,576,256]{2,1,0:T(8,128)(2,1)S(1)} %pad_maximum_fusion.t0), channel_id=1, source_target_pairs={{0,12},{1,13},{2,14},{3,15},{4,0},{5,1},{6,2},{7,3},{8,4},{9,5},{1... | collective-permute-start | bytes 3538952 | tf_op jit(solution)/shard_map/ppermute | solution.py:44
  40.3 17.5 %collective-permute-start.7 = (bf16[4,576,256]{2,1,0:T(8,128)(2,1)S(1)}, bf16[4,576,256]{2,1,0:T(8,128)(2,1)S(1)}, u32[]{:S(2)}, u32[]{:S(2)}) collective-permute-start(bf16[4,576,256]{2,1,0:T(8,128)(2,1)S(1)} %pad_maximum_fusion.t0), channel_id=1, source_target_pairs={{0,4},{1,5},{2,6},{3,7},{4,8},{5,9},{6,10},{7,11},{8,12},{9,13},{1... | collective-permute-start | bytes 3538952 | tf_op jit(solution)/shard_map/ppermute | solution.py:44
  54.1 11.2 %collective-permute-start.10 = (bf16[2,576,256]{2,1,0:T(8,128)(2,1)S(1)}, bf16[2,576,256]{2,1,0:T(8,128)(2,1)S(1)}, u32[]{:S(2)}, u32[]{:S(2)}) collective-permute-start(bf16[2,576,256]{2,1,0:T(8,128)(2,1)S(1)} %slice.279), channel_id=1, source_target_pairs={{0,12},{1,13},{2,14},{3,15},{4,0},{5,1},{6,2},{7,3},{8,4},{9,5},{1... | collective-permute-start | bytes 1769480 | tf_op jit(solution)/shard_map/ppermute | solution.py:44
  57.9 11.4 %collective-permute-start.9 = (bf16[2,576,256]{2,1,0:T(8,128)(2,1)S(1)}, bf16[2,576,256]{2,1,0:T(8,128)(2,1)S(1)}, u32[]{:S(2)}, u32[]{:S(2)}) collective-permute-start(bf16[2,576,256]{2,1,0:T(8,128)(2,1)S(1)} %slice.278), channel_id=1, source_target_pairs={{0,4},{1,5},{2,6},{3,7},{4,8},{5,9},{6,10},{7,11},{8,12},{9,13},{1... | collective-permute-start | bytes 1769480 | tf_op jit(solution)/shard_map/ppermute | solution.py:44
  84.7 6.7 %collective-permute-start.14 = (f32[8,256]{1,0:T(8,128)S(1)}, f32[8,256]{1,0:T(8,128)S(1)}, u32[]{:S(2)}, u32[]{:S(2)}) collective-permute-start(f32[8,256]{1,0:T(8,128)S(1)} %pad_maximum_fusion.7), channel_id=1, source_target_pairs={{0,1},{1,2},{2,3},{3,0},{4,5},{5,6},{6,7},{7,4},{8,9},{9,10},{10,1... | collective-permute-start | bytes 24584 | tf_op jit(solution)/shard_map/ppermute | solution.py:44
  86.9 7.6 %collective-permute-start.15 = (f32[8,256]{1,0:T(8,128)S(1)}, f32[8,256]{1,0:T(8,128)S(1)}, u32[]{:S(2)}, u32[]{:S(2)}) collective-permute-start(f32[8,256]{1,0:T(8,128)S(1)} %pad_maximum_fusion.7), channel_id=1, source_target_pairs={{0,2},{1,3},{2,0},{3,1},{4,6},{5,7},{6,4},{7,5},{8,10},{9,11},{10,... | collective-permute-start | bytes 24584 | tf_op jit(solution)/shard_map/ppermute | solution.py:44
  104.8 25.3 %collective-permute-start.28 = (bf16[5120,256]{1,0:T(8,128)(2,1)}, bf16[5120,256]{1,0:T(8,128)(2,1)S(1)}, u32[]{:S(2)}, u32[]{:S(2)}) collective-permute-start(bf16[5120,256]{1,0:T(8,128)(2,1)} %copy-done.3), channel_id=1, source_target_pairs={{0,64},{1,65},{2,66},{3,67},{4,68},{5,69},{6,70},{7,71},{8,72},{9,... | collective-permute-start | bytes 7864328 | tf_op jit(solution)/shard_map/ppermute | solution.py:44
  117.2 7.3 %collective-permute-start.25 = (bf16[2,320,256]{2,1,0:T(8,128)(2,1)S(1)}, bf16[2,320,256]{2,1,0:T(8,128)(2,1)S(1)}, u32[]{:S(2)}, u32[]{:S(2)}) collective-permute-start(bf16[2,320,256]{2,1,0:T(8,128)(2,1)S(1)} %get-tuple-element.24), channel_id=1, source_target_pairs={{0,12},{1,13},{2,14},{3,15},{4,0},{5,1},{6,2},{7,3},{8,4},{9,5},{1... | collective-permute-start | bytes 983048 | tf_op jit(solution)/shard_map/ppermute | solution.py:44
  119.8 8.5 %collective-permute-start.23 = (bf16[2,320,256]{2,1,0:T(8,128)(2,1)S(1)}, bf16[2,320,256]{2,1,0:T(8,128)(2,1)S(1)}, u32[]{:S(2)}, u32[]{:S(2)}) collective-permute-start(bf16[2,320,256]{2,1,0:T(8,128)(2,1)S(1)} %get-tuple-element.22), channel_id=1, source_target_pairs={{0,4},{1,5},{2,6},{3,7},{4,8},{5,9},{6,10},{7,11},{8,12},{9,13},{1... | collective-permute-start | bytes 983048 | tf_op jit(solution)/shard_map/ppermute | solution.py:44
  124.6 11.9 %collective-permute-start.26 = (bf16[4,320,256]{2,1,0:T(8,128)(2,1)S(1)}, bf16[4,320,256]{2,1,0:T(8,128)(2,1)S(1)}, u32[]{:S(2)}, u32[]{:S(2)}) collective-permute-start(bf16[4,320,256]{2,1,0:T(8,128)(2,1)S(1)} %pad_maximum_fusion.2), channel_id=1, source_target_pairs={{0,12},{1,13},{2,14},{3,15},{4,0},{5,1},{6,2},{7,3},{8,4},{9,5},{1... | collective-permute-start | bytes 1966088 | tf_op jit(solution)/shard_map/ppermute | solution.py:44
  128.5 11.9 %collective-permute-start.24 = (bf16[4,320,256]{2,1,0:T(8,128)(2,1)S(1)}, bf16[4,320,256]{2,1,0:T(8,128)(2,1)S(1)}, u32[]{:S(2)}, u32[]{:S(2)}) collective-permute-start(bf16[4,320,256]{2,1,0:T(8,128)(2,1)S(1)} %pad_maximum_fusion.1), channel_id=1, source_target_pairs={{0,4},{1,5},{2,6},{3,7},{4,8},{5,9},{6,10},{7,11},{8,12},{9,13},{1... | collective-permute-start | bytes 1966088 | tf_op jit(solution)/shard_map/ppermute | solution.py:44
  140.7 5.4 %collective-permute-start.29 = (bf16[320,256]{1,0:T(8,128)(2,1)S(1)}, bf16[320,256]{1,0:T(8,128)(2,1)S(1)}, u32[]{:S(2)}, u32[]{:S(2)}) collective-permute-start(bf16[320,256]{1,0:T(8,128)(2,1)S(1)} %get-tuple-element.41), channel_id=1, source_target_pairs={{0,16},{1,17},{2,18},{3,19},{4,20},{5,21},{6,22},{7,23},{8,24},{9,... | collective-permute-start | bytes 491528 | tf_op jit(solution)/shard_map/ppermute | solution.py:44
  141.4 6.5 %collective-permute-start.30 = (bf16[320,256]{1,0:T(8,128)(2,1)S(1)}, bf16[320,256]{1,0:T(8,128)(2,1)S(1)}, u32[]{:S(2)}, u32[]{:S(2)}) collective-permute-start(bf16[320,256]{1,0:T(8,128)(2,1)S(1)} %get-tuple-element.43), channel_id=1, source_target_pairs={{0,48},{1,49},{2,50},{3,51},{4,52},{5,53},{6,54},{7,55},{8,56},{9,... | collective-permute-start | bytes 491528 | tf_op jit(solution)/shard_map/ppermute | solution.py:44
  142.8 8.3 %collective-permute-start.31 = (bf16[320,256]{1,0:T(8,128)(2,1)S(1)}, bf16[320,256]{1,0:T(8,128)(2,1)S(1)}, u32[]{:S(2)}, u32[]{:S(2)}) collective-permute-start(bf16[320,256]{1,0:T(8,128)(2,1)S(1)} %get-tuple-element.42), channel_id=1, source_target_pairs={{0,32},{1,33},{2,34},{3,35},{4,36},{5,37},{6,38},{7,39},{8,40},{9,... | collective-permute-start | bytes 491528 | tf_op jit(solution)/shard_map/ppermute | solution.py:44
  151.2 7.1 %collective-permute-start.32 = (bf16[80,256]{1,0:T(8,128)(2,1)S(1)}, bf16[80,256]{1,0:T(8,128)(2,1)S(1)}, u32[]{:S(2)}, u32[]{:S(2)}) collective-permute-start(bf16[80,256]{1,0:T(8,128)(2,1)S(1)} %get-tuple-element.47), channel_id=1, source_target_pairs={{0,1},{1,2},{2,3},{3,0},{4,5},{5,6},{6,7},{7,4},{8,9},{9,10},{10,1... | collective-permute-start | bytes 122888 | tf_op jit(solution)/shard_map/ppermute | solution.py:44
  155.4 7.9 %collective-permute-start.34 = (bf16[80,256]{1,0:T(8,128)(2,1)S(1)}, bf16[80,256]{1,0:T(8,128)(2,1)S(1)}, u32[]{:S(2)}, u32[]{:S(2)}) collective-permute-start(bf16[80,256]{1,0:T(8,128)(2,1)S(1)} %get-tuple-element.48), channel_id=1, source_target_pairs={{0,2},{1,3},{2,0},{3,1},{4,6},{5,7},{6,4},{7,5},{8,10},{9,11},{10,... | collective-permute-start | bytes 122888 | tf_op jit(solution)/shard_map/ppermute | solution.py:44
  (22 other events, 149.1 us)

commit v3 on v2

--- a/solution.py
+++ b/solution.py
@@ -11,7 +11,7 @@
 NS, NT = 320, 256
 AXES = ("pipe", "vocab")
 F32, BF16 = jnp.float32, jnp.bfloat16
-VMEM_LIMIT = 20 * 1024 * 1024
+VMEM_LIMIT = 24 * 1024 * 1024
 
 
 def coords(i):
@@ -64,19 +64,28 @@
     return lax.dot_general(a, b, (dims, ((), ())), preferred_element_type=F32)
 
 
-def logits_kernel(t0, t1, t3, t2a, t2b, ws, wso, wt, wto, es_ref, et_ref, st_ref, hs, ht):
+def logits_kernel(
+    t0, t1, t3, t2a, t2b, ws, wso, wto, wt, es_out, et_out, st_ref, hs_out, wso_out, hs, ht, es_ref, et_ref, wtb, sem
+):
     _, c, x, y, _ = place()
+    teacher_in = pltpu.make_async_copy(wt, wtb, sem.at[0])
+    keep = pltpu.make_async_copy(wso, wso_out, sem.at[1])
+    teacher_in.start()
+    keep.start()
     parts = [(0, t0, 0, range(4)), (1, t1, 0, range(4)), (3, t3, 0, range(4))]
     parts += [(2, t2a, 0, range(2)), (2, t2b, 2, range(2, 4))]
     for j, t, base, lines in parts:
         for i in lines:
             at = block_at(c, x, y, (4 - i) & 3, (4 - j) & 3)
+            hs[pl.ds(pl.multiple_of(at * NS, NS), NS)] = t[i - base, 0:NS]
             ht[pl.ds(pl.multiple_of(at * NT, NT), NT)] = t[i - base, NS : NS + NT]
-            hs[pl.ds(pl.multiple_of(at * NS, NS), NS)] = t[i - base, 0:NS]
-    et_ref[:ROWS] = dot(wt[...], ht[...], ((1,), (0,)))
-    et_ref[ROWS:] = dot(wto[...], ht[...], ((1,), (0,)))
+    hidden = pltpu.make_async_copy(hs, hs_out, sem.at[2])
+    hidden.start()
     es_ref[:ROWS] = dot(ws[...], hs[...], ((1,), (0,)))
     es_ref[ROWS:] = dot(wso[...], hs[...], ((1,), (0,)))
+    et_ref[ROWS:] = dot(wto[...], ht[...], ((1,), (0,)))
+    teacher_in.wait()
+    et_ref[:ROWS] = dot(wtb[...], ht[...], ((1,), (0,)))
     s, t = es_ref[...], et_ref[...]
     sm = jnp.max(s, axis=0, keepdims=True)
     tm = jnp.max(t, axis=0, keepdims=True)
@@ -89,10 +98,17 @@
     st_ref[5:8] = jnp.zeros((3, TOK), F32)
     es_ref[...] = es
     et_ref[...] = et
+    student_out = pltpu.make_async_copy(es_ref, es_out, sem.at[3])
+    teacher_out = pltpu.make_async_copy(et_ref, et_out, sem.at[4])
+    student_out.start()
+    teacher_out.start()
+    for copy in (keep, hidden, student_out, teacher_out):
+        copy.wait()
 
 
 def logits_call(parts, ws, wso, wt, wto):
     vmem = pl.BlockSpec(memory_space=pltpu.VMEM)
+    hbm = pl.BlockSpec(memory_space=pltpu.HBM)
     return pl.pallas_call(
         logits_kernel,
         out_shape=(
@@ -100,30 +116,96 @@
             jax.ShapeDtypeStruct((2 * ROWS, TOK), F32),
             jax.ShapeDtypeStruct((8, TOK), F32),
             jax.ShapeDtypeStruct((DS, TOK), BF16),
-        ),
-        in_specs=[vmem] * 9,
-        out_specs=(vmem,) * 4,
-        scratch_shapes=[pltpu.VMEM((DT, TOK), BF16)],
+            jax.ShapeDtypeStruct((ROWS, DS), BF16),
+        ),
+        in_specs=[vmem] * 8 + [hbm],
+        out_specs=(hbm, hbm, vmem, hbm, hbm),
+        scratch_shapes=[
+            pltpu.VMEM((DS, TOK), BF16),
+            pltpu.VMEM((DT, TOK), BF16),
+            pltpu.VMEM((2 * ROWS, TOK), F32),
+            pltpu.VMEM((2 * ROWS, TOK), F32),
+            pltpu.VMEM((ROWS, DT), BF16),
+            pltpu.SemaphoreType.DMA((5,)),
+        ],
         compiler_params=pltpu.CompilerParams(vmem_limit_bytes=VMEM_LIMIT),
         cost_estimate=pl.CostEstimate(
             flops=2 * 2 * ROWS * TOK * (DS + DT), bytes_accessed=22_000_000, transcendentals=4 * ROWS * TOK
         ),
         name="logits",
-    )(*parts, ws, wso, wt, wto)
+    )(*parts, ws, wso, wto, wt)
+
+
+def merged(stats):
+    top = stats[0][0:2]
+    for s in stats[1:]:
+        top = jnp.maximum(top, s[0:2])
+    totals, cross = jnp.zeros_like(top), jnp.zeros_like(top[0:1])
+    for s in stats:
+        scale = jnp.exp(s[0:2] - top)
+        totals = totals + s[2:4] * scale
+        cross = cross + s[4:5] * scale[1:2]
+    return top, totals, cross
+
+
+def merge_kernel(*refs):
+    top, totals, cross = merged([r[...] for r in refs[:-1]])
+    refs[-1][0:2] = top
+    refs[-1][2:4] = totals
+    refs[-1][4:5] = cross
+    refs[-1][5:8] = jnp.zeros((3, TOK), F32)
+
+
+def merge(stats):
+    vmem = pl.BlockSpec(memory_space=pltpu.VMEM)
+    return pl.pallas_call(
+        merge_kernel,
+        out_shape=jax.ShapeDtypeStruct((8, TOK), F32),
+        in_specs=[vmem] * len(stats),
+        out_specs=vmem,
+        name="merge",
+    )(*stats)
 
 
 CHUNK = 1280
 
 
-def grads_kernel(es_ref, et_ref, coef_ref, ws, wso, g_own, g_oth, o0, o1, o3, o2a, o2b, acc):
+def grads_kernel(
+    s0, s1, s2, s3, local, weight, es_in, et_in, ws, wso,
+    st_out, g_own, g_oth, o0, o1, o3, o2a, o2b, es, et, wsb, acc, esem, wsem,
+):
     _, c, x, y, _ = place()
-    g = (es_ref[...] * coef_ref[0:1] - et_ref[...] * coef_ref[1:2]).astype(BF16)
+    terms = [
+        pltpu.make_async_copy(es_in, es, esem.at[0]),
+        pltpu.make_async_copy(et_in, et, esem.at[1]),
+    ]
+    weights = []
+    for n in range(DS // CHUNK):
+        cols = pl.ds(n * CHUNK, CHUNK)
+        for half, src in enumerate((ws, wso)):
+            weights.append(
+                pltpu.make_async_copy(
+                    src.at[:, cols], wsb.at[pl.ds(half * ROWS, ROWS), cols], wsem.at[2 * n + half]
+                )
+            )
+    for copy in terms + weights:
+        copy.start()
+    top, totals, cross = merged([s0[...], s1[...], s2[...], s3[...]])
+    st_out[0:2] = top
+    st_out[2:4] = totals
+    st_out[4:5] = cross
+    st_out[5:8] = jnp.zeros((3, TOK), F32)
+    coef = weight[0:1] * (jnp.exp(local[0:2] - top) / totals)
+    for copy in terms:
+        copy.wait()
+    g = (es[...] * coef[0:1] - et[...] * coef[1:2]).astype(BF16)
     g_own[...] = g[:ROWS]
     g_oth[...] = g[ROWS:]
     for n in range(DS // CHUNK):
+        weights[2 * n].wait()
+        weights[2 * n + 1].wait()
         cols = slice(n * CHUNK, (n + 1) * CHUNK)
-        part = dot(g[:ROWS], ws[:, cols], ((0,), (0,))) + dot(g[ROWS:], wso[:, cols], ((0,), (0,)))
-        acc[cols] = part.astype(BF16).T
+        acc[cols] = dot(g, wsb[:, cols], ((0,), (0,))).astype(BF16).T
     outs = [(0, o0, 0, range(4)), (1, o1, 0, range(4)), (3, o3, 0, range(4))]
     outs += [(2, o2a, 0, range(2)), (2, o2b, 2, range(2, 4))]
     for k, o, base, lines in outs:
@@ -132,23 +214,33 @@
             o[r - base] = acc[pl.ds(pl.multiple_of(at * NS, NS), NS)]
 
 
-def grads_call(es, et, coef, ws, wso):
+def grads_call(stats, local, weight, es, et, ws, wso):
     vmem = pl.BlockSpec(memory_space=pltpu.VMEM)
+    hbm = pl.BlockSpec(memory_space=pltpu.HBM)
     whole = jax.ShapeDtypeStruct((4, NS, TOK), BF16)
     half = jax.ShapeDtypeStruct((2, NS, TOK), BF16)
     rows = jax.ShapeDtypeStruct((ROWS, TOK), BF16)
     return pl.pallas_call(
         grads_kernel,
-        out_shape=(rows, rows, whole, whole, whole, half, half),
-        in_specs=[vmem] * 5,
-        out_specs=(vmem,) * 7,
-        scratch_shapes=[pltpu.VMEM((DS, TOK), BF16)],
+        out_shape=(
+            jax.ShapeDtypeStruct((8, TOK), F32), rows, rows, whole, whole, whole, half, half,
+        ),
+        in_specs=[vmem] * 6 + [hbm] * 4,
+        out_specs=(vmem,) * 8,
+        scratch_shapes=[
+            pltpu.VMEM((2 * ROWS, TOK), F32),
+            pltpu.VMEM((2 * ROWS, TOK), F32),
+            pltpu.VMEM((2 * ROWS, DS), BF16),
+            pltpu.VMEM((DS, TOK), BF16),
+            pltpu.SemaphoreType.DMA((2,)),
+            pltpu.SemaphoreType.DMA((8,)),
+        ],
         compiler_params=pltpu.CompilerParams(vmem_limit_bytes=VMEM_LIMIT),
         cost_estimate=pl.CostEstimate(
             flops=2 * 2 * ROWS * TOK * DS, bytes_accessed=14_000_000, transcendentals=0
         ),
         name="grads",
-    )(es, et, coef, ws, wso)
+    )(*stats, local, weight, es, et, ws, wso)
 
 
 def head_kernel(g_own, g_got, h_own, h_got, out):
@@ -175,17 +267,6 @@
     )(g_own, g_got, h_own, h_got)
 
 
-def merge(stats):
-    top = stats[0][0:2]
-    for s in stats[1:]:
-        top = jnp.maximum(top, s[0:2])
-    total = jnp.zeros_like(stats[0][2:5])
-    for s in stats:
-        scale = jnp.exp(s[0:2] - top)
-        total = total + s[2:5] * jnp.concatenate([scale, scale[1:2]], axis=0)
-    return jnp.concatenate([top, total, stats[0][5:8]], axis=0)
-
-
 def per_device(student_hidden, teacher_hidden, student_head, teacher_head, row_weight):
     zl, c, x, y, zh = place()
 
@@ -205,14 +286,20 @@
     far_low, far_high = send(before[:2], SECOND[1]), send(after[2:], SECOND[3])
     parts = (line, before, after, far_low, far_high)
 
-    es, et, local, hidden_own = logits_call(
+    es, et, local, hidden_own, student_other = logits_call(
         parts, student_head, student_other, teacher_head, teacher_other
     )
     hidden_got = send(hidden_own, CORE)
 
     stats = merge((local, send(local, PAIR)))
-    for perms in (ZH, FIRST, SECOND):
+    for perms in (ZH, FIRST):
         stats = merge((stats,) + ring(stats, perms))
+    weight = lax.dynamic_index_in_dim(row_weight.reshape(2, 2, 128), c, 1, False).reshape(1, TOK)
+    weight = jnp.broadcast_to(weight, (8, TOK))
+
+    stats, g_own, g_oth, o0, o1, o3, o2a, o2b = grads_call(
+        (stats,) + ring(stats, SECOND), local, weight, es, et, student_head, student_other
+    )
     student_max, teacher_max, student_total, teacher_total, cross = (stats[i] for i in range(5))
     kl_both = (
         cross / teacher_total
@@ -222,16 +309,6 @@
         + jnp.log(student_total)
     )
     kl_rows = lax.dynamic_slice_in_dim(kl_both, zl * 128, 128, 0)
-    weight = lax.dynamic_index_in_dim(row_weight.reshape(2, 2, 128), c, 1, False).reshape(TOK)
-    coef = jnp.stack(
-        [
-            weight * (jnp.exp(local[0] - student_max) / student_total),
-            weight * (jnp.exp(local[1] - teacher_max) / teacher_total),
-        ]
-    )
-    coef = jnp.concatenate([coef, jnp.zeros((6, TOK), F32)], axis=0)
-
-    g_own, g_oth, o0, o1, o3, o2a, o2b = grads_call(es, et, coef, student_head, student_other)
     low, high = send(o2a, SECOND[1]), send(o2b, SECOND[3])
     g_got = send(g_oth, CORE)
     r1 = send(jnp.concatenate([(o1[:2].astype(F32) + low.astype(F32)).astype(BF16), o1[2:]]), SECOND[1])

time: 169 us -> 181 us (1.071)
  Pallas kernels: 17.4 us -> 25.7 us
  local copies, waits for them, and re-layouts: 9.9 us -> 16.7 us
    unnamed x27 -> x47, local copies, waits for them, and re-layouts: 9.58 us -> 16.5 us
    pallas_call x1 -> x4, Pallas kernels: 5.27 us -> 8.57 us  [the longest x1 4.52 us: grads_call(): pl.pallas_call(grads_kernel, out_shape=(jax.ShapeDtypeStruct((8, TOK), F3...]
    pallas_call x1, Pallas kernels: 6.52 us -> 9.22 us  [logits_call(): pl.pallas_call(logits_kernel, out_shape=(jax.ShapeDtypeStruct((2 * ROWS,...]
    pallas_call x1, Pallas kernels: 5.62 us -> 7.87 us  [head_call(): pl.pallas_call(head_kernel, out_shape=jax.ShapeDtypeStruct((ROWS, DS), BF...]
    ppermute x36, starting transfers between devices: 59.7 us -> 57.9 us  [send(): return lax.ppermute(value, AXES, pairs)]
  transfers between devices with their start and end apart: 36 -> 36, of which waited for: 25 -> 24; matrix products, arithmetic and copies ran while one was open for 1% -> 1% of each run, Pallas kernels for 6% -> 9%
where the time goes in v3:
time: 181 us
  waiting for transfers between devices  75.7 us (42%)
  starting transfers between devices  57.9 us (32%)
  Pallas kernels  25.7 us (14%)
  local copies, waits for them, and re-layouts  16.7 us (9%)
  other arithmetic  3.67 us (2%)
    ppermute x36, waiting for transfers between devices, send(): return lax.ppermute(value, AXES, pairs)  75.7 us
    ppermute x36, starting transfers between devices, send(): return lax.ppermute(value, AXES, pairs)  57.9 us
    unnamed x47, local copies, waits for them, and re-layouts  16.5 us
    pallas_call x1, Pallas kernels, logits_call(): pl.pallas_call(logits_kernel, out_shape=(jax.ShapeDtypeStruct((2 * ROWS,...  9.22 us
    pallas_call x1, Pallas kernels, head_call(): pl.pallas_call(head_kernel, out_shape=jax.ShapeDtypeStruct((ROWS, DS), BF...  7.87 us
    pallas_call x1, Pallas kernels, grads_call(): pl.pallas_call(grads_kernel, out_shape=(jax.ShapeDtypeStruct((8, TOK), F3...  4.52 us
    pallas_call x3, Pallas kernels, merge(): pl.pallas_call(merge_kernel, out_shape=jax.ShapeDtypeStruct((8, TOK), F32...  4.05 us
  transfers between devices with their start and end apart: 36, of which 24 were waited for; matrix products, arithmetic and copies ran while one was open for 1% of the time, Pallas kernels for 9%

profile of v3, /device:TPU:2, one launch (start us, length us, event | category | flops | bytes accessed | tf_op | source)
XLA Modules:
  0.0 180.6 jit_solution(10555213070130044765)
XLA Ops:
  6.1 3.3 %collective-permute-start.1 = (bf16[144,256]{1,0:T(8,128)(2,1)S(1)}, bf16[144,256]{1,0:T(8,128)(2,1)S(1)}, u32[]{:S(2)}, u32[]{:S(2)}) collective-permute-start(bf16[144,256]{1,0:T(8,128)(2,1)S(1)} %pad_maximum_fusion.3), channel_id=1, source_target_pairs={{0,1},{1,2},{2,3},{3,0},{4,5},{5,6},{6,7},{7,4},{8,9},{9,10},{10,1... | collective-permute-start | bytes 221192 | tf_op jit(solution)/shard_map/ppermute | solution.py:44
  9.5 5.4 %collective-permute-start.2 = (bf16[144,256]{1,0:T(8,128)(2,1)S(1)}, bf16[144,256]{1,0:T(8,128)(2,1)S(1)}, u32[]{:S(2)}, u32[]{:S(2)}) collective-permute-start(bf16[144,256]{1,0:T(8,128)(2,1)S(1)} %pad_maximum_fusion.3), channel_id=1, source_target_pairs={{0,2},{1,3},{2,0},{3,1},{4,6},{5,7},{6,4},{7,5},{8,10},{9,11},{10,... | collective-permute-start | bytes 221192 | tf_op jit(solution)/shard_map/ppermute | solution.py:44
  14.9 2.7 %collective-permute-start.3 = (bf16[144,256]{1,0:T(8,128)(2,1)S(1)}, bf16[144,256]{1,0:T(8,128)(2,1)S(1)}, u32[]{:S(2)}, u32[]{:S(2)}) collective-permute-start(bf16[144,256]{1,0:T(8,128)(2,1)S(1)} %pad_maximum_fusion.3), channel_id=1, source_target_pairs={{0,3},{1,0},{2,1},{3,2},{4,7},{5,4},{6,5},{7,6},{8,11},{9,8},{10,9... | collective-permute-start | bytes 221192 | tf_op jit(solution)/shard_map/ppermute | solution.py:44
  28.7 3.1 %collective-permute-done.5 = bf16[576,256]{1,0:T(8,128)(2,1)S(1)} collective-permute-done((bf16[576,256]{1,0:T(8,128)(2,1)S(1)}, bf16[576,256]{1,0:T(8,128)(2,1)S(1)}, u32[]{:S(2)}, u32[]{:S(2)}) %collective-permute-start.5) | collective-permute-done | bytes 294944 | tf_op jit(solution)/shard_map/ppermute | solution.py:44
  31.8 4.6 %collective-permute-done.6 = bf16[576,256]{1,0:T(8,128)(2,1)S(1)} collective-permute-done((bf16[576,256]{1,0:T(8,128)(2,1)S(1)}, bf16[576,256]{1,0:T(8,128)(2,1)S(1)}, u32[]{:S(2)}, u32[]{:S(2)}) %collective-permute-start.6) | collective-permute-done | bytes 294944 | tf_op jit(solution)/shard_map/ppermute | solution.py:44
  36.6 3.7 %collective-permute-start.8 = (bf16[4,576,256]{2,1,0:T(8,128)(2,1)S(1)}, bf16[4,576,256]{2,1,0:T(8,128)(2,1)S(1)}, u32[]{:S(2)}, u32[]{:S(2)}) collective-permute-start(bf16[4,576,256]{2,1,0:T(8,128)(2,1)S(1)} %pad_maximum_fusion.t0), channel_id=1, source_target_pairs={{0,12},{1,13},{2,14},{3,15},{4,0},{5,1},{6,2},{7,3},{8,4},{9,5},{1... | collective-permute-start | bytes 3538952 | tf_op jit(solution)/shard_map/ppermute | solution.py:44
  40.4 13.7 %collective-permute-done.8.t3 = bf16[4,576,256]{2,1,0:T(8,128)(2,1)S(1)} collective-permute-done((bf16[4,576,256]{2,1,0:T(8,128)(2,1)S(1)}, bf16[4,576,256]{2,1,0:T(8,128)(2,1)S(1)}, u32[]{:S(2)}, u32[]{:S(2)}) %collective-permute-start.8) | collective-permute-done | bytes 1179680 | tf_op jit(solution)/shard_map/ppermute | solution.py:44
  54.1 3.8 %collective-permute-start.10 = (bf16[2,576,256]{2,1,0:T(8,128)(2,1)S(1)}, bf16[2,576,256]{2,1,0:T(8,128)(2,1)S(1)}, u32[]{:S(2)}, u32[]{:S(2)}) collective-permute-start(bf16[2,576,256]{2,1,0:T(8,128)(2,1)S(1)} %slice.112), channel_id=1, source_target_pairs={{0,12},{1,13},{2,14},{3,15},{4,0},{5,1},{6,2},{7,3},{8,4},{9,5},{1... | collective-permute-start | bytes 1769480 | tf_op jit(solution)/shard_map/ppermute | solution.py:44
  58.2 7.1 %collective-permute-done.10.t2b = bf16[2,576,256]{2,1,0:T(8,128)(2,1)S(1)} collective-permute-done((bf16[2,576,256]{2,1,0:T(8,128)(2,1)S(1)}, bf16[2,576,256]{2,1,0:T(8,128)(2,1)S(1)}, u32[]{:S(2)}, u32[]{:S(2)}) %collective-permute-start.10) | collective-permute-done | bytes 589856 | tf_op jit(solution)/shard_map/ppermute | solution.py:44
  65.3 4.0 %collective-permute-done.9.t2a = bf16[2,576,256]{2,1,0:T(8,128)(2,1)S(1)} collective-permute-done((bf16[2,576,256]{2,1,0:T(8,128)(2,1)S(1)}, bf16[2,576,256]{2,1,0:T(8,128)(2,1)S(1)}, u32[]{:S(2)}, u32[]{:S(2)}) %collective-permute-start.9) | collective-permute-done | bytes 589856 | tf_op jit(solution)/shard_map/ppermute | solution.py:44
  71.2 9.2 %logits.1 = (f32[768,256]{1,0:T(8,128)S(1)}, f32[768,256]{1,0:T(8,128)S(1)}, f32[8,256]{1,0:T(8,128)S(1)}, bf16[5120,256]{1,0:T(8,128)(2,1)}, bf16[384,5120]{1,0:T(8,128)(2,1)S(1)}) custom-call(bf16[4,576,256]{2,1,0:T(8,128)(2,1)S(1)} %pad_maximum_fusion.t0, bf16[4,576,256]{2,1,0:T(8,128)(2,1)S(1)} %collective-permute-done.7.t1, ...), custom_call_target="tpu_custom_call" | custom-call | flops 3623878656 | bytes 22000000 | tf_op jit(solution)/shard_map/logits/pallas_call | solution.py:112
  84.2 3.6 %collective-permute-done.13.refs_1_ = f32[8,256]{1,0:T(8,128)S(1)} collective-permute-done((f32[8,256]{1,0:T(8,128)S(1)}, f32[8,256]{1,0:T(8,128)S(1)}, u32[]{:S(2)}, u32[]{:S(2)}) %collective-permute-start.13) | collective-permute-done | bytes 8224 | tf_op jit(solution)/shard_map/ppermute | solution.py:44
  91.9 2.7 %collective-permute-start.15 = (f32[8,256]{1,0:T(8,128)}, f32[8,256]{1,0:T(8,128)S(1)}, u32[]{:S(2)}, u32[]{:S(2)}) collective-permute-start(f32[8,256]{1,0:T(8,128)} %merge.3.refs_0_), channel_id=1, source_target_pairs={{0,2},{1,3},{2,0},{3,1},{4,6},{5,7},{6,4},{7,5},{8,10},{9,11},{10,... | collective-permute-start | bytes 24584 | tf_op jit(solution)/shard_map/ppermute | solution.py:44
  96.4 3.3 %collective-permute-done.15.refs_2_ = f32[8,256]{1,0:T(8,128)S(1)} collective-permute-done((f32[8,256]{1,0:T(8,128)}, f32[8,256]{1,0:T(8,128)S(1)}, u32[]{:S(2)}, u32[]{:S(2)}) %collective-permute-start.15) | collective-permute-done | bytes 8224 | tf_op jit(solution)/shard_map/ppermute | solution.py:44
  106.1 2.9 %collective-permute-done.18.refs_2_ = f32[8,256]{1,0:T(8,128)S(1)} collective-permute-done((f32[8,256]{1,0:T(8,128)}, f32[8,256]{1,0:T(8,128)S(1)}, u32[]{:S(2)}, u32[]{:S(2)}) %collective-permute-start.18) | collective-permute-done | bytes 8224 | tf_op jit(solution)/shard_map/ppermute | solution.py:44
  125.5 4.5 %grads.1 = (f32[8,256]{1,0:T(8,128)S(1)}, bf16[384,256]{1,0:T(8,128)(2,1)S(1)}, bf16[384,256]{1,0:T(8,128)(2,1)S(1)}, bf16[4,320,256]{2,1,0:T(8,128)(2,1)S(1)}, ...) custom-call(f32[8,256]{1,0:T(8,128)S(1)} %copy-done.12, ...), custom_call_target="tpu_custom_call" | custom-call | flops 2013265920 | bytes 14000000 | tf_op jit(solution)/shard_map/grads/pallas_call | solution.py:223
  130.0 2.7 %collective-permute-start.25 = (bf16[2,320,256]{2,1,0:T(8,128)(2,1)S(1)}, bf16[2,320,256]{2,1,0:T(8,128)(2,1)S(1)}, u32[]{:S(2)}, u32[]{:S(2)}) collective-permute-start(bf16[2,320,256]{2,1,0:T(8,128)(2,1)S(1)} %get-tuple-element.28), channel_id=1, source_target_pairs={{0,12},{1,13},{2,14},{3,15},{4,0},{5,1},{6,2},{7,3},{8,4},{9,5},{1... | collective-permute-start | bytes 983048 | tf_op jit(solution)/shard_map/ppermute | solution.py:44
  132.8 4.4 %collective-permute-done.25 = bf16[2,320,256]{2,1,0:T(8,128)(2,1)S(1)} collective-permute-done((bf16[2,320,256]{2,1,0:T(8,128)(2,1)S(1)}, bf16[2,320,256]{2,1,0:T(8,128)(2,1)S(1)}, u32[]{:S(2)}, u32[]{:S(2)}) %collective-permute-start.25) | collective-permute-done | bytes 327712 | tf_op jit(solution)/shard_map/ppermute | solution.py:44
  137.4 3.8 %collective-permute-start.26 = (bf16[4,320,256]{2,1,0:T(8,128)(2,1)S(1)}, bf16[4,320,256]{2,1,0:T(8,128)(2,1)S(1)}, u32[]{:S(2)}, u32[]{:S(2)}) collective-permute-start(bf16[4,320,256]{2,1,0:T(8,128)(2,1)S(1)} %pad_maximum_fusion.2), channel_id=1, source_target_pairs={{0,12},{1,13},{2,14},{3,15},{4,0},{5,1},{6,2},{7,3},{8,4},{9,5},{1... | collective-permute-start | bytes 1966088 | tf_op jit(solution)/shard_map/ppermute | solution.py:44
  143.0 7.9 %head.1 = bf16[384,5120]{1,0:T(8,128)(2,1)} custom-call(bf16[384,256]{1,0:T(8,128)(2,1)S(1)} %get-tuple-element.29.g_own, bf16[384,256]{1,0:T(8,128)(2,1)S(1)} %collective-permute-done.27.g_got, bf16[5120,256]{1,0:T(8,128)(2,1)} %get-tuple-element.31.h_own, bf16[5120,256]{1,0:T(8,128)(2,1)S(1)} %collective-permute-done.28.h_got), custom_call_target="tpu_custom_call" | custom-call | flops 2013265920 | bytes 10000000 | tf_op jit(solution)/shard_map/head/pallas_call | solution.py:256
  160.1 3.2 %collective-permute-done.31 = bf16[320,256]{1,0:T(8,128)(2,1)S(1)} collective-permute-done((bf16[320,256]{1,0:T(8,128)(2,1)S(1)}, bf16[320,256]{1,0:T(8,128)(2,1)S(1)}, u32[]{:S(2)}, u32[]{:S(2)}) %collective-permute-start.31) | collective-permute-done | bytes 163872 | tf_op jit(solution)/shard_map/ppermute | solution.py:44
  164.7 3.0 %collective-permute-start.33 = (bf16[80,256]{1,0:T(8,128)(2,1)S(1)}, bf16[80,256]{1,0:T(8,128)(2,1)S(1)}, u32[]{:S(2)}, u32[]{:S(2)}) collective-permute-start(bf16[80,256]{1,0:T(8,128)(2,1)S(1)} %get-tuple-element.45), channel_id=1, source_target_pairs={{0,3},{1,0},{2,1},{3,2},{4,7},{5,4},{6,5},{7,6},{8,11},{9,8},{10,9... | collective-permute-start | bytes 122888 | tf_op jit(solution)/shard_map/ppermute | solution.py:44
  170.1 5.8 %collective-permute-done.34 = bf16[80,256]{1,0:T(8,128)(2,1)S(1)} collective-permute-done((bf16[80,256]{1,0:T(8,128)(2,1)S(1)}, bf16[80,256]{1,0:T(8,128)(2,1)S(1)}, u32[]{:S(2)}, u32[]{:S(2)}) %collective-permute-start.34) | collective-permute-done | bytes 40992 | tf_op jit(solution)/shard_map/ppermute | solution.py:44
  176.5 3.5 %collective-permute-done.35 = f32[80,128]{1,0:T(8,128)S(1)} collective-permute-done((f32[80,128]{1,0:T(8,128)S(1)}, f32[80,128]{1,0:T(8,128)S(1)}, u32[]{:S(2)}, u32[]{:S(2)}) %collective-permute-start.35) | collective-permute-done | bytes 40992 | tf_op jit(solution)/shard_map/ppermute | solution.py:44
  (128 shorter events, 67.7 us)
Async XLA Ops:
  6.1 11.9 %collective-permute-start.1 = (bf16[144,256]{1,0:T(8,128)(2,1)S(1)}, bf16[144,256]{1,0:T(8,128)(2,1)S(1)}, u32[]{:S(2)}, u32[]{:S(2)}) collective-permute-start(bf16[144,256]{1,0:T(8,128)(2,1)S(1)} %pad_maximum_fusion.3), channel_id=1, source_target_pairs={{0,1},{1,2},{2,3},{3,0},{4,5},{5,6},{6,7},{7,4},{8,9},{9,10},{10,1... | collective-permute-start | bytes 221192 | tf_op jit(solution)/shard_map/ppermute | solution.py:44
  9.5 9.9 %collective-permute-start.2 = (bf16[144,256]{1,0:T(8,128)(2,1)S(1)}, bf16[144,256]{1,0:T(8,128)(2,1)S(1)}, u32[]{:S(2)}, u32[]{:S(2)}) collective-permute-start(bf16[144,256]{1,0:T(8,128)(2,1)S(1)} %pad_maximum_fusion.3), channel_id=1, source_target_pairs={{0,2},{1,3},{2,0},{3,1},{4,6},{5,7},{6,4},{7,5},{8,10},{9,11},{10,... | collective-permute-start | bytes 221192 | tf_op jit(solution)/shard_map/ppermute | solution.py:44
  14.9 6.8 %collective-permute-start.3 = (bf16[144,256]{1,0:T(8,128)(2,1)S(1)}, bf16[144,256]{1,0:T(8,128)(2,1)S(1)}, u32[]{:S(2)}, u32[]{:S(2)}) collective-permute-start(bf16[144,256]{1,0:T(8,128)(2,1)S(1)} %pad_maximum_fusion.3), channel_id=1, source_target_pairs={{0,3},{1,0},{2,1},{3,2},{4,7},{5,4},{6,5},{7,6},{8,11},{9,8},{10,9... | collective-permute-start | bytes 221192 | tf_op jit(solution)/shard_map/ppermute | solution.py:44
  17.6 51.7 %collective-permute-start.11 = (bf16[384,5120]{1,0:T(8,128)(2,1)}, bf16[384,5120]{1,0:T(8,128)(2,1)}, u32[]{:S(2)}, u32[]{:S(2)}) collective-permute-start(bf16[384,5120]{1,0:T(8,128)(2,1)} %ws.3), channel_id=1, source_target_pairs={{0,64},{1,65},{2,66},{3,67},{4,68},{5,69},{6,70},{7,71},{8,72},{9,... | collective-permute-start | bytes 11796488 | tf_op jit(solution)/shard_map/ppermute | solution.py:44
  17.6 51.7 %collective-permute-start.12 = (bf16[384,4096]{1,0:T(8,128)(2,1)}, bf16[384,4096]{1,0:T(8,128)(2,1)S(1)}, u32[]{:S(2)}, u32[]{:S(2)}) collective-permute-start(bf16[384,4096]{1,0:T(8,128)(2,1)} %wt.1), channel_id=1, source_target_pairs={{0,64},{1,65},{2,66},{3,67},{4,68},{5,69},{6,70},{7,71},{8,72},{9,... | collective-permute-start | bytes 9437192 | tf_op jit(solution)/shard_map/ppermute | solution.py:44
  21.9 6.8 %collective-permute-start.4 = (bf16[576,256]{1,0:T(8,128)(2,1)S(1)}, bf16[576,256]{1,0:T(8,128)(2,1)S(1)}, u32[]{:S(2)}, u32[]{:S(2)}) collective-permute-start(bf16[576,256]{1,0:T(8,128)(2,1)S(1)} %slice_dynamic-update-slice_fusion.4), channel_id=1, source_target_pairs={{0,16},{1,17},{2,18},{3,19},{4,20},{5,21},{6,22},{7,23},{8,24},{9,... | collective-permute-start | bytes 884744 | tf_op jit(solution)/shard_map/ppermute | solution.py:44
  23.5 8.3 %collective-permute-start.5 = (bf16[576,256]{1,0:T(8,128)(2,1)S(1)}, bf16[576,256]{1,0:T(8,128)(2,1)S(1)}, u32[]{:S(2)}, u32[]{:S(2)}) collective-permute-start(bf16[576,256]{1,0:T(8,128)(2,1)S(1)} %slice_dynamic-update-slice_fusion.4), channel_id=1, source_target_pairs={{0,32},{1,33},{2,34},{3,35},{4,36},{5,37},{6,38},{7,39},{8,40},{9,... | collective-permute-start | bytes 884744 | tf_op jit(solution)/shard_map/ppermute | solution.py:44
  24.6 11.9 %collective-permute-start.6 = (bf16[576,256]{1,0:T(8,128)(2,1)S(1)}, bf16[576,256]{1,0:T(8,128)(2,1)S(1)}, u32[]{:S(2)}, u32[]{:S(2)}) collective-permute-start(bf16[576,256]{1,0:T(8,128)(2,1)S(1)} %slice_dynamic-update-slice_fusion.4), channel_id=1, source_target_pairs={{0,48},{1,49},{2,50},{3,51},{4,52},{5,53},{6,54},{7,55},{8,56},{9,... | collective-permute-start | bytes 884744 | tf_op jit(solution)/shard_map/ppermute | solution.py:44
  36.6 17.4 %collective-permute-start.8 = (bf16[4,576,256]{2,1,0:T(8,128)(2,1)S(1)}, bf16[4,576,256]{2,1,0:T(8,128)(2,1)S(1)}, u32[]{:S(2)}, u32[]{:S(2)}) collective-permute-start(bf16[4,576,256]{2,1,0:T(8,128)(2,1)S(1)} %pad_maximum_fusion.t0), channel_id=1, source_target_pairs={{0,12},{1,13},{2,14},{3,15},{4,0},{5,1},{6,2},{7,3},{8,4},{9,5},{1... | collective-permute-start | bytes 3538952 | tf_op jit(solution)/shard_map/ppermute | solution.py:44
  40.3 17.5 %collective-permute-start.7 = (bf16[4,576,256]{2,1,0:T(8,128)(2,1)S(1)}, bf16[4,576,256]{2,1,0:T(8,128)(2,1)S(1)}, u32[]{:S(2)}, u32[]{:S(2)}) collective-permute-start(bf16[4,576,256]{2,1,0:T(8,128)(2,1)S(1)} %pad_maximum_fusion.t0), channel_id=1, source_target_pairs={{0,4},{1,5},{2,6},{3,7},{4,8},{5,9},{6,10},{7,11},{8,12},{9,13},{1... | collective-permute-start | bytes 3538952 | tf_op jit(solution)/shard_map/ppermute | solution.py:44
  54.1 11.2 %collective-permute-start.10 = (bf16[2,576,256]{2,1,0:T(8,128)(2,1)S(1)}, bf16[2,576,256]{2,1,0:T(8,128)(2,1)S(1)}, u32[]{:S(2)}, u32[]{:S(2)}) collective-permute-start(bf16[2,576,256]{2,1,0:T(8,128)(2,1)S(1)} %slice.112), channel_id=1, source_target_pairs={{0,12},{1,13},{2,14},{3,15},{4,0},{5,1},{6,2},{7,3},{8,4},{9,5},{1... | collective-permute-start | bytes 1769480 | tf_op jit(solution)/shard_map/ppermute | solution.py:44
  57.9 11.4 %collective-permute-start.9 = (bf16[2,576,256]{2,1,0:T(8,128)(2,1)S(1)}, bf16[2,576,256]{2,1,0:T(8,128)(2,1)S(1)}, u32[]{:S(2)}, u32[]{:S(2)}) collective-permute-start(bf16[2,576,256]{2,1,0:T(8,128)(2,1)S(1)} %slice.111), channel_id=1, source_target_pairs={{0,4},{1,5},{2,6},{3,7},{4,8},{5,9},{6,10},{7,11},{8,12},{9,13},{1... | collective-permute-start | bytes 1769480 | tf_op jit(solution)/shard_map/ppermute | solution.py:44
  84.2 58.8 %collective-permute-start.28 = (bf16[5120,256]{1,0:T(8,128)(2,1)}, bf16[5120,256]{1,0:T(8,128)(2,1)S(1)}, u32[]{:S(2)}, u32[]{:S(2)}) collective-permute-start(bf16[5120,256]{1,0:T(8,128)(2,1)} %get-tuple-element.31.h_own), channel_id=1, source_target_pairs={{0,64},{1,65},{2,66},{3,67},{4,68},{5,69},{6,70},{7,71},{8,72},{9,... | collective-permute-start | bytes 7864328 | tf_op jit(solution)/shard_map/ppermute | solution.py:44
  89.7 6.6 %collective-permute-start.14 = (f32[8,256]{1,0:T(8,128)}, f32[8,256]{1,0:T(8,128)S(1)}, u32[]{:S(2)}, u32[]{:S(2)}) collective-permute-start(f32[8,256]{1,0:T(8,128)} %merge.3.refs_0_), channel_id=1, source_target_pairs={{0,1},{1,2},{2,3},{3,0},{4,5},{5,6},{6,7},{7,4},{8,9},{9,10},{10,1... | collective-permute-start | bytes 24584 | tf_op jit(solution)/shard_map/ppermute | solution.py:44
  91.9 7.8 %collective-permute-start.15 = (f32[8,256]{1,0:T(8,128)}, f32[8,256]{1,0:T(8,128)S(1)}, u32[]{:S(2)}, u32[]{:S(2)}) collective-permute-start(f32[8,256]{1,0:T(8,128)} %merge.3.refs_0_), channel_id=1, source_target_pairs={{0,2},{1,3},{2,0},{3,1},{4,6},{5,7},{6,4},{7,5},{8,10},{9,11},{10,... | collective-permute-start | bytes 24584 | tf_op jit(solution)/shard_map/ppermute | solution.py:44
  130.0 7.3 %collective-permute-start.25 = (bf16[2,320,256]{2,1,0:T(8,128)(2,1)S(1)}, bf16[2,320,256]{2,1,0:T(8,128)(2,1)S(1)}, u32[]{:S(2)}, u32[]{:S(2)}) collective-permute-start(bf16[2,320,256]{2,1,0:T(8,128)(2,1)S(1)} %get-tuple-element.28), channel_id=1, source_target_pairs={{0,12},{1,13},{2,14},{3,15},{4,0},{5,1},{6,2},{7,3},{8,4},{9,5},{1... | collective-permute-start | bytes 983048 | tf_op jit(solution)/shard_map/ppermute | solution.py:44
  132.7 8.5 %collective-permute-start.23 = (bf16[2,320,256]{2,1,0:T(8,128)(2,1)S(1)}, bf16[2,320,256]{2,1,0:T(8,128)(2,1)S(1)}, u32[]{:S(2)}, u32[]{:S(2)}) collective-permute-start(bf16[2,320,256]{2,1,0:T(8,128)(2,1)S(1)} %get-tuple-element.26), channel_id=1, source_target_pairs={{0,4},{1,5},{2,6},{3,7},{4,8},{5,9},{6,10},{7,11},{8,12},{9,13},{1... | collective-permute-start | bytes 983048 | tf_op jit(solution)/shard_map/ppermute | solution.py:44
  137.4 13.4 %collective-permute-start.26 = (bf16[4,320,256]{2,1,0:T(8,128)(2,1)S(1)}, bf16[4,320,256]{2,1,0:T(8,128)(2,1)S(1)}, u32[]{:S(2)}, u32[]{:S(2)}) collective-permute-start(bf16[4,320,256]{2,1,0:T(8,128)(2,1)S(1)} %pad_maximum_fusion.2), channel_id=1, source_target_pairs={{0,12},{1,13},{2,14},{3,15},{4,0},{5,1},{6,2},{7,3},{8,4},{9,5},{1... | collective-permute-start | bytes 1966088 | tf_op jit(solution)/shard_map/ppermute | solution.py:44
  141.3 11.9 %collective-permute-start.24 = (bf16[4,320,256]{2,1,0:T(8,128)(2,1)S(1)}, bf16[4,320,256]{2,1,0:T(8,128)(2,1)S(1)}, u32[]{:S(2)}, u32[]{:S(2)}) collective-permute-start(bf16[4,320,256]{2,1,0:T(8,128)(2,1)S(1)} %pad_maximum_fusion.1), channel_id=1, source_target_pairs={{0,4},{1,5},{2,6},{3,7},{4,8},{5,9},{6,10},{7,11},{8,12},{9,13},{1... | collective-permute-start | bytes 1966088 | tf_op jit(solution)/shard_map/ppermute | solution.py:44
  153.6 5.4 %collective-permute-start.29 = (bf16[320,256]{1,0:T(8,128)(2,1)S(1)}, bf16[320,256]{1,0:T(8,128)(2,1)S(1)}, u32[]{:S(2)}, u32[]{:S(2)}) collective-permute-start(bf16[320,256]{1,0:T(8,128)(2,1)S(1)} %get-tuple-element.37), channel_id=1, source_target_pairs={{0,16},{1,17},{2,18},{3,19},{4,20},{5,21},{6,22},{7,23},{8,24},{9,... | collective-permute-start | bytes 491528 | tf_op jit(solution)/shard_map/ppermute | solution.py:44
  153.7 6.5 %collective-permute-start.30 = (bf16[320,256]{1,0:T(8,128)(2,1)S(1)}, bf16[320,256]{1,0:T(8,128)(2,1)S(1)}, u32[]{:S(2)}, u32[]{:S(2)}) collective-permute-start(bf16[320,256]{1,0:T(8,128)(2,1)S(1)} %get-tuple-element.39), channel_id=1, source_target_pairs={{0,48},{1,49},{2,50},{3,51},{4,52},{5,53},{6,54},{7,55},{8,56},{9,... | collective-permute-start | bytes 491528 | tf_op jit(solution)/shard_map/ppermute | solution.py:44
  155.7 7.7 %collective-permute-start.31 = (bf16[320,256]{1,0:T(8,128)(2,1)S(1)}, bf16[320,256]{1,0:T(8,128)(2,1)S(1)}, u32[]{:S(2)}, u32[]{:S(2)}) collective-permute-start(bf16[320,256]{1,0:T(8,128)(2,1)S(1)} %get-tuple-element.38), channel_id=1, source_target_pairs={{0,32},{1,33},{2,34},{3,35},{4,36},{5,37},{6,38},{7,39},{8,40},{9,... | collective-permute-start | bytes 491528 | tf_op jit(solution)/shard_map/ppermute | solution.py:44
  163.5 6.6 %collective-permute-start.32 = (bf16[80,256]{1,0:T(8,128)(2,1)S(1)}, bf16[80,256]{1,0:T(8,128)(2,1)S(1)}, u32[]{:S(2)}, u32[]{:S(2)}) collective-permute-start(bf16[80,256]{1,0:T(8,128)(2,1)S(1)} %get-tuple-element.43), channel_id=1, source_target_pairs={{0,1},{1,2},{2,3},{3,0},{4,5},{5,6},{6,7},{7,4},{8,9},{9,10},{10,1... | collective-permute-start | bytes 122888 | tf_op jit(solution)/shard_map/ppermute | solution.py:44
  167.7 8.1 %collective-permute-start.34 = (bf16[80,256]{1,0:T(8,128)(2,1)S(1)}, bf16[80,256]{1,0:T(8,128)(2,1)S(1)}, u32[]{:S(2)}, u32[]{:S(2)}) collective-permute-start(bf16[80,256]{1,0:T(8,128)(2,1)S(1)} %get-tuple-element.44), channel_id=1, source_target_pairs={{0,2},{1,3},{2,0},{3,1},{4,6},{5,7},{6,4},{7,5},{8,10},{9,11},{10,... | collective-permute-start | bytes 122888 | tf_op jit(solution)/shard_map/ppermute | solution.py:44
  (32 other events, 226.2 us)

commit v4 on v2

--- a/solution.py
+++ b/solution.py
@@ -9,7 +9,7 @@
 ROWS = 384
 TOK = 256
 NS, NT = 320, 256
-AXES = ("pipe", "vocab")
+AXES = ("zl", "c", "x", "y", "zh")
 F32, BF16 = jnp.float32, jnp.bfloat16
 VMEM_LIMIT = 20 * 1024 * 1024
 
@@ -50,8 +50,7 @@
 
 
 def place():
-    p, v = lax.axis_index("pipe"), lax.axis_index("vocab")
-    return p >> 1, p & 1, v >> 4, (v >> 2) & 3, v & 3
+    return tuple(lax.axis_index(a) for a in AXES)
 
 
 def block_at(c, x, y, first, second):
@@ -115,9 +114,18 @@
 CHUNK = 1280
 
 
-def grads_kernel(es_ref, et_ref, coef_ref, ws, wso, g_own, g_oth, o0, o1, o3, o2a, o2b, acc):
-    _, c, x, y, _ = place()
-    g = (es_ref[...] * coef_ref[0:1] - et_ref[...] * coef_ref[1:2]).astype(BF16)
+def grads_kernel(
+    stats, local, weights, es_ref, et_ref, ws, wso, kl_ref, g_own, g_oth, o0, o1, o3, o2a, o2b, acc
+):
+    zl, c, x, y, _ = place()
+    top, totals = stats[0:2], stats[2:4]
+    kl = stats[4:5] / totals[1:2] - top[1:2] - jnp.log(totals[1:2]) + top[0:1] + jnp.log(totals[0:1])
+    kl_ref[...] = jnp.where(zl == 0, kl[:, :128], kl[:, 128:])
+    weight = jnp.concatenate(
+        [jnp.where(c == 0, weights[i : i + 1], weights[i + 1 : i + 2]) for i in (0, 2)], axis=1
+    )
+    coef = weight * (jnp.exp(local[0:2] - top) / totals)
+    g = (es_ref[...] * coef[0:1] - et_ref[...] * coef[1:2]).astype(BF16)
     g_own[...] = g[:ROWS]
     g_oth[...] = g[ROWS:]
     for n in range(DS // CHUNK):
@@ -132,23 +140,23 @@
             o[r - base] = acc[pl.ds(pl.multiple_of(at * NS, NS), NS)]
 
 
-def grads_call(es, et, coef, ws, wso):
+def grads_call(stats, local, weights, es, et, ws, wso):
     vmem = pl.BlockSpec(memory_space=pltpu.VMEM)
     whole = jax.ShapeDtypeStruct((4, NS, TOK), BF16)
     half = jax.ShapeDtypeStruct((2, NS, TOK), BF16)
     rows = jax.ShapeDtypeStruct((ROWS, TOK), BF16)
     return pl.pallas_call(
         grads_kernel,
-        out_shape=(rows, rows, whole, whole, whole, half, half),
-        in_specs=[vmem] * 5,
-        out_specs=(vmem,) * 7,
+        out_shape=(jax.ShapeDtypeStruct((1, 128), F32), rows, rows, whole, whole, whole, half, half),
+        in_specs=[vmem] * 7,
+        out_specs=(vmem,) * 8,
         scratch_shapes=[pltpu.VMEM((DS, TOK), BF16)],
         compiler_params=pltpu.CompilerParams(vmem_limit_bytes=VMEM_LIMIT),
         cost_estimate=pl.CostEstimate(
             flops=2 * 2 * ROWS * TOK * DS, bytes_accessed=14_000_000, transcendentals=0
         ),
         name="grads",
-    )(es, et, coef, ws, wso)
+    )(stats, local, weights, es, et, ws, wso)
 
 
 def head_kernel(g_own, g_got, h_own, h_got, out):
@@ -187,19 +195,13 @@
 
 
 def per_device(student_hidden, teacher_hidden, student_head, teacher_head, row_weight):
-    zl, c, x, y, zh = place()
-
     teacher_other = send(teacher_head, CORE)
     student_other = send(student_head, CORE)
 
     mine = jnp.concatenate([student_hidden.T, teacher_hidden.T], axis=0)
-    pair = send(mine, PAIR)
-    both = jnp.concatenate(
-        [jnp.where(zl == 0, mine, pair), jnp.where(zl == 0, pair, mine)], axis=1
-    )
-    around = (both,) + ring(both, ZH)
-    ordered = [lax.select_n((zh - q) & 3, *around) for q in range(4)]
-    block = jnp.concatenate([o[:80] for o in ordered] + [o[80:] for o in ordered], axis=0)
+    along = lax.all_to_all(jnp.broadcast_to(mine, (8, 144, 128)), ("zl", "zh"), 0, 0)
+    along = jnp.concatenate([along[:4], along[4:]], axis=2)
+    block = jnp.concatenate([along[:, :80].reshape(NS, TOK), along[:, 80:].reshape(NT, TOK)], axis=0)
     line = jnp.stack((block,) + ring(block, FIRST))
     before, after = send(line, SECOND[1]), send(line, SECOND[3])
     far_low, far_high = send(before[:2], SECOND[1]), send(after[2:], SECOND[3])
@@ -213,25 +215,9 @@
     stats = merge((local, send(local, PAIR)))
     for perms in (ZH, FIRST, SECOND):
         stats = merge((stats,) + ring(stats, perms))
-    student_max, teacher_max, student_total, teacher_total, cross = (stats[i] for i in range(5))
-    kl_both = (
-        cross / teacher_total
-        - teacher_max
-        - jnp.log(teacher_total)
-        + student_max
-        + jnp.log(student_total)
-    )
-    kl_rows = lax.dynamic_slice_in_dim(kl_both, zl * 128, 128, 0)
-    weight = lax.dynamic_index_in_dim(row_weight.reshape(2, 2, 128), c, 1, False).reshape(TOK)
-    coef = jnp.stack(
-        [
-            weight * (jnp.exp(local[0] - student_max) / student_total),
-            weight * (jnp.exp(local[1] - teacher_max) / teacher_total),
-        ]
-    )
-    coef = jnp.concatenate([coef, jnp.zeros((6, TOK), F32)], axis=0)
-
-    g_own, g_oth, o0, o1, o3, o2a, o2b = grads_call(es, et, coef, student_head, student_other)
+    kl_rows, g_own, g_oth, o0, o1, o3, o2a, o2b = grads_call(
+        stats, local, row_weight.reshape(4, 128), es, et, student_head, student_other
+    )
     low, high = send(o2a, SECOND[1]), send(o2b, SECOND[3])
     g_got = send(g_oth, CORE)
     r1 = send(jnp.concatenate([(o1[:2].astype(F32) + low.astype(F32)).astype(BF16), o1[2:]]), SECOND[1])
@@ -241,30 +227,20 @@
 
     sums = o0.astype(F32) + (r1.astype(F32) + r3.astype(F32))
     r1, r3, r2 = (send(sums[k].astype(BF16), FIRST[k]) for k in (1, 3, 2))
-    sums = (sums[0] + (r1.astype(F32) + r3.astype(F32)) + r2.astype(F32)).reshape(4, 80, TOK)
-    narrow = sums.astype(BF16)
-    r1, r3, r2 = (
-        send(lax.dynamic_index_in_dim(narrow, (zh + k) & 3, 0, False), ZH[k]) for k in (1, 3, 2)
-    )
-    sums = lax.dynamic_index_in_dim(sums, zh, 0, False) + (r1.astype(F32) + r3.astype(F32)) + r2.astype(F32)
-    low, high = sums[:, :128], sums[:, 128:]
-    got = send(jnp.where(zl == 0, high, low), PAIR)
-    hidden_grad = (jnp.where(zl == 0, low, high) + got).T
-    return (kl_rows, hidden_grad, head_grad)
+    sums = sums[0] + (r1.astype(F32) + r3.astype(F32)) + r2.astype(F32)
+    sums = jnp.concatenate([sums[:, :128], sums[:, 128:]], axis=0).reshape(8, 80, 128)
+    hidden_grad = jnp.sum(lax.all_to_all(sums, ("zl", "zh"), 0, 0), axis=0).T
+    return (kl_rows.reshape(128), hidden_grad, head_grad)
 
 
 def solution(mesh):
-    placed = (
-        P("pipe", "vocab"),
-        P("pipe", "vocab"),
-        P(("pipe", "vocab"), None),
-        P(("pipe", "vocab"), None),
-        P(),
-    )
+    fine = jax.sharding.Mesh(mesh.devices.reshape(2, 2, 4, 4, 4), AXES)
+    pipe, vocab = AXES[:2], AXES[2:]
+    placed = (P(pipe, vocab), P(pipe, vocab), P(AXES, None), P(AXES, None), P())
     return jax.shard_map(
         per_device,
-        mesh=mesh,
+        mesh=fine,
         in_specs=placed,
-        out_specs=(P("pipe"), P("pipe", "vocab"), P(("pipe", "vocab"), None)),
+        out_specs=(P(pipe), P(pipe, vocab), P(AXES, None)),
         check_vma=False,
     )

time: 169 us -> 156 us (0.923)
  blocking collectives: 0 us -> 15.2 us
  starting transfers between devices: 59.7 us -> 46.1 us
  local copies, waits for them, and re-layouts: 9.9 us -> 1.04 us
  waiting for transfers between devices: 76.1 us -> 71 us
    ppermute x36 -> x28, starting transfers between devices: 59.7 us -> 37.6 us  [send(): return lax.ppermute(value, AXES, pairs)]
    ppermute x36 -> x28, waiting for transfers between devices: 76.1 us -> 60.7 us  [send(): return lax.ppermute(value, AXES, pairs)]
    all_to_all x0 -> x1, blocking collectives: none -> 15.2 us  [per_device(): hidden_grad = jnp.sum(lax.all_to_all(sums, ('zl', 'zh'), 0, 0), axis=0).T]
    all_to_all x0 -> x1, waiting for transfers between devices: none -> 10.3 us  [per_device(): lax.all_to_all(jnp.broadcast_to(mine, (8, 144, 128)), ('zl', 'zh'), 0, 0)]
    unnamed x27 -> x6, local copies, waits for them, and re-layouts: 9.58 us -> 0.01 us
    all_to_all x0 -> x1, starting transfers between devices: none -> 8.47 us  [per_device(): lax.all_to_all(jnp.broadcast_to(mine, (8, 144, 128)), ('zl', 'zh'), 0, 0)]
  transfers between devices with their start and end apart: 36 -> 29, of which waited for: 25 -> 21; matrix products, arithmetic and copies ran while one was open for 1% -> 1% of each run, Pallas kernels for 6% -> 7%
where the time goes in v4:
time: 156 us; the launch traced here: 155 us
  waiting for transfers between devices  71 us (46%)
  starting transfers between devices  46.1 us (30%)
  Pallas kernels  18.1 us (12%)
  blocking collectives  15.2 us (10%)
  other arithmetic  2.55 us (2%)
    ppermute x28, waiting for transfers between devices, send(): return lax.ppermute(value, AXES, pairs)  60.7 us
    ppermute x28, starting transfers between devices, send(): return lax.ppermute(value, AXES, pairs)  37.6 us
    all_to_all x1, blocking collectives, per_device(): hidden_grad = jnp.sum(lax.all_to_all(sums, ('zl', 'zh'), 0, 0), axis=0).T  15.2 us
    all_to_all x1, waiting for transfers between devices, per_device(): lax.all_to_all(jnp.broadcast_to(mine, (8, 144, 128)), ('zl', 'zh'), 0, 0)  10.3 us
    all_to_all x1, starting transfers between devices, per_device(): lax.all_to_all(jnp.broadcast_to(mine, (8, 144, 128)), ('zl', 'zh'), 0, 0)  8.47 us
    pallas_call x1, Pallas kernels, logits_call(): pl.pallas_call(logits_kernel, out_shape=(jax.ShapeDtypeStruct((2 * ROWS,...  6.56 us
    pallas_call x1, Pallas kernels, grads_call(): pl.pallas_call(grads_kernel, out_shape=(jax.ShapeDtypeStruct((1, 128), F3...  5.86 us
    pallas_call x1, Pallas kernels, head_call(): pl.pallas_call(head_kernel, out_shape=jax.ShapeDtypeStruct((ROWS, DS), BF...  5.63 us
  transfers between devices with their start and end apart: 29, of which 21 were waited for; matrix products, arithmetic and copies ran while one was open for 1% of the time, Pallas kernels for 7%

profile of v4, /device:TPU:2, one launch (start us, length us, event | category | flops | bytes accessed | tf_op | source)
XLA Modules:
  0.0 155.0 jit_solution(2728129086197939327)
XLA Ops:
  2.2 8.5 %all-to-all-start = ((bf16[8,144,128]{2,1,0:T(8,128)(2,1)}), bf16[8,144,128]{2,1,0:T(8,128)(2,1)S(1)}, u32[]{:S(2)}, u32[]{:S(2)}) async-start(bf16[8,144,128]{2,1,0:T(8,128)(2,1)} %broadcast_in_dim.3), calls=%async_computation | async-start | bytes 589824 | tf_op jit(solution)/shard_map/all_to_all | solution.py:202
  10.9 10.3 %all-to-all-done = bf16[8,144,128]{2,1,0:T(8,128)(2,1)S(1)} async-done(((bf16[8,144,128]{2,1,0:T(8,128)(2,1)}), bf16[8,144,128]{2,1,0:T(8,128)(2,1)S(1)}, u32[]{:S(2)}, u32[]{:S(2)}) %all-to-all-start) | async-done | bytes 294944 | tf_op jit(solution)/shard_map/all_to_all | solution.py:202
  21.4 2.2 %collective-permute-start.1 = (bf16[576,256]{1,0:T(8,128)(2,1)S(1)}, bf16[576,256]{1,0:T(8,128)(2,1)S(1)}, u32[]{:S(2)}, u32[]{:S(2)}) collective-permute-start(bf16[576,256]{1,0:T(8,128)(2,1)S(1)} %get-tuple-element.49), channel_id=1, source_target_pairs={{0,32},{1,33},{2,34},{3,35},{4,36},{5,37},{6,38},{7,39},{8,40},{9,... | collective-permute-start | bytes 884744 | tf_op jit(solution)/shard_map/ppermute | solution.py:44
  25.6 4.2 %collective-permute-done.1 = bf16[576,256]{1,0:T(8,128)(2,1)S(1)} collective-permute-done((bf16[576,256]{1,0:T(8,128)(2,1)S(1)}, bf16[576,256]{1,0:T(8,128)(2,1)S(1)}, u32[]{:S(2)}, u32[]{:S(2)}) %collective-permute-start.1) | collective-permute-done | bytes 294944 | tf_op jit(solution)/shard_map/ppermute | solution.py:44
  29.8 3.1 %collective-permute-done = bf16[576,256]{1,0:T(8,128)(2,1)S(1)} collective-permute-done((bf16[576,256]{1,0:T(8,128)(2,1)S(1)}, bf16[576,256]{1,0:T(8,128)(2,1)S(1)}, u32[]{:S(2)}, u32[]{:S(2)}) %collective-permute-start) | collective-permute-done | bytes 294944 | tf_op jit(solution)/shard_map/ppermute | solution.py:44
  33.1 3.1 %collective-permute-start.4 = (bf16[4,576,256]{2,1,0:T(8,128)(2,1)S(1)}, bf16[4,576,256]{2,1,0:T(8,128)(2,1)S(1)}, u32[]{:S(2)}, u32[]{:S(2)}) collective-permute-start(bf16[4,576,256]{2,1,0:T(8,128)(2,1)S(1)} %pad_maximum_fusion.t0), channel_id=1, source_target_pairs={{0,12},{1,13},{2,14},{3,15},{4,0},{5,1},{6,2},{7,3},{8,4},{9,5},{1... | collective-permute-start | bytes 3538952 | tf_op jit(solution)/shard_map/ppermute | solution.py:44
  36.2 13.7 %collective-permute-done.4.t3 = bf16[4,576,256]{2,1,0:T(8,128)(2,1)S(1)} collective-permute-done((bf16[4,576,256]{2,1,0:T(8,128)(2,1)S(1)}, bf16[4,576,256]{2,1,0:T(8,128)(2,1)S(1)}, u32[]{:S(2)}, u32[]{:S(2)}) %collective-permute-start.4) | collective-permute-done | bytes 1179680 | tf_op jit(solution)/shard_map/ppermute | solution.py:44
  49.9 3.8 %collective-permute-start.6 = (bf16[2,576,256]{2,1,0:T(8,128)(2,1)S(1)}, bf16[2,576,256]{2,1,0:T(8,128)(2,1)S(1)}, u32[]{:S(2)}, u32[]{:S(2)}) collective-permute-start(bf16[2,576,256]{2,1,0:T(8,128)(2,1)S(1)} %slice.231), channel_id=1, source_target_pairs={{0,12},{1,13},{2,14},{3,15},{4,0},{5,1},{6,2},{7,3},{8,4},{9,5},{1... | collective-permute-start | bytes 1769480 | tf_op jit(solution)/shard_map/ppermute | solution.py:44
  53.9 7.3 %collective-permute-done.6.t2b = bf16[2,576,256]{2,1,0:T(8,128)(2,1)S(1)} collective-permute-done((bf16[2,576,256]{2,1,0:T(8,128)(2,1)S(1)}, bf16[2,576,256]{2,1,0:T(8,128)(2,1)S(1)}, u32[]{:S(2)}, u32[]{:S(2)}) %collective-permute-start.6) | collective-permute-done | bytes 589856 | tf_op jit(solution)/shard_map/ppermute | solution.py:44
  61.1 3.8 %collective-permute-done.5.t2a = bf16[2,576,256]{2,1,0:T(8,128)(2,1)S(1)} collective-permute-done((bf16[2,576,256]{2,1,0:T(8,128)(2,1)S(1)}, bf16[2,576,256]{2,1,0:T(8,128)(2,1)S(1)}, u32[]{:S(2)}, u32[]{:S(2)}) %collective-permute-start.5) | collective-permute-done | bytes 589856 | tf_op jit(solution)/shard_map/ppermute | solution.py:44
  65.0 6.6 %logits.1 = (f32[768,256]{1,0:T(8,128)S(1)}, f32[768,256]{1,0:T(8,128)S(1)}, f32[8,256]{1,0:T(8,128)S(1)}, bf16[5120,256]{1,0:T(8,128)(2,1)S(1)}) custom-call(bf16[4,576,256]{2,1,0:T(8,128)(2,1)S(1)} %pad_maximum_fusion.t0, bf16[4,576,256]{2,1,0:T(8,128)(2,1)S(1)} %collective-permute-done.3.t1, bf16[4,576,256]{2,1,0:T(8,128)(2,1)S(1)} %collective-permute-done.4.t3, ...), custom_call_target="tpu_custom_call" | custom-call | flops 3623878656 | bytes 22000000 | tf_op jit(solution)/shard_map/logits/pallas_call | solution.py:95
  71.5 3.3 %collective-permute-start.9 = (f32[8,256]{1,0:T(8,128)S(1)}, f32[8,256]{1,0:T(8,128)S(1)}, u32[]{:S(2)}, u32[]{:S(2)}) collective-permute-start(f32[8,256]{1,0:T(8,128)S(1)} %get-tuple-element.18.local), channel_id=1, source_target_pairs={{0,128},{1,129},{2,130},{3,131},{4,132},{5,133},{6,134},{7,135},{8... | collective-permute-start | bytes 24584 | tf_op jit(solution)/shard_map/ppermute | solution.py:44
  77.6 2.9 %collective-permute-start.11 = (f32[8,256]{1,0:T(8,128)S(1)}, f32[8,256]{1,0:T(8,128)S(1)}, u32[]{:S(2)}, u32[]{:S(2)}) collective-permute-start(f32[8,256]{1,0:T(8,128)S(1)} %pad_maximum_fusion.10), channel_id=1, source_target_pairs={{0,2},{1,3},{2,0},{3,1},{4,6},{5,7},{6,4},{7,5},{8,10},{9,11},{10,... | collective-permute-start | bytes 24584 | tf_op jit(solution)/shard_map/ppermute | solution.py:44
  81.6 3.6 %collective-permute-done.11 = f32[8,256]{1,0:T(8,128)S(1)} collective-permute-done((f32[8,256]{1,0:T(8,128)S(1)}, f32[8,256]{1,0:T(8,128)S(1)}, u32[]{:S(2)}, u32[]{:S(2)}) %collective-permute-start.11) | collective-permute-done | bytes 8224 | tf_op jit(solution)/shard_map/ppermute | solution.py:44
  88.6 2.5 %collective-permute-start.13 = (f32[8,256]{1,0:T(8,128)S(1)}, f32[8,256]{1,0:T(8,128)S(1)}, u32[]{:S(2)}, u32[]{:S(2)}) collective-permute-start(f32[8,256]{1,0:T(8,128)S(1)} %pad_maximum_fusion.9), channel_id=1, source_target_pairs={{0,16},{1,17},{2,18},{3,19},{4,20},{5,21},{6,22},{7,23},{8,24},{9,... | collective-permute-start | bytes 24584 | tf_op jit(solution)/shard_map/ppermute | solution.py:44
  99.2 5.9 %grads.1 = (f32[1,128]{1,0:T(1,128)}, bf16[384,256]{1,0:T(8,128)(2,1)S(1)}, bf16[384,256]{1,0:T(8,128)(2,1)S(1)}, bf16[4,320,256]{2,1,0:T(8,128)(2,1)S(1)}, bf16...) custom-call(f32[8,256]{1,0:T(8,128)S(1)} %pad_maximum_fusion.7.stats, ...), custom_call_target="tpu_custom_call" | custom-call | flops 2013265920 | bytes 14000000 | tf_op jit(solution)/shard_map/grads/pallas_call | solution.py:148
  107.2 4.9 %collective-permute-done.21 = bf16[2,320,256]{2,1,0:T(8,128)(2,1)S(1)} collective-permute-done((bf16[2,320,256]{2,1,0:T(8,128)(2,1)S(1)}, bf16[2,320,256]{2,1,0:T(8,128)(2,1)S(1)}, u32[]{:S(2)}, u32[]{:S(2)}) %collective-permute-start.21) | collective-permute-done | bytes 327712 | tf_op jit(solution)/shard_map/ppermute | solution.py:44
  112.3 3.3 %collective-permute-start.22 = (bf16[4,320,256]{2,1,0:T(8,128)(2,1)S(1)}, bf16[4,320,256]{2,1,0:T(8,128)(2,1)S(1)}, u32[]{:S(2)}, u32[]{:S(2)}) collective-permute-start(bf16[4,320,256]{2,1,0:T(8,128)(2,1)S(1)} %pad_maximum_fusion.2), channel_id=1, source_target_pairs={{0,12},{1,13},{2,14},{3,15},{4,0},{5,1},{6,2},{7,3},{8,4},{9,5},{1... | collective-permute-start | bytes 1966088 | tf_op jit(solution)/shard_map/ppermute | solution.py:44
  117.6 5.6 %head.1 = bf16[384,5120]{1,0:T(8,128)(2,1)} custom-call(bf16[384,256]{1,0:T(8,128)(2,1)S(1)} %get-tuple-element.27.g_own, bf16[384,256]{1,0:T(8,128)(2,1)S(1)} %collective-permute-done.23.g_got, bf16[5120,256]{1,0:T(8,128)(2,1)S(1)} %get-tuple-element.29.h_own, bf16[5120,256]{1,0:T(8,128)(2,1)S(1)} %collective-permute-done.24.h_got), custom_call_target="tpu_custom_call" | custom-call | flops 2013265920 | bytes 10000000 | tf_op jit(solution)/shard_map/head/pallas_call | solution.py:172
  123.7 3.9 %collective-permute-done.20 = bf16[4,320,256]{2,1,0:T(8,128)(2,1)S(1)} collective-permute-done((bf16[4,320,256]{2,1,0:T(8,128)(2,1)S(1)}, bf16[4,320,256]{2,1,0:T(8,128)(2,1)S(1)}, u32[]{:S(2)}, u32[]{:S(2)}) %collective-permute-start.20) | collective-permute-done | bytes 655392 | tf_op jit(solution)/shard_map/ppermute | solution.py:44
  128.0 2.4 %collective-permute-start.25 = (bf16[320,256]{1,0:T(8,128)(2,1)S(1)}, bf16[320,256]{1,0:T(8,128)(2,1)S(1)}, u32[]{:S(2)}, u32[]{:S(2)}) collective-permute-start(bf16[320,256]{1,0:T(8,128)(2,1)S(1)} %get-tuple-element.43), channel_id=1, source_target_pairs={{0,16},{1,17},{2,18},{3,19},{4,20},{5,21},{6,22},{7,23},{8,24},{9,... | collective-permute-start | bytes 491528 | tf_op jit(solution)/shard_map/ppermute | solution.py:44
  130.4 2.6 %collective-permute-start.27 = (bf16[320,256]{1,0:T(8,128)(2,1)S(1)}, bf16[320,256]{1,0:T(8,128)(2,1)S(1)}, u32[]{:S(2)}, u32[]{:S(2)}) collective-permute-start(bf16[320,256]{1,0:T(8,128)(2,1)S(1)} %get-tuple-element.44), channel_id=1, source_target_pairs={{0,32},{1,33},{2,34},{3,35},{4,36},{5,37},{6,38},{7,39},{8,40},{9,... | collective-permute-start | bytes 491528 | tf_op jit(solution)/shard_map/ppermute | solution.py:44
  134.2 3.0 %collective-permute-done.27 = bf16[320,256]{1,0:T(8,128)(2,1)S(1)} collective-permute-done((bf16[320,256]{1,0:T(8,128)(2,1)S(1)}, bf16[320,256]{1,0:T(8,128)(2,1)S(1)}, u32[]{:S(2)}, u32[]{:S(2)}) %collective-permute-start.27) | collective-permute-done | bytes 163872 | tf_op jit(solution)/shard_map/ppermute | solution.py:44
  139.1 15.2 %all_to_all.10 = f32[8,80,128]{2,1,0:T(8,128)S(1)} all-to-all(f32[8,80,128]{2,1,0:T(8,128)S(1)} %bitcast.26), channel_id=1, replica_groups=mesh['zl'=2,'c'=2,'x'=4,'y'=4,'zh'=4] {'zl','zh'}, dimensions={0} | all-to-all | bytes 655360 | tf_op jit(solution)/shard_map/all_to_all | solution.py:232
  (95 shorter events, 28.3 us)
Async XLA Ops:
  0.6 64.3 %collective-permute-start.7 = (bf16[384,5120]{1,0:T(8,128)(2,1)}, bf16[384,5120]{1,0:T(8,128)(2,1)}, u32[]{:S(2)}, u32[]{:S(2)}) collective-permute-start(bf16[384,5120]{1,0:T(8,128)(2,1)} %ws.3), channel_id=1, source_target_pairs={{0,64},{1,65},{2,66},{3,67},{4,68},{5,69},{6,70},{7,71},{8,72},{9,... | collective-permute-start | bytes 11796488 | tf_op jit(solution)/shard_map/ppermute | solution.py:44
  2.2 19.0 %all-to-all-start = ((bf16[8,144,128]{2,1,0:T(8,128)(2,1)}), bf16[8,144,128]{2,1,0:T(8,128)(2,1)S(1)}, u32[]{:S(2)}, u32[]{:S(2)}) async-start(bf16[8,144,128]{2,1,0:T(8,128)(2,1)} %broadcast_in_dim.3), calls=%async_computation | async-start | bytes 589824 | tf_op jit(solution)/shard_map/all_to_all | solution.py:202
  10.7 54.2 %collective-permute-start.8 = (bf16[384,4096]{1,0:T(8,128)(2,1)}, bf16[384,4096]{1,0:T(8,128)(2,1)S(1)}, u32[]{:S(2)}, u32[]{:S(2)}) collective-permute-start(bf16[384,4096]{1,0:T(8,128)(2,1)} %wt.1), channel_id=1, source_target_pairs={{0,64},{1,65},{2,66},{3,67},{4,68},{5,69},{6,70},{7,71},{8,72},{9,... | collective-permute-start | bytes 9437192 | tf_op jit(solution)/shard_map/ppermute | solution.py:44
  21.4 8.4 %collective-permute-start.1 = (bf16[576,256]{1,0:T(8,128)(2,1)S(1)}, bf16[576,256]{1,0:T(8,128)(2,1)S(1)}, u32[]{:S(2)}, u32[]{:S(2)}) collective-permute-start(bf16[576,256]{1,0:T(8,128)(2,1)S(1)} %get-tuple-element.49), channel_id=1, source_target_pairs={{0,32},{1,33},{2,34},{3,35},{4,36},{5,37},{6,38},{7,39},{8,40},{9,... | collective-permute-start | bytes 884744 | tf_op jit(solution)/shard_map/ppermute | solution.py:44
  23.6 9.3 %collective-permute-start = (bf16[576,256]{1,0:T(8,128)(2,1)S(1)}, bf16[576,256]{1,0:T(8,128)(2,1)S(1)}, u32[]{:S(2)}, u32[]{:S(2)}) collective-permute-start(bf16[576,256]{1,0:T(8,128)(2,1)S(1)} %get-tuple-element.49), channel_id=1, source_target_pairs={{0,16},{1,17},{2,18},{3,19},{4,20},{5,21},{6,22},{7,23},{8,24},{9,... | collective-permute-start | bytes 884744 | tf_op jit(solution)/shard_map/ppermute | solution.py:44
  23.6 9.3 %collective-permute-start.2 = (bf16[576,256]{1,0:T(8,128)(2,1)S(1)}, bf16[576,256]{1,0:T(8,128)(2,1)S(1)}, u32[]{:S(2)}, u32[]{:S(2)}) collective-permute-start(bf16[576,256]{1,0:T(8,128)(2,1)S(1)} %get-tuple-element.49), channel_id=1, source_target_pairs={{0,48},{1,49},{2,50},{3,51},{4,52},{5,53},{6,54},{7,55},{8,56},{9,... | collective-permute-start | bytes 884744 | tf_op jit(solution)/shard_map/ppermute | solution.py:44
  33.1 16.8 %collective-permute-start.4 = (bf16[4,576,256]{2,1,0:T(8,128)(2,1)S(1)}, bf16[4,576,256]{2,1,0:T(8,128)(2,1)S(1)}, u32[]{:S(2)}, u32[]{:S(2)}) collective-permute-start(bf16[4,576,256]{2,1,0:T(8,128)(2,1)S(1)} %pad_maximum_fusion.t0), channel_id=1, source_target_pairs={{0,12},{1,13},{2,14},{3,15},{4,0},{5,1},{6,2},{7,3},{8,4},{9,5},{1... | collective-permute-start | bytes 3538952 | tf_op jit(solution)/shard_map/ppermute | solution.py:44
  36.2 17.5 %collective-permute-start.3 = (bf16[4,576,256]{2,1,0:T(8,128)(2,1)S(1)}, bf16[4,576,256]{2,1,0:T(8,128)(2,1)S(1)}, u32[]{:S(2)}, u32[]{:S(2)}) collective-permute-start(bf16[4,576,256]{2,1,0:T(8,128)(2,1)S(1)} %pad_maximum_fusion.t0), channel_id=1, source_target_pairs={{0,4},{1,5},{2,6},{3,7},{4,8},{5,9},{6,10},{7,11},{8,12},{9,13},{1... | collective-permute-start | bytes 3538952 | tf_op jit(solution)/shard_map/ppermute | solution.py:44
  49.9 11.2 %collective-permute-start.6 = (bf16[2,576,256]{2,1,0:T(8,128)(2,1)S(1)}, bf16[2,576,256]{2,1,0:T(8,128)(2,1)S(1)}, u32[]{:S(2)}, u32[]{:S(2)}) collective-permute-start(bf16[2,576,256]{2,1,0:T(8,128)(2,1)S(1)} %slice.231), channel_id=1, source_target_pairs={{0,12},{1,13},{2,14},{3,15},{4,0},{5,1},{6,2},{7,3},{8,4},{9,5},{1... | collective-permute-start | bytes 1769480 | tf_op jit(solution)/shard_map/ppermute | solution.py:44
  53.8 11.2 %collective-permute-start.5 = (bf16[2,576,256]{2,1,0:T(8,128)(2,1)S(1)}, bf16[2,576,256]{2,1,0:T(8,128)(2,1)S(1)}, u32[]{:S(2)}, u32[]{:S(2)}) collective-permute-start(bf16[2,576,256]{2,1,0:T(8,128)(2,1)S(1)} %slice.230), channel_id=1, source_target_pairs={{0,4},{1,5},{2,6},{3,7},{4,8},{5,9},{6,10},{7,11},{8,12},{9,13},{1... | collective-permute-start | bytes 1769480 | tf_op jit(solution)/shard_map/ppermute | solution.py:44
  76.6 5.0 %collective-permute-start.12 = (f32[8,256]{1,0:T(8,128)S(1)}, f32[8,256]{1,0:T(8,128)S(1)}, u32[]{:S(2)}, u32[]{:S(2)}) collective-permute-start(f32[8,256]{1,0:T(8,128)S(1)} %pad_maximum_fusion.10), channel_id=1, source_target_pairs={{0,3},{1,0},{2,1},{3,2},{4,7},{5,4},{6,5},{7,6},{8,11},{9,8},{10,9... | collective-permute-start | bytes 24584 | tf_op jit(solution)/shard_map/ppermute | solution.py:44
  77.6 7.6 %collective-permute-start.11 = (f32[8,256]{1,0:T(8,128)S(1)}, f32[8,256]{1,0:T(8,128)S(1)}, u32[]{:S(2)}, u32[]{:S(2)}) collective-permute-start(f32[8,256]{1,0:T(8,128)S(1)} %pad_maximum_fusion.10), channel_id=1, source_target_pairs={{0,2},{1,3},{2,0},{3,1},{4,6},{5,7},{6,4},{7,5},{8,10},{9,11},{10,... | collective-permute-start | bytes 24584 | tf_op jit(solution)/shard_map/ppermute | solution.py:44
  80.5 5.8 %collective-permute-start.10 = (f32[8,256]{1,0:T(8,128)S(1)}, f32[8,256]{1,0:T(8,128)S(1)}, u32[]{:S(2)}, u32[]{:S(2)}) collective-permute-start(f32[8,256]{1,0:T(8,128)S(1)} %pad_maximum_fusion.10), channel_id=1, source_target_pairs={{0,1},{1,2},{2,3},{3,0},{4,5},{5,6},{6,7},{7,4},{8,9},{9,10},{10,1... | collective-permute-start | bytes 24584 | tf_op jit(solution)/shard_map/ppermute | solution.py:44
  87.0 5.2 %collective-permute-start.14 = (f32[8,256]{1,0:T(8,128)S(1)}, f32[8,256]{1,0:T(8,128)S(1)}, u32[]{:S(2)}, u32[]{:S(2)}) collective-permute-start(f32[8,256]{1,0:T(8,128)S(1)} %pad_maximum_fusion.9), channel_id=1, source_target_pairs={{0,32},{1,33},{2,34},{3,35},{4,36},{5,37},{6,38},{7,39},{8,40},{9,... | collective-permute-start | bytes 24584 | tf_op jit(solution)/shard_map/ppermute | solution.py:44
  91.2 26.4 %collective-permute-start.24 = (bf16[5120,256]{1,0:T(8,128)(2,1)S(1)}, bf16[5120,256]{1,0:T(8,128)(2,1)S(1)}, u32[]{:S(2)}, u32[]{:S(2)}) collective-permute-start(bf16[5120,256]{1,0:T(8,128)(2,1)S(1)} %get-tuple-element.29.h_own), channel_id=1, source_target_pairs={{0,64},{1,65},{2,66},{3,67},{4,68},{5,69},{6,70},{7,71},{8,72},{9,... | collective-permute-start | bytes 7864328 | tf_op jit(solution)/shard_map/ppermute | solution.py:44
  92.7 5.2 %collective-permute-start.17 = (f32[8,256]{1,0:T(8,128)S(1)}, f32[8,256]{1,0:T(8,128)S(1)}, u32[]{:S(2)}, u32[]{:S(2)}) collective-permute-start(f32[8,256]{1,0:T(8,128)S(1)} %pad_maximum_fusion.8), channel_id=1, source_target_pairs={{0,8},{1,9},{2,10},{3,11},{4,12},{5,13},{6,14},{7,15},{8,0},{9,1},... | collective-permute-start | bytes 24584 | tf_op jit(solution)/shard_map/ppermute | solution.py:44
  93.6 5.5 %collective-permute-start.16 = (f32[8,256]{1,0:T(8,128)S(1)}, f32[8,256]{1,0:T(8,128)S(1)}, u32[]{:S(2)}, u32[]{:S(2)}) collective-permute-start(f32[8,256]{1,0:T(8,128)S(1)} %pad_maximum_fusion.8), channel_id=1, source_target_pairs={{0,4},{1,5},{2,6},{3,7},{4,8},{5,9},{6,10},{7,11},{8,12},{9,13},{1... | collective-permute-start | bytes 24584 | tf_op jit(solution)/shard_map/ppermute | solution.py:44
  105.0 7.1 %collective-permute-start.21 = (bf16[2,320,256]{2,1,0:T(8,128)(2,1)S(1)}, bf16[2,320,256]{2,1,0:T(8,128)(2,1)S(1)}, u32[]{:S(2)}, u32[]{:S(2)}) collective-permute-start(bf16[2,320,256]{2,1,0:T(8,128)(2,1)S(1)} %get-tuple-element.26), channel_id=1, source_target_pairs={{0,12},{1,13},{2,14},{3,15},{4,0},{5,1},{6,2},{7,3},{8,4},{9,5},{1... | collective-permute-start | bytes 983048 | tf_op jit(solution)/shard_map/ppermute | solution.py:44
  107.1 8.5 %collective-permute-start.19 = (bf16[2,320,256]{2,1,0:T(8,128)(2,1)S(1)}, bf16[2,320,256]{2,1,0:T(8,128)(2,1)S(1)}, u32[]{:S(2)}, u32[]{:S(2)}) collective-permute-start(bf16[2,320,256]{2,1,0:T(8,128)(2,1)S(1)} %get-tuple-element.24), channel_id=1, source_target_pairs={{0,4},{1,5},{2,6},{3,7},{4,8},{5,9},{6,10},{7,11},{8,12},{9,13},{1... | collective-permute-start | bytes 983048 | tf_op jit(solution)/shard_map/ppermute | solution.py:44
  112.3 11.4 %collective-permute-start.22 = (bf16[4,320,256]{2,1,0:T(8,128)(2,1)S(1)}, bf16[4,320,256]{2,1,0:T(8,128)(2,1)S(1)}, u32[]{:S(2)}, u32[]{:S(2)}) collective-permute-start(bf16[4,320,256]{2,1,0:T(8,128)(2,1)S(1)} %pad_maximum_fusion.2), channel_id=1, source_target_pairs={{0,12},{1,13},{2,14},{3,15},{4,0},{5,1},{6,2},{7,3},{8,4},{9,5},{1... | collective-permute-start | bytes 1966088 | tf_op jit(solution)/shard_map/ppermute | solution.py:44
  115.8 11.9 %collective-permute-start.20 = (bf16[4,320,256]{2,1,0:T(8,128)(2,1)S(1)}, bf16[4,320,256]{2,1,0:T(8,128)(2,1)S(1)}, u32[]{:S(2)}, u32[]{:S(2)}) collective-permute-start(bf16[4,320,256]{2,1,0:T(8,128)(2,1)S(1)} %pad_maximum_fusion.1), channel_id=1, source_target_pairs={{0,4},{1,5},{2,6},{3,7},{4,8},{5,9},{6,10},{7,11},{8,12},{9,13},{1... | collective-permute-start | bytes 1966088 | tf_op jit(solution)/shard_map/ppermute | solution.py:44
  128.0 6.2 %collective-permute-start.25 = (bf16[320,256]{1,0:T(8,128)(2,1)S(1)}, bf16[320,256]{1,0:T(8,128)(2,1)S(1)}, u32[]{:S(2)}, u32[]{:S(2)}) collective-permute-start(bf16[320,256]{1,0:T(8,128)(2,1)S(1)} %get-tuple-element.43), channel_id=1, source_target_pairs={{0,16},{1,17},{2,18},{3,19},{4,20},{5,21},{6,22},{7,23},{8,24},{9,... | collective-permute-start | bytes 491528 | tf_op jit(solution)/shard_map/ppermute | solution.py:44
  130.4 6.9 %collective-permute-start.27 = (bf16[320,256]{1,0:T(8,128)(2,1)S(1)}, bf16[320,256]{1,0:T(8,128)(2,1)S(1)}, u32[]{:S(2)}, u32[]{:S(2)}) collective-permute-start(bf16[320,256]{1,0:T(8,128)(2,1)S(1)} %get-tuple-element.44), channel_id=1, source_target_pairs={{0,32},{1,33},{2,34},{3,35},{4,36},{5,37},{6,38},{7,39},{8,40},{9,... | collective-permute-start | bytes 491528 | tf_op jit(solution)/shard_map/ppermute | solution.py:44
  133.0 5.9 %collective-permute-start.26 = (bf16[320,256]{1,0:T(8,128)(2,1)S(1)}, bf16[320,256]{1,0:T(8,128)(2,1)S(1)}, u32[]{:S(2)}, u32[]{:S(2)}) collective-permute-start(bf16[320,256]{1,0:T(8,128)(2,1)S(1)} %get-tuple-element.45), channel_id=1, source_target_pairs={{0,48},{1,49},{2,50},{3,51},{4,52},{5,53},{6,54},{7,55},{8,56},{9,... | collective-permute-start | bytes 491528 | tf_op jit(solution)/shard_map/ppermute | solution.py:44
  (8 other events, 140.3 us)

commit v5 on v4

--- a/solution.py
+++ b/solution.py
@@ -9,6 +9,7 @@
 ROWS = 384
 TOK = 256
 NS, NT = 320, 256
+WIDE = 384
 AXES = ("zl", "c", "x", "y", "zh")
 F32, BF16 = jnp.float32, jnp.bfloat16
 VMEM_LIMIT = 20 * 1024 * 1024
@@ -63,20 +64,51 @@
     return lax.dot_general(a, b, (dims, ((), ())), preferred_element_type=F32)
 
 
-def logits_kernel(t0, t1, t3, t2a, t2b, ws, wso, wt, wto, es_ref, et_ref, st_ref, hs, ht):
+def window(at):
+    start = pl.multiple_of(((at * 5) >> 1) * 128, 128)
+    return pl.ds(start, WIDE), pl.multiple_of((at & 1) * 64, 64)
+
+
+def near_kernel(t0, t1, t3, ws, wso, wt, wto, s_ref, t_ref, hs, ht):
     _, c, x, y, _ = place()
-    parts = [(0, t0, 0, range(4)), (1, t1, 0, range(4)), (3, t3, 0, range(4))]
-    parts += [(2, t2a, 0, range(2)), (2, t2b, 2, range(2, 4))]
-    for j, t, base, lines in parts:
-        for i in lines:
+    for j, t in ((0, t0), (1, t1), (3, t3), (2, None)):
+        for i in range(4):
             at = block_at(c, x, y, (4 - i) & 3, (4 - j) & 3)
-            ht[pl.ds(pl.multiple_of(at * NT, NT), NT)] = t[i - base, NS : NS + NT]
-            hs[pl.ds(pl.multiple_of(at * NS, NS), NS)] = t[i - base, 0:NS]
-    et_ref[:ROWS] = dot(wt[...], ht[...], ((1,), (0,)))
-    et_ref[ROWS:] = dot(wto[...], ht[...], ((1,), (0,)))
-    es_ref[:ROWS] = dot(ws[...], hs[...], ((1,), (0,)))
-    es_ref[ROWS:] = dot(wso[...], hs[...], ((1,), (0,)))
-    s, t = es_ref[...], et_ref[...]
+            rows_s = pl.ds(pl.multiple_of(at * NS, NS), NS)
+            rows_t = pl.ds(pl.multiple_of(at * NT, NT), NT)
+            if t is None:
+                hs[rows_s] = jnp.zeros((NS, TOK), BF16)
+                ht[rows_t] = jnp.zeros((NT, TOK), BF16)
+            else:
+                hs[rows_s] = t[i, 0:NS]
+                ht[rows_t] = t[i, NS : NS + NT]
+    t_ref[:ROWS] = dot(wt[...], ht[...], ((1,), (0,)))
+    t_ref[ROWS:] = dot(wto[...], ht[...], ((1,), (0,)))
+    s_ref[:ROWS] = dot(ws[...], hs[...], ((1,), (0,)))
+    s_ref[ROWS:] = dot(wso[...], hs[...], ((1,), (0,)))
+
+
+def far_kernel(
+    t2a, t2b, s_in, t_in, hs_in, ws, wso, wt, wto, es_ref, et_ref, st_ref, hs, pads
+):
+    _, c, x, y, _ = place()
+    s_ref, t_ref = es_ref, et_ref
+    hs[...] = hs_in[...]
+    s_ref[...] = s_in[...]
+    t_ref[...] = t_in[...]
+    for i in range(4):
+        line = t2a[i] if i < 2 else t2b[i - 2]
+        at = block_at(c, x, y, (4 - i) & 3, 2)
+        hs[pl.ds(pl.multiple_of(at * NS, NS), NS)] = line[0:NS]
+        cols, first = window(at)
+        pads[i] = jnp.zeros((WIDE, TOK), BF16)
+        pads[i, pl.ds(first, NS)] = line[0:NS]
+        cols_t = pl.ds(pl.multiple_of(at * NT, NT), NT)
+        s_ref[:ROWS] += dot(ws[:, cols], pads[i], ((1,), (0,)))
+        s_ref[ROWS:] += dot(wso[:, cols], pads[i], ((1,), (0,)))
+        t_ref[:ROWS] += dot(wt[:, cols_t], line[NS:], ((1,), (0,)))
+        t_ref[ROWS:] += dot(wto[:, cols_t], line[NS:], ((1,), (0,)))
+    s, t = s_ref[...], t_ref[...]
     sm = jnp.max(s, axis=0, keepdims=True)
     tm = jnp.max(t, axis=0, keepdims=True)
     es, et = jnp.exp(s - sm), jnp.exp(t - tm)
@@ -90,32 +122,41 @@
     et_ref[...] = et
 
 
-def logits_call(parts, ws, wso, wt, wto):
+def vmem_call(kernel, name, outs, scratch, flops, *args):
     vmem = pl.BlockSpec(memory_space=pltpu.VMEM)
     return pl.pallas_call(
-        logits_kernel,
-        out_shape=(
-            jax.ShapeDtypeStruct((2 * ROWS, TOK), F32),
-            jax.ShapeDtypeStruct((2 * ROWS, TOK), F32),
-            jax.ShapeDtypeStruct((8, TOK), F32),
-            jax.ShapeDtypeStruct((DS, TOK), BF16),
-        ),
-        in_specs=[vmem] * 9,
-        out_specs=(vmem,) * 4,
-        scratch_shapes=[pltpu.VMEM((DT, TOK), BF16)],
+        kernel,
+        out_shape=tuple(jax.ShapeDtypeStruct(*o) for o in outs),
+        in_specs=[vmem] * len(args),
+        out_specs=(vmem,) * len(outs),
+        scratch_shapes=[pltpu.VMEM(*o) for o in scratch],
         compiler_params=pltpu.CompilerParams(vmem_limit_bytes=VMEM_LIMIT),
-        cost_estimate=pl.CostEstimate(
-            flops=2 * 2 * ROWS * TOK * (DS + DT), bytes_accessed=22_000_000, transcendentals=4 * ROWS * TOK
-        ),
-        name="logits",
-    )(*parts, ws, wso, wt, wto)
+        cost_estimate=pl.CostEstimate(flops=flops, bytes_accessed=14_000_000, transcendentals=0),
+        name=name,
+    )(*args)
+
+
+LOGITS = ((2 * ROWS, TOK), F32)
+HIDDEN = ((DS, TOK), BF16)
+
+
+def near_call(t0, t1, t3, *weights):
+    flops = 2 * 2 * ROWS * TOK * (DS + DT)
+    outs = (LOGITS, LOGITS, HIDDEN)
+    return vmem_call(near_kernel, "near", outs, [((DT, TOK), BF16)], flops, t0, t1, t3, *weights)
+
+
+def far_call(*args):
+    flops = 2 * 2 * ROWS * TOK * (DS + DT) // 3
+    outs = (LOGITS, LOGITS, ((8, TOK), F32), HIDDEN)
+    return vmem_call(far_kernel, "far", outs, [((4, WIDE, TOK), BF16)], flops, *args)
 
 
 CHUNK = 1280
 
 
-def grads_kernel(
-    stats, local, weights, es_ref, et_ref, ws, wso, kl_ref, g_own, g_oth, o0, o1, o3, o2a, o2b, acc
+def opposite_kernel(
+    stats, local, weights, es_ref, et_ref, ws, wso, kl_ref, g_own, g_oth, o2a, o2b, part
 ):
     zl, c, x, y, _ = place()
     top, totals = stats[0:2], stats[2:4]
@@ -128,35 +169,38 @@
     g = (es_ref[...] * coef[0:1] - et_ref[...] * coef[1:2]).astype(BF16)
     g_own[...] = g[:ROWS]
     g_oth[...] = g[ROWS:]
+    for r in range(4):
+        cols, first = window(block_at(c, x, y, r, 2))
+        whole = dot(g[:ROWS], ws[:, cols], ((0,), (0,))) + dot(g[ROWS:], wso[:, cols], ((0,), (0,)))
+        part[r] = whole.astype(BF16).T
+        if r < 2:
+            o2a[r] = part[r, pl.ds(first, NS)]
+        else:
+            o2b[r - 2] = part[r, pl.ds(first, NS)]
+
+
+def rest_kernel(g_own, g_oth, ws, wso, o0, o1, o3, acc):
+    _, c, x, y, _ = place()
     for n in range(DS // CHUNK):
         cols = slice(n * CHUNK, (n + 1) * CHUNK)
-        part = dot(g[:ROWS], ws[:, cols], ((0,), (0,))) + dot(g[ROWS:], wso[:, cols], ((0,), (0,)))
+        part = dot(g_own[...], ws[:, cols], ((0,), (0,))) + dot(g_oth[...], wso[:, cols], ((0,), (0,)))
         acc[cols] = part.astype(BF16).T
-    outs = [(0, o0, 0, range(4)), (1, o1, 0, range(4)), (3, o3, 0, range(4))]
-    outs += [(2, o2a, 0, range(2)), (2, o2b, 2, range(2, 4))]
-    for k, o, base, lines in outs:
-        for r in lines:
+    for k, o in ((0, o0), (1, o1), (3, o3)):
+        for r in range(4):
             at = block_at(c, x, y, r, k)
-            o[r - base] = acc[pl.ds(pl.multiple_of(at * NS, NS), NS)]
-
-
-def grads_call(stats, local, weights, es, et, ws, wso):
-    vmem = pl.BlockSpec(memory_space=pltpu.VMEM)
-    whole = jax.ShapeDtypeStruct((4, NS, TOK), BF16)
-    half = jax.ShapeDtypeStruct((2, NS, TOK), BF16)
-    rows = jax.ShapeDtypeStruct((ROWS, TOK), BF16)
-    return pl.pallas_call(
-        grads_kernel,
-        out_shape=(jax.ShapeDtypeStruct((1, 128), F32), rows, rows, whole, whole, whole, half, half),
-        in_specs=[vmem] * 7,
-        out_specs=(vmem,) * 8,
-        scratch_shapes=[pltpu.VMEM((DS, TOK), BF16)],
-        compiler_params=pltpu.CompilerParams(vmem_limit_bytes=VMEM_LIMIT),
-        cost_estimate=pl.CostEstimate(
-            flops=2 * 2 * ROWS * TOK * DS, bytes_accessed=14_000_000, transcendentals=0
-        ),
-        name="grads",
-    )(stats, local, weights, es, et, ws, wso)
+            o[r] = acc[pl.ds(pl.multiple_of(at * NS, NS), NS)]
+
+
+def opposite_call(*args):
+    rows, half = ((ROWS, TOK), BF16), ((2, NS, TOK), BF16)
+    outs = (((1, 128), F32), rows, rows, half, half)
+    flops = 2 * 2 * ROWS * TOK * DS // 3
+    return vmem_call(opposite_kernel, "opposite", outs, [((4, WIDE, TOK), BF16)], flops, *args)
+
+
+def rest_call(*args):
+    outs = (((4, NS, TOK), BF16),) * 3
+    return vmem_call(rest_kernel, "rest", outs, [HIDDEN], 2 * 2 * ROWS * TOK * DS, *args)
 
 
 def head_kernel(g_own, g_got, h_own, h_got, out):
@@ -198,28 +242,30 @@
     teacher_other = send(teacher_head, CORE)
     student_other = send(student_head, CORE)
 
-    mine = jnp.concatenate([student_hidden.T, teacher_hidden.T], axis=0)
-    along = lax.all_to_all(jnp.broadcast_to(mine, (8, 144, 128)), ("zl", "zh"), 0, 0)
+    mine = jnp.concatenate([jnp.broadcast_to(h.T, (8,) + h.T.shape) for h in (student_hidden, teacher_hidden)], axis=1)
+    along = lax.all_to_all(mine, ("zl", "zh"), 0, 0)
     along = jnp.concatenate([along[:4], along[4:]], axis=2)
     block = jnp.concatenate([along[:, :80].reshape(NS, TOK), along[:, 80:].reshape(NT, TOK)], axis=0)
     line = jnp.stack((block,) + ring(block, FIRST))
     before, after = send(line, SECOND[1]), send(line, SECOND[3])
     far_low, far_high = send(before[:2], SECOND[1]), send(after[2:], SECOND[3])
-    parts = (line, before, after, far_low, far_high)
-
-    es, et, local, hidden_own = logits_call(
-        parts, student_head, student_other, teacher_head, teacher_other
-    )
+
+    heads = (student_head, student_other, teacher_head, teacher_other)
+    near = near_call(line, before, after, *heads)
+    es, et, local, hidden_own = far_call(far_low, far_high, *near, *heads)
     hidden_got = send(hidden_own, CORE)
 
     stats = merge((local, send(local, PAIR)))
     for perms in (ZH, FIRST, SECOND):
         stats = merge((stats,) + ring(stats, perms))
-    kl_rows, g_own, g_oth, o0, o1, o3, o2a, o2b = grads_call(
+    kl_rows, g_own, g_oth, o2a, o2b = opposite_call(
         stats, local, row_weight.reshape(4, 128), es, et, student_head, student_other
     )
     low, high = send(o2a, SECOND[1]), send(o2b, SECOND[3])
     g_got = send(g_oth, CORE)
+    low, high, g_got, o0, o1, o3 = lax.optimization_barrier(
+        (low, high, g_got, *rest_call(g_own, g_oth, student_head, student_other))
+    )
     r1 = send(jnp.concatenate([(o1[:2].astype(F32) + low.astype(F32)).astype(BF16), o1[2:]]), SECOND[1])
     r3 = send(jnp.concatenate([o3[:2], (o3[2:].astype(F32) + high.astype(F32)).astype(BF16)]), SECOND[3])
     head_grad = head_call(g_own, g_got, hidden_own, hidden_got)

time: 156 us -> 152 us (0.974)
  blocking collectives: 15.2 us -> 35.6 us
  waiting for transfers between devices: 71 us -> 56.8 us
  starting transfers between devices: 46.1 us -> 38.4 us
    all_to_all x0 -> x1, blocking collectives: none -> 21 us  [per_device(): along = lax.all_to_all(mine, ('zl', 'zh'), 0, 0)]
    all_to_all x1 -> x0, waiting for transfers between devices: 10.3 us -> none  [per_device(): lax.all_to_all(jnp.broadcast_to(mine, (8, 144, 128)), ('zl', 'zh'), 0, 0)]
    all_to_all x1 -> x0, starting transfers between devices: 8.47 us -> none  [per_device(): lax.all_to_all(jnp.broadcast_to(mine, (8, 144, 128)), ('zl', 'zh'), 0, 0)]
    ppermute x28, waiting for transfers between devices: 60.7 us -> 56.8 us  [send(): return lax.ppermute(value, AXES, pairs)]
    pallas_call x2 -> x4, Pallas kernels: 12.4 us -> 11 us  [vmem_call(): pl.pallas_call(kernel, out_shape=tuple((jax.ShapeDtypeStruct(*o) for o in...]
  transfers between devices with their start and end apart: 29 -> 28, of which waited for: 21 -> 20; matrix products, arithmetic and copies ran while one was open for 1% -> 2% of each run, Pallas kernels for 7% -> 10%
where the time goes in v5:
time: 152 us
  waiting for transfers between devices  56.8 us (37%)
  starting transfers between devices  38.4 us (25%)
  blocking collectives  35.6 us (23%)
  Pallas kernels  16.7 us (11%)
  other arithmetic  1.78 us (1%)
  local copies, waits for them, and re-layouts  1.77 us (1%)
    ppermute x28, waiting for transfers between devices, send(): return lax.ppermute(value, AXES, pairs)  56.8 us
    ppermute x28, starting transfers between devices, send(): return lax.ppermute(value, AXES, pairs)  38.4 us
    all_to_all x1, blocking collectives, per_device(): along = lax.all_to_all(mine, ('zl', 'zh'), 0, 0)  21 us
    all_to_all x1, blocking collectives, per_device(): hidden_grad = jnp.sum(lax.all_to_all(sums, ('zl', 'zh'), 0, 0), axis=0).T  14.6 us
    pallas_call x4, Pallas kernels, vmem_call(): pl.pallas_call(kernel, out_shape=tuple((jax.ShapeDtypeStruct(*o) for o in...  11 us
    pallas_call x1, Pallas kernels, head_call(): pl.pallas_call(head_kernel, out_shape=jax.ShapeDtypeStruct((ROWS, DS), BF...  5.65 us
  transfers between devices with their start and end apart: 28, of which 20 were waited for; matrix products, arithmetic and copies ran while one was open for 2% of the time, Pallas kernels for 10%

profile of v5, /device:TPU:2, one launch (start us, length us, event | category | flops | bytes accessed | tf_op | source)
XLA Modules:
  0.0 152.1 jit_solution(1674329437245142253)
XLA Ops:
  2.7 21.0 %all_to_all.10 = bf16[8,144,128]{2,1,0:T(8,128)(2,1)S(1)} all-to-all(bf16[8,144,128]{2,1,0:T(8,128)(2,1)S(1)} %pad_maximum_fusion.4), channel_id=1, replica_groups=mesh['zl'=2,'c'=2,'x'=4,'y'=4,'zh'=4] {'zl','zh'}, dimensions={0} | all-to-all | bytes 589824 | tf_op jit(solution)/shard_map/all_to_all | solution.py:246
  23.9 2.2 %collective-permute-start.1 = (bf16[576,256]{1,0:T(8,128)(2,1)S(1)}, bf16[576,256]{1,0:T(8,128)(2,1)S(1)}, u32[]{:S(2)}, u32[]{:S(2)}) collective-permute-start(bf16[576,256]{1,0:T(8,128)(2,1)S(1)} %get-tuple-element.67), channel_id=1, source_target_pairs={{0,32},{1,33},{2,34},{3,35},{4,36},{5,37},{6,38},{7,39},{8,40},{9,... | collective-permute-start | bytes 884744 | tf_op jit(solution)/shard_map/ppermute | solution.py:45
  28.1 4.2 %collective-permute-done.1 = bf16[576,256]{1,0:T(8,128)(2,1)S(1)} collective-permute-done((bf16[576,256]{1,0:T(8,128)(2,1)S(1)}, bf16[576,256]{1,0:T(8,128)(2,1)S(1)}, u32[]{:S(2)}, u32[]{:S(2)}) %collective-permute-start.1) | collective-permute-done | bytes 294944 | tf_op jit(solution)/shard_map/ppermute | solution.py:45
  32.3 3.1 %collective-permute-done = bf16[576,256]{1,0:T(8,128)(2,1)S(1)} collective-permute-done((bf16[576,256]{1,0:T(8,128)(2,1)S(1)}, bf16[576,256]{1,0:T(8,128)(2,1)S(1)}, u32[]{:S(2)}, u32[]{:S(2)}) %collective-permute-start) | collective-permute-done | bytes 294944 | tf_op jit(solution)/shard_map/ppermute | solution.py:45
  35.6 3.1 %collective-permute-start.5 = (bf16[4,576,256]{2,1,0:T(8,128)(2,1)S(1)}, bf16[4,576,256]{2,1,0:T(8,128)(2,1)S(1)}, u32[]{:S(2)}, u32[]{:S(2)}) collective-permute-start(bf16[4,576,256]{2,1,0:T(8,128)(2,1)S(1)} %pad_maximum_fusion.t0), channel_id=1, source_target_pairs={{0,12},{1,13},{2,14},{3,15},{4,0},{5,1},{6,2},{7,3},{8,4},{9,5},{1... | collective-permute-start | bytes 3538952 | tf_op jit(solution)/shard_map/ppermute | solution.py:45
  38.7 13.7 %collective-permute-done.5.t3 = bf16[4,576,256]{2,1,0:T(8,128)(2,1)S(1)} collective-permute-done((bf16[4,576,256]{2,1,0:T(8,128)(2,1)S(1)}, bf16[4,576,256]{2,1,0:T(8,128)(2,1)S(1)}, u32[]{:S(2)}, u32[]{:S(2)}) %collective-permute-start.5) | collective-permute-done | bytes 1179680 | tf_op jit(solution)/shard_map/ppermute | solution.py:45
  52.4 3.8 %collective-permute-start.6 = (bf16[2,576,256]{2,1,0:T(8,128)(2,1)S(1)}, bf16[2,576,256]{2,1,0:T(8,128)(2,1)S(1)}, u32[]{:S(2)}, u32[]{:S(2)}) collective-permute-start(bf16[2,576,256]{2,1,0:T(8,128)(2,1)S(1)} %slice.231), channel_id=1, source_target_pairs={{0,12},{1,13},{2,14},{3,15},{4,0},{5,1},{6,2},{7,3},{8,4},{9,5},{1... | collective-permute-start | bytes 1769480 | tf_op jit(solution)/shard_map/ppermute | solution.py:45
  56.4 4.1 %near.1 = (f32[768,256]{1,0:T(8,128)S(1)}, f32[768,256]{1,0:T(8,128)S(1)}, bf16[5120,256]{1,0:T(8,128)(2,1)S(1)}) custom-call(bf16[4,576,256]{2,1,0:T(8,128)(2,1)S(1)} %pad_maximum_fusion.t0, bf16[4,576,256]{2,1,0:T(8,128)(2,1)S(1)} %collective-permute-done.3.t1, bf16[4,576,256]{2,1,0:T(8,128)(2,1)S(1)} %collective-permute-done.5.t3, ...), custom_call_target="tpu_custom_call" | custom-call | flops 3623878656 | bytes 14000000 | tf_op jit(solution)/shard_map/near/pallas_call | solution.py:127
  60.5 3.1 %collective-permute-done.6.t2b = bf16[2,576,256]{2,1,0:T(8,128)(2,1)S(1)} collective-permute-done((bf16[2,576,256]{2,1,0:T(8,128)(2,1)S(1)}, bf16[2,576,256]{2,1,0:T(8,128)(2,1)S(1)}, u32[]{:S(2)}, u32[]{:S(2)}) %collective-permute-start.6) | collective-permute-done | bytes 589856 | tf_op jit(solution)/shard_map/ppermute | solution.py:45
  63.6 3.8 %collective-permute-done.4.t2a = bf16[2,576,256]{2,1,0:T(8,128)(2,1)S(1)} collective-permute-done((bf16[2,576,256]{2,1,0:T(8,128)(2,1)S(1)}, bf16[2,576,256]{2,1,0:T(8,128)(2,1)S(1)}, u32[]{:S(2)}, u32[]{:S(2)}) %collective-permute-start.4) | collective-permute-done | bytes 589856 | tf_op jit(solution)/shard_map/ppermute | solution.py:45
  70.4 3.0 %collective-permute-done.9 = f32[8,256]{1,0:T(8,128)S(1)} collective-permute-done((f32[8,256]{1,0:T(8,128)S(1)}, f32[8,256]{1,0:T(8,128)S(1)}, u32[]{:S(2)}, u32[]{:S(2)}) %collective-permute-start.9) | collective-permute-done | bytes 8224 | tf_op jit(solution)/shard_map/ppermute | solution.py:45
  74.2 3.7 %collective-permute-start.11 = (f32[8,256]{1,0:T(8,128)S(1)}, f32[8,256]{1,0:T(8,128)S(1)}, u32[]{:S(2)}, u32[]{:S(2)}) collective-permute-start(f32[8,256]{1,0:T(8,128)S(1)} %pad_maximum_fusion.10), channel_id=1, source_target_pairs={{0,2},{1,3},{2,0},{3,1},{4,6},{5,7},{6,4},{7,5},{8,10},{9,11},{10,... | collective-permute-start | bytes 24584 | tf_op jit(solution)/shard_map/ppermute | solution.py:45
  78.1 3.7 %collective-permute-done.11 = f32[8,256]{1,0:T(8,128)S(1)} collective-permute-done((f32[8,256]{1,0:T(8,128)S(1)}, f32[8,256]{1,0:T(8,128)S(1)}, u32[]{:S(2)}, u32[]{:S(2)}) %collective-permute-start.11) | collective-permute-done | bytes 8224 | tf_op jit(solution)/shard_map/ppermute | solution.py:45
  85.9 2.5 %collective-permute-start.13 = (f32[8,256]{1,0:T(8,128)S(1)}, f32[8,256]{1,0:T(8,128)S(1)}, u32[]{:S(2)}, u32[]{:S(2)}) collective-permute-start(f32[8,256]{1,0:T(8,128)S(1)} %pad_maximum_fusion.9), channel_id=1, source_target_pairs={{0,16},{1,17},{2,18},{3,19},{4,20},{5,21},{6,22},{7,23},{8,24},{9,... | collective-permute-start | bytes 24584 | tf_op jit(solution)/shard_map/ppermute | solution.py:45
  99.0 2.4 %collective-permute-start.20 = (bf16[2,320,256]{2,1,0:T(8,128)(2,1)S(1)}, bf16[2,320,256]{2,1,0:T(8,128)(2,1)S(1)}, u32[]{:S(2)}, u32[]{:S(2)}) collective-permute-start(bf16[2,320,256]{2,1,0:T(8,128)(2,1)S(1)} %get-tuple-element.35), channel_id=1, source_target_pairs={{0,12},{1,13},{2,14},{3,15},{4,0},{5,1},{6,2},{7,3},{8,4},{9,5},{1... | collective-permute-start | bytes 983048 | tf_op jit(solution)/shard_map/ppermute | solution.py:45
  101.4 3.1 %rest.1 = (bf16[4,320,256]{2,1,0:T(8,128)(2,1)S(1)}, bf16[4,320,256]{2,1,0:T(8,128)(2,1)S(1)}, bf16[4,320,256]{2,1,0:T(8,128)(2,1)S(1)}) custom-call(bf16[384,256]{1,0:T(8,128)(2,1)S(1)} %get-tuple-element.37.g_own, bf16[384,256]{1,0:T(8,128)(2,1)S(1)} %get-tuple-element.36.g_oth, bf16[384,5120]{1,0:T(8,128)(2,1)S(1)} %copy-done, ...), custom_call_target="tpu_custom_call" | custom-call | flops 2013265920 | bytes 14000000 | tf_op jit(solution)/shard_map/rest/pallas_call | solution.py:127
  106.7 3.3 %collective-permute-start.23 = (bf16[4,320,256]{2,1,0:T(8,128)(2,1)S(1)}, bf16[4,320,256]{2,1,0:T(8,128)(2,1)S(1)}, u32[]{:S(2)}, u32[]{:S(2)}) collective-permute-start(bf16[4,320,256]{2,1,0:T(8,128)(2,1)S(1)} %pad_maximum_fusion.2), channel_id=1, source_target_pairs={{0,12},{1,13},{2,14},{3,15},{4,0},{5,1},{6,2},{7,3},{8,4},{9,5},{1... | collective-permute-start | bytes 1966088 | tf_op jit(solution)/shard_map/ppermute | solution.py:45
  110.2 5.7 %head.1 = bf16[384,5120]{1,0:T(8,128)(2,1)} custom-call(bf16[384,256]{1,0:T(8,128)(2,1)S(1)} %get-tuple-element.37.g_own, bf16[384,256]{1,0:T(8,128)(2,1)S(1)} %collective-permute-done.21.g_got, bf16[5120,256]{1,0:T(8,128)(2,1)S(1)} %get-tuple-element.47.h_own, bf16[5120,256]{1,0:T(8,128)(2,1)S(1)} %collective-permute-done.24.h_got), custom_call_target="tpu_custom_call" | custom-call | flops 2013265920 | bytes 10000000 | tf_op jit(solution)/shard_map/head/pallas_call | solution.py:216
  115.9 2.2 %collective-permute-done.23 = bf16[4,320,256]{2,1,0:T(8,128)(2,1)S(1)} collective-permute-done((bf16[4,320,256]{2,1,0:T(8,128)(2,1)S(1)}, bf16[4,320,256]{2,1,0:T(8,128)(2,1)S(1)}, u32[]{:S(2)}, u32[]{:S(2)}) %collective-permute-start.23) | collective-permute-done | bytes 655392 | tf_op jit(solution)/shard_map/ppermute | solution.py:45
  118.1 3.9 %collective-permute-done.22 = bf16[4,320,256]{2,1,0:T(8,128)(2,1)S(1)} collective-permute-done((bf16[4,320,256]{2,1,0:T(8,128)(2,1)S(1)}, bf16[4,320,256]{2,1,0:T(8,128)(2,1)S(1)}, u32[]{:S(2)}, u32[]{:S(2)}) %collective-permute-start.22) | collective-permute-done | bytes 655392 | tf_op jit(solution)/shard_map/ppermute | solution.py:45
  122.3 5.7 %collective-permute-start.25 = (bf16[320,256]{1,0:T(8,128)(2,1)S(1)}, bf16[320,256]{1,0:T(8,128)(2,1)S(1)}, u32[]{:S(2)}, u32[]{:S(2)}) collective-permute-start(bf16[320,256]{1,0:T(8,128)(2,1)S(1)} %get-tuple-element.61), channel_id=1, source_target_pairs={{0,16},{1,17},{2,18},{3,19},{4,20},{5,21},{6,22},{7,23},{8,24},{9,... | collective-permute-start | bytes 491528 | tf_op jit(solution)/shard_map/ppermute | solution.py:45
  128.1 2.1 %collective-permute-start.27 = (bf16[320,256]{1,0:T(8,128)(2,1)S(1)}, bf16[320,256]{1,0:T(8,128)(2,1)S(1)}, u32[]{:S(2)}, u32[]{:S(2)}) collective-permute-start(bf16[320,256]{1,0:T(8,128)(2,1)S(1)} %get-tuple-element.62), channel_id=1, source_target_pairs={{0,32},{1,33},{2,34},{3,35},{4,36},{5,37},{6,38},{7,39},{8,40},{9,... | collective-permute-start | bytes 491528 | tf_op jit(solution)/shard_map/ppermute | solution.py:45
  131.4 3.6 %collective-permute-done.27 = bf16[320,256]{1,0:T(8,128)(2,1)S(1)} collective-permute-done((bf16[320,256]{1,0:T(8,128)(2,1)S(1)}, bf16[320,256]{1,0:T(8,128)(2,1)S(1)}, u32[]{:S(2)}, u32[]{:S(2)}) %collective-permute-start.27) | collective-permute-done | bytes 163872 | tf_op jit(solution)/shard_map/ppermute | solution.py:45
  136.8 14.6 %all_to_all.11 = f32[8,80,128]{2,1,0:T(8,128)S(1)} all-to-all(f32[8,80,128]{2,1,0:T(8,128)S(1)} %bitcast.26), channel_id=1, replica_groups=mesh['zl'=2,'c'=2,'x'=4,'y'=4,'zh'=4] {'zl','zh'}, dimensions={0} | all-to-all | bytes 655360 | tf_op jit(solution)/shard_map/all_to_all | solution.py:278
  (97 shorter events, 29.4 us)
Async XLA Ops:
  0.6 55.7 %collective-permute-start.7 = (bf16[384,5120]{1,0:T(8,128)(2,1)}, bf16[384,5120]{1,0:T(8,128)(2,1)S(1)}, u32[]{:S(2)}, u32[]{:S(2)}) collective-permute-start(bf16[384,5120]{1,0:T(8,128)(2,1)} %ws.7), channel_id=1, source_target_pairs={{0,64},{1,65},{2,66},{3,67},{4,68},{5,69},{6,70},{7,71},{8,72},{9,... | collective-permute-start | bytes 11796488 | tf_op jit(solution)/shard_map/ppermute | solution.py:45
  0.7 55.6 %collective-permute-start.8 = (bf16[384,4096]{1,0:T(8,128)(2,1)}, bf16[384,4096]{1,0:T(8,128)(2,1)S(1)}, u32[]{:S(2)}, u32[]{:S(2)}) collective-permute-start(bf16[384,4096]{1,0:T(8,128)(2,1)} %wt.3), channel_id=1, source_target_pairs={{0,64},{1,65},{2,66},{3,67},{4,68},{5,69},{6,70},{7,71},{8,72},{9,... | collective-permute-start | bytes 9437192 | tf_op jit(solution)/shard_map/ppermute | solution.py:45
  23.9 8.4 %collective-permute-start.1 = (bf16[576,256]{1,0:T(8,128)(2,1)S(1)}, bf16[576,256]{1,0:T(8,128)(2,1)S(1)}, u32[]{:S(2)}, u32[]{:S(2)}) collective-permute-start(bf16[576,256]{1,0:T(8,128)(2,1)S(1)} %get-tuple-element.67), channel_id=1, source_target_pairs={{0,32},{1,33},{2,34},{3,35},{4,36},{5,37},{6,38},{7,39},{8,40},{9,... | collective-permute-start | bytes 884744 | tf_op jit(solution)/shard_map/ppermute | solution.py:45
  26.1 9.3 %collective-permute-start = (bf16[576,256]{1,0:T(8,128)(2,1)S(1)}, bf16[576,256]{1,0:T(8,128)(2,1)S(1)}, u32[]{:S(2)}, u32[]{:S(2)}) collective-permute-start(bf16[576,256]{1,0:T(8,128)(2,1)S(1)} %get-tuple-element.67), channel_id=1, source_target_pairs={{0,16},{1,17},{2,18},{3,19},{4,20},{5,21},{6,22},{7,23},{8,24},{9,... | collective-permute-start | bytes 884744 | tf_op jit(solution)/shard_map/ppermute | solution.py:45
  26.1 9.3 %collective-permute-start.2 = (bf16[576,256]{1,0:T(8,128)(2,1)S(1)}, bf16[576,256]{1,0:T(8,128)(2,1)S(1)}, u32[]{:S(2)}, u32[]{:S(2)}) collective-permute-start(bf16[576,256]{1,0:T(8,128)(2,1)S(1)} %get-tuple-element.67), channel_id=1, source_target_pairs={{0,48},{1,49},{2,50},{3,51},{4,52},{5,53},{6,54},{7,55},{8,56},{9,... | collective-permute-start | bytes 884744 | tf_op jit(solution)/shard_map/ppermute | solution.py:45
  35.6 16.8 %collective-permute-start.5 = (bf16[4,576,256]{2,1,0:T(8,128)(2,1)S(1)}, bf16[4,576,256]{2,1,0:T(8,128)(2,1)S(1)}, u32[]{:S(2)}, u32[]{:S(2)}) collective-permute-start(bf16[4,576,256]{2,1,0:T(8,128)(2,1)S(1)} %pad_maximum_fusion.t0), channel_id=1, source_target_pairs={{0,12},{1,13},{2,14},{3,15},{4,0},{5,1},{6,2},{7,3},{8,4},{9,5},{1... | collective-permute-start | bytes 3538952 | tf_op jit(solution)/shard_map/ppermute | solution.py:45
  38.7 17.5 %collective-permute-start.3 = (bf16[4,576,256]{2,1,0:T(8,128)(2,1)S(1)}, bf16[4,576,256]{2,1,0:T(8,128)(2,1)S(1)}, u32[]{:S(2)}, u32[]{:S(2)}) collective-permute-start(bf16[4,576,256]{2,1,0:T(8,128)(2,1)S(1)} %pad_maximum_fusion.t0), channel_id=1, source_target_pairs={{0,4},{1,5},{2,6},{3,7},{4,8},{5,9},{6,10},{7,11},{8,12},{9,13},{1... | collective-permute-start | bytes 3538952 | tf_op jit(solution)/shard_map/ppermute | solution.py:45
  52.4 11.2 %collective-permute-start.6 = (bf16[2,576,256]{2,1,0:T(8,128)(2,1)S(1)}, bf16[2,576,256]{2,1,0:T(8,128)(2,1)S(1)}, u32[]{:S(2)}, u32[]{:S(2)}) collective-permute-start(bf16[2,576,256]{2,1,0:T(8,128)(2,1)S(1)} %slice.231), channel_id=1, source_target_pairs={{0,12},{1,13},{2,14},{3,15},{4,0},{5,1},{6,2},{7,3},{8,4},{9,5},{1... | collective-permute-start | bytes 1769480 | tf_op jit(solution)/shard_map/ppermute | solution.py:45
  56.2 11.2 %collective-permute-start.4 = (bf16[2,576,256]{2,1,0:T(8,128)(2,1)S(1)}, bf16[2,576,256]{2,1,0:T(8,128)(2,1)S(1)}, u32[]{:S(2)}, u32[]{:S(2)}) collective-permute-start(bf16[2,576,256]{2,1,0:T(8,128)(2,1)S(1)} %slice.230), channel_id=1, source_target_pairs={{0,4},{1,5},{2,6},{3,7},{4,8},{5,9},{6,10},{7,11},{8,12},{9,13},{1... | collective-permute-start | bytes 1769480 | tf_op jit(solution)/shard_map/ppermute | solution.py:45
  73.5 4.6 %collective-permute-start.12 = (f32[8,256]{1,0:T(8,128)S(1)}, f32[8,256]{1,0:T(8,128)S(1)}, u32[]{:S(2)}, u32[]{:S(2)}) collective-permute-start(f32[8,256]{1,0:T(8,128)S(1)} %pad_maximum_fusion.10), channel_id=1, source_target_pairs={{0,3},{1,0},{2,1},{3,2},{4,7},{5,4},{6,5},{7,6},{8,11},{9,8},{10,9... | collective-permute-start | bytes 24584 | tf_op jit(solution)/shard_map/ppermute | solution.py:45
  74.2 7.6 %collective-permute-start.11 = (f32[8,256]{1,0:T(8,128)S(1)}, f32[8,256]{1,0:T(8,128)S(1)}, u32[]{:S(2)}, u32[]{:S(2)}) collective-permute-start(f32[8,256]{1,0:T(8,128)S(1)} %pad_maximum_fusion.10), channel_id=1, source_target_pairs={{0,2},{1,3},{2,0},{3,1},{4,6},{5,7},{6,4},{7,5},{8,10},{9,11},{10,... | collective-permute-start | bytes 24584 | tf_op jit(solution)/shard_map/ppermute | solution.py:45
  77.9 5.8 %collective-permute-start.10 = (f32[8,256]{1,0:T(8,128)S(1)}, f32[8,256]{1,0:T(8,128)S(1)}, u32[]{:S(2)}, u32[]{:S(2)}) collective-permute-start(f32[8,256]{1,0:T(8,128)S(1)} %pad_maximum_fusion.10), channel_id=1, source_target_pairs={{0,1},{1,2},{2,3},{3,0},{4,5},{5,6},{6,7},{7,4},{8,9},{9,10},{10,1... | collective-permute-start | bytes 24584 | tf_op jit(solution)/shard_map/ppermute | solution.py:45
  83.8 4.7 %collective-permute-start.15 = (f32[8,256]{1,0:T(8,128)S(1)}, f32[8,256]{1,0:T(8,128)S(1)}, u32[]{:S(2)}, u32[]{:S(2)}) collective-permute-start(f32[8,256]{1,0:T(8,128)S(1)} %pad_maximum_fusion.9), channel_id=1, source_target_pairs={{0,48},{1,49},{2,50},{3,51},{4,52},{5,53},{6,54},{7,55},{8,56},{9,... | collective-permute-start | bytes 24584 | tf_op jit(solution)/shard_map/ppermute | solution.py:45
  84.4 5.2 %collective-permute-start.14 = (f32[8,256]{1,0:T(8,128)S(1)}, f32[8,256]{1,0:T(8,128)S(1)}, u32[]{:S(2)}, u32[]{:S(2)}) collective-permute-start(f32[8,256]{1,0:T(8,128)S(1)} %pad_maximum_fusion.9), channel_id=1, source_target_pairs={{0,32},{1,33},{2,34},{3,35},{4,36},{5,37},{6,38},{7,39},{8,40},{9,... | collective-permute-start | bytes 24584 | tf_op jit(solution)/shard_map/ppermute | solution.py:45
  88.4 21.8 %collective-permute-start.24 = (bf16[5120,256]{1,0:T(8,128)(2,1)S(1)}, bf16[5120,256]{1,0:T(8,128)(2,1)S(1)}, u32[]{:S(2)}, u32[]{:S(2)}) collective-permute-start(bf16[5120,256]{1,0:T(8,128)(2,1)S(1)} %get-tuple-element.47.h_own), channel_id=1, source_target_pairs={{0,64},{1,65},{2,66},{3,67},{4,68},{5,69},{6,70},{7,71},{8,72},{9,... | collective-permute-start | bytes 7864328 | tf_op jit(solution)/shard_map/ppermute | solution.py:45
  90.0 5.2 %collective-permute-start.17 = (f32[8,256]{1,0:T(8,128)S(1)}, f32[8,256]{1,0:T(8,128)S(1)}, u32[]{:S(2)}, u32[]{:S(2)}) collective-permute-start(f32[8,256]{1,0:T(8,128)S(1)} %pad_maximum_fusion.8), channel_id=1, source_target_pairs={{0,8},{1,9},{2,10},{3,11},{4,12},{5,13},{6,14},{7,15},{8,0},{9,1},... | collective-permute-start | bytes 24584 | tf_op jit(solution)/shard_map/ppermute | solution.py:45
  90.8 5.5 %collective-permute-start.16 = (f32[8,256]{1,0:T(8,128)S(1)}, f32[8,256]{1,0:T(8,128)S(1)}, u32[]{:S(2)}, u32[]{:S(2)}) collective-permute-start(f32[8,256]{1,0:T(8,128)S(1)} %pad_maximum_fusion.8), channel_id=1, source_target_pairs={{0,4},{1,5},{2,6},{3,7},{4,8},{5,9},{6,10},{7,11},{8,12},{9,13},{1... | collective-permute-start | bytes 24584 | tf_op jit(solution)/shard_map/ppermute | solution.py:45
  98.2 8.3 %collective-permute-start.19 = (bf16[2,320,256]{2,1,0:T(8,128)(2,1)S(1)}, bf16[2,320,256]{2,1,0:T(8,128)(2,1)S(1)}, u32[]{:S(2)}, u32[]{:S(2)}) collective-permute-start(bf16[2,320,256]{2,1,0:T(8,128)(2,1)S(1)} %get-tuple-element.34), channel_id=1, source_target_pairs={{0,4},{1,5},{2,6},{3,7},{4,8},{5,9},{6,10},{7,11},{8,12},{9,13},{1... | collective-permute-start | bytes 983048 | tf_op jit(solution)/shard_map/ppermute | solution.py:45
  99.0 7.4 %collective-permute-start.20 = (bf16[2,320,256]{2,1,0:T(8,128)(2,1)S(1)}, bf16[2,320,256]{2,1,0:T(8,128)(2,1)S(1)}, u32[]{:S(2)}, u32[]{:S(2)}) collective-permute-start(bf16[2,320,256]{2,1,0:T(8,128)(2,1)S(1)} %get-tuple-element.35), channel_id=1, source_target_pairs={{0,12},{1,13},{2,14},{3,15},{4,0},{5,1},{6,2},{7,3},{8,4},{9,5},{1... | collective-permute-start | bytes 983048 | tf_op jit(solution)/shard_map/ppermute | solution.py:45
  106.7 11.4 %collective-permute-start.23 = (bf16[4,320,256]{2,1,0:T(8,128)(2,1)S(1)}, bf16[4,320,256]{2,1,0:T(8,128)(2,1)S(1)}, u32[]{:S(2)}, u32[]{:S(2)}) collective-permute-start(bf16[4,320,256]{2,1,0:T(8,128)(2,1)S(1)} %pad_maximum_fusion.2), channel_id=1, source_target_pairs={{0,12},{1,13},{2,14},{3,15},{4,0},{5,1},{6,2},{7,3},{8,4},{9,5},{1... | collective-permute-start | bytes 1966088 | tf_op jit(solution)/shard_map/ppermute | solution.py:45
  110.1 11.9 %collective-permute-start.22 = (bf16[4,320,256]{2,1,0:T(8,128)(2,1)S(1)}, bf16[4,320,256]{2,1,0:T(8,128)(2,1)S(1)}, u32[]{:S(2)}, u32[]{:S(2)}) collective-permute-start(bf16[4,320,256]{2,1,0:T(8,128)(2,1)S(1)} %pad_maximum_fusion.1), channel_id=1, source_target_pairs={{0,4},{1,5},{2,6},{3,7},{4,8},{5,9},{6,10},{7,11},{8,12},{9,13},{1... | collective-permute-start | bytes 1966088 | tf_op jit(solution)/shard_map/ppermute | solution.py:45
  122.3 9.1 %collective-permute-start.25 = (bf16[320,256]{1,0:T(8,128)(2,1)S(1)}, bf16[320,256]{1,0:T(8,128)(2,1)S(1)}, u32[]{:S(2)}, u32[]{:S(2)}) collective-permute-start(bf16[320,256]{1,0:T(8,128)(2,1)S(1)} %get-tuple-element.61), channel_id=1, source_target_pairs={{0,16},{1,17},{2,18},{3,19},{4,20},{5,21},{6,22},{7,23},{8,24},{9,... | collective-permute-start | bytes 491528 | tf_op jit(solution)/shard_map/ppermute | solution.py:45
  128.1 6.9 %collective-permute-start.27 = (bf16[320,256]{1,0:T(8,128)(2,1)S(1)}, bf16[320,256]{1,0:T(8,128)(2,1)S(1)}, u32[]{:S(2)}, u32[]{:S(2)}) collective-permute-start(bf16[320,256]{1,0:T(8,128)(2,1)S(1)} %get-tuple-element.62), channel_id=1, source_target_pairs={{0,32},{1,33},{2,34},{3,35},{4,36},{5,37},{6,38},{7,39},{8,40},{9,... | collective-permute-start | bytes 491528 | tf_op jit(solution)/shard_map/ppermute | solution.py:45
  130.2 6.5 %collective-permute-start.26 = (bf16[320,256]{1,0:T(8,128)(2,1)S(1)}, bf16[320,256]{1,0:T(8,128)(2,1)S(1)}, u32[]{:S(2)}, u32[]{:S(2)}) collective-permute-start(bf16[320,256]{1,0:T(8,128)(2,1)S(1)} %get-tuple-element.63), channel_id=1, source_target_pairs={{0,48},{1,49},{2,50},{3,51},{4,52},{5,53},{6,54},{7,55},{8,56},{9,... | collective-permute-start | bytes 491528 | tf_op jit(solution)/shard_map/ppermute | solution.py:45
  (7 other events, 97.3 us)

commit v6 on v5

--- a/solution.py
+++ b/solution.py
@@ -67,6 +67,19 @@
 def window(at):
     start = pl.multiple_of(((at * 5) >> 1) * 128, 128)
     return pl.ds(start, WIDE), pl.multiple_of((at & 1) * 64, 64)
+
+
+def spread_kernel(mine, out):
+    for i in range(8):
+        out[i] = mine[...]
+
+
+def weave_kernel(along, out):
+    for zh in range(4):
+        for zl in range(2):
+            tokens = slice(zl * 128, (zl + 1) * 128)
+            out[zh * 80 : (zh + 1) * 80, tokens] = along[zl * 4 + zh, 0:80]
+            out[NS + zh * 64 : NS + (zh + 1) * 64, tokens] = along[zl * 4 + zh, 80:144]
 
 
 def near_kernel(t0, t1, t3, ws, wso, wt, wto, s_ref, t_ref, hs, ht):
@@ -159,8 +172,15 @@
     stats, local, weights, es_ref, et_ref, ws, wso, kl_ref, g_own, g_oth, o2a, o2b, part
 ):
     zl, c, x, y, _ = place()
-    top, totals = stats[0:2], stats[2:4]
-    kl = stats[4:5] / totals[1:2] - top[1:2] - jnp.log(totals[1:2]) + top[0:1] + jnp.log(totals[0:1])
+    top = stats[0, 0:2]
+    for i in range(1, 16):
+        top = jnp.maximum(top, stats[i, 0:2])
+    totals, cross = jnp.zeros((2, TOK), F32), jnp.zeros((1, TOK), F32)
+    for i in range(16):
+        scale = jnp.exp(stats[i, 0:2] - top)
+        totals += stats[i, 2:4] * scale
+        cross += stats[i, 4:5] * scale[1:2]
+    kl = cross / totals[1:2] - top[1:2] - jnp.log(totals[1:2]) + top[0:1] + jnp.log(totals[0:1])
     kl_ref[...] = jnp.where(zl == 0, kl[:, :128], kl[:, 128:])
     weight = jnp.concatenate(
         [jnp.where(c == 0, weights[i : i + 1], weights[i + 1 : i + 2]) for i in (0, 2)], axis=1
@@ -242,10 +262,10 @@
     teacher_other = send(teacher_head, CORE)
     student_other = send(student_head, CORE)
 
-    mine = jnp.concatenate([jnp.broadcast_to(h.T, (8,) + h.T.shape) for h in (student_hidden, teacher_hidden)], axis=1)
-    along = lax.all_to_all(mine, ("zl", "zh"), 0, 0)
-    along = jnp.concatenate([along[:4], along[4:]], axis=2)
-    block = jnp.concatenate([along[:, :80].reshape(NS, TOK), along[:, 80:].reshape(NT, TOK)], axis=0)
+    mine = jnp.concatenate([student_hidden.T, teacher_hidden.T], axis=0)
+    copies = vmem_call(spread_kernel, "spread", [((8, 144, 128), BF16)], [], 1, mine)[0]
+    along = lax.all_to_all(copies, ("zl", "zh"), 0, 0)
+    block = vmem_call(weave_kernel, "weave", [((NS + NT, TOK), BF16)], [], 1, along)[0]
     line = jnp.stack((block,) + ring(block, FIRST))
     before, after = send(line, SECOND[1]), send(line, SECOND[3])
     far_low, far_high = send(before[:2], SECOND[1]), send(after[2:], SECOND[3])
@@ -253,21 +273,20 @@
     heads = (student_head, student_other, teacher_head, teacher_other)
     near = near_call(line, before, after, *heads)
     es, et, local, hidden_own = far_call(far_low, far_high, *near, *heads)
-    hidden_got = send(hidden_own, CORE)
-
     stats = merge((local, send(local, PAIR)))
-    for perms in (ZH, FIRST, SECOND):
-        stats = merge((stats,) + ring(stats, perms))
+    stats = merge((stats,) + ring(stats, ZH))
+    stats = lax.all_to_all(jnp.broadcast_to(stats, (16, 8, TOK)), ("x", "y"), 0, 0)
     kl_rows, g_own, g_oth, o2a, o2b = opposite_call(
         stats, local, row_weight.reshape(4, 128), es, et, student_head, student_other
     )
     low, high = send(o2a, SECOND[1]), send(o2b, SECOND[3])
-    g_got = send(g_oth, CORE)
-    low, high, g_got, o0, o1, o3 = lax.optimization_barrier(
-        (low, high, g_got, *rest_call(g_own, g_oth, student_head, student_other))
+    g_got, hidden_got = send(g_oth, CORE), send(hidden_own, CORE)
+    low, high, g_got, hidden_got, o0, o1, o3 = lax.optimization_barrier(
+        (low, high, g_got, hidden_got, *rest_call(g_own, g_oth, student_head, student_other))
     )
-    r1 = send(jnp.concatenate([(o1[:2].astype(F32) + low.astype(F32)).astype(BF16), o1[2:]]), SECOND[1])
-    r3 = send(jnp.concatenate([o3[:2], (o3[2:].astype(F32) + high.astype(F32)).astype(BF16)]), SECOND[3])
+    o1 = jnp.concatenate([(o1[:2].astype(F32) + low.astype(F32)).astype(BF16), o1[2:]])
+    o3 = jnp.concatenate([o3[:2], (o3[2:].astype(F32) + high.astype(F32)).astype(BF16)])
+    r1, r3 = send(o1, SECOND[1]), send(o3, SECOND[3])
     head_grad = head_call(g_own, g_got, hidden_own, hidden_got)
     r1, r3, head_grad = lax.optimization_barrier((r1, r3, head_grad))
 

time: 152 us -> 149 us (0.980)
  blocking collectives: 35.6 us -> 47 us
  starting transfers between devices: 38.4 us -> 28.7 us
  waiting for transfers between devices: 56.8 us -> 50.9 us
    all_to_all x1 -> x2, blocking collectives: 21 us -> 32.5 us  [the longest x1 21 us: per_device(): along = lax.all_to_all(copies, ('zl', 'zh'), 0, 0)]
    ppermute x28 -> x22, starting transfers between devices: 38.4 us -> 28.7 us  [send(): return lax.ppermute(value, AXES, pairs)]
    ppermute x28 -> x22, waiting for transfers between devices: 56.8 us -> 50.9 us  [send(): return lax.ppermute(value, AXES, pairs)]
    unnamed x6, local copies, waits for them, and re-layouts: 0.01 us -> 1.89 us
    pallas_call x4 -> x6, Pallas kernels: 11 us -> 11.2 us  [vmem_call(): pl.pallas_call(kernel, out_shape=tuple((jax.ShapeDtypeStruct(*o) for o in...]
  transfers between devices with their start and end apart: 28 -> 22, of which waited for: 20 -> 16; matrix products, arithmetic and copies ran while one was open for 2% -> 1% of each run, Pallas kernels for 10% -> 10%
where the time goes in v6:
time: 149 us
  waiting for transfers between devices  50.9 us (34%)
  blocking collectives  47 us (32%)
  starting transfers between devices  28.7 us (19%)
  Pallas kernels  16.8 us (11%)
  other arithmetic  2.32 us (2%)
  local copies, waits for them, and re-layouts  2.11 us (1%)
    ppermute x22, waiting for transfers between devices, send(): return lax.ppermute(value, AXES, pairs)  50.9 us
    ppermute x22, starting transfers between devices, send(): return lax.ppermute(value, AXES, pairs)  28.7 us
    all_to_all x1, blocking collectives, per_device(): along = lax.all_to_all(copies, ('zl', 'zh'), 0, 0)  21 us
    all_to_all x1, blocking collectives, per_device(): hidden_grad = jnp.sum(lax.all_to_all(sums, ('zl', 'zh'), 0, 0), axis=0).T  14.4 us
    all_to_all x1, blocking collectives, per_device(): lax.all_to_all(jnp.broadcast_to(stats, (16, 8, TOK)), ('x', 'y'), 0, 0)  11.6 us
    pallas_call x6, Pallas kernels, vmem_call(): pl.pallas_call(kernel, out_shape=tuple((jax.ShapeDtypeStruct(*o) for o in...  11.2 us
    pallas_call x1, Pallas kernels, head_call(): pl.pallas_call(head_kernel, out_shape=jax.ShapeDtypeStruct((ROWS, DS), BF...  5.65 us
  transfers between devices with their start and end apart: 22, of which 16 were waited for; matrix products, arithmetic and copies ran while one was open for 1% of the time, Pallas kernels for 10%

profile of v6, /device:TPU:2, one launch (start us, length us, event | category | flops | bytes accessed | tf_op | source)
XLA Modules:
  0.0 148.7 jit_solution(5568856368026546632)
XLA Ops:
  2.0 21.0 %all_to_all.15.along = bf16[8,144,128]{2,1,0:T(8,128)(2,1)S(1)} all-to-all(bf16[8,144,128]{2,1,0:T(8,128)(2,1)S(1)} %spread.1), channel_id=1, replica_groups=mesh['zl'=2,'c'=2,'x'=4,'y'=4,'zh'=4] {'zl','zh'}, dimensions={0} | all-to-all | bytes 589824 | tf_op jit(solution)/shard_map/all_to_all | solution.py:267
  23.7 2.4 %collective-permute-start.1 = (bf16[576,256]{1,0:T(8,128)(2,1)S(1)}, bf16[576,256]{1,0:T(8,128)(2,1)S(1)}, u32[]{:S(2)}, u32[]{:S(2)}) collective-permute-start(bf16[576,256]{1,0:T(8,128)(2,1)S(1)} %weave.1), channel_id=1, source_target_pairs={{0,32},{1,33},{2,34},{3,35},{4,36},{5,37},{6,38},{7,39},{8,40},{9,... | collective-permute-start | bytes 884744 | tf_op jit(solution)/shard_map/ppermute | solution.py:45
  27.9 2.0 %collective-permute-done.2 = bf16[576,256]{1,0:T(8,128)(2,1)S(1)} collective-permute-done((bf16[576,256]{1,0:T(8,128)(2,1)S(1)}, bf16[576,256]{1,0:T(8,128)(2,1)S(1)}, u32[]{:S(2)}, u32[]{:S(2)}) %collective-permute-start.2) | collective-permute-done | bytes 294944 | tf_op jit(solution)/shard_map/ppermute | solution.py:45
  29.9 4.1 %collective-permute-done.1 = bf16[576,256]{1,0:T(8,128)(2,1)S(1)} collective-permute-done((bf16[576,256]{1,0:T(8,128)(2,1)S(1)}, bf16[576,256]{1,0:T(8,128)(2,1)S(1)}, u32[]{:S(2)}, u32[]{:S(2)}) %collective-permute-start.1) | collective-permute-done | bytes 294944 | tf_op jit(solution)/shard_map/ppermute | solution.py:45
  35.3 3.1 %collective-permute-start.5 = (bf16[4,576,256]{2,1,0:T(8,128)(2,1)S(1)}, bf16[4,576,256]{2,1,0:T(8,128)(2,1)S(1)}, u32[]{:S(2)}, u32[]{:S(2)}) collective-permute-start(bf16[4,576,256]{2,1,0:T(8,128)(2,1)S(1)} %pad_maximum_fusion.t0), channel_id=1, source_target_pairs={{0,12},{1,13},{2,14},{3,15},{4,0},{5,1},{6,2},{7,3},{8,4},{9,5},{1... | collective-permute-start | bytes 3538952 | tf_op jit(solution)/shard_map/ppermute | solution.py:45
  38.4 13.7 %collective-permute-done.5.t3 = bf16[4,576,256]{2,1,0:T(8,128)(2,1)S(1)} collective-permute-done((bf16[4,576,256]{2,1,0:T(8,128)(2,1)S(1)}, bf16[4,576,256]{2,1,0:T(8,128)(2,1)S(1)}, u32[]{:S(2)}, u32[]{:S(2)}) %collective-permute-start.5) | collective-permute-done | bytes 1179680 | tf_op jit(solution)/shard_map/ppermute | solution.py:45
  52.1 3.8 %collective-permute-start.6 = (bf16[2,576,256]{2,1,0:T(8,128)(2,1)S(1)}, bf16[2,576,256]{2,1,0:T(8,128)(2,1)S(1)}, u32[]{:S(2)}, u32[]{:S(2)}) collective-permute-start(bf16[2,576,256]{2,1,0:T(8,128)(2,1)S(1)} %slice.125), channel_id=1, source_target_pairs={{0,12},{1,13},{2,14},{3,15},{4,0},{5,1},{6,2},{7,3},{8,4},{9,5},{1... | collective-permute-start | bytes 1769480 | tf_op jit(solution)/shard_map/ppermute | solution.py:45
  56.1 1.9 %copy-done.1 = bf16[384,4096]{1,0:T(8,128)(2,1)S(1)} copy-done((bf16[384,4096]{1,0:T(8,128)(2,1)S(1)}, bf16[384,4096]{1,0:T(8,128)(2,1)}, u32[]{:S(2)}) %copy-start.1) | copy-done | bytes 3145752
  58.0 4.1 %near.1 = (f32[768,256]{1,0:T(8,128)S(1)}, f32[768,256]{1,0:T(8,128)S(1)}, bf16[5120,256]{1,0:T(8,128)(2,1)S(1)}) custom-call(bf16[4,576,256]{2,1,0:T(8,128)(2,1)S(1)} %pad_maximum_fusion.t0, bf16[4,576,256]{2,1,0:T(8,128)(2,1)S(1)} %collective-permute-done.3.t1, bf16[4,576,256]{2,1,0:T(8,128)(2,1)S(1)} %collective-permute-done.5.t3, ...), custom_call_target="tpu_custom_call" | custom-call | flops 3623878656 | bytes 14000000 | tf_op jit(solution)/shard_map/near/pallas_call | solution.py:140
  63.3 3.8 %collective-permute-done.4.t2a = bf16[2,576,256]{2,1,0:T(8,128)(2,1)S(1)} collective-permute-done((bf16[2,576,256]{2,1,0:T(8,128)(2,1)S(1)}, bf16[2,576,256]{2,1,0:T(8,128)(2,1)S(1)}, u32[]{:S(2)}, u32[]{:S(2)}) %collective-permute-start.4) | collective-permute-done | bytes 589856 | tf_op jit(solution)/shard_map/ppermute | solution.py:45
  67.1 2.1 %far.1 = (f32[768,256]{1,0:T(8,128)S(1)}, f32[768,256]{1,0:T(8,128)S(1)}, f32[8,256]{1,0:T(8,128)S(1)}, bf16[5120,256]{1,0:T(8,128)(2,1)S(1)}) custom-call(bf16[2,576,256]{2,1,0:T(8,128)(2,1)S(1)} %collective-permute-done.4.t2a, bf16[2,576,256]{2,1,0:T(8,128)(2,1)S(1)} %collective-permute-done.6.t2b, f32[768,256]{1,0:T(8,128)S(1)} %get-tuple-element.28.s_in, ...), custom_call_target="tpu_custom_call" | custom-call | flops 1207959552 | bytes 14000000 | tf_op jit(solution)/shard_map/far/pallas_call | solution.py:140
  70.2 3.0 %collective-permute-done.9 = f32[8,256]{1,0:T(8,128)S(1)} collective-permute-done((f32[8,256]{1,0:T(8,128)S(1)}, f32[8,256]{1,0:T(8,128)S(1)}, u32[]{:S(2)}, u32[]{:S(2)}) %collective-permute-start.9) | collective-permute-done | bytes 8224 | tf_op jit(solution)/shard_map/ppermute | solution.py:45
  74.0 3.5 %collective-permute-start.11 = (f32[8,256]{1,0:T(8,128)S(1)}, f32[8,256]{1,0:T(8,128)S(1)}, u32[]{:S(2)}, u32[]{:S(2)}) collective-permute-start(f32[8,256]{1,0:T(8,128)S(1)} %pad_maximum_fusion.6), channel_id=1, source_target_pairs={{0,2},{1,3},{2,0},{3,1},{4,6},{5,7},{6,4},{7,5},{8,10},{9,11},{10,... | collective-permute-start | bytes 24584 | tf_op jit(solution)/shard_map/ppermute | solution.py:45
  77.9 3.7 %collective-permute-done.11 = f32[8,256]{1,0:T(8,128)S(1)} collective-permute-done((f32[8,256]{1,0:T(8,128)S(1)}, f32[8,256]{1,0:T(8,128)S(1)}, u32[]{:S(2)}, u32[]{:S(2)}) %collective-permute-start.11) | collective-permute-done | bytes 8224 | tf_op jit(solution)/shard_map/ppermute | solution.py:45
  83.4 11.6 %all_to_all.16.stats = f32[16,8,256]{2,1,0:T(8,128)S(1)} all-to-all(f32[16,8,256]{2,1,0:T(8,128)S(1)} %broadcast_in_dim.3), channel_id=1, replica_groups=mesh['zl'=2,'c'=2,'x'=4,'y'=4,'zh'=4] {'x','y'}, dimensions={0} | all-to-all | bytes 262144 | tf_op jit(solution)/shard_map/all_to_all | solution.py:278
  97.3 2.8 %collective-permute-start.14 = (bf16[2,320,256]{2,1,0:T(8,128)(2,1)S(1)}, bf16[2,320,256]{2,1,0:T(8,128)(2,1)S(1)}, u32[]{:S(2)}, u32[]{:S(2)}) collective-permute-start(bf16[2,320,256]{2,1,0:T(8,128)(2,1)S(1)} %get-tuple-element.36), channel_id=1, source_target_pairs={{0,12},{1,13},{2,14},{3,15},{4,0},{5,1},{6,2},{7,3},{8,4},{9,5},{1... | collective-permute-start | bytes 983048 | tf_op jit(solution)/shard_map/ppermute | solution.py:45
  100.0 3.1 %rest.1 = (bf16[4,320,256]{2,1,0:T(8,128)(2,1)S(1)}, bf16[4,320,256]{2,1,0:T(8,128)(2,1)S(1)}, bf16[4,320,256]{2,1,0:T(8,128)(2,1)S(1)}) custom-call(bf16[384,256]{1,0:T(8,128)(2,1)S(1)} %get-tuple-element.39.g_own, bf16[384,256]{1,0:T(8,128)(2,1)S(1)} %get-tuple-element.37.g_oth, bf16[384,5120]{1,0:T(8,128)(2,1)S(1)} %copy-done, ...), custom_call_target="tpu_custom_call" | custom-call | flops 2013265920 | bytes 14000000 | tf_op jit(solution)/shard_map/rest/pallas_call | solution.py:140
  103.2 1.9 %collective-permute-done.13 = bf16[2,320,256]{2,1,0:T(8,128)(2,1)S(1)} collective-permute-done((bf16[2,320,256]{2,1,0:T(8,128)(2,1)S(1)}, bf16[2,320,256]{2,1,0:T(8,128)(2,1)S(1)}, u32[]{:S(2)}, u32[]{:S(2)}) %collective-permute-start.13) | collective-permute-done | bytes 327712 | tf_op jit(solution)/shard_map/ppermute | solution.py:45
  105.4 3.3 %collective-permute-start.18 = (bf16[4,320,256]{2,1,0:T(8,128)(2,1)S(1)}, bf16[4,320,256]{2,1,0:T(8,128)(2,1)S(1)}, u32[]{:S(2)}, u32[]{:S(2)}) collective-permute-start(bf16[4,320,256]{2,1,0:T(8,128)(2,1)S(1)} %pad_maximum_fusion.2), channel_id=1, source_target_pairs={{0,12},{1,13},{2,14},{3,15},{4,0},{5,1},{6,2},{7,3},{8,4},{9,5},{1... | collective-permute-start | bytes 1966088 | tf_op jit(solution)/shard_map/ppermute | solution.py:45
  108.8 5.7 %head.1 = bf16[384,5120]{1,0:T(8,128)(2,1)} custom-call(bf16[384,256]{1,0:T(8,128)(2,1)S(1)} %get-tuple-element.39.g_own, bf16[384,256]{1,0:T(8,128)(2,1)S(1)} %collective-permute-done.15.g_got, bf16[5120,256]{1,0:T(8,128)(2,1)S(1)} %get-tuple-element.38.h_own, bf16[5120,256]{1,0:T(8,128)(2,1)S(1)} %collective-permute-done.16.h_got), custom_call_target="tpu_custom_call" | custom-call | flops 2013265920 | bytes 10000000 | tf_op jit(solution)/shard_map/head/pallas_call | solution.py:236
  114.5 2.3 %collective-permute-done.18 = bf16[4,320,256]{2,1,0:T(8,128)(2,1)S(1)} collective-permute-done((bf16[4,320,256]{2,1,0:T(8,128)(2,1)S(1)}, bf16[4,320,256]{2,1,0:T(8,128)(2,1)S(1)}, u32[]{:S(2)}, u32[]{:S(2)}) %collective-permute-start.18) | collective-permute-done | bytes 655392 | tf_op jit(solution)/shard_map/ppermute | solution.py:45
  116.8 6.7 %collective-permute-done.17 = bf16[4,320,256]{2,1,0:T(8,128)(2,1)S(1)} collective-permute-done((bf16[4,320,256]{2,1,0:T(8,128)(2,1)S(1)}, bf16[4,320,256]{2,1,0:T(8,128)(2,1)S(1)}, u32[]{:S(2)}, u32[]{:S(2)}) %collective-permute-start.17) | collective-permute-done | bytes 655392 | tf_op jit(solution)/shard_map/ppermute | solution.py:45
  129.2 2.6 %collective-permute-done.21 = bf16[320,256]{1,0:T(8,128)(2,1)S(1)} collective-permute-done((bf16[320,256]{1,0:T(8,128)(2,1)S(1)}, bf16[320,256]{1,0:T(8,128)(2,1)S(1)}, u32[]{:S(2)}, u32[]{:S(2)}) %collective-permute-start.21) | collective-permute-done | bytes 163872 | tf_op jit(solution)/shard_map/ppermute | solution.py:45
  133.6 14.4 %all_to_all.17 = f32[8,80,128]{2,1,0:T(8,128)S(1)} all-to-all(f32[8,80,128]{2,1,0:T(8,128)S(1)} %bitcast.24), channel_id=1, replica_groups=mesh['zl'=2,'c'=2,'x'=4,'y'=4,'zh'=4] {'zl','zh'}, dimensions={0} | all-to-all | bytes 655360 | tf_op jit(solution)/shard_map/all_to_all | solution.py:297
  (67 shorter events, 21.4 us)
Async XLA Ops:
  0.6 55.4 %collective-permute-start.7 = (bf16[384,5120]{1,0:T(8,128)(2,1)}, bf16[384,5120]{1,0:T(8,128)(2,1)S(1)}, u32[]{:S(2)}, u32[]{:S(2)}) collective-permute-start(bf16[384,5120]{1,0:T(8,128)(2,1)} %ws.7), channel_id=1, source_target_pairs={{0,64},{1,65},{2,66},{3,67},{4,68},{5,69},{6,70},{7,71},{8,72},{9,... | collective-permute-start | bytes 11796488 | tf_op jit(solution)/shard_map/ppermute | solution.py:45
  0.7 55.3 %collective-permute-start.8 = (bf16[384,4096]{1,0:T(8,128)(2,1)}, bf16[384,4096]{1,0:T(8,128)(2,1)S(1)}, u32[]{:S(2)}, u32[]{:S(2)}) collective-permute-start(bf16[384,4096]{1,0:T(8,128)(2,1)} %wt.3), channel_id=1, source_target_pairs={{0,64},{1,65},{2,66},{3,67},{4,68},{5,69},{6,70},{7,71},{8,72},{9,... | collective-permute-start | bytes 9437192 | tf_op jit(solution)/shard_map/ppermute | solution.py:45
  23.1 6.8 %collective-permute-start.2 = (bf16[576,256]{1,0:T(8,128)(2,1)S(1)}, bf16[576,256]{1,0:T(8,128)(2,1)S(1)}, u32[]{:S(2)}, u32[]{:S(2)}) collective-permute-start(bf16[576,256]{1,0:T(8,128)(2,1)S(1)} %weave.1), channel_id=1, source_target_pairs={{0,48},{1,49},{2,50},{3,51},{4,52},{5,53},{6,54},{7,55},{8,56},{9,... | collective-permute-start | bytes 884744 | tf_op jit(solution)/shard_map/ppermute | solution.py:45
  23.7 10.3 %collective-permute-start.1 = (bf16[576,256]{1,0:T(8,128)(2,1)S(1)}, bf16[576,256]{1,0:T(8,128)(2,1)S(1)}, u32[]{:S(2)}, u32[]{:S(2)}) collective-permute-start(bf16[576,256]{1,0:T(8,128)(2,1)S(1)} %weave.1), channel_id=1, source_target_pairs={{0,32},{1,33},{2,34},{3,35},{4,36},{5,37},{6,38},{7,39},{8,40},{9,... | collective-permute-start | bytes 884744 | tf_op jit(solution)/shard_map/ppermute | solution.py:45
  26.1 9.0 %collective-permute-start = (bf16[576,256]{1,0:T(8,128)(2,1)S(1)}, bf16[576,256]{1,0:T(8,128)(2,1)S(1)}, u32[]{:S(2)}, u32[]{:S(2)}) collective-permute-start(bf16[576,256]{1,0:T(8,128)(2,1)S(1)} %weave.1), channel_id=1, source_target_pairs={{0,16},{1,17},{2,18},{3,19},{4,20},{5,21},{6,22},{7,23},{8,24},{9,... | collective-permute-start | bytes 884744 | tf_op jit(solution)/shard_map/ppermute | solution.py:45
  35.1 20.9 %copy-start = (bf16[384,5120]{1,0:T(8,128)(2,1)S(1)}, bf16[384,5120]{1,0:T(8,128)(2,1)}, u32[]{:S(2)}) copy-start(bf16[384,5120]{1,0:T(8,128)(2,1)} %ws.7) | copy-start | bytes 11796484
  35.3 16.8 %collective-permute-start.5 = (bf16[4,576,256]{2,1,0:T(8,128)(2,1)S(1)}, bf16[4,576,256]{2,1,0:T(8,128)(2,1)S(1)}, u32[]{:S(2)}, u32[]{:S(2)}) collective-permute-start(bf16[4,576,256]{2,1,0:T(8,128)(2,1)S(1)} %pad_maximum_fusion.t0), channel_id=1, source_target_pairs={{0,12},{1,13},{2,14},{3,15},{4,0},{5,1},{6,2},{7,3},{8,4},{9,5},{1... | collective-permute-start | bytes 3538952 | tf_op jit(solution)/shard_map/ppermute | solution.py:45
  38.4 17.5 %collective-permute-start.3 = (bf16[4,576,256]{2,1,0:T(8,128)(2,1)S(1)}, bf16[4,576,256]{2,1,0:T(8,128)(2,1)S(1)}, u32[]{:S(2)}, u32[]{:S(2)}) collective-permute-start(bf16[4,576,256]{2,1,0:T(8,128)(2,1)S(1)} %pad_maximum_fusion.t0), channel_id=1, source_target_pairs={{0,4},{1,5},{2,6},{3,7},{4,8},{5,9},{6,10},{7,11},{8,12},{9,13},{1... | collective-permute-start | bytes 3538952 | tf_op jit(solution)/shard_map/ppermute | solution.py:45
  52.1 11.2 %collective-permute-start.6 = (bf16[2,576,256]{2,1,0:T(8,128)(2,1)S(1)}, bf16[2,576,256]{2,1,0:T(8,128)(2,1)S(1)}, u32[]{:S(2)}, u32[]{:S(2)}) collective-permute-start(bf16[2,576,256]{2,1,0:T(8,128)(2,1)S(1)} %slice.125), channel_id=1, source_target_pairs={{0,12},{1,13},{2,14},{3,15},{4,0},{5,1},{6,2},{7,3},{8,4},{9,5},{1... | collective-permute-start | bytes 1769480 | tf_op jit(solution)/shard_map/ppermute | solution.py:45
  56.0 11.2 %collective-permute-start.4 = (bf16[2,576,256]{2,1,0:T(8,128)(2,1)S(1)}, bf16[2,576,256]{2,1,0:T(8,128)(2,1)S(1)}, u32[]{:S(2)}, u32[]{:S(2)}) collective-permute-start(bf16[2,576,256]{2,1,0:T(8,128)(2,1)S(1)} %slice.124), channel_id=1, source_target_pairs={{0,4},{1,5},{2,6},{3,7},{4,8},{5,9},{6,10},{7,11},{8,12},{9,13},{1... | collective-permute-start | bytes 1769480 | tf_op jit(solution)/shard_map/ppermute | solution.py:45
  67.1 27.9 %copy-start.2 = (f32[512]{0:T(512)S(1)}, f32[512]{0:T(512)}, u32[]{:S(2)}) copy-start(f32[512]{0:T(512)} %param.9) | copy-start | bytes 6148
  69.2 35.9 %collective-permute-start.16 = (bf16[5120,256]{1,0:T(8,128)(2,1)S(1)}, bf16[5120,256]{1,0:T(8,128)(2,1)S(1)}, u32[]{:S(2)}, u32[]{:S(2)}) collective-permute-start(bf16[5120,256]{1,0:T(8,128)(2,1)S(1)} %get-tuple-element.38.h_own), channel_id=1, source_target_pairs={{0,64},{1,65},{2,66},{3,67},{4,68},{5,69},{6,70},{7,71},{8,72},{9,... | collective-permute-start | bytes 7864328 | tf_op jit(solution)/shard_map/ppermute | solution.py:45
  69.3 3.9 %collective-permute-start.9 = (f32[8,256]{1,0:T(8,128)S(1)}, f32[8,256]{1,0:T(8,128)S(1)}, u32[]{:S(2)}, u32[]{:S(2)}) collective-permute-start(f32[8,256]{1,0:T(8,128)S(1)} %get-tuple-element.31.local), channel_id=1, source_target_pairs={{0,128},{1,129},{2,130},{3,131},{4,132},{5,133},{6,134},{7,135},{8... | collective-permute-start | bytes 24584 | tf_op jit(solution)/shard_map/ppermute | solution.py:45
  73.3 4.6 %collective-permute-start.12 = (f32[8,256]{1,0:T(8,128)S(1)}, f32[8,256]{1,0:T(8,128)S(1)}, u32[]{:S(2)}, u32[]{:S(2)}) collective-permute-start(f32[8,256]{1,0:T(8,128)S(1)} %pad_maximum_fusion.6), channel_id=1, source_target_pairs={{0,3},{1,0},{2,1},{3,2},{4,7},{5,4},{6,5},{7,6},{8,11},{9,8},{10,9... | collective-permute-start | bytes 24584 | tf_op jit(solution)/shard_map/ppermute | solution.py:45
  74.0 7.6 %collective-permute-start.11 = (f32[8,256]{1,0:T(8,128)S(1)}, f32[8,256]{1,0:T(8,128)S(1)}, u32[]{:S(2)}, u32[]{:S(2)}) collective-permute-start(f32[8,256]{1,0:T(8,128)S(1)} %pad_maximum_fusion.6), channel_id=1, source_target_pairs={{0,2},{1,3},{2,0},{3,1},{4,6},{5,7},{6,4},{7,5},{8,10},{9,11},{10,... | collective-permute-start | bytes 24584 | tf_op jit(solution)/shard_map/ppermute | solution.py:45
  77.5 5.8 %collective-permute-start.10 = (f32[8,256]{1,0:T(8,128)S(1)}, f32[8,256]{1,0:T(8,128)S(1)}, u32[]{:S(2)}, u32[]{:S(2)}) collective-permute-start(f32[8,256]{1,0:T(8,128)S(1)} %pad_maximum_fusion.6), channel_id=1, source_target_pairs={{0,1},{1,2},{2,3},{3,0},{4,5},{5,6},{6,7},{7,4},{8,9},{9,10},{10,1... | collective-permute-start | bytes 24584 | tf_op jit(solution)/shard_map/ppermute | solution.py:45
  96.8 8.3 %collective-permute-start.13 = (bf16[2,320,256]{2,1,0:T(8,128)(2,1)S(1)}, bf16[2,320,256]{2,1,0:T(8,128)(2,1)S(1)}, u32[]{:S(2)}, u32[]{:S(2)}) collective-permute-start(bf16[2,320,256]{2,1,0:T(8,128)(2,1)S(1)} %get-tuple-element.35), channel_id=1, source_target_pairs={{0,4},{1,5},{2,6},{3,7},{4,8},{5,9},{6,10},{7,11},{8,12},{9,13},{1... | collective-permute-start | bytes 983048 | tf_op jit(solution)/shard_map/ppermute | solution.py:45
  97.3 7.8 %collective-permute-start.14 = (bf16[2,320,256]{2,1,0:T(8,128)(2,1)S(1)}, bf16[2,320,256]{2,1,0:T(8,128)(2,1)S(1)}, u32[]{:S(2)}, u32[]{:S(2)}) collective-permute-start(bf16[2,320,256]{2,1,0:T(8,128)(2,1)S(1)} %get-tuple-element.36), channel_id=1, source_target_pairs={{0,12},{1,13},{2,14},{3,15},{4,0},{5,1},{6,2},{7,3},{8,4},{9,5},{1... | collective-permute-start | bytes 983048 | tf_op jit(solution)/shard_map/ppermute | solution.py:45
  100.0 3.2 %collective-permute-start.15 = (bf16[384,256]{1,0:T(8,128)(2,1)S(1)}, bf16[384,256]{1,0:T(8,128)(2,1)S(1)}, u32[]{:S(2)}, u32[]{:S(2)}) collective-permute-start(bf16[384,256]{1,0:T(8,128)(2,1)S(1)} %get-tuple-element.37.g_oth), channel_id=1, source_target_pairs={{0,64},{1,65},{2,66},{3,67},{4,68},{5,69},{6,70},{7,71},{8,72},{9,... | collective-permute-start | bytes 589832 | tf_op jit(solution)/shard_map/ppermute | solution.py:45
  105.4 11.4 %collective-permute-start.18 = (bf16[4,320,256]{2,1,0:T(8,128)(2,1)S(1)}, bf16[4,320,256]{2,1,0:T(8,128)(2,1)S(1)}, u32[]{:S(2)}, u32[]{:S(2)}) collective-permute-start(bf16[4,320,256]{2,1,0:T(8,128)(2,1)S(1)} %pad_maximum_fusion.2), channel_id=1, source_target_pairs={{0,12},{1,13},{2,14},{3,15},{4,0},{5,1},{6,2},{7,3},{8,4},{9,5},{1... | collective-permute-start | bytes 1966088 | tf_op jit(solution)/shard_map/ppermute | solution.py:45
  108.8 14.8 %collective-permute-start.17 = (bf16[4,320,256]{2,1,0:T(8,128)(2,1)S(1)}, bf16[4,320,256]{2,1,0:T(8,128)(2,1)S(1)}, u32[]{:S(2)}, u32[]{:S(2)}) collective-permute-start(bf16[4,320,256]{2,1,0:T(8,128)(2,1)S(1)} %pad_maximum_fusion.1), channel_id=1, source_target_pairs={{0,4},{1,5},{2,6},{3,7},{4,8},{5,9},{6,10},{7,11},{8,12},{9,13},{1... | collective-permute-start | bytes 1966088 | tf_op jit(solution)/shard_map/ppermute | solution.py:45
  123.8 5.4 %collective-permute-start.19 = (bf16[320,256]{1,0:T(8,128)(2,1)S(1)}, bf16[320,256]{1,0:T(8,128)(2,1)S(1)}, u32[]{:S(2)}, u32[]{:S(2)}) collective-permute-start(bf16[320,256]{1,0:T(8,128)(2,1)S(1)} %get-tuple-element.59), channel_id=1, source_target_pairs={{0,16},{1,17},{2,18},{3,19},{4,20},{5,21},{6,22},{7,23},{8,24},{9,... | collective-permute-start | bytes 491528 | tf_op jit(solution)/shard_map/ppermute | solution.py:45
  124.9 6.9 %collective-permute-start.21 = (bf16[320,256]{1,0:T(8,128)(2,1)S(1)}, bf16[320,256]{1,0:T(8,128)(2,1)S(1)}, u32[]{:S(2)}, u32[]{:S(2)}) collective-permute-start(bf16[320,256]{1,0:T(8,128)(2,1)S(1)} %get-tuple-element.60), channel_id=1, source_target_pairs={{0,32},{1,33},{2,34},{3,35},{4,36},{5,37},{6,38},{7,39},{8,40},{9,... | collective-permute-start | bytes 491528 | tf_op jit(solution)/shard_map/ppermute | solution.py:45
  126.7 6.8 %collective-permute-start.20 = (bf16[320,256]{1,0:T(8,128)(2,1)S(1)}, bf16[320,256]{1,0:T(8,128)(2,1)S(1)}, u32[]{:S(2)}, u32[]{:S(2)}) collective-permute-start(bf16[320,256]{1,0:T(8,128)(2,1)S(1)} %get-tuple-element.61), channel_id=1, source_target_pairs={{0,48},{1,49},{2,50},{3,51},{4,52},{5,53},{6,54},{7,55},{8,56},{9,... | collective-permute-start | bytes 491528 | tf_op jit(solution)/shard_map/ppermute | solution.py:45
  (1 other events, 1.9 us)

commit v7 on v6

--- a/solution.py
+++ b/solution.py
@@ -30,13 +30,13 @@
 
 PAIR = perm(lambda zl, c, x, y, zh: (1 - zl, c, x, y, zh))
 CORE = perm(lambda zl, c, x, y, zh: (zl, 1 - c, x, y, zh))
-ZH = {k: perm(lambda zl, c, x, y, zh, k=k: (zl, c, x, y, (zh + k) % 4)) for k in (1, 2, 3)}
+ZH = {k: perm(lambda zl, c, x, y, zh, k=k: (zl, c, x, y, zh ^ k)) for k in (1, 2, 3)}
 FIRST = {
-    k: perm(lambda zl, c, x, y, zh, k=k: (zl, c, (x + k * (1 - c)) % 4, (y + k * c) % 4, zh))
+    k: perm(lambda zl, c, x, y, zh, k=k: (zl, c, x ^ (k * (1 - c)), y ^ (k * c), zh))
     for k in (1, 2, 3)
 }
 SECOND = {
-    k: perm(lambda zl, c, x, y, zh, k=k: (zl, c, (x + k * c) % 4, (y + k * (1 - c)) % 4, zh))
+    k: perm(lambda zl, c, x, y, zh, k=k: (zl, c, x ^ (k * c), y ^ (k * (1 - c)), zh))
     for k in (1, 2, 3)
 }
 
@@ -57,7 +57,7 @@
 def block_at(c, x, y, first, second):
     in_x = jnp.where(c == 0, first, second)
     in_y = jnp.where(c == 0, second, first)
-    return ((x + in_x) & 3) * 4 + ((y + in_y) & 3)
+    return (x ^ in_x) * 4 + (y ^ in_y)
 
 
 def dot(a, b, dims):
@@ -86,7 +86,7 @@
     _, c, x, y, _ = place()
     for j, t in ((0, t0), (1, t1), (3, t3), (2, None)):
         for i in range(4):
-            at = block_at(c, x, y, (4 - i) & 3, (4 - j) & 3)
+            at = block_at(c, x, y, i, j)
             rows_s = pl.ds(pl.multiple_of(at * NS, NS), NS)
             rows_t = pl.ds(pl.multiple_of(at * NT, NT), NT)
             if t is None:
@@ -111,7 +111,7 @@
     t_ref[...] = t_in[...]
     for i in range(4):
         line = t2a[i] if i < 2 else t2b[i - 2]
-        at = block_at(c, x, y, (4 - i) & 3, 2)
+        at = block_at(c, x, y, i, 2)
         hs[pl.ds(pl.multiple_of(at * NS, NS), NS)] = line[0:NS]
         cols, first = window(at)
         pads[i] = jnp.zeros((WIDE, TOK), BF16)
@@ -268,7 +268,7 @@
     block = vmem_call(weave_kernel, "weave", [((NS + NT, TOK), BF16)], [], 1, along)[0]
     line = jnp.stack((block,) + ring(block, FIRST))
     before, after = send(line, SECOND[1]), send(line, SECOND[3])
-    far_low, far_high = send(before[:2], SECOND[1]), send(after[2:], SECOND[3])
+    far_low, far_high = send(after[:2], SECOND[1]), send(before[2:], SECOND[3])
 
     heads = (student_head, student_other, teacher_head, teacher_other)
     near = near_call(line, before, after, *heads)
@@ -284,8 +284,8 @@
     low, high, g_got, hidden_got, o0, o1, o3 = lax.optimization_barrier(
         (low, high, g_got, hidden_got, *rest_call(g_own, g_oth, student_head, student_other))
     )
-    o1 = jnp.concatenate([(o1[:2].astype(F32) + low.astype(F32)).astype(BF16), o1[2:]])
-    o3 = jnp.concatenate([o3[:2], (o3[2:].astype(F32) + high.astype(F32)).astype(BF16)])
+    o3 = jnp.concatenate([(o3[:2].astype(F32) + low.astype(F32)).astype(BF16), o3[2:]])
+    o1 = jnp.concatenate([o1[:2], (o1[2:].astype(F32) + high.astype(F32)).astype(BF16)])
     r1, r3 = send(o1, SECOND[1]), send(o3, SECOND[3])
     head_grad = head_call(g_own, g_got, hidden_own, hidden_got)
     r1, r3, head_grad = lax.optimization_barrier((r1, r3, head_grad))

time: 149 us -> 143 us (0.960)
  waiting for transfers between devices: 50.9 us -> 44.9 us
  starting transfers between devices: 28.7 us -> 26.8 us
    ppermute x22, waiting for transfers between devices: 50.9 us -> 44.9 us  [send(): return lax.ppermute(value, AXES, pairs)]
    ppermute x22, starting transfers between devices: 28.7 us -> 26.8 us  [send(): return lax.ppermute(value, AXES, pairs)]
  transfers between devices with their start and end apart: 22 -> 22, of which waited for: 16 -> 15; matrix products, arithmetic and copies ran while one was open for 1% -> 1% of each run, Pallas kernels for 10% -> 10%
where the time goes in v7:
time: 143 us; the launch traced here: 142 us
  blocking collectives  48.2 us (34%)
  waiting for transfers between devices  44.9 us (31%)
  starting transfers between devices  26.8 us (19%)
  Pallas kernels  16.8 us (12%)
  other arithmetic  2.32 us (2%)
  local copies, waits for them, and re-layouts  2.11 us (1%)
    ppermute x22, waiting for transfers between devices, send(): return lax.ppermute(value, AXES, pairs)  44.9 us
    ppermute x22, starting transfers between devices, send(): return lax.ppermute(value, AXES, pairs)  26.8 us
    all_to_all x1, blocking collectives, per_device(): along = lax.all_to_all(copies, ('zl', 'zh'), 0, 0)  21 us
    all_to_all x1, blocking collectives, per_device(): hidden_grad = jnp.sum(lax.all_to_all(sums, ('zl', 'zh'), 0, 0), axis=0).T  14.9 us
    all_to_all x1, blocking collectives, per_device(): lax.all_to_all(jnp.broadcast_to(stats, (16, 8, TOK)), ('x', 'y'), 0, 0)  12.3 us
    pallas_call x6, Pallas kernels, vmem_call(): pl.pallas_call(kernel, out_shape=tuple((jax.ShapeDtypeStruct(*o) for o in...  11.2 us
    pallas_call x1, Pallas kernels, head_call(): pl.pallas_call(head_kernel, out_shape=jax.ShapeDtypeStruct((ROWS, DS), BF...  5.65 us
  transfers between devices with their start and end apart: 22, of which 15 were waited for; matrix products, arithmetic and copies ran while one was open for 1% of the time, Pallas kernels for 10%

profile of v7, /device:TPU:2, one launch (start us, length us, event | category | flops | bytes accessed | tf_op | source)
XLA Modules:
  0.0 142.1 jit_solution(744646273874219234)
XLA Ops:
  2.0 21.0 %all_to_all.15.along = bf16[8,144,128]{2,1,0:T(8,128)(2,1)S(1)} all-to-all(bf16[8,144,128]{2,1,0:T(8,128)(2,1)S(1)} %spread.1), channel_id=1, replica_groups=mesh['zl'=2,'c'=2,'x'=4,'y'=4,'zh'=4] {'zl','zh'}, dimensions={0} | all-to-all | bytes 589824 | tf_op jit(solution)/shard_map/all_to_all | solution.py:267
  27.2 5.8 %collective-permute-done.2 = bf16[576,256]{1,0:T(8,128)(2,1)S(1)} collective-permute-done((bf16[576,256]{1,0:T(8,128)(2,1)S(1)}, bf16[576,256]{1,0:T(8,128)(2,1)S(1)}, u32[]{:S(2)}, u32[]{:S(2)}) %collective-permute-start.2) | collective-permute-done | bytes 294944 | tf_op jit(solution)/shard_map/ppermute | solution.py:45
  33.0 2.1 %collective-permute-done = bf16[576,256]{1,0:T(8,128)(2,1)S(1)} collective-permute-done((bf16[576,256]{1,0:T(8,128)(2,1)S(1)}, bf16[576,256]{1,0:T(8,128)(2,1)S(1)}, u32[]{:S(2)}, u32[]{:S(2)}) %collective-permute-start) | collective-permute-done | bytes 294944 | tf_op jit(solution)/shard_map/ppermute | solution.py:45
  37.0 2.2 %collective-permute-start.3 = (bf16[4,576,256]{2,1,0:T(8,128)(2,1)S(1)}, bf16[4,576,256]{2,1,0:T(8,128)(2,1)S(1)}, u32[]{:S(2)}, u32[]{:S(2)}) collective-permute-start(bf16[4,576,256]{2,1,0:T(8,128)(2,1)S(1)} %pad_maximum_fusion.t0), channel_id=1, source_target_pairs={{0,12},{1,13},{2,14},{3,15},{4,8},{5,9},{6,10},{7,11},{8,4},{9,5},... | collective-permute-start | bytes 3538952 | tf_op jit(solution)/shard_map/ppermute | solution.py:45
  39.1 12.4 %collective-permute-done.5.t1 = bf16[4,576,256]{2,1,0:T(8,128)(2,1)S(1)} collective-permute-done((bf16[4,576,256]{2,1,0:T(8,128)(2,1)S(1)}, bf16[4,576,256]{2,1,0:T(8,128)(2,1)S(1)}, u32[]{:S(2)}, u32[]{:S(2)}) %collective-permute-start.5) | collective-permute-done | bytes 1179680 | tf_op jit(solution)/shard_map/ppermute | solution.py:45
  51.6 3.1 %collective-permute-start.6 = (bf16[2,576,256]{2,1,0:T(8,128)(2,1)S(1)}, bf16[2,576,256]{2,1,0:T(8,128)(2,1)S(1)}, u32[]{:S(2)}, u32[]{:S(2)}) collective-permute-start(bf16[2,576,256]{2,1,0:T(8,128)(2,1)S(1)} %slice.125), channel_id=1, source_target_pairs={{0,12},{1,13},{2,14},{3,15},{4,8},{5,9},{6,10},{7,11},{8,4},{9,5},... | collective-permute-start | bytes 1769480 | tf_op jit(solution)/shard_map/ppermute | solution.py:45
  55.0 1.9 %copy-done.1 = bf16[384,4096]{1,0:T(8,128)(2,1)S(1)} copy-done((bf16[384,4096]{1,0:T(8,128)(2,1)S(1)}, bf16[384,4096]{1,0:T(8,128)(2,1)}, u32[]{:S(2)}) %copy-start.1) | copy-done | bytes 3145752
  56.9 4.1 %near.1 = (f32[768,256]{1,0:T(8,128)S(1)}, f32[768,256]{1,0:T(8,128)S(1)}, bf16[5120,256]{1,0:T(8,128)(2,1)S(1)}) custom-call(bf16[4,576,256]{2,1,0:T(8,128)(2,1)S(1)} %pad_maximum_fusion.t0, bf16[4,576,256]{2,1,0:T(8,128)(2,1)S(1)} %collective-permute-done.5.t1, bf16[4,576,256]{2,1,0:T(8,128)(2,1)S(1)} %collective-permute-done.3.t3, ...), custom_call_target="tpu_custom_call" | custom-call | flops 3623878656 | bytes 14000000 | tf_op jit(solution)/shard_map/near/pallas_call | solution.py:140
  61.0 1.8 %collective-permute-done.6.t2b = bf16[2,576,256]{2,1,0:T(8,128)(2,1)S(1)} collective-permute-done((bf16[2,576,256]{2,1,0:T(8,128)(2,1)S(1)}, bf16[2,576,256]{2,1,0:T(8,128)(2,1)S(1)}, u32[]{:S(2)}, u32[]{:S(2)}) %collective-permute-start.6) | collective-permute-done | bytes 589856 | tf_op jit(solution)/shard_map/ppermute | solution.py:45
  62.8 1.9 %collective-permute-done.4.t2a = bf16[2,576,256]{2,1,0:T(8,128)(2,1)S(1)} collective-permute-done((bf16[2,576,256]{2,1,0:T(8,128)(2,1)S(1)}, bf16[2,576,256]{2,1,0:T(8,128)(2,1)S(1)}, u32[]{:S(2)}, u32[]{:S(2)}) %collective-permute-start.4) | collective-permute-done | bytes 589856 | tf_op jit(solution)/shard_map/ppermute | solution.py:45
  64.7 2.0 %far.1 = (f32[768,256]{1,0:T(8,128)S(1)}, f32[768,256]{1,0:T(8,128)S(1)}, f32[8,256]{1,0:T(8,128)S(1)}, bf16[5120,256]{1,0:T(8,128)(2,1)S(1)}) custom-call(bf16[2,576,256]{2,1,0:T(8,128)(2,1)S(1)} %collective-permute-done.4.t2a, bf16[2,576,256]{2,1,0:T(8,128)(2,1)S(1)} %collective-permute-done.6.t2b, f32[768,256]{1,0:T(8,128)S(1)} %get-tuple-element.28.s_in, ...), custom_call_target="tpu_custom_call" | custom-call | flops 1207959552 | bytes 14000000 | tf_op jit(solution)/shard_map/far/pallas_call | solution.py:140
  67.7 3.0 %collective-permute-done.9 = f32[8,256]{1,0:T(8,128)S(1)} collective-permute-done((f32[8,256]{1,0:T(8,128)S(1)}, f32[8,256]{1,0:T(8,128)S(1)}, u32[]{:S(2)}, u32[]{:S(2)}) %collective-permute-start.9) | collective-permute-done | bytes 8224 | tf_op jit(solution)/shard_map/ppermute | solution.py:45
  71.4 3.9 %collective-permute-start.11 = (f32[8,256]{1,0:T(8,128)S(1)}, f32[8,256]{1,0:T(8,128)S(1)}, u32[]{:S(2)}, u32[]{:S(2)}) collective-permute-start(f32[8,256]{1,0:T(8,128)S(1)} %pad_maximum_fusion.6), channel_id=1, source_target_pairs={{0,2},{1,3},{2,0},{3,1},{4,6},{5,7},{6,4},{7,5},{8,10},{9,11},{10,... | collective-permute-start | bytes 24584 | tf_op jit(solution)/shard_map/ppermute | solution.py:45
  75.3 2.0 %collective-permute-start.10 = (f32[8,256]{1,0:T(8,128)S(1)}, f32[8,256]{1,0:T(8,128)S(1)}, u32[]{:S(2)}, u32[]{:S(2)}) collective-permute-start(f32[8,256]{1,0:T(8,128)S(1)} %pad_maximum_fusion.6), channel_id=1, source_target_pairs={{0,1},{1,0},{2,3},{3,2},{4,5},{5,4},{6,7},{7,6},{8,9},{9,8},{10,11... | collective-permute-start | bytes 24584 | tf_op jit(solution)/shard_map/ppermute | solution.py:45
  80.1 12.3 %all_to_all.16.stats = f32[16,8,256]{2,1,0:T(8,128)S(1)} all-to-all(f32[16,8,256]{2,1,0:T(8,128)S(1)} %broadcast_in_dim.3), channel_id=1, replica_groups=mesh['zl'=2,'c'=2,'x'=4,'y'=4,'zh'=4] {'x','y'}, dimensions={0} | all-to-all | bytes 262144 | tf_op jit(solution)/shard_map/all_to_all | solution.py:278
  96.2 3.1 %rest.1 = (bf16[4,320,256]{2,1,0:T(8,128)(2,1)S(1)}, bf16[4,320,256]{2,1,0:T(8,128)(2,1)S(1)}, bf16[4,320,256]{2,1,0:T(8,128)(2,1)S(1)}) custom-call(bf16[384,256]{1,0:T(8,128)(2,1)S(1)} %get-tuple-element.39.g_own, bf16[384,256]{1,0:T(8,128)(2,1)S(1)} %get-tuple-element.37.g_oth, bf16[384,5120]{1,0:T(8,128)(2,1)S(1)} %copy-done, ...), custom_call_target="tpu_custom_call" | custom-call | flops 2013265920 | bytes 14000000 | tf_op jit(solution)/shard_map/rest/pallas_call | solution.py:140
  99.4 1.8 %collective-permute-done.13 = bf16[2,320,256]{2,1,0:T(8,128)(2,1)S(1)} collective-permute-done((bf16[2,320,256]{2,1,0:T(8,128)(2,1)S(1)}, bf16[2,320,256]{2,1,0:T(8,128)(2,1)S(1)}, u32[]{:S(2)}, u32[]{:S(2)}) %collective-permute-start.13) | collective-permute-done | bytes 327712 | tf_op jit(solution)/shard_map/ppermute | solution.py:45
  105.1 5.7 %head.1 = bf16[384,5120]{1,0:T(8,128)(2,1)} custom-call(bf16[384,256]{1,0:T(8,128)(2,1)S(1)} %get-tuple-element.39.g_own, bf16[384,256]{1,0:T(8,128)(2,1)S(1)} %collective-permute-done.15.g_got, bf16[5120,256]{1,0:T(8,128)(2,1)S(1)} %get-tuple-element.38.h_own, bf16[5120,256]{1,0:T(8,128)(2,1)S(1)} %collective-permute-done.16.h_got), custom_call_target="tpu_custom_call" | custom-call | flops 2013265920 | bytes 10000000 | tf_op jit(solution)/shard_map/head/pallas_call | solution.py:236
  110.7 4.4 %collective-permute-done.18 = bf16[4,320,256]{2,1,0:T(8,128)(2,1)S(1)} collective-permute-done((bf16[4,320,256]{2,1,0:T(8,128)(2,1)S(1)}, bf16[4,320,256]{2,1,0:T(8,128)(2,1)S(1)}, u32[]{:S(2)}, u32[]{:S(2)}) %collective-permute-start.18) | collective-permute-done | bytes 655392 | tf_op jit(solution)/shard_map/ppermute | solution.py:45
  115.1 2.3 %collective-permute-done.17 = bf16[4,320,256]{2,1,0:T(8,128)(2,1)S(1)} collective-permute-done((bf16[4,320,256]{2,1,0:T(8,128)(2,1)S(1)}, bf16[4,320,256]{2,1,0:T(8,128)(2,1)S(1)}, u32[]{:S(2)}, u32[]{:S(2)}) %collective-permute-start.17) | collective-permute-done | bytes 655392 | tf_op jit(solution)/shard_map/ppermute | solution.py:45
  119.2 2.1 %collective-permute-start.20 = (bf16[320,256]{1,0:T(8,128)(2,1)S(1)}, bf16[320,256]{1,0:T(8,128)(2,1)S(1)}, u32[]{:S(2)}, u32[]{:S(2)}) collective-permute-start(bf16[320,256]{1,0:T(8,128)(2,1)S(1)} %get-tuple-element.61), channel_id=1, source_target_pairs={{0,48},{1,49},{2,50},{3,51},{4,52},{5,53},{6,54},{7,55},{8,56},{9,... | collective-permute-start | bytes 491528 | tf_op jit(solution)/shard_map/ppermute | solution.py:45
  121.3 1.8 %collective-permute-done.19 = bf16[320,256]{1,0:T(8,128)(2,1)S(1)} collective-permute-done((bf16[320,256]{1,0:T(8,128)(2,1)S(1)}, bf16[320,256]{1,0:T(8,128)(2,1)S(1)}, u32[]{:S(2)}, u32[]{:S(2)}) %collective-permute-start.19) | collective-permute-done | bytes 163872 | tf_op jit(solution)/shard_map/ppermute | solution.py:45
  123.1 2.7 %collective-permute-done.21 = bf16[320,256]{1,0:T(8,128)(2,1)S(1)} collective-permute-done((bf16[320,256]{1,0:T(8,128)(2,1)S(1)}, bf16[320,256]{1,0:T(8,128)(2,1)S(1)}, u32[]{:S(2)}, u32[]{:S(2)}) %collective-permute-start.21) | collective-permute-done | bytes 163872 | tf_op jit(solution)/shard_map/ppermute | solution.py:45
  126.5 14.9 %all_to_all.17 = f32[8,80,128]{2,1,0:T(8,128)S(1)} all-to-all(f32[8,80,128]{2,1,0:T(8,128)S(1)} %bitcast.24), channel_id=1, replica_groups=mesh['zl'=2,'c'=2,'x'=4,'y'=4,'zh'=4] {'zl','zh'}, dimensions={0} | all-to-all | bytes 655360 | tf_op jit(solution)/shard_map/all_to_all | solution.py:297
  (67 shorter events, 22.9 us)
Async XLA Ops:
  0.6 54.4 %collective-permute-start.7 = (bf16[384,5120]{1,0:T(8,128)(2,1)}, bf16[384,5120]{1,0:T(8,128)(2,1)S(1)}, u32[]{:S(2)}, u32[]{:S(2)}) collective-permute-start(bf16[384,5120]{1,0:T(8,128)(2,1)} %ws.7), channel_id=1, source_target_pairs={{0,64},{1,65},{2,66},{3,67},{4,68},{5,69},{6,70},{7,71},{8,72},{9,... | collective-permute-start | bytes 11796488 | tf_op jit(solution)/shard_map/ppermute | solution.py:45
  0.7 54.3 %collective-permute-start.8 = (bf16[384,4096]{1,0:T(8,128)(2,1)}, bf16[384,4096]{1,0:T(8,128)(2,1)S(1)}, u32[]{:S(2)}, u32[]{:S(2)}) collective-permute-start(bf16[384,4096]{1,0:T(8,128)(2,1)} %wt.3), channel_id=1, source_target_pairs={{0,64},{1,65},{2,66},{3,67},{4,68},{5,69},{6,70},{7,71},{8,72},{9,... | collective-permute-start | bytes 9437192 | tf_op jit(solution)/shard_map/ppermute | solution.py:45
  23.1 10.0 %collective-permute-start.2 = (bf16[576,256]{1,0:T(8,128)(2,1)S(1)}, bf16[576,256]{1,0:T(8,128)(2,1)S(1)}, u32[]{:S(2)}, u32[]{:S(2)}) collective-permute-start(bf16[576,256]{1,0:T(8,128)(2,1)S(1)} %weave.1), channel_id=1, source_target_pairs={{0,48},{1,49},{2,50},{3,51},{4,52},{5,53},{6,54},{7,55},{8,56},{9,... | collective-permute-start | bytes 884744 | tf_op jit(solution)/shard_map/ppermute | solution.py:45
  24.6 8.4 %collective-permute-start.1 = (bf16[576,256]{1,0:T(8,128)(2,1)S(1)}, bf16[576,256]{1,0:T(8,128)(2,1)S(1)}, u32[]{:S(2)}, u32[]{:S(2)}) collective-permute-start(bf16[576,256]{1,0:T(8,128)(2,1)S(1)} %weave.1), channel_id=1, source_target_pairs={{0,32},{1,33},{2,34},{3,35},{4,36},{5,37},{6,38},{7,39},{8,40},{9,... | collective-permute-start | bytes 884744 | tf_op jit(solution)/shard_map/ppermute | solution.py:45
  25.7 9.4 %collective-permute-start = (bf16[576,256]{1,0:T(8,128)(2,1)S(1)}, bf16[576,256]{1,0:T(8,128)(2,1)S(1)}, u32[]{:S(2)}, u32[]{:S(2)}) collective-permute-start(bf16[576,256]{1,0:T(8,128)(2,1)S(1)} %weave.1), channel_id=1, source_target_pairs={{0,16},{1,17},{2,18},{3,19},{4,20},{5,21},{6,22},{7,23},{8,24},{9,... | collective-permute-start | bytes 884744 | tf_op jit(solution)/shard_map/ppermute | solution.py:45
  35.1 19.9 %copy-start = (bf16[384,5120]{1,0:T(8,128)(2,1)S(1)}, bf16[384,5120]{1,0:T(8,128)(2,1)}, u32[]{:S(2)}) copy-start(bf16[384,5120]{1,0:T(8,128)(2,1)} %ws.7) | copy-start | bytes 11796484
  35.3 16.3 %collective-permute-start.5 = (bf16[4,576,256]{2,1,0:T(8,128)(2,1)S(1)}, bf16[4,576,256]{2,1,0:T(8,128)(2,1)S(1)}, u32[]{:S(2)}, u32[]{:S(2)}) collective-permute-start(bf16[4,576,256]{2,1,0:T(8,128)(2,1)S(1)} %pad_maximum_fusion.t0), channel_id=1, source_target_pairs={{0,4},{1,5},{2,6},{3,7},{4,0},{5,1},{6,2},{7,3},{8,12},{9,13},{10,... | collective-permute-start | bytes 3538952 | tf_op jit(solution)/shard_map/ppermute | solution.py:45
  37.0 17.8 %collective-permute-start.3 = (bf16[4,576,256]{2,1,0:T(8,128)(2,1)S(1)}, bf16[4,576,256]{2,1,0:T(8,128)(2,1)S(1)}, u32[]{:S(2)}, u32[]{:S(2)}) collective-permute-start(bf16[4,576,256]{2,1,0:T(8,128)(2,1)S(1)} %pad_maximum_fusion.t0), channel_id=1, source_target_pairs={{0,12},{1,13},{2,14},{3,15},{4,8},{5,9},{6,10},{7,11},{8,4},{9,5},... | collective-permute-start | bytes 3538952 | tf_op jit(solution)/shard_map/ppermute | solution.py:45
  51.6 11.2 %collective-permute-start.6 = (bf16[2,576,256]{2,1,0:T(8,128)(2,1)S(1)}, bf16[2,576,256]{2,1,0:T(8,128)(2,1)S(1)}, u32[]{:S(2)}, u32[]{:S(2)}) collective-permute-start(bf16[2,576,256]{2,1,0:T(8,128)(2,1)S(1)} %slice.125), channel_id=1, source_target_pairs={{0,12},{1,13},{2,14},{3,15},{4,8},{5,9},{6,10},{7,11},{8,4},{9,5},... | collective-permute-start | bytes 1769480 | tf_op jit(solution)/shard_map/ppermute | solution.py:45
  54.8 10.0 %collective-permute-start.4 = (bf16[2,576,256]{2,1,0:T(8,128)(2,1)S(1)}, bf16[2,576,256]{2,1,0:T(8,128)(2,1)S(1)}, u32[]{:S(2)}, u32[]{:S(2)}) collective-permute-start(bf16[2,576,256]{2,1,0:T(8,128)(2,1)S(1)} %slice.124), channel_id=1, source_target_pairs={{0,4},{1,5},{2,6},{3,7},{4,0},{5,1},{6,2},{7,3},{8,12},{9,13},{10,... | collective-permute-start | bytes 1769480 | tf_op jit(solution)/shard_map/ppermute | solution.py:45
  64.7 27.6 %copy-start.2 = (f32[512]{0:T(512)S(1)}, f32[512]{0:T(512)}, u32[]{:S(2)}) copy-start(f32[512]{0:T(512)} %param.9) | copy-start | bytes 6148
  66.8 36.1 %collective-permute-start.16 = (bf16[5120,256]{1,0:T(8,128)(2,1)S(1)}, bf16[5120,256]{1,0:T(8,128)(2,1)S(1)}, u32[]{:S(2)}, u32[]{:S(2)}) collective-permute-start(bf16[5120,256]{1,0:T(8,128)(2,1)S(1)} %get-tuple-element.38.h_own), channel_id=1, source_target_pairs={{0,64},{1,65},{2,66},{3,67},{4,68},{5,69},{6,70},{7,71},{8,72},{9,... | collective-permute-start | bytes 7864328 | tf_op jit(solution)/shard_map/ppermute | solution.py:45
  66.9 3.7 %collective-permute-start.9 = (f32[8,256]{1,0:T(8,128)S(1)}, f32[8,256]{1,0:T(8,128)S(1)}, u32[]{:S(2)}, u32[]{:S(2)}) collective-permute-start(f32[8,256]{1,0:T(8,128)S(1)} %get-tuple-element.31.local), channel_id=1, source_target_pairs={{0,128},{1,129},{2,130},{3,131},{4,132},{5,133},{6,134},{7,135},{8... | collective-permute-start | bytes 24584 | tf_op jit(solution)/shard_map/ppermute | solution.py:45
  70.7 6.6 %collective-permute-start.12 = (f32[8,256]{1,0:T(8,128)S(1)}, f32[8,256]{1,0:T(8,128)S(1)}, u32[]{:S(2)}, u32[]{:S(2)}) collective-permute-start(f32[8,256]{1,0:T(8,128)S(1)} %pad_maximum_fusion.6), channel_id=1, source_target_pairs={{0,3},{1,2},{2,1},{3,0},{4,7},{5,6},{6,5},{7,4},{8,11},{9,10},{10,... | collective-permute-start | bytes 24584 | tf_op jit(solution)/shard_map/ppermute | solution.py:45
  71.4 7.6 %collective-permute-start.11 = (f32[8,256]{1,0:T(8,128)S(1)}, f32[8,256]{1,0:T(8,128)S(1)}, u32[]{:S(2)}, u32[]{:S(2)}) collective-permute-start(f32[8,256]{1,0:T(8,128)S(1)} %pad_maximum_fusion.6), channel_id=1, source_target_pairs={{0,2},{1,3},{2,0},{3,1},{4,6},{5,7},{6,4},{7,5},{8,10},{9,11},{10,... | collective-permute-start | bytes 24584 | tf_op jit(solution)/shard_map/ppermute | solution.py:45
  75.3 4.6 %collective-permute-start.10 = (f32[8,256]{1,0:T(8,128)S(1)}, f32[8,256]{1,0:T(8,128)S(1)}, u32[]{:S(2)}, u32[]{:S(2)}) collective-permute-start(f32[8,256]{1,0:T(8,128)S(1)} %pad_maximum_fusion.6), channel_id=1, source_target_pairs={{0,1},{1,0},{2,3},{3,2},{4,5},{5,4},{6,7},{7,6},{8,9},{9,8},{10,11... | collective-permute-start | bytes 24584 | tf_op jit(solution)/shard_map/ppermute | solution.py:45
  94.1 7.1 %collective-permute-start.13 = (bf16[2,320,256]{2,1,0:T(8,128)(2,1)S(1)}, bf16[2,320,256]{2,1,0:T(8,128)(2,1)S(1)}, u32[]{:S(2)}, u32[]{:S(2)}) collective-permute-start(bf16[2,320,256]{2,1,0:T(8,128)(2,1)S(1)} %get-tuple-element.35), channel_id=1, source_target_pairs={{0,4},{1,5},{2,6},{3,7},{4,0},{5,1},{6,2},{7,3},{8,12},{9,13},{10,... | collective-permute-start | bytes 983048 | tf_op jit(solution)/shard_map/ppermute | solution.py:45
  94.6 8.3 %collective-permute-start.14 = (bf16[2,320,256]{2,1,0:T(8,128)(2,1)S(1)}, bf16[2,320,256]{2,1,0:T(8,128)(2,1)S(1)}, u32[]{:S(2)}, u32[]{:S(2)}) collective-permute-start(bf16[2,320,256]{2,1,0:T(8,128)(2,1)S(1)} %get-tuple-element.36), channel_id=1, source_target_pairs={{0,12},{1,13},{2,14},{3,15},{4,8},{5,9},{6,10},{7,11},{8,4},{9,5},... | collective-permute-start | bytes 983048 | tf_op jit(solution)/shard_map/ppermute | solution.py:45
  96.2 3.2 %collective-permute-start.15 = (bf16[384,256]{1,0:T(8,128)(2,1)S(1)}, bf16[384,256]{1,0:T(8,128)(2,1)S(1)}, u32[]{:S(2)}, u32[]{:S(2)}) collective-permute-start(bf16[384,256]{1,0:T(8,128)(2,1)S(1)} %get-tuple-element.37.g_oth), channel_id=1, source_target_pairs={{0,64},{1,65},{2,66},{3,67},{4,68},{5,69},{6,70},{7,71},{8,72},{9,... | collective-permute-start | bytes 589832 | tf_op jit(solution)/shard_map/ppermute | solution.py:45
  103.2 11.9 %collective-permute-start.18 = (bf16[4,320,256]{2,1,0:T(8,128)(2,1)S(1)}, bf16[4,320,256]{2,1,0:T(8,128)(2,1)S(1)}, u32[]{:S(2)}, u32[]{:S(2)}) collective-permute-start(bf16[4,320,256]{2,1,0:T(8,128)(2,1)S(1)} %pad_maximum_fusion.2), channel_id=1, source_target_pairs={{0,12},{1,13},{2,14},{3,15},{4,8},{5,9},{6,10},{7,11},{8,4},{9,5},... | collective-permute-start | bytes 1966088 | tf_op jit(solution)/shard_map/ppermute | solution.py:45
  105.0 12.4 %collective-permute-start.17 = (bf16[4,320,256]{2,1,0:T(8,128)(2,1)S(1)}, bf16[4,320,256]{2,1,0:T(8,128)(2,1)S(1)}, u32[]{:S(2)}, u32[]{:S(2)}) collective-permute-start(bf16[4,320,256]{2,1,0:T(8,128)(2,1)S(1)} %pad_maximum_fusion.1), channel_id=1, source_target_pairs={{0,4},{1,5},{2,6},{3,7},{4,0},{5,1},{6,2},{7,3},{8,12},{9,13},{10,... | collective-permute-start | bytes 1966088 | tf_op jit(solution)/shard_map/ppermute | solution.py:45
  117.7 5.4 %collective-permute-start.19 = (bf16[320,256]{1,0:T(8,128)(2,1)S(1)}, bf16[320,256]{1,0:T(8,128)(2,1)S(1)}, u32[]{:S(2)}, u32[]{:S(2)}) collective-permute-start(bf16[320,256]{1,0:T(8,128)(2,1)S(1)} %get-tuple-element.59), channel_id=1, source_target_pairs={{0,16},{1,17},{2,18},{3,19},{4,20},{5,21},{6,22},{7,23},{8,24},{9,... | collective-permute-start | bytes 491528 | tf_op jit(solution)/shard_map/ppermute | solution.py:45
  118.9 6.9 %collective-permute-start.21 = (bf16[320,256]{1,0:T(8,128)(2,1)S(1)}, bf16[320,256]{1,0:T(8,128)(2,1)S(1)}, u32[]{:S(2)}, u32[]{:S(2)}) collective-permute-start(bf16[320,256]{1,0:T(8,128)(2,1)S(1)} %get-tuple-element.60), channel_id=1, source_target_pairs={{0,32},{1,33},{2,34},{3,35},{4,36},{5,37},{6,38},{7,39},{8,40},{9,... | collective-permute-start | bytes 491528 | tf_op jit(solution)/shard_map/ppermute | solution.py:45
  119.2 7.2 %collective-permute-start.20 = (bf16[320,256]{1,0:T(8,128)(2,1)S(1)}, bf16[320,256]{1,0:T(8,128)(2,1)S(1)}, u32[]{:S(2)}, u32[]{:S(2)}) collective-permute-start(bf16[320,256]{1,0:T(8,128)(2,1)S(1)} %get-tuple-element.61), channel_id=1, source_target_pairs={{0,48},{1,49},{2,50},{3,51},{4,52},{5,53},{6,54},{7,55},{8,56},{9,... | collective-permute-start | bytes 491528 | tf_op jit(solution)/shard_map/ppermute | solution.py:45
  (1 other events, 1.9 us)

commit v8 on v7

--- a/solution.py
+++ b/solution.py
@@ -69,17 +69,17 @@
     return pl.ds(start, WIDE), pl.multiple_of((at & 1) * 64, 64)
 
 
-def spread_kernel(mine, out):
-    for i in range(8):
-        out[i] = mine[...]
-
-
-def weave_kernel(along, out):
-    for zh in range(4):
-        for zl in range(2):
-            tokens = slice(zl * 128, (zl + 1) * 128)
-            out[zh * 80 : (zh + 1) * 80, tokens] = along[zl * 4 + zh, 0:80]
-            out[NS + zh * 64 : NS + (zh + 1) * 64, tokens] = along[zl * 4 + zh, 80:144]
+def beside_kernel(mine, pair, out):
+    first = lax.axis_index("zl") == 0
+    out[:, :128] = jnp.where(first, mine[...], pair[...])
+    out[:, 128:] = jnp.where(first, pair[...], mine[...])
+
+
+def weave_kernel(r0, r1, r2, r3, out):
+    zh = lax.axis_index("zh")
+    for k, r in enumerate((r0, r1, r2, r3)):
+        out[pl.ds(pl.multiple_of((zh ^ k) * 80, 16), 80)] = r[0:80]
+        out[pl.ds(pl.multiple_of(NS + (zh ^ k) * 64, 64), 64)] = r[80:144]
 
 
 def near_kernel(t0, t1, t3, ws, wso, wt, wto, s_ref, t_ref, hs, ht):
@@ -263,9 +263,12 @@
     student_other = send(student_head, CORE)
 
     mine = jnp.concatenate([student_hidden.T, teacher_hidden.T], axis=0)
-    copies = vmem_call(spread_kernel, "spread", [((8, 144, 128), BF16)], [], 1, mine)[0]
-    along = lax.all_to_all(copies, ("zl", "zh"), 0, 0)
-    block = vmem_call(weave_kernel, "weave", [((NS + NT, TOK), BF16)], [], 1, along)[0]
+    both = vmem_call(
+        beside_kernel, "beside", [((144, TOK), BF16)], [], 1, mine, send(mine, PAIR)
+    )[0]
+    block = vmem_call(
+        weave_kernel, "weave", [((NS + NT, TOK), BF16)], [], 1, both, *ring(both, ZH)
+    )[0]
     line = jnp.stack((block,) + ring(block, FIRST))
     before, after = send(line, SECOND[1]), send(line, SECOND[3])
     far_low, far_high = send(after[:2], SECOND[1]), send(before[2:], SECOND[3])

time: 143 us -> 143 us (level)
  blocking collectives: 48.2 us -> 27.7 us
  starting transfers between devices: 26.8 us -> 38.5 us
  waiting for transfers between devices: 44.9 us -> 53.6 us
    all_to_all x1 -> x0, blocking collectives: 21 us -> none  [per_device(): along = lax.all_to_all(copies, ('zl', 'zh'), 0, 0)]
    ppermute x22 -> x26, starting transfers between devices: 26.8 us -> 38.5 us  [send(): return lax.ppermute(value, AXES, pairs)]
    ppermute x22 -> x26, waiting for transfers between devices: 44.9 us -> 53.6 us  [send(): return lax.ppermute(value, AXES, pairs)]
  transfers between devices with their start and end apart: 22 -> 26, of which waited for: 15 -> 19; matrix products, arithmetic and copies ran while one was open for 1% -> 1% of each run, Pallas kernels for 10% -> 10%
where the time goes in v8:
time: 143 us; the launch traced here: 142 us
  waiting for transfers between devices  53.6 us (37%)
  starting transfers between devices  38.5 us (27%)
  blocking collectives  27.7 us (19%)
  Pallas kernels  16.8 us (12%)
  other arithmetic  2.32 us (2%)
  local copies, waits for them, and re-layouts  2.11 us (1%)
    ppermute x26, waiting for transfers between devices, send(): return lax.ppermute(value, AXES, pairs)  53.6 us
    ppermute x26, starting transfers between devices, send(): return lax.ppermute(value, AXES, pairs)  38.5 us
    all_to_all x1, blocking collectives, per_device(): hidden_grad = jnp.sum(lax.all_to_all(sums, ('zl', 'zh'), 0, 0), axis=0).T  15.4 us
    all_to_all x1, blocking collectives, per_device(): lax.all_to_all(jnp.broadcast_to(stats, (16, 8, TOK)), ('x', 'y'), 0, 0)  12.3 us
    pallas_call x6, Pallas kernels, vmem_call(): pl.pallas_call(kernel, out_shape=tuple((jax.ShapeDtypeStruct(*o) for o in...  11.1 us
    pallas_call x1, Pallas kernels, head_call(): pl.pallas_call(head_kernel, out_shape=jax.ShapeDtypeStruct((ROWS, DS), BF...  5.65 us
  transfers between devices with their start and end apart: 26, of which 19 were waited for; matrix products, arithmetic and copies ran while one was open for 1% of the time, Pallas kernels for 10%

profile of v8, /device:TPU:2, one launch (start us, length us, event | category | flops | bytes accessed | tf_op | source)
XLA Modules:
  0.0 141.9 jit_solution(4789697713596758158)
XLA Ops:
  3.9 2.0 %collective-permute-done.pair = bf16[144,128]{1,0:T(8,128)(2,1)S(1)} collective-permute-done((bf16[144,128]{1,0:T(8,128)(2,1)S(1)}, bf16[144,128]{1,0:T(8,128)(2,1)S(1)}, u32[]{:S(2)}, u32[]{:S(2)}) %collective-permute-start) | collective-permute-done | bytes 36896 | tf_op jit(solution)/shard_map/ppermute | solution.py:45
  6.0 6.4 %collective-permute-start.3 = (bf16[144,256]{1,0:T(8,128)(2,1)S(1)}, bf16[144,256]{1,0:T(8,128)(2,1)S(1)}, u32[]{:S(2)}, u32[]{:S(2)}) collective-permute-start(bf16[144,256]{1,0:T(8,128)(2,1)S(1)} %beside.1.r0), channel_id=1, source_target_pairs={{0,3},{1,2},{2,1},{3,0},{4,7},{5,6},{6,5},{7,4},{8,11},{9,10},{10,... | collective-permute-start | bytes 221192 | tf_op jit(solution)/shard_map/ppermute | solution.py:45
  14.8 3.0 %collective-permute-done.3.r3 = bf16[144,256]{1,0:T(8,128)(2,1)S(1)} collective-permute-done((bf16[144,256]{1,0:T(8,128)(2,1)S(1)}, bf16[144,256]{1,0:T(8,128)(2,1)S(1)}, u32[]{:S(2)}, u32[]{:S(2)}) %collective-permute-start.3) | collective-permute-done | bytes 73760 | tf_op jit(solution)/shard_map/ppermute | solution.py:45
  17.8 3.6 %collective-permute-done.2.r2 = bf16[144,256]{1,0:T(8,128)(2,1)S(1)} collective-permute-done((bf16[144,256]{1,0:T(8,128)(2,1)S(1)}, bf16[144,256]{1,0:T(8,128)(2,1)S(1)}, u32[]{:S(2)}, u32[]{:S(2)}) %collective-permute-start.2) | collective-permute-done | bytes 73760 | tf_op jit(solution)/shard_map/ppermute | solution.py:45
  26.0 5.8 %collective-permute-done.6 = bf16[576,256]{1,0:T(8,128)(2,1)S(1)} collective-permute-done((bf16[576,256]{1,0:T(8,128)(2,1)S(1)}, bf16[576,256]{1,0:T(8,128)(2,1)S(1)}, u32[]{:S(2)}, u32[]{:S(2)}) %collective-permute-start.6) | collective-permute-done | bytes 294944 | tf_op jit(solution)/shard_map/ppermute | solution.py:45
  31.8 2.1 %collective-permute-done.4 = bf16[576,256]{1,0:T(8,128)(2,1)S(1)} collective-permute-done((bf16[576,256]{1,0:T(8,128)(2,1)S(1)}, bf16[576,256]{1,0:T(8,128)(2,1)S(1)}, u32[]{:S(2)}, u32[]{:S(2)}) %collective-permute-start.4) | collective-permute-done | bytes 294944 | tf_op jit(solution)/shard_map/ppermute | solution.py:45
  35.7 2.2 %collective-permute-start.7 = (bf16[4,576,256]{2,1,0:T(8,128)(2,1)S(1)}, bf16[4,576,256]{2,1,0:T(8,128)(2,1)S(1)}, u32[]{:S(2)}, u32[]{:S(2)}) collective-permute-start(bf16[4,576,256]{2,1,0:T(8,128)(2,1)S(1)} %pad_maximum_fusion.t0), channel_id=1, source_target_pairs={{0,12},{1,13},{2,14},{3,15},{4,8},{5,9},{6,10},{7,11},{8,4},{9,5},... | collective-permute-start | bytes 3538952 | tf_op jit(solution)/shard_map/ppermute | solution.py:45
  37.9 12.4 %collective-permute-done.9.t1 = bf16[4,576,256]{2,1,0:T(8,128)(2,1)S(1)} collective-permute-done((bf16[4,576,256]{2,1,0:T(8,128)(2,1)S(1)}, bf16[4,576,256]{2,1,0:T(8,128)(2,1)S(1)}, u32[]{:S(2)}, u32[]{:S(2)}) %collective-permute-start.9) | collective-permute-done | bytes 1179680 | tf_op jit(solution)/shard_map/ppermute | solution.py:45
  50.4 3.1 %collective-permute-start.10 = (bf16[2,576,256]{2,1,0:T(8,128)(2,1)S(1)}, bf16[2,576,256]{2,1,0:T(8,128)(2,1)S(1)}, u32[]{:S(2)}, u32[]{:S(2)}) collective-permute-start(bf16[2,576,256]{2,1,0:T(8,128)(2,1)S(1)} %slice.125), channel_id=1, source_target_pairs={{0,12},{1,13},{2,14},{3,15},{4,8},{5,9},{6,10},{7,11},{8,4},{9,5},... | collective-permute-start | bytes 1769480 | tf_op jit(solution)/shard_map/ppermute | solution.py:45
  55.8 4.1 %near.1 = (f32[768,256]{1,0:T(8,128)S(1)}, f32[768,256]{1,0:T(8,128)S(1)}, bf16[5120,256]{1,0:T(8,128)(2,1)S(1)}) custom-call(bf16[4,576,256]{2,1,0:T(8,128)(2,1)S(1)} %pad_maximum_fusion.t0, bf16[4,576,256]{2,1,0:T(8,128)(2,1)S(1)} %collective-permute-done.9.t1, bf16[4,576,256]{2,1,0:T(8,128)(2,1)S(1)} %collective-permute-done.7.t3, ...), custom_call_target="tpu_custom_call" | custom-call | flops 3623878656 | bytes 14000000 | tf_op jit(solution)/shard_map/near/pallas_call | solution.py:140
  61.5 2.1 %collective-permute-done.8.t2a = bf16[2,576,256]{2,1,0:T(8,128)(2,1)S(1)} collective-permute-done((bf16[2,576,256]{2,1,0:T(8,128)(2,1)S(1)}, bf16[2,576,256]{2,1,0:T(8,128)(2,1)S(1)}, u32[]{:S(2)}, u32[]{:S(2)}) %collective-permute-start.8) | collective-permute-done | bytes 589856 | tf_op jit(solution)/shard_map/ppermute | solution.py:45
  63.7 2.0 %far.1 = (f32[768,256]{1,0:T(8,128)S(1)}, f32[768,256]{1,0:T(8,128)S(1)}, f32[8,256]{1,0:T(8,128)S(1)}, bf16[5120,256]{1,0:T(8,128)(2,1)S(1)}) custom-call(bf16[2,576,256]{2,1,0:T(8,128)(2,1)S(1)} %collective-permute-done.8.t2a, bf16[2,576,256]{2,1,0:T(8,128)(2,1)S(1)} %collective-permute-done.10.t2b, f32[768,256]{1,0:T(8,128)S(1)} %get-tuple-element.28.s_in, ...), custom_call_target="tpu_custom_call" | custom-call | flops 1207959552 | bytes 14000000 | tf_op jit(solution)/shard_map/far/pallas_call | solution.py:140
  67.3 2.2 %collective-permute-done.13 = f32[8,256]{1,0:T(8,128)S(1)} collective-permute-done((f32[8,256]{1,0:T(8,128)S(1)}, f32[8,256]{1,0:T(8,128)S(1)}, u32[]{:S(2)}, u32[]{:S(2)}) %collective-permute-start.13) | collective-permute-done | bytes 8224 | tf_op jit(solution)/shard_map/ppermute | solution.py:45
  69.6 2.0 %collective-permute-start.16 = (f32[8,256]{1,0:T(8,128)S(1)}, f32[8,256]{1,0:T(8,128)S(1)}, u32[]{:S(2)}, u32[]{:S(2)}) collective-permute-start(f32[8,256]{1,0:T(8,128)S(1)} %pad_maximum_fusion.6), channel_id=1, source_target_pairs={{0,3},{1,2},{2,1},{3,0},{4,7},{5,6},{6,5},{7,4},{8,11},{9,10},{10,... | collective-permute-start | bytes 24584 | tf_op jit(solution)/shard_map/ppermute | solution.py:45
  71.7 3.1 %collective-permute-start.15 = (f32[8,256]{1,0:T(8,128)S(1)}, f32[8,256]{1,0:T(8,128)S(1)}, u32[]{:S(2)}, u32[]{:S(2)}) collective-permute-start(f32[8,256]{1,0:T(8,128)S(1)} %pad_maximum_fusion.6), channel_id=1, source_target_pairs={{0,2},{1,3},{2,0},{3,1},{4,6},{5,7},{6,4},{7,5},{8,10},{9,11},{10,... | collective-permute-start | bytes 24584 | tf_op jit(solution)/shard_map/ppermute | solution.py:45
  76.2 3.0 %collective-permute-done.15 = f32[8,256]{1,0:T(8,128)S(1)} collective-permute-done((f32[8,256]{1,0:T(8,128)S(1)}, f32[8,256]{1,0:T(8,128)S(1)}, u32[]{:S(2)}, u32[]{:S(2)}) %collective-permute-start.15) | collective-permute-done | bytes 8224 | tf_op jit(solution)/shard_map/ppermute | solution.py:45
  79.5 12.3 %all_to_all.10.stats = f32[16,8,256]{2,1,0:T(8,128)S(1)} all-to-all(f32[16,8,256]{2,1,0:T(8,128)S(1)} %broadcast_in_dim.3), channel_id=1, replica_groups=mesh['zl'=2,'c'=2,'x'=4,'y'=4,'zh'=4] {'x','y'}, dimensions={0} | all-to-all | bytes 262144 | tf_op jit(solution)/shard_map/all_to_all | solution.py:281
  95.6 3.1 %rest.1 = (bf16[4,320,256]{2,1,0:T(8,128)(2,1)S(1)}, bf16[4,320,256]{2,1,0:T(8,128)(2,1)S(1)}, bf16[4,320,256]{2,1,0:T(8,128)(2,1)S(1)}) custom-call(bf16[384,256]{1,0:T(8,128)(2,1)S(1)} %get-tuple-element.39.g_own, bf16[384,256]{1,0:T(8,128)(2,1)S(1)} %get-tuple-element.37.g_oth, bf16[384,5120]{1,0:T(8,128)(2,1)S(1)} %copy-done, ...), custom_call_target="tpu_custom_call" | custom-call | flops 2013265920 | bytes 14000000 | tf_op jit(solution)/shard_map/rest/pallas_call | solution.py:140
  104.4 5.7 %head.1 = bf16[384,5120]{1,0:T(8,128)(2,1)} custom-call(bf16[384,256]{1,0:T(8,128)(2,1)S(1)} %get-tuple-element.39.g_own, bf16[384,256]{1,0:T(8,128)(2,1)S(1)} %collective-permute-done.19.g_got, bf16[5120,256]{1,0:T(8,128)(2,1)S(1)} %get-tuple-element.38.h_own, bf16[5120,256]{1,0:T(8,128)(2,1)S(1)} %collective-permute-done.20.h_got), custom_call_target="tpu_custom_call" | custom-call | flops 2013265920 | bytes 10000000 | tf_op jit(solution)/shard_map/head/pallas_call | solution.py:236
  110.1 4.4 %collective-permute-done.22 = bf16[4,320,256]{2,1,0:T(8,128)(2,1)S(1)} collective-permute-done((bf16[4,320,256]{2,1,0:T(8,128)(2,1)S(1)}, bf16[4,320,256]{2,1,0:T(8,128)(2,1)S(1)}, u32[]{:S(2)}, u32[]{:S(2)}) %collective-permute-start.22) | collective-permute-done | bytes 655392 | tf_op jit(solution)/shard_map/ppermute | solution.py:45
  114.5 2.3 %collective-permute-done.21 = bf16[4,320,256]{2,1,0:T(8,128)(2,1)S(1)} collective-permute-done((bf16[4,320,256]{2,1,0:T(8,128)(2,1)S(1)}, bf16[4,320,256]{2,1,0:T(8,128)(2,1)S(1)}, u32[]{:S(2)}, u32[]{:S(2)}) %collective-permute-start.21) | collective-permute-done | bytes 655392 | tf_op jit(solution)/shard_map/ppermute | solution.py:45
  118.5 2.1 %collective-permute-start.24 = (bf16[320,256]{1,0:T(8,128)(2,1)S(1)}, bf16[320,256]{1,0:T(8,128)(2,1)S(1)}, u32[]{:S(2)}, u32[]{:S(2)}) collective-permute-start(bf16[320,256]{1,0:T(8,128)(2,1)S(1)} %get-tuple-element.61), channel_id=1, source_target_pairs={{0,48},{1,49},{2,50},{3,51},{4,52},{5,53},{6,54},{7,55},{8,56},{9,... | collective-permute-start | bytes 491528 | tf_op jit(solution)/shard_map/ppermute | solution.py:45
  122.5 2.7 %collective-permute-done.25 = bf16[320,256]{1,0:T(8,128)(2,1)S(1)} collective-permute-done((bf16[320,256]{1,0:T(8,128)(2,1)S(1)}, bf16[320,256]{1,0:T(8,128)(2,1)S(1)}, u32[]{:S(2)}, u32[]{:S(2)}) %collective-permute-start.25) | collective-permute-done | bytes 163872 | tf_op jit(solution)/shard_map/ppermute | solution.py:45
  125.9 15.4 %all_to_all.11 = f32[8,80,128]{2,1,0:T(8,128)S(1)} all-to-all(f32[8,80,128]{2,1,0:T(8,128)S(1)} %bitcast.24), channel_id=1, replica_groups=mesh['zl'=2,'c'=2,'x'=4,'y'=4,'zh'=4] {'zl','zh'}, dimensions={0} | all-to-all | bytes 655360 | tf_op jit(solution)/shard_map/all_to_all | solution.py:300
  (74 shorter events, 33.8 us)
Async XLA Ops:
  0.6 53.3 %collective-permute-start.11 = (bf16[384,5120]{1,0:T(8,128)(2,1)}, bf16[384,5120]{1,0:T(8,128)(2,1)S(1)}, u32[]{:S(2)}, u32[]{:S(2)}) collective-permute-start(bf16[384,5120]{1,0:T(8,128)(2,1)} %ws.7), channel_id=1, source_target_pairs={{0,64},{1,65},{2,66},{3,67},{4,68},{5,69},{6,70},{7,71},{8,72},{9,... | collective-permute-start | bytes 11796488 | tf_op jit(solution)/shard_map/ppermute | solution.py:45
  0.7 53.2 %collective-permute-start.12 = (bf16[384,4096]{1,0:T(8,128)(2,1)}, bf16[384,4096]{1,0:T(8,128)(2,1)S(1)}, u32[]{:S(2)}, u32[]{:S(2)}) collective-permute-start(bf16[384,4096]{1,0:T(8,128)(2,1)} %wt.3), channel_id=1, source_target_pairs={{0,64},{1,65},{2,66},{3,67},{4,68},{5,69},{6,70},{7,71},{8,72},{9,... | collective-permute-start | bytes 9437192 | tf_op jit(solution)/shard_map/ppermute | solution.py:45
  2.0 4.0 %collective-permute-start = (bf16[144,128]{1,0:T(8,128)(2,1)S(1)}, bf16[144,128]{1,0:T(8,128)(2,1)S(1)}, u32[]{:S(2)}, u32[]{:S(2)}) collective-permute-start(bf16[144,128]{1,0:T(8,128)(2,1)S(1)} %pad_maximum_fusion.4.mine), channel_id=1, source_target_pairs={{0,128},{1,129},{2,130},{3,131},{4,132},{5,133},{6,134},{7,135},{8... | collective-permute-start | bytes 110600 | tf_op jit(solution)/shard_map/ppermute | solution.py:45
  6.0 11.8 %collective-permute-start.3 = (bf16[144,256]{1,0:T(8,128)(2,1)S(1)}, bf16[144,256]{1,0:T(8,128)(2,1)S(1)}, u32[]{:S(2)}, u32[]{:S(2)}) collective-permute-start(bf16[144,256]{1,0:T(8,128)(2,1)S(1)} %beside.1.r0), channel_id=1, source_target_pairs={{0,3},{1,2},{2,1},{3,0},{4,7},{5,6},{6,5},{7,4},{8,11},{9,10},{10,... | collective-permute-start | bytes 221192 | tf_op jit(solution)/shard_map/ppermute | solution.py:45
  12.3 9.1 %collective-permute-start.2 = (bf16[144,256]{1,0:T(8,128)(2,1)S(1)}, bf16[144,256]{1,0:T(8,128)(2,1)S(1)}, u32[]{:S(2)}, u32[]{:S(2)}) collective-permute-start(bf16[144,256]{1,0:T(8,128)(2,1)S(1)} %beside.1.r0), channel_id=1, source_target_pairs={{0,2},{1,3},{2,0},{3,1},{4,6},{5,7},{6,4},{7,5},{8,10},{9,11},{10,... | collective-permute-start | bytes 221192 | tf_op jit(solution)/shard_map/ppermute | solution.py:45
  13.3 8.4 %collective-permute-start.1 = (bf16[144,256]{1,0:T(8,128)(2,1)S(1)}, bf16[144,256]{1,0:T(8,128)(2,1)S(1)}, u32[]{:S(2)}, u32[]{:S(2)}) collective-permute-start(bf16[144,256]{1,0:T(8,128)(2,1)S(1)} %beside.1.r0), channel_id=1, source_target_pairs={{0,1},{1,0},{2,3},{3,2},{4,5},{5,4},{6,7},{7,6},{8,9},{9,8},{10,11... | collective-permute-start | bytes 221192 | tf_op jit(solution)/shard_map/ppermute | solution.py:45
  21.8 10.0 %collective-permute-start.6 = (bf16[576,256]{1,0:T(8,128)(2,1)S(1)}, bf16[576,256]{1,0:T(8,128)(2,1)S(1)}, u32[]{:S(2)}, u32[]{:S(2)}) collective-permute-start(bf16[576,256]{1,0:T(8,128)(2,1)S(1)} %weave.1), channel_id=1, source_target_pairs={{0,48},{1,49},{2,50},{3,51},{4,52},{5,53},{6,54},{7,55},{8,56},{9,... | collective-permute-start | bytes 884744 | tf_op jit(solution)/shard_map/ppermute | solution.py:45
  23.4 8.4 %collective-permute-start.5 = (bf16[576,256]{1,0:T(8,128)(2,1)S(1)}, bf16[576,256]{1,0:T(8,128)(2,1)S(1)}, u32[]{:S(2)}, u32[]{:S(2)}) collective-permute-start(bf16[576,256]{1,0:T(8,128)(2,1)S(1)} %weave.1), channel_id=1, source_target_pairs={{0,32},{1,33},{2,34},{3,35},{4,36},{5,37},{6,38},{7,39},{8,40},{9,... | collective-permute-start | bytes 884744 | tf_op jit(solution)/shard_map/ppermute | solution.py:45
  24.5 9.4 %collective-permute-start.4 = (bf16[576,256]{1,0:T(8,128)(2,1)S(1)}, bf16[576,256]{1,0:T(8,128)(2,1)S(1)}, u32[]{:S(2)}, u32[]{:S(2)}) collective-permute-start(bf16[576,256]{1,0:T(8,128)(2,1)S(1)} %weave.1), channel_id=1, source_target_pairs={{0,16},{1,17},{2,18},{3,19},{4,20},{5,21},{6,22},{7,23},{8,24},{9,... | collective-permute-start | bytes 884744 | tf_op jit(solution)/shard_map/ppermute | solution.py:45
  34.0 16.3 %collective-permute-start.9 = (bf16[4,576,256]{2,1,0:T(8,128)(2,1)S(1)}, bf16[4,576,256]{2,1,0:T(8,128)(2,1)S(1)}, u32[]{:S(2)}, u32[]{:S(2)}) collective-permute-start(bf16[4,576,256]{2,1,0:T(8,128)(2,1)S(1)} %pad_maximum_fusion.t0), channel_id=1, source_target_pairs={{0,4},{1,5},{2,6},{3,7},{4,0},{5,1},{6,2},{7,3},{8,12},{9,13},{10,... | collective-permute-start | bytes 3538952 | tf_op jit(solution)/shard_map/ppermute | solution.py:45
  35.7 17.8 %collective-permute-start.7 = (bf16[4,576,256]{2,1,0:T(8,128)(2,1)S(1)}, bf16[4,576,256]{2,1,0:T(8,128)(2,1)S(1)}, u32[]{:S(2)}, u32[]{:S(2)}) collective-permute-start(bf16[4,576,256]{2,1,0:T(8,128)(2,1)S(1)} %pad_maximum_fusion.t0), channel_id=1, source_target_pairs={{0,12},{1,13},{2,14},{3,15},{4,8},{5,9},{6,10},{7,11},{8,4},{9,5},... | collective-permute-start | bytes 3538952 | tf_op jit(solution)/shard_map/ppermute | solution.py:45
  50.4 11.2 %collective-permute-start.10 = (bf16[2,576,256]{2,1,0:T(8,128)(2,1)S(1)}, bf16[2,576,256]{2,1,0:T(8,128)(2,1)S(1)}, u32[]{:S(2)}, u32[]{:S(2)}) collective-permute-start(bf16[2,576,256]{2,1,0:T(8,128)(2,1)S(1)} %slice.125), channel_id=1, source_target_pairs={{0,12},{1,13},{2,14},{3,15},{4,8},{5,9},{6,10},{7,11},{8,4},{9,5},... | collective-permute-start | bytes 1769480 | tf_op jit(solution)/shard_map/ppermute | solution.py:45
  53.5 10.2 %collective-permute-start.8 = (bf16[2,576,256]{2,1,0:T(8,128)(2,1)S(1)}, bf16[2,576,256]{2,1,0:T(8,128)(2,1)S(1)}, u32[]{:S(2)}, u32[]{:S(2)}) collective-permute-start(bf16[2,576,256]{2,1,0:T(8,128)(2,1)S(1)} %slice.124), channel_id=1, source_target_pairs={{0,4},{1,5},{2,6},{3,7},{4,0},{5,1},{6,2},{7,3},{8,12},{9,13},{10,... | collective-permute-start | bytes 1769480 | tf_op jit(solution)/shard_map/ppermute | solution.py:45
  65.7 36.6 %collective-permute-start.20 = (bf16[5120,256]{1,0:T(8,128)(2,1)S(1)}, bf16[5120,256]{1,0:T(8,128)(2,1)S(1)}, u32[]{:S(2)}, u32[]{:S(2)}) collective-permute-start(bf16[5120,256]{1,0:T(8,128)(2,1)S(1)} %get-tuple-element.38.h_own), channel_id=1, source_target_pairs={{0,64},{1,65},{2,66},{3,67},{4,68},{5,69},{6,70},{7,71},{8,72},{9,... | collective-permute-start | bytes 7864328 | tf_op jit(solution)/shard_map/ppermute | solution.py:45
  69.6 6.6 %collective-permute-start.16 = (f32[8,256]{1,0:T(8,128)S(1)}, f32[8,256]{1,0:T(8,128)S(1)}, u32[]{:S(2)}, u32[]{:S(2)}) collective-permute-start(f32[8,256]{1,0:T(8,128)S(1)} %pad_maximum_fusion.6), channel_id=1, source_target_pairs={{0,3},{1,2},{2,1},{3,0},{4,7},{5,6},{6,5},{7,4},{8,11},{9,10},{10,... | collective-permute-start | bytes 24584 | tf_op jit(solution)/shard_map/ppermute | solution.py:45
  71.7 7.6 %collective-permute-start.15 = (f32[8,256]{1,0:T(8,128)S(1)}, f32[8,256]{1,0:T(8,128)S(1)}, u32[]{:S(2)}, u32[]{:S(2)}) collective-permute-start(f32[8,256]{1,0:T(8,128)S(1)} %pad_maximum_fusion.6), channel_id=1, source_target_pairs={{0,2},{1,3},{2,0},{3,1},{4,6},{5,7},{6,4},{7,5},{8,10},{9,11},{10,... | collective-permute-start | bytes 24584 | tf_op jit(solution)/shard_map/ppermute | solution.py:45
  74.8 4.5 %collective-permute-start.14 = (f32[8,256]{1,0:T(8,128)S(1)}, f32[8,256]{1,0:T(8,128)S(1)}, u32[]{:S(2)}, u32[]{:S(2)}) collective-permute-start(f32[8,256]{1,0:T(8,128)S(1)} %pad_maximum_fusion.6), channel_id=1, source_target_pairs={{0,1},{1,0},{2,3},{3,2},{4,5},{5,4},{6,7},{7,6},{8,9},{9,8},{10,11... | collective-permute-start | bytes 24584 | tf_op jit(solution)/shard_map/ppermute | solution.py:45
  93.5 7.1 %collective-permute-start.17 = (bf16[2,320,256]{2,1,0:T(8,128)(2,1)S(1)}, bf16[2,320,256]{2,1,0:T(8,128)(2,1)S(1)}, u32[]{:S(2)}, u32[]{:S(2)}) collective-permute-start(bf16[2,320,256]{2,1,0:T(8,128)(2,1)S(1)} %get-tuple-element.35), channel_id=1, source_target_pairs={{0,4},{1,5},{2,6},{3,7},{4,0},{5,1},{6,2},{7,3},{8,12},{9,13},{10,... | collective-permute-start | bytes 983048 | tf_op jit(solution)/shard_map/ppermute | solution.py:45
  94.0 8.3 %collective-permute-start.18 = (bf16[2,320,256]{2,1,0:T(8,128)(2,1)S(1)}, bf16[2,320,256]{2,1,0:T(8,128)(2,1)S(1)}, u32[]{:S(2)}, u32[]{:S(2)}) collective-permute-start(bf16[2,320,256]{2,1,0:T(8,128)(2,1)S(1)} %get-tuple-element.36), channel_id=1, source_target_pairs={{0,12},{1,13},{2,14},{3,15},{4,8},{5,9},{6,10},{7,11},{8,4},{9,5},... | collective-permute-start | bytes 983048 | tf_op jit(solution)/shard_map/ppermute | solution.py:45
  102.6 11.9 %collective-permute-start.22 = (bf16[4,320,256]{2,1,0:T(8,128)(2,1)S(1)}, bf16[4,320,256]{2,1,0:T(8,128)(2,1)S(1)}, u32[]{:S(2)}, u32[]{:S(2)}) collective-permute-start(bf16[4,320,256]{2,1,0:T(8,128)(2,1)S(1)} %pad_maximum_fusion.2), channel_id=1, source_target_pairs={{0,12},{1,13},{2,14},{3,15},{4,8},{5,9},{6,10},{7,11},{8,4},{9,5},... | collective-permute-start | bytes 1966088 | tf_op jit(solution)/shard_map/ppermute | solution.py:45
  104.3 12.4 %collective-permute-start.21 = (bf16[4,320,256]{2,1,0:T(8,128)(2,1)S(1)}, bf16[4,320,256]{2,1,0:T(8,128)(2,1)S(1)}, u32[]{:S(2)}, u32[]{:S(2)}) collective-permute-start(bf16[4,320,256]{2,1,0:T(8,128)(2,1)S(1)} %pad_maximum_fusion.1), channel_id=1, source_target_pairs={{0,4},{1,5},{2,6},{3,7},{4,0},{5,1},{6,2},{7,3},{8,12},{9,13},{10,... | collective-permute-start | bytes 1966088 | tf_op jit(solution)/shard_map/ppermute | solution.py:45
  117.1 5.4 %collective-permute-start.23 = (bf16[320,256]{1,0:T(8,128)(2,1)S(1)}, bf16[320,256]{1,0:T(8,128)(2,1)S(1)}, u32[]{:S(2)}, u32[]{:S(2)}) collective-permute-start(bf16[320,256]{1,0:T(8,128)(2,1)S(1)} %get-tuple-element.59), channel_id=1, source_target_pairs={{0,16},{1,17},{2,18},{3,19},{4,20},{5,21},{6,22},{7,23},{8,24},{9,... | collective-permute-start | bytes 491528 | tf_op jit(solution)/shard_map/ppermute | solution.py:45
  118.3 6.9 %collective-permute-start.25 = (bf16[320,256]{1,0:T(8,128)(2,1)S(1)}, bf16[320,256]{1,0:T(8,128)(2,1)S(1)}, u32[]{:S(2)}, u32[]{:S(2)}) collective-permute-start(bf16[320,256]{1,0:T(8,128)(2,1)S(1)} %get-tuple-element.60), channel_id=1, source_target_pairs={{0,32},{1,33},{2,34},{3,35},{4,36},{5,37},{6,38},{7,39},{8,40},{9,... | collective-permute-start | bytes 491528 | tf_op jit(solution)/shard_map/ppermute | solution.py:45
  118.5 7.2 %collective-permute-start.24 = (bf16[320,256]{1,0:T(8,128)(2,1)S(1)}, bf16[320,256]{1,0:T(8,128)(2,1)S(1)}, u32[]{:S(2)}, u32[]{:S(2)}) collective-permute-start(bf16[320,256]{1,0:T(8,128)(2,1)S(1)} %get-tuple-element.61), channel_id=1, source_target_pairs={{0,48},{1,49},{2,50},{3,51},{4,52},{5,53},{6,54},{7,55},{8,56},{9,... | collective-permute-start | bytes 491528 | tf_op jit(solution)/shard_map/ppermute | solution.py:45
  (5 other events, 56.9 us)

commit v9 on v7

--- a/solution.py
+++ b/solution.py
@@ -169,7 +169,7 @@
 
 
 def opposite_kernel(
-    stats, local, weights, es_ref, et_ref, ws, wso, kl_ref, g_own, g_oth, o2a, o2b, part
+    stats, local, weights, es_ref, et_ref, ws, wso, kl_ref, g_own, g_oth, o2, part
 ):
     zl, c, x, y, _ = place()
     top = stats[0, 0:2]
@@ -193,10 +193,7 @@
         cols, first = window(block_at(c, x, y, r, 2))
         whole = dot(g[:ROWS], ws[:, cols], ((0,), (0,))) + dot(g[ROWS:], wso[:, cols], ((0,), (0,)))
         part[r] = whole.astype(BF16).T
-        if r < 2:
-            o2a[r] = part[r, pl.ds(first, NS)]
-        else:
-            o2b[r - 2] = part[r, pl.ds(first, NS)]
+        o2[r] = part[r, pl.ds(first, NS)]
 
 
 def rest_kernel(g_own, g_oth, ws, wso, o0, o1, o3, acc):
@@ -212,8 +209,8 @@
 
 
 def opposite_call(*args):
-    rows, half = ((ROWS, TOK), BF16), ((2, NS, TOK), BF16)
-    outs = (((1, 128), F32), rows, rows, half, half)
+    rows = ((ROWS, TOK), BF16)
+    outs = (((1, 128), F32), rows, rows, ((4, NS, TOK), BF16))
     flops = 2 * 2 * ROWS * TOK * DS // 3
     return vmem_call(opposite_kernel, "opposite", outs, [((4, WIDE, TOK), BF16)], flops, *args)
 
@@ -276,21 +273,19 @@
     stats = merge((local, send(local, PAIR)))
     stats = merge((stats,) + ring(stats, ZH))
     stats = lax.all_to_all(jnp.broadcast_to(stats, (16, 8, TOK)), ("x", "y"), 0, 0)
-    kl_rows, g_own, g_oth, o2a, o2b = opposite_call(
+    kl_rows, g_own, g_oth, o2 = opposite_call(
         stats, local, row_weight.reshape(4, 128), es, et, student_head, student_other
     )
-    low, high = send(o2a, SECOND[1]), send(o2b, SECOND[3])
+    r2 = send(o2, SECOND[2])
     g_got, hidden_got = send(g_oth, CORE), send(hidden_own, CORE)
-    low, high, g_got, hidden_got, o0, o1, o3 = lax.optimization_barrier(
-        (low, high, g_got, hidden_got, *rest_call(g_own, g_oth, student_head, student_other))
+    g_got, hidden_got, o0, o1, o3 = lax.optimization_barrier(
+        (g_got, hidden_got, *rest_call(g_own, g_oth, student_head, student_other))
     )
-    o3 = jnp.concatenate([(o3[:2].astype(F32) + low.astype(F32)).astype(BF16), o3[2:]])
-    o1 = jnp.concatenate([o1[:2], (o1[2:].astype(F32) + high.astype(F32)).astype(BF16)])
     r1, r3 = send(o1, SECOND[1]), send(o3, SECOND[3])
     head_grad = head_call(g_own, g_got, hidden_own, hidden_got)
-    r1, r3, head_grad = lax.optimization_barrier((r1, r3, head_grad))
-
-    sums = o0.astype(F32) + (r1.astype(F32) + r3.astype(F32))
+    r1, r2, r3, head_grad = lax.optimization_barrier((r1, r2, r3, head_grad))
+
+    sums = o0.astype(F32) + (r1.astype(F32) + r3.astype(F32)) + r2.astype(F32)
     r1, r3, r2 = (send(sums[k].astype(BF16), FIRST[k]) for k in (1, 3, 2))
     sums = sums[0] + (r1.astype(F32) + r3.astype(F32)) + r2.astype(F32)
     sums = jnp.concatenate([sums[:, :128], sums[:, 128:]], axis=0).reshape(8, 80, 128)

time: 143 us -> 140 us (0.979)
  waiting for transfers between devices: 44.9 us -> 41.6 us
    ppermute x22 -> x21, waiting for transfers between devices: 44.9 us -> 41.6 us  [send(): return lax.ppermute(value, AXES, pairs)]
    ppermute x22 -> x21, starting transfers between devices: 26.8 us -> 27.2 us  [send(): return lax.ppermute(value, AXES, pairs)]
  transfers between devices with their start and end apart: 22 -> 21, of which waited for: 15 -> 13; matrix products, arithmetic and copies ran while one was open for 1% -> 1% of each run, Pallas kernels for 10% -> 11%
where the time goes in v9:
time: 140 us
  blocking collectives  49.3 us (35%)
  waiting for transfers between devices  41.6 us (30%)
  starting transfers between devices  27.2 us (19%)
  Pallas kernels  16.8 us (12%)
  other arithmetic  2.14 us (2%)
  local copies, waits for them, and re-layouts  2.07 us (1%)
    ppermute x21, waiting for transfers between devices, send(): return lax.ppermute(value, AXES, pairs)  41.6 us
    ppermute x21, starting transfers between devices, send(): return lax.ppermute(value, AXES, pairs)  27.2 us
    all_to_all x1, blocking collectives, per_device(): along = lax.all_to_all(copies, ('zl', 'zh'), 0, 0)  21 us
    all_to_all x1, blocking collectives, per_device(): hidden_grad = jnp.sum(lax.all_to_all(sums, ('zl', 'zh'), 0, 0), axis=0).T  16 us
    all_to_all x1, blocking collectives, per_device(): lax.all_to_all(jnp.broadcast_to(stats, (16, 8, TOK)), ('x', 'y'), 0, 0)  12.3 us
    pallas_call x6, Pallas kernels, vmem_call(): pl.pallas_call(kernel, out_shape=tuple((jax.ShapeDtypeStruct(*o) for o in...  11.2 us
    pallas_call x1, Pallas kernels, head_call(): pl.pallas_call(head_kernel, out_shape=jax.ShapeDtypeStruct((ROWS, DS), BF...  5.63 us
  transfers between devices with their start and end apart: 21, of which 13 were waited for; matrix products, arithmetic and copies ran while one was open for 1% of the time, Pallas kernels for 11%

profile of v9, /device:TPU:2, one launch (start us, length us, event | category | flops | bytes accessed | tf_op | source)
XLA Modules:
  0.0 139.9 jit_solution(937645709048649451)
XLA Ops:
  2.0 21.0 %all_to_all.15.along = bf16[8,144,128]{2,1,0:T(8,128)(2,1)S(1)} all-to-all(bf16[8,144,128]{2,1,0:T(8,128)(2,1)S(1)} %spread.1), channel_id=1, replica_groups=mesh['zl'=2,'c'=2,'x'=4,'y'=4,'zh'=4] {'zl','zh'}, dimensions={0} | all-to-all | bytes 589824 | tf_op jit(solution)/shard_map/all_to_all | solution.py:264
  27.2 5.8 %collective-permute-done.2 = bf16[576,256]{1,0:T(8,128)(2,1)S(1)} collective-permute-done((bf16[576,256]{1,0:T(8,128)(2,1)S(1)}, bf16[576,256]{1,0:T(8,128)(2,1)S(1)}, u32[]{:S(2)}, u32[]{:S(2)}) %collective-permute-start.2) | collective-permute-done | bytes 294944 | tf_op jit(solution)/shard_map/ppermute | solution.py:45
  33.0 2.1 %collective-permute-done = bf16[576,256]{1,0:T(8,128)(2,1)S(1)} collective-permute-done((bf16[576,256]{1,0:T(8,128)(2,1)S(1)}, bf16[576,256]{1,0:T(8,128)(2,1)S(1)}, u32[]{:S(2)}, u32[]{:S(2)}) %collective-permute-start) | collective-permute-done | bytes 294944 | tf_op jit(solution)/shard_map/ppermute | solution.py:45
  37.0 2.2 %collective-permute-start.3 = (bf16[4,576,256]{2,1,0:T(8,128)(2,1)S(1)}, bf16[4,576,256]{2,1,0:T(8,128)(2,1)S(1)}, u32[]{:S(2)}, u32[]{:S(2)}) collective-permute-start(bf16[4,576,256]{2,1,0:T(8,128)(2,1)S(1)} %pad_maximum_fusion.t0), channel_id=1, source_target_pairs={{0,12},{1,13},{2,14},{3,15},{4,8},{5,9},{6,10},{7,11},{8,4},{9,5},... | collective-permute-start | bytes 3538952 | tf_op jit(solution)/shard_map/ppermute | solution.py:45
  39.1 12.4 %collective-permute-done.5.t1 = bf16[4,576,256]{2,1,0:T(8,128)(2,1)S(1)} collective-permute-done((bf16[4,576,256]{2,1,0:T(8,128)(2,1)S(1)}, bf16[4,576,256]{2,1,0:T(8,128)(2,1)S(1)}, u32[]{:S(2)}, u32[]{:S(2)}) %collective-permute-start.5) | collective-permute-done | bytes 1179680 | tf_op jit(solution)/shard_map/ppermute | solution.py:45
  51.6 3.1 %collective-permute-start.6 = (bf16[2,576,256]{2,1,0:T(8,128)(2,1)S(1)}, bf16[2,576,256]{2,1,0:T(8,128)(2,1)S(1)}, u32[]{:S(2)}, u32[]{:S(2)}) collective-permute-start(bf16[2,576,256]{2,1,0:T(8,128)(2,1)S(1)} %slice.109), channel_id=1, source_target_pairs={{0,12},{1,13},{2,14},{3,15},{4,8},{5,9},{6,10},{7,11},{8,4},{9,5},... | collective-permute-start | bytes 1769480 | tf_op jit(solution)/shard_map/ppermute | solution.py:45
  55.0 1.9 %copy-done.1 = bf16[384,4096]{1,0:T(8,128)(2,1)S(1)} copy-done((bf16[384,4096]{1,0:T(8,128)(2,1)S(1)}, bf16[384,4096]{1,0:T(8,128)(2,1)}, u32[]{:S(2)}) %copy-start.1) | copy-done | bytes 3145752
  56.9 4.1 %near.1 = (f32[768,256]{1,0:T(8,128)S(1)}, f32[768,256]{1,0:T(8,128)S(1)}, bf16[5120,256]{1,0:T(8,128)(2,1)S(1)}) custom-call(bf16[4,576,256]{2,1,0:T(8,128)(2,1)S(1)} %pad_maximum_fusion.t0, bf16[4,576,256]{2,1,0:T(8,128)(2,1)S(1)} %collective-permute-done.5.t1, bf16[4,576,256]{2,1,0:T(8,128)(2,1)S(1)} %collective-permute-done.3.t3, ...), custom_call_target="tpu_custom_call" | custom-call | flops 3623878656 | bytes 14000000 | tf_op jit(solution)/shard_map/near/pallas_call | solution.py:140
  61.0 1.8 %collective-permute-done.6.t2b = bf16[2,576,256]{2,1,0:T(8,128)(2,1)S(1)} collective-permute-done((bf16[2,576,256]{2,1,0:T(8,128)(2,1)S(1)}, bf16[2,576,256]{2,1,0:T(8,128)(2,1)S(1)}, u32[]{:S(2)}, u32[]{:S(2)}) %collective-permute-start.6) | collective-permute-done | bytes 589856 | tf_op jit(solution)/shard_map/ppermute | solution.py:45
  62.8 1.9 %collective-permute-done.4.t2a = bf16[2,576,256]{2,1,0:T(8,128)(2,1)S(1)} collective-permute-done((bf16[2,576,256]{2,1,0:T(8,128)(2,1)S(1)}, bf16[2,576,256]{2,1,0:T(8,128)(2,1)S(1)}, u32[]{:S(2)}, u32[]{:S(2)}) %collective-permute-start.4) | collective-permute-done | bytes 589856 | tf_op jit(solution)/shard_map/ppermute | solution.py:45
  64.7 2.0 %far.1 = (f32[768,256]{1,0:T(8,128)S(1)}, f32[768,256]{1,0:T(8,128)S(1)}, f32[8,256]{1,0:T(8,128)S(1)}, bf16[5120,256]{1,0:T(8,128)(2,1)S(1)}) custom-call(bf16[2,576,256]{2,1,0:T(8,128)(2,1)S(1)} %collective-permute-done.4.t2a, bf16[2,576,256]{2,1,0:T(8,128)(2,1)S(1)} %collective-permute-done.6.t2b, f32[768,256]{1,0:T(8,128)S(1)} %get-tuple-element.26.s_in, ...), custom_call_target="tpu_custom_call" | custom-call | flops 1207959552 | bytes 14000000 | tf_op jit(solution)/shard_map/far/pallas_call | solution.py:140
  67.7 3.0 %collective-permute-done.9 = f32[8,256]{1,0:T(8,128)S(1)} collective-permute-done((f32[8,256]{1,0:T(8,128)S(1)}, f32[8,256]{1,0:T(8,128)S(1)}, u32[]{:S(2)}, u32[]{:S(2)}) %collective-permute-start.9) | collective-permute-done | bytes 8224 | tf_op jit(solution)/shard_map/ppermute | solution.py:45
  71.4 3.9 %collective-permute-start.11 = (f32[8,256]{1,0:T(8,128)S(1)}, f32[8,256]{1,0:T(8,128)S(1)}, u32[]{:S(2)}, u32[]{:S(2)}) collective-permute-start(f32[8,256]{1,0:T(8,128)S(1)} %pad_maximum_fusion.4), channel_id=1, source_target_pairs={{0,2},{1,3},{2,0},{3,1},{4,6},{5,7},{6,4},{7,5},{8,10},{9,11},{10,... | collective-permute-start | bytes 24584 | tf_op jit(solution)/shard_map/ppermute | solution.py:45
  75.3 2.0 %collective-permute-start.10 = (f32[8,256]{1,0:T(8,128)S(1)}, f32[8,256]{1,0:T(8,128)S(1)}, u32[]{:S(2)}, u32[]{:S(2)}) collective-permute-start(f32[8,256]{1,0:T(8,128)S(1)} %pad_maximum_fusion.4), channel_id=1, source_target_pairs={{0,1},{1,0},{2,3},{3,2},{4,5},{5,4},{6,7},{7,6},{8,9},{9,8},{10,11... | collective-permute-start | bytes 24584 | tf_op jit(solution)/shard_map/ppermute | solution.py:45
  77.3 1.7 %collective-permute-done.11 = f32[8,256]{1,0:T(8,128)S(1)} collective-permute-done((f32[8,256]{1,0:T(8,128)S(1)}, f32[8,256]{1,0:T(8,128)S(1)}, u32[]{:S(2)}, u32[]{:S(2)}) %collective-permute-start.11) | collective-permute-done | bytes 8224 | tf_op jit(solution)/shard_map/ppermute | solution.py:45
  80.1 12.3 %all_to_all.16.stats = f32[16,8,256]{2,1,0:T(8,128)S(1)} all-to-all(f32[16,8,256]{2,1,0:T(8,128)S(1)} %broadcast_in_dim.3), channel_id=1, replica_groups=mesh['zl'=2,'c'=2,'x'=4,'y'=4,'zh'=4] {'x','y'}, dimensions={0} | all-to-all | bytes 262144 | tf_op jit(solution)/shard_map/all_to_all | solution.py:275
  92.4 1.8 %opposite.1 = (f32[1,128]{1,0:T(1,128)}, bf16[384,256]{1,0:T(8,128)(2,1)S(1)}, bf16[384,256]{1,0:T(8,128)(2,1)S(1)}, bf16[4,320,256]{2,1,0:T(8,128)(2,1)S(1)}) custom-call(f32[16,8,256]{2,1,0:T(8,128)S(1)} %all_to_all.16.stats, f32[8,256]{1,0:T(8,128)S(1)} %get-tuple-element.29.local, f32[4,128]{1,0:T(4,128)S(1)} %bitcast.23, ...), custom_call_target="tpu_custom_call" | custom-call | flops 671088640 | bytes 14000000 | tf_op jit(solution)/shard_map/opposite/pallas_call | solution.py:140
  95.7 3.1 %rest.1 = (bf16[4,320,256]{2,1,0:T(8,128)(2,1)S(1)}, bf16[4,320,256]{2,1,0:T(8,128)(2,1)S(1)}, bf16[4,320,256]{2,1,0:T(8,128)(2,1)S(1)}) custom-call(bf16[384,256]{1,0:T(8,128)(2,1)S(1)} %get-tuple-element.35.g_own, bf16[384,256]{1,0:T(8,128)(2,1)S(1)} %get-tuple-element.33.g_oth, bf16[384,5120]{1,0:T(8,128)(2,1)S(1)} %copy-done, ...), custom_call_target="tpu_custom_call" | custom-call | flops 2013265920 | bytes 14000000 | tf_op jit(solution)/shard_map/rest/pallas_call | solution.py:140
  99.4 2.1 %collective-permute-start.17 = (bf16[4,320,256]{2,1,0:T(8,128)(2,1)S(1)}, bf16[4,320,256]{2,1,0:T(8,128)(2,1)S(1)}, u32[]{:S(2)}, u32[]{:S(2)}) collective-permute-start(bf16[4,320,256]{2,1,0:T(8,128)(2,1)S(1)} %get-tuple-element.42), channel_id=1, source_target_pairs={{0,12},{1,13},{2,14},{3,15},{4,8},{5,9},{6,10},{7,11},{8,4},{9,5},... | collective-permute-start | bytes 1966088 | tf_op jit(solution)/shard_map/ppermute | solution.py:45
  101.5 5.6 %head.1 = bf16[384,5120]{1,0:T(8,128)(2,1)} custom-call(bf16[384,256]{1,0:T(8,128)(2,1)S(1)} %get-tuple-element.35.g_own, bf16[384,256]{1,0:T(8,128)(2,1)S(1)} %collective-permute-done.13.g_got, bf16[5120,256]{1,0:T(8,128)(2,1)S(1)} %get-tuple-element.34.h_own, bf16[5120,256]{1,0:T(8,128)(2,1)S(1)} %collective-permute-done.14.h_got), custom_call_target="tpu_custom_call" | custom-call | flops 2013265920 | bytes 10000000 | tf_op jit(solution)/shard_map/head/pallas_call | solution.py:233
  107.1 4.6 %collective-permute-done.15 = bf16[4,320,256]{2,1,0:T(8,128)(2,1)S(1)} collective-permute-done((bf16[4,320,256]{2,1,0:T(8,128)(2,1)S(1)}, bf16[4,320,256]{2,1,0:T(8,128)(2,1)S(1)}, u32[]{:S(2)}, u32[]{:S(2)}) %collective-permute-start.15) | collective-permute-done | bytes 655392 | tf_op jit(solution)/shard_map/ppermute | solution.py:45
  117.3 1.8 %collective-permute-done.18 = bf16[320,256]{1,0:T(8,128)(2,1)S(1)} collective-permute-done((bf16[320,256]{1,0:T(8,128)(2,1)S(1)}, bf16[320,256]{1,0:T(8,128)(2,1)S(1)}, u32[]{:S(2)}, u32[]{:S(2)}) %collective-permute-start.18) | collective-permute-done | bytes 163872 | tf_op jit(solution)/shard_map/ppermute | solution.py:45
  119.1 3.1 %collective-permute-done.20 = bf16[320,256]{1,0:T(8,128)(2,1)S(1)} collective-permute-done((bf16[320,256]{1,0:T(8,128)(2,1)S(1)}, bf16[320,256]{1,0:T(8,128)(2,1)S(1)}, u32[]{:S(2)}, u32[]{:S(2)}) %collective-permute-start.20) | collective-permute-done | bytes 163872 | tf_op jit(solution)/shard_map/ppermute | solution.py:45
  123.2 16.0 %all_to_all.17 = f32[8,80,128]{2,1,0:T(8,128)S(1)} all-to-all(f32[8,80,128]{2,1,0:T(8,128)S(1)} %bitcast.24), channel_id=1, replica_groups=mesh['zl'=2,'c'=2,'x'=4,'y'=4,'zh'=4] {'zl','zh'}, dimensions={0} | all-to-all | bytes 655360 | tf_op jit(solution)/shard_map/all_to_all | solution.py:292
  (59 shorter events, 19.7 us)
Async XLA Ops:
  0.6 54.4 %collective-permute-start.7 = (bf16[384,5120]{1,0:T(8,128)(2,1)}, bf16[384,5120]{1,0:T(8,128)(2,1)S(1)}, u32[]{:S(2)}, u32[]{:S(2)}) collective-permute-start(bf16[384,5120]{1,0:T(8,128)(2,1)} %ws.7), channel_id=1, source_target_pairs={{0,64},{1,65},{2,66},{3,67},{4,68},{5,69},{6,70},{7,71},{8,72},{9,... | collective-permute-start | bytes 11796488 | tf_op jit(solution)/shard_map/ppermute | solution.py:45
  0.7 54.3 %collective-permute-start.8 = (bf16[384,4096]{1,0:T(8,128)(2,1)}, bf16[384,4096]{1,0:T(8,128)(2,1)S(1)}, u32[]{:S(2)}, u32[]{:S(2)}) collective-permute-start(bf16[384,4096]{1,0:T(8,128)(2,1)} %wt.3), channel_id=1, source_target_pairs={{0,64},{1,65},{2,66},{3,67},{4,68},{5,69},{6,70},{7,71},{8,72},{9,... | collective-permute-start | bytes 9437192 | tf_op jit(solution)/shard_map/ppermute | solution.py:45
  23.1 10.0 %collective-permute-start.2 = (bf16[576,256]{1,0:T(8,128)(2,1)S(1)}, bf16[576,256]{1,0:T(8,128)(2,1)S(1)}, u32[]{:S(2)}, u32[]{:S(2)}) collective-permute-start(bf16[576,256]{1,0:T(8,128)(2,1)S(1)} %weave.1), channel_id=1, source_target_pairs={{0,48},{1,49},{2,50},{3,51},{4,52},{5,53},{6,54},{7,55},{8,56},{9,... | collective-permute-start | bytes 884744 | tf_op jit(solution)/shard_map/ppermute | solution.py:45
  24.6 8.4 %collective-permute-start.1 = (bf16[576,256]{1,0:T(8,128)(2,1)S(1)}, bf16[576,256]{1,0:T(8,128)(2,1)S(1)}, u32[]{:S(2)}, u32[]{:S(2)}) collective-permute-start(bf16[576,256]{1,0:T(8,128)(2,1)S(1)} %weave.1), channel_id=1, source_target_pairs={{0,32},{1,33},{2,34},{3,35},{4,36},{5,37},{6,38},{7,39},{8,40},{9,... | collective-permute-start | bytes 884744 | tf_op jit(solution)/shard_map/ppermute | solution.py:45
  25.7 9.4 %collective-permute-start = (bf16[576,256]{1,0:T(8,128)(2,1)S(1)}, bf16[576,256]{1,0:T(8,128)(2,1)S(1)}, u32[]{:S(2)}, u32[]{:S(2)}) collective-permute-start(bf16[576,256]{1,0:T(8,128)(2,1)S(1)} %weave.1), channel_id=1, source_target_pairs={{0,16},{1,17},{2,18},{3,19},{4,20},{5,21},{6,22},{7,23},{8,24},{9,... | collective-permute-start | bytes 884744 | tf_op jit(solution)/shard_map/ppermute | solution.py:45
  35.1 19.9 %copy-start = (bf16[384,5120]{1,0:T(8,128)(2,1)S(1)}, bf16[384,5120]{1,0:T(8,128)(2,1)}, u32[]{:S(2)}) copy-start(bf16[384,5120]{1,0:T(8,128)(2,1)} %ws.7) | copy-start | bytes 11796484
  35.3 16.3 %collective-permute-start.5 = (bf16[4,576,256]{2,1,0:T(8,128)(2,1)S(1)}, bf16[4,576,256]{2,1,0:T(8,128)(2,1)S(1)}, u32[]{:S(2)}, u32[]{:S(2)}) collective-permute-start(bf16[4,576,256]{2,1,0:T(8,128)(2,1)S(1)} %pad_maximum_fusion.t0), channel_id=1, source_target_pairs={{0,4},{1,5},{2,6},{3,7},{4,0},{5,1},{6,2},{7,3},{8,12},{9,13},{10,... | collective-permute-start | bytes 3538952 | tf_op jit(solution)/shard_map/ppermute | solution.py:45
  37.0 17.8 %collective-permute-start.3 = (bf16[4,576,256]{2,1,0:T(8,128)(2,1)S(1)}, bf16[4,576,256]{2,1,0:T(8,128)(2,1)S(1)}, u32[]{:S(2)}, u32[]{:S(2)}) collective-permute-start(bf16[4,576,256]{2,1,0:T(8,128)(2,1)S(1)} %pad_maximum_fusion.t0), channel_id=1, source_target_pairs={{0,12},{1,13},{2,14},{3,15},{4,8},{5,9},{6,10},{7,11},{8,4},{9,5},... | collective-permute-start | bytes 3538952 | tf_op jit(solution)/shard_map/ppermute | solution.py:45
  51.6 11.2 %collective-permute-start.6 = (bf16[2,576,256]{2,1,0:T(8,128)(2,1)S(1)}, bf16[2,576,256]{2,1,0:T(8,128)(2,1)S(1)}, u32[]{:S(2)}, u32[]{:S(2)}) collective-permute-start(bf16[2,576,256]{2,1,0:T(8,128)(2,1)S(1)} %slice.109), channel_id=1, source_target_pairs={{0,12},{1,13},{2,14},{3,15},{4,8},{5,9},{6,10},{7,11},{8,4},{9,5},... | collective-permute-start | bytes 1769480 | tf_op jit(solution)/shard_map/ppermute | solution.py:45
  54.8 10.0 %collective-permute-start.4 = (bf16[2,576,256]{2,1,0:T(8,128)(2,1)S(1)}, bf16[2,576,256]{2,1,0:T(8,128)(2,1)S(1)}, u32[]{:S(2)}, u32[]{:S(2)}) collective-permute-start(bf16[2,576,256]{2,1,0:T(8,128)(2,1)S(1)} %slice.108), channel_id=1, source_target_pairs={{0,4},{1,5},{2,6},{3,7},{4,0},{5,1},{6,2},{7,3},{8,12},{9,13},{10,... | collective-permute-start | bytes 1769480 | tf_op jit(solution)/shard_map/ppermute | solution.py:45
  55.0 1.9 %copy-start.1 = (bf16[384,4096]{1,0:T(8,128)(2,1)S(1)}, bf16[384,4096]{1,0:T(8,128)(2,1)}, u32[]{:S(2)}) copy-start(bf16[384,4096]{1,0:T(8,128)(2,1)} %wt.3) | copy-start | bytes 9437188
  64.7 27.6 %copy-start.2 = (f32[512]{0:T(512)S(1)}, f32[512]{0:T(512)}, u32[]{:S(2)}) copy-start(f32[512]{0:T(512)} %param.9) | copy-start | bytes 6148
  66.8 32.0 %collective-permute-start.14 = (bf16[5120,256]{1,0:T(8,128)(2,1)S(1)}, bf16[5120,256]{1,0:T(8,128)(2,1)S(1)}, u32[]{:S(2)}, u32[]{:S(2)}) collective-permute-start(bf16[5120,256]{1,0:T(8,128)(2,1)S(1)} %get-tuple-element.34.h_own), channel_id=1, source_target_pairs={{0,64},{1,65},{2,66},{3,67},{4,68},{5,69},{6,70},{7,71},{8,72},{9,... | collective-permute-start | bytes 7864328 | tf_op jit(solution)/shard_map/ppermute | solution.py:45
  66.9 3.7 %collective-permute-start.9 = (f32[8,256]{1,0:T(8,128)S(1)}, f32[8,256]{1,0:T(8,128)S(1)}, u32[]{:S(2)}, u32[]{:S(2)}) collective-permute-start(f32[8,256]{1,0:T(8,128)S(1)} %get-tuple-element.29.local), channel_id=1, source_target_pairs={{0,128},{1,129},{2,130},{3,131},{4,132},{5,133},{6,134},{7,135},{8... | collective-permute-start | bytes 24584 | tf_op jit(solution)/shard_map/ppermute | solution.py:45
  70.7 6.6 %collective-permute-start.12 = (f32[8,256]{1,0:T(8,128)S(1)}, f32[8,256]{1,0:T(8,128)S(1)}, u32[]{:S(2)}, u32[]{:S(2)}) collective-permute-start(f32[8,256]{1,0:T(8,128)S(1)} %pad_maximum_fusion.4), channel_id=1, source_target_pairs={{0,3},{1,2},{2,1},{3,0},{4,7},{5,6},{6,5},{7,4},{8,11},{9,10},{10,... | collective-permute-start | bytes 24584 | tf_op jit(solution)/shard_map/ppermute | solution.py:45
  71.4 7.6 %collective-permute-start.11 = (f32[8,256]{1,0:T(8,128)S(1)}, f32[8,256]{1,0:T(8,128)S(1)}, u32[]{:S(2)}, u32[]{:S(2)}) collective-permute-start(f32[8,256]{1,0:T(8,128)S(1)} %pad_maximum_fusion.4), channel_id=1, source_target_pairs={{0,2},{1,3},{2,0},{3,1},{4,6},{5,7},{6,4},{7,5},{8,10},{9,11},{10,... | collective-permute-start | bytes 24584 | tf_op jit(solution)/shard_map/ppermute | solution.py:45
  75.3 4.6 %collective-permute-start.10 = (f32[8,256]{1,0:T(8,128)S(1)}, f32[8,256]{1,0:T(8,128)S(1)}, u32[]{:S(2)}, u32[]{:S(2)}) collective-permute-start(f32[8,256]{1,0:T(8,128)S(1)} %pad_maximum_fusion.4), channel_id=1, source_target_pairs={{0,1},{1,0},{2,3},{3,2},{4,5},{5,4},{6,7},{7,6},{8,9},{9,8},{10,11... | collective-permute-start | bytes 24584 | tf_op jit(solution)/shard_map/ppermute | solution.py:45
  94.1 4.7 %collective-permute-start.13 = (bf16[384,256]{1,0:T(8,128)(2,1)S(1)}, bf16[384,256]{1,0:T(8,128)(2,1)S(1)}, u32[]{:S(2)}, u32[]{:S(2)}) collective-permute-start(bf16[384,256]{1,0:T(8,128)(2,1)S(1)} %get-tuple-element.33.g_oth), channel_id=1, source_target_pairs={{0,64},{1,65},{2,66},{3,67},{4,68},{5,69},{6,70},{7,71},{8,72},{9,... | collective-permute-start | bytes 589832 | tf_op jit(solution)/shard_map/ppermute | solution.py:45
  94.1 13.0 %collective-permute-start.16 = (bf16[4,320,256]{2,1,0:T(8,128)(2,1)S(1)}, bf16[4,320,256]{2,1,0:T(8,128)(2,1)S(1)}, u32[]{:S(2)}, u32[]{:S(2)}) collective-permute-start(bf16[4,320,256]{2,1,0:T(8,128)(2,1)S(1)} %get-tuple-element.41), channel_id=1, source_target_pairs={{0,8},{1,9},{2,10},{3,11},{4,12},{5,13},{6,14},{7,15},{8,0},{9,1},... | collective-permute-start | bytes 1966088 | tf_op jit(solution)/shard_map/ppermute | solution.py:45
  98.8 12.9 %collective-permute-start.15 = (bf16[4,320,256]{2,1,0:T(8,128)(2,1)S(1)}, bf16[4,320,256]{2,1,0:T(8,128)(2,1)S(1)}, u32[]{:S(2)}, u32[]{:S(2)}) collective-permute-start(bf16[4,320,256]{2,1,0:T(8,128)(2,1)S(1)} %get-tuple-element.40), channel_id=1, source_target_pairs={{0,4},{1,5},{2,6},{3,7},{4,0},{5,1},{6,2},{7,3},{8,12},{9,13},{10,... | collective-permute-start | bytes 1966088 | tf_op jit(solution)/shard_map/ppermute | solution.py:45
  99.4 13.8 %collective-permute-start.17 = (bf16[4,320,256]{2,1,0:T(8,128)(2,1)S(1)}, bf16[4,320,256]{2,1,0:T(8,128)(2,1)S(1)}, u32[]{:S(2)}, u32[]{:S(2)}) collective-permute-start(bf16[4,320,256]{2,1,0:T(8,128)(2,1)S(1)} %get-tuple-element.42), channel_id=1, source_target_pairs={{0,12},{1,13},{2,14},{3,15},{4,8},{5,9},{6,10},{7,11},{8,4},{9,5},... | collective-permute-start | bytes 1966088 | tf_op jit(solution)/shard_map/ppermute | solution.py:45
  113.7 5.4 %collective-permute-start.18 = (bf16[320,256]{1,0:T(8,128)(2,1)S(1)}, bf16[320,256]{1,0:T(8,128)(2,1)S(1)}, u32[]{:S(2)}, u32[]{:S(2)}) collective-permute-start(bf16[320,256]{1,0:T(8,128)(2,1)S(1)} %get-tuple-element.55), channel_id=1, source_target_pairs={{0,16},{1,17},{2,18},{3,19},{4,20},{5,21},{6,22},{7,23},{8,24},{9,... | collective-permute-start | bytes 491528 | tf_op jit(solution)/shard_map/ppermute | solution.py:45
  115.3 6.9 %collective-permute-start.20 = (bf16[320,256]{1,0:T(8,128)(2,1)S(1)}, bf16[320,256]{1,0:T(8,128)(2,1)S(1)}, u32[]{:S(2)}, u32[]{:S(2)}) collective-permute-start(bf16[320,256]{1,0:T(8,128)(2,1)S(1)} %get-tuple-element.56), channel_id=1, source_target_pairs={{0,32},{1,33},{2,34},{3,35},{4,36},{5,37},{6,38},{7,39},{8,40},{9,... | collective-permute-start | bytes 491528 | tf_op jit(solution)/shard_map/ppermute | solution.py:45
  116.0 7.1 %collective-permute-start.19 = (bf16[320,256]{1,0:T(8,128)(2,1)S(1)}, bf16[320,256]{1,0:T(8,128)(2,1)S(1)}, u32[]{:S(2)}, u32[]{:S(2)}) collective-permute-start(bf16[320,256]{1,0:T(8,128)(2,1)S(1)} %get-tuple-element.57), channel_id=1, source_target_pairs={{0,48},{1,49},{2,50},{3,51},{4,52},{5,53},{6,54},{7,55},{8,56},{9,... | collective-permute-start | bytes 491528 | tf_op jit(solution)/shard_map/ppermute | solution.py:45

commit v10 on v9

--- a/solution.py
+++ b/solution.py
@@ -28,9 +28,7 @@
     return [(i, index(*move(*coords(i)))) for i in range(256)]
 
 
-PAIR = perm(lambda zl, c, x, y, zh: (1 - zl, c, x, y, zh))
 CORE = perm(lambda zl, c, x, y, zh: (zl, 1 - c, x, y, zh))
-ZH = {k: perm(lambda zl, c, x, y, zh, k=k: (zl, c, x, y, zh ^ k)) for k in (1, 2, 3)}
 FIRST = {
     k: perm(lambda zl, c, x, y, zh, k=k: (zl, c, x ^ (k * (1 - c)), y ^ (k * c), zh))
     for k in (1, 2, 3)
@@ -125,12 +123,14 @@
     sm = jnp.max(s, axis=0, keepdims=True)
     tm = jnp.max(t, axis=0, keepdims=True)
     es, et = jnp.exp(s - sm), jnp.exp(t - tm)
-    st_ref[0:1] = sm
-    st_ref[1:2] = tm
-    st_ref[2:3] = jnp.sum(es, axis=0, keepdims=True)
-    st_ref[3:4] = jnp.sum(et, axis=0, keepdims=True)
-    st_ref[4:5] = jnp.sum(et * (t - s), axis=0, keepdims=True)
-    st_ref[5:8] = jnp.zeros((3, TOK), F32)
+    st_ref[0, 0:1] = sm
+    st_ref[0, 1:2] = tm
+    st_ref[0, 2:3] = jnp.sum(es, axis=0, keepdims=True)
+    st_ref[0, 3:4] = jnp.sum(et, axis=0, keepdims=True)
+    st_ref[0, 4:5] = jnp.sum(et * (t - s), axis=0, keepdims=True)
+    st_ref[0, 5:8] = jnp.zeros((3, TOK), F32)
+    for i in range(1, 8):
+        st_ref[i] = st_ref[0]
     es_ref[...] = es
     et_ref[...] = et
 
@@ -161,8 +161,27 @@
 
 def far_call(*args):
     flops = 2 * 2 * ROWS * TOK * (DS + DT) // 3
-    outs = (LOGITS, LOGITS, ((8, TOK), F32), HIDDEN)
+    outs = (LOGITS, LOGITS, ((8, 8, TOK), F32), HIDDEN)
     return vmem_call(far_kernel, "far", outs, [((4, WIDE, TOK), BF16)], flops, *args)
+
+
+def merged(stats, n):
+    top = stats[0, 0:2]
+    for i in range(1, n):
+        top = jnp.maximum(top, stats[i, 0:2])
+    totals, cross = jnp.zeros((2, TOK), F32), jnp.zeros((1, TOK), F32)
+    for i in range(n):
+        scale = jnp.exp(stats[i, 0:2] - top)
+        totals += stats[i, 2:4] * scale
+        cross += stats[i, 4:5] * scale[1:2]
+    return top, totals, cross
+
+
+def merge_kernel(stats, out):
+    out[0, 0:2], out[0, 2:4], out[0, 4:5] = merged(stats, 8)
+    out[0, 5:8] = jnp.zeros((3, TOK), F32)
+    for i in range(1, 16):
+        out[i] = out[0]
 
 
 CHUNK = 1280
@@ -172,20 +191,13 @@
     stats, local, weights, es_ref, et_ref, ws, wso, kl_ref, g_own, g_oth, o2, part
 ):
     zl, c, x, y, _ = place()
-    top = stats[0, 0:2]
-    for i in range(1, 16):
-        top = jnp.maximum(top, stats[i, 0:2])
-    totals, cross = jnp.zeros((2, TOK), F32), jnp.zeros((1, TOK), F32)
-    for i in range(16):
-        scale = jnp.exp(stats[i, 0:2] - top)
-        totals += stats[i, 2:4] * scale
-        cross += stats[i, 4:5] * scale[1:2]
+    top, totals, cross = merged(stats, 16)
     kl = cross / totals[1:2] - top[1:2] - jnp.log(totals[1:2]) + top[0:1] + jnp.log(totals[0:1])
     kl_ref[...] = jnp.where(zl == 0, kl[:, :128], kl[:, 128:])
     weight = jnp.concatenate(
         [jnp.where(c == 0, weights[i : i + 1], weights[i + 1 : i + 2]) for i in (0, 2)], axis=1
     )
-    coef = weight * (jnp.exp(local[0:2] - top) / totals)
+    coef = weight * (jnp.exp(local[0, 0:2] - top) / totals)
     g = (es_ref[...] * coef[0:1] - et_ref[...] * coef[1:2]).astype(BF16)
     g_own[...] = g[:ROWS]
     g_oth[...] = g[ROWS:]
@@ -244,17 +256,6 @@
     )(g_own, g_got, h_own, h_got)
 
 
-def merge(stats):
-    top = stats[0][0:2]
-    for s in stats[1:]:
-        top = jnp.maximum(top, s[0:2])
-    total = jnp.zeros_like(stats[0][2:5])
-    for s in stats:
-        scale = jnp.exp(s[0:2] - top)
-        total = total + s[2:5] * jnp.concatenate([scale, scale[1:2]], axis=0)
-    return jnp.concatenate([top, total, stats[0][5:8]], axis=0)
-
-
 def per_device(student_hidden, teacher_hidden, student_head, teacher_head, row_weight):
     teacher_other = send(teacher_head, CORE)
     student_other = send(student_head, CORE)
@@ -270,9 +271,9 @@
     heads = (student_head, student_other, teacher_head, teacher_other)
     near = near_call(line, before, after, *heads)
     es, et, local, hidden_own = far_call(far_low, far_high, *near, *heads)
-    stats = merge((local, send(local, PAIR)))
-    stats = merge((stats,) + ring(stats, ZH))
-    stats = lax.all_to_all(jnp.broadcast_to(stats, (16, 8, TOK)), ("x", "y"), 0, 0)
+    stats = lax.all_to_all(local, ("zl", "zh"), 0, 0)
+    stats = vmem_call(merge_kernel, "merge", [((16, 8, TOK), F32)], [], 1, stats)[0]
+    stats = lax.all_to_all(stats, ("x", "y"), 0, 0)
     kl_rows, g_own, g_oth, o2 = opposite_call(
         stats, local, row_weight.reshape(4, 128), es, et, student_head, student_other
     )

time: 140 us -> 136 us (0.971)
  blocking collectives: 49.3 us -> 58.1 us
  starting transfers between devices: 27.2 us -> 19.8 us
  waiting for transfers between devices: 41.6 us -> 36.1 us
    all_to_all x1 -> x2, blocking collectives: 12.3 us -> 22.6 us  [the longest x1 12.3 us: per_device(): stats = lax.all_to_all(stats, ('x', 'y'), 0, 0)]
    ppermute x21 -> x17, starting transfers between devices: 27.2 us -> 19.8 us  [send(): return lax.ppermute(value, AXES, pairs)]
    ppermute x21 -> x17, waiting for transfers between devices: 41.6 us -> 36.1 us  [send(): return lax.ppermute(value, AXES, pairs)]
    all_to_all x1, blocking collectives: 16 us -> 14.6 us  [per_device(): hidden_grad = jnp.sum(lax.all_to_all(sums, ('zl', 'zh'), 0, 0), axis=0).T]
    pallas_call x6 -> x7, Pallas kernels: 11.2 us -> 11.2 us  [vmem_call(): pl.pallas_call(kernel, out_shape=tuple((jax.ShapeDtypeStruct(*o) for o in...]
  transfers between devices with their start and end apart: 21 -> 17, of which waited for: 13 -> 10; matrix products, arithmetic and copies ran while one was open for 1% -> 1% of each run, Pallas kernels for 11% -> 11%
where the time goes in v10:
time: 136 us
  blocking collectives  58.1 us (43%)
  waiting for transfers between devices  36.1 us (27%)
  starting transfers between devices  19.8 us (15%)
  Pallas kernels  16.8 us (12%)
  other arithmetic  2.03 us (1%)
  local copies, waits for them, and re-layouts  2.03 us (1%)
    ppermute x17, waiting for transfers between devices, send(): return lax.ppermute(value, AXES, pairs)  36.1 us
    all_to_all x1, blocking collectives, per_device(): along = lax.all_to_all(copies, ('zl', 'zh'), 0, 0)  21 us
    ppermute x17, starting transfers between devices, send(): return lax.ppermute(value, AXES, pairs)  19.8 us
    all_to_all x1, blocking collectives, per_device(): hidden_grad = jnp.sum(lax.all_to_all(sums, ('zl', 'zh'), 0, 0), axis=0).T  14.6 us
    all_to_all x1, blocking collectives, per_device(): stats = lax.all_to_all(stats, ('x', 'y'), 0, 0)  12.3 us
    pallas_call x7, Pallas kernels, vmem_call(): pl.pallas_call(kernel, out_shape=tuple((jax.ShapeDtypeStruct(*o) for o in...  11.2 us
    all_to_all x1, blocking collectives, per_device(): stats = lax.all_to_all(local, ('zl', 'zh'), 0, 0)  10.3 us
    pallas_call x1, Pallas kernels, head_call(): pl.pallas_call(head_kernel, out_shape=jax.ShapeDtypeStruct((ROWS, DS), BF...  5.63 us
  transfers between devices with their start and end apart: 17, of which 10 were waited for; matrix products, arithmetic and copies ran while one was open for 1% of the time, Pallas kernels for 11%

profile of v10, /device:TPU:2, one launch (start us, length us, event | category | flops | bytes accessed | tf_op | source)
XLA Modules:
  0.0 135.6 jit_solution(16879092563449875423)
XLA Ops:
  2.0 21.0 %all_to_all.20.along = bf16[8,144,128]{2,1,0:T(8,128)(2,1)S(1)} all-to-all(bf16[8,144,128]{2,1,0:T(8,128)(2,1)S(1)} %spread.1), channel_id=1, replica_groups=mesh['zl'=2,'c'=2,'x'=4,'y'=4,'zh'=4] {'zl','zh'}, dimensions={0} | all-to-all | bytes 589824 | tf_op jit(solution)/shard_map/all_to_all | solution.py:265
  23.1 1.6 %collective-permute-start.2 = (bf16[576,256]{1,0:T(8,128)(2,1)S(1)}, bf16[576,256]{1,0:T(8,128)(2,1)S(1)}, u32[]{:S(2)}, u32[]{:S(2)}) collective-permute-start(bf16[576,256]{1,0:T(8,128)(2,1)S(1)} %weave.1), channel_id=1, source_target_pairs={{0,48},{1,49},{2,50},{3,51},{4,52},{5,53},{6,54},{7,55},{8,56},{9,... | collective-permute-start | bytes 884744 | tf_op jit(solution)/shard_map/ppermute | solution.py:43
  27.2 5.8 %collective-permute-done.2 = bf16[576,256]{1,0:T(8,128)(2,1)S(1)} collective-permute-done((bf16[576,256]{1,0:T(8,128)(2,1)S(1)}, bf16[576,256]{1,0:T(8,128)(2,1)S(1)}, u32[]{:S(2)}, u32[]{:S(2)}) %collective-permute-start.2) | collective-permute-done | bytes 294944 | tf_op jit(solution)/shard_map/ppermute | solution.py:43
  33.0 2.1 %collective-permute-done = bf16[576,256]{1,0:T(8,128)(2,1)S(1)} collective-permute-done((bf16[576,256]{1,0:T(8,128)(2,1)S(1)}, bf16[576,256]{1,0:T(8,128)(2,1)S(1)}, u32[]{:S(2)}, u32[]{:S(2)}) %collective-permute-start) | collective-permute-done | bytes 294944 | tf_op jit(solution)/shard_map/ppermute | solution.py:43
  35.3 1.7 %collective-permute-start.5 = (bf16[4,576,256]{2,1,0:T(8,128)(2,1)S(1)}, bf16[4,576,256]{2,1,0:T(8,128)(2,1)S(1)}, u32[]{:S(2)}, u32[]{:S(2)}) collective-permute-start(bf16[4,576,256]{2,1,0:T(8,128)(2,1)S(1)} %pad_maximum_fusion.t0), channel_id=1, source_target_pairs={{0,4},{1,5},{2,6},{3,7},{4,0},{5,1},{6,2},{7,3},{8,12},{9,13},{10,... | collective-permute-start | bytes 3538952 | tf_op jit(solution)/shard_map/ppermute | solution.py:43
  37.0 2.2 %collective-permute-start.3 = (bf16[4,576,256]{2,1,0:T(8,128)(2,1)S(1)}, bf16[4,576,256]{2,1,0:T(8,128)(2,1)S(1)}, u32[]{:S(2)}, u32[]{:S(2)}) collective-permute-start(bf16[4,576,256]{2,1,0:T(8,128)(2,1)S(1)} %pad_maximum_fusion.t0), channel_id=1, source_target_pairs={{0,12},{1,13},{2,14},{3,15},{4,8},{5,9},{6,10},{7,11},{8,4},{9,5},... | collective-permute-start | bytes 3538952 | tf_op jit(solution)/shard_map/ppermute | solution.py:43
  39.1 12.4 %collective-permute-done.5.t1 = bf16[4,576,256]{2,1,0:T(8,128)(2,1)S(1)} collective-permute-done((bf16[4,576,256]{2,1,0:T(8,128)(2,1)S(1)}, bf16[4,576,256]{2,1,0:T(8,128)(2,1)S(1)}, u32[]{:S(2)}, u32[]{:S(2)}) %collective-permute-start.5) | collective-permute-done | bytes 1179680 | tf_op jit(solution)/shard_map/ppermute | solution.py:43
  51.6 3.1 %collective-permute-start.6 = (bf16[2,576,256]{2,1,0:T(8,128)(2,1)S(1)}, bf16[2,576,256]{2,1,0:T(8,128)(2,1)S(1)}, u32[]{:S(2)}, u32[]{:S(2)}) collective-permute-start(bf16[2,576,256]{2,1,0:T(8,128)(2,1)S(1)} %slice.36), channel_id=1, source_target_pairs={{0,12},{1,13},{2,14},{3,15},{4,8},{5,9},{6,10},{7,11},{8,4},{9,5},... | collective-permute-start | bytes 1769480 | tf_op jit(solution)/shard_map/ppermute | solution.py:43
  55.0 1.9 %copy-done.1 = bf16[384,4096]{1,0:T(8,128)(2,1)S(1)} copy-done((bf16[384,4096]{1,0:T(8,128)(2,1)S(1)}, bf16[384,4096]{1,0:T(8,128)(2,1)}, u32[]{:S(2)}) %copy-start.1) | copy-done | bytes 3145752
  56.9 4.1 %near.1 = (f32[768,256]{1,0:T(8,128)S(1)}, f32[768,256]{1,0:T(8,128)S(1)}, bf16[5120,256]{1,0:T(8,128)(2,1)S(1)}) custom-call(bf16[4,576,256]{2,1,0:T(8,128)(2,1)S(1)} %pad_maximum_fusion.t0, bf16[4,576,256]{2,1,0:T(8,128)(2,1)S(1)} %collective-permute-done.5.t1, bf16[4,576,256]{2,1,0:T(8,128)(2,1)S(1)} %collective-permute-done.3.t3, ...), custom_call_target="tpu_custom_call" | custom-call | flops 3623878656 | bytes 14000000 | tf_op jit(solution)/shard_map/near/pallas_call | solution.py:140
  61.0 1.8 %collective-permute-done.6.t2b = bf16[2,576,256]{2,1,0:T(8,128)(2,1)S(1)} collective-permute-done((bf16[2,576,256]{2,1,0:T(8,128)(2,1)S(1)}, bf16[2,576,256]{2,1,0:T(8,128)(2,1)S(1)}, u32[]{:S(2)}, u32[]{:S(2)}) %collective-permute-start.6) | collective-permute-done | bytes 589856 | tf_op jit(solution)/shard_map/ppermute | solution.py:43
  62.8 1.9 %collective-permute-done.4.t2a = bf16[2,576,256]{2,1,0:T(8,128)(2,1)S(1)} collective-permute-done((bf16[2,576,256]{2,1,0:T(8,128)(2,1)S(1)}, bf16[2,576,256]{2,1,0:T(8,128)(2,1)S(1)}, u32[]{:S(2)}, u32[]{:S(2)}) %collective-permute-start.4) | collective-permute-done | bytes 589856 | tf_op jit(solution)/shard_map/ppermute | solution.py:43
  64.7 2.1 %far.1 = (f32[768,256]{1,0:T(8,128)S(1)}, f32[768,256]{1,0:T(8,128)S(1)}, f32[8,8,256]{2,1,0:T(8,128)S(1)}, bf16[5120,256]{1,0:T(8,128)(2,1)S(1)}) custom-call(bf16[2,576,256]{2,1,0:T(8,128)(2,1)S(1)} %collective-permute-done.4.t2a, bf16[2,576,256]{2,1,0:T(8,128)(2,1)S(1)} %collective-permute-done.6.t2b, f32[768,256]{1,0:T(8,128)S(1)} %get-tuple-element.26.s_in, ...), custom_call_target="tpu_custom_call" | custom-call | flops 1207959552 | bytes 14000000 | tf_op jit(solution)/shard_map/far/pallas_call | solution.py:140
  66.9 10.3 %all_to_all.21.stats = f32[8,8,256]{2,1,0:T(8,128)S(1)} all-to-all(f32[8,8,256]{2,1,0:T(8,128)S(1)} %get-tuple-element.29.local), channel_id=1, replica_groups=mesh['zl'=2,'c'=2,'x'=4,'y'=4,'zh'=4] {'zl','zh'}, dimensions={0} | all-to-all | bytes 131072 | tf_op jit(solution)/shard_map/all_to_all | solution.py:274
  77.2 12.3 %all_to_all.22.stats = f32[16,8,256]{2,1,0:T(8,128)S(1)} all-to-all(f32[16,8,256]{2,1,0:T(8,128)S(1)} %merge.1), channel_id=1, replica_groups=mesh['zl'=2,'c'=2,'x'=4,'y'=4,'zh'=4] {'x','y'}, dimensions={0} | all-to-all | bytes 262144 | tf_op jit(solution)/shard_map/all_to_all | solution.py:276
  89.5 1.8 %opposite.1 = (f32[1,128]{1,0:T(1,128)}, bf16[384,256]{1,0:T(8,128)(2,1)S(1)}, bf16[384,256]{1,0:T(8,128)(2,1)S(1)}, bf16[4,320,256]{2,1,0:T(8,128)(2,1)S(1)}) custom-call(f32[16,8,256]{2,1,0:T(8,128)S(1)} %all_to_all.22.stats, f32[8,8,256]{2,1,0:T(8,128)S(1)} %get-tuple-element.29.local, f32[4,128]{1,0:T(4,128)S(1)} %bitcast.23, ...), custom_call_target="tpu_custom_call" | custom-call | flops 671088640 | bytes 14000000 | tf_op jit(solution)/shard_map/opposite/pallas_call | solution.py:140
  92.8 3.1 %rest.1 = (bf16[4,320,256]{2,1,0:T(8,128)(2,1)S(1)}, bf16[4,320,256]{2,1,0:T(8,128)(2,1)S(1)}, bf16[4,320,256]{2,1,0:T(8,128)(2,1)S(1)}) custom-call(bf16[384,256]{1,0:T(8,128)(2,1)S(1)} %get-tuple-element.35.g_own, bf16[384,256]{1,0:T(8,128)(2,1)S(1)} %get-tuple-element.33.g_oth, bf16[384,5120]{1,0:T(8,128)(2,1)S(1)} %copy-done, ...), custom_call_target="tpu_custom_call" | custom-call | flops 2013265920 | bytes 14000000 | tf_op jit(solution)/shard_map/rest/pallas_call | solution.py:140
  96.6 2.1 %collective-permute-start.13 = (bf16[4,320,256]{2,1,0:T(8,128)(2,1)S(1)}, bf16[4,320,256]{2,1,0:T(8,128)(2,1)S(1)}, u32[]{:S(2)}, u32[]{:S(2)}) collective-permute-start(bf16[4,320,256]{2,1,0:T(8,128)(2,1)S(1)} %get-tuple-element.42), channel_id=1, source_target_pairs={{0,12},{1,13},{2,14},{3,15},{4,8},{5,9},{6,10},{7,11},{8,4},{9,5},... | collective-permute-start | bytes 1966088 | tf_op jit(solution)/shard_map/ppermute | solution.py:43
  98.6 5.6 %head.1 = bf16[384,5120]{1,0:T(8,128)(2,1)} custom-call(bf16[384,256]{1,0:T(8,128)(2,1)S(1)} %get-tuple-element.35.g_own, bf16[384,256]{1,0:T(8,128)(2,1)S(1)} %collective-permute-done.9.g_got, bf16[5120,256]{1,0:T(8,128)(2,1)S(1)} %get-tuple-element.34.h_own, bf16[5120,256]{1,0:T(8,128)(2,1)S(1)} %collective-permute-done.10.h_got), custom_call_target="tpu_custom_call" | custom-call | flops 2013265920 | bytes 10000000 | tf_op jit(solution)/shard_map/head/pallas_call | solution.py:245
  104.3 4.6 %collective-permute-done.11 = bf16[4,320,256]{2,1,0:T(8,128)(2,1)S(1)} collective-permute-done((bf16[4,320,256]{2,1,0:T(8,128)(2,1)S(1)}, bf16[4,320,256]{2,1,0:T(8,128)(2,1)S(1)}, u32[]{:S(2)}, u32[]{:S(2)}) %collective-permute-start.11) | collective-permute-done | bytes 655392 | tf_op jit(solution)/shard_map/ppermute | solution.py:43
  110.8 1.6 %collective-permute-start.14 = (bf16[320,256]{1,0:T(8,128)(2,1)S(1)}, bf16[320,256]{1,0:T(8,128)(2,1)S(1)}, u32[]{:S(2)}, u32[]{:S(2)}) collective-permute-start(bf16[320,256]{1,0:T(8,128)(2,1)S(1)} %get-tuple-element.51), channel_id=1, source_target_pairs={{0,16},{1,17},{2,18},{3,19},{4,20},{5,21},{6,22},{7,23},{8,24},{9,... | collective-permute-start | bytes 491528 | tf_op jit(solution)/shard_map/ppermute | solution.py:43
  114.4 1.8 %collective-permute-done.14 = bf16[320,256]{1,0:T(8,128)(2,1)S(1)} collective-permute-done((bf16[320,256]{1,0:T(8,128)(2,1)S(1)}, bf16[320,256]{1,0:T(8,128)(2,1)S(1)}, u32[]{:S(2)}, u32[]{:S(2)}) %collective-permute-start.14) | collective-permute-done | bytes 163872 | tf_op jit(solution)/shard_map/ppermute | solution.py:43
  116.2 3.2 %collective-permute-done.16 = bf16[320,256]{1,0:T(8,128)(2,1)S(1)} collective-permute-done((bf16[320,256]{1,0:T(8,128)(2,1)S(1)}, bf16[320,256]{1,0:T(8,128)(2,1)S(1)}, u32[]{:S(2)}, u32[]{:S(2)}) %collective-permute-start.16) | collective-permute-done | bytes 163872 | tf_op jit(solution)/shard_map/ppermute | solution.py:43
  120.4 14.6 %all_to_all.23 = f32[8,80,128]{2,1,0:T(8,128)S(1)} all-to-all(f32[8,80,128]{2,1,0:T(8,128)S(1)} %bitcast.24), channel_id=1, replica_groups=mesh['zl'=2,'c'=2,'x'=4,'y'=4,'zh'=4] {'zl','zh'}, dimensions={0} | all-to-all | bytes 655360 | tf_op jit(solution)/shard_map/all_to_all | solution.py:293
  (38 shorter events, 12.2 us)
Async XLA Ops:
  0.6 54.4 %collective-permute-start.7 = (bf16[384,5120]{1,0:T(8,128)(2,1)}, bf16[384,5120]{1,0:T(8,128)(2,1)S(1)}, u32[]{:S(2)}, u32[]{:S(2)}) collective-permute-start(bf16[384,5120]{1,0:T(8,128)(2,1)} %ws.7), channel_id=1, source_target_pairs={{0,64},{1,65},{2,66},{3,67},{4,68},{5,69},{6,70},{7,71},{8,72},{9,... | collective-permute-start | bytes 11796488 | tf_op jit(solution)/shard_map/ppermute | solution.py:43
  0.7 54.3 %collective-permute-start.8 = (bf16[384,4096]{1,0:T(8,128)(2,1)}, bf16[384,4096]{1,0:T(8,128)(2,1)S(1)}, u32[]{:S(2)}, u32[]{:S(2)}) collective-permute-start(bf16[384,4096]{1,0:T(8,128)(2,1)} %wt.3), channel_id=1, source_target_pairs={{0,64},{1,65},{2,66},{3,67},{4,68},{5,69},{6,70},{7,71},{8,72},{9,... | collective-permute-start | bytes 9437192 | tf_op jit(solution)/shard_map/ppermute | solution.py:43
  23.1 10.0 %collective-permute-start.2 = (bf16[576,256]{1,0:T(8,128)(2,1)S(1)}, bf16[576,256]{1,0:T(8,128)(2,1)S(1)}, u32[]{:S(2)}, u32[]{:S(2)}) collective-permute-start(bf16[576,256]{1,0:T(8,128)(2,1)S(1)} %weave.1), channel_id=1, source_target_pairs={{0,48},{1,49},{2,50},{3,51},{4,52},{5,53},{6,54},{7,55},{8,56},{9,... | collective-permute-start | bytes 884744 | tf_op jit(solution)/shard_map/ppermute | solution.py:43
  24.6 8.4 %collective-permute-start.1 = (bf16[576,256]{1,0:T(8,128)(2,1)S(1)}, bf16[576,256]{1,0:T(8,128)(2,1)S(1)}, u32[]{:S(2)}, u32[]{:S(2)}) collective-permute-start(bf16[576,256]{1,0:T(8,128)(2,1)S(1)} %weave.1), channel_id=1, source_target_pairs={{0,32},{1,33},{2,34},{3,35},{4,36},{5,37},{6,38},{7,39},{8,40},{9,... | collective-permute-start | bytes 884744 | tf_op jit(solution)/shard_map/ppermute | solution.py:43
  25.7 9.4 %collective-permute-start = (bf16[576,256]{1,0:T(8,128)(2,1)S(1)}, bf16[576,256]{1,0:T(8,128)(2,1)S(1)}, u32[]{:S(2)}, u32[]{:S(2)}) collective-permute-start(bf16[576,256]{1,0:T(8,128)(2,1)S(1)} %weave.1), channel_id=1, source_target_pairs={{0,16},{1,17},{2,18},{3,19},{4,20},{5,21},{6,22},{7,23},{8,24},{9,... | collective-permute-start | bytes 884744 | tf_op jit(solution)/shard_map/ppermute | solution.py:43
  35.1 19.9 %copy-start = (bf16[384,5120]{1,0:T(8,128)(2,1)S(1)}, bf16[384,5120]{1,0:T(8,128)(2,1)}, u32[]{:S(2)}) copy-start(bf16[384,5120]{1,0:T(8,128)(2,1)} %ws.7) | copy-start | bytes 11796484
  35.3 16.3 %collective-permute-start.5 = (bf16[4,576,256]{2,1,0:T(8,128)(2,1)S(1)}, bf16[4,576,256]{2,1,0:T(8,128)(2,1)S(1)}, u32[]{:S(2)}, u32[]{:S(2)}) collective-permute-start(bf16[4,576,256]{2,1,0:T(8,128)(2,1)S(1)} %pad_maximum_fusion.t0), channel_id=1, source_target_pairs={{0,4},{1,5},{2,6},{3,7},{4,0},{5,1},{6,2},{7,3},{8,12},{9,13},{10,... | collective-permute-start | bytes 3538952 | tf_op jit(solution)/shard_map/ppermute | solution.py:43
  37.0 17.8 %collective-permute-start.3 = (bf16[4,576,256]{2,1,0:T(8,128)(2,1)S(1)}, bf16[4,576,256]{2,1,0:T(8,128)(2,1)S(1)}, u32[]{:S(2)}, u32[]{:S(2)}) collective-permute-start(bf16[4,576,256]{2,1,0:T(8,128)(2,1)S(1)} %pad_maximum_fusion.t0), channel_id=1, source_target_pairs={{0,12},{1,13},{2,14},{3,15},{4,8},{5,9},{6,10},{7,11},{8,4},{9,5},... | collective-permute-start | bytes 3538952 | tf_op jit(solution)/shard_map/ppermute | solution.py:43
  51.6 11.2 %collective-permute-start.6 = (bf16[2,576,256]{2,1,0:T(8,128)(2,1)S(1)}, bf16[2,576,256]{2,1,0:T(8,128)(2,1)S(1)}, u32[]{:S(2)}, u32[]{:S(2)}) collective-permute-start(bf16[2,576,256]{2,1,0:T(8,128)(2,1)S(1)} %slice.36), channel_id=1, source_target_pairs={{0,12},{1,13},{2,14},{3,15},{4,8},{5,9},{6,10},{7,11},{8,4},{9,5},... | collective-permute-start | bytes 1769480 | tf_op jit(solution)/shard_map/ppermute | solution.py:43
  54.8 10.0 %collective-permute-start.4 = (bf16[2,576,256]{2,1,0:T(8,128)(2,1)S(1)}, bf16[2,576,256]{2,1,0:T(8,128)(2,1)S(1)}, u32[]{:S(2)}, u32[]{:S(2)}) collective-permute-start(bf16[2,576,256]{2,1,0:T(8,128)(2,1)S(1)} %slice.35), channel_id=1, source_target_pairs={{0,4},{1,5},{2,6},{3,7},{4,0},{5,1},{6,2},{7,3},{8,12},{9,13},{10,... | collective-permute-start | bytes 1769480 | tf_op jit(solution)/shard_map/ppermute | solution.py:43
  55.0 1.9 %copy-start.1 = (bf16[384,4096]{1,0:T(8,128)(2,1)S(1)}, bf16[384,4096]{1,0:T(8,128)(2,1)}, u32[]{:S(2)}) copy-start(bf16[384,4096]{1,0:T(8,128)(2,1)} %wt.3) | copy-start | bytes 9437188
  64.7 24.8 %copy-start.2 = (f32[512]{0:T(512)S(1)}, f32[512]{0:T(512)}, u32[]{:S(2)}) copy-start(f32[512]{0:T(512)} %param.9) | copy-start | bytes 6148
  66.8 29.2 %collective-permute-start.10 = (bf16[5120,256]{1,0:T(8,128)(2,1)S(1)}, bf16[5120,256]{1,0:T(8,128)(2,1)S(1)}, u32[]{:S(2)}, u32[]{:S(2)}) collective-permute-start(bf16[5120,256]{1,0:T(8,128)(2,1)S(1)} %get-tuple-element.34.h_own), channel_id=1, source_target_pairs={{0,64},{1,65},{2,66},{3,67},{4,68},{5,69},{6,70},{7,71},{8,72},{9,... | collective-permute-start | bytes 7864328 | tf_op jit(solution)/shard_map/ppermute | solution.py:43
  91.3 4.7 %collective-permute-start.9 = (bf16[384,256]{1,0:T(8,128)(2,1)S(1)}, bf16[384,256]{1,0:T(8,128)(2,1)S(1)}, u32[]{:S(2)}, u32[]{:S(2)}) collective-permute-start(bf16[384,256]{1,0:T(8,128)(2,1)S(1)} %get-tuple-element.33.g_oth), channel_id=1, source_target_pairs={{0,64},{1,65},{2,66},{3,67},{4,68},{5,69},{6,70},{7,71},{8,72},{9,... | collective-permute-start | bytes 589832 | tf_op jit(solution)/shard_map/ppermute | solution.py:43
  91.3 13.0 %collective-permute-start.12 = (bf16[4,320,256]{2,1,0:T(8,128)(2,1)S(1)}, bf16[4,320,256]{2,1,0:T(8,128)(2,1)S(1)}, u32[]{:S(2)}, u32[]{:S(2)}) collective-permute-start(bf16[4,320,256]{2,1,0:T(8,128)(2,1)S(1)} %get-tuple-element.41), channel_id=1, source_target_pairs={{0,8},{1,9},{2,10},{3,11},{4,12},{5,13},{6,14},{7,15},{8,0},{9,1},... | collective-permute-start | bytes 1966088 | tf_op jit(solution)/shard_map/ppermute | solution.py:43
  96.0 12.9 %collective-permute-start.11 = (bf16[4,320,256]{2,1,0:T(8,128)(2,1)S(1)}, bf16[4,320,256]{2,1,0:T(8,128)(2,1)S(1)}, u32[]{:S(2)}, u32[]{:S(2)}) collective-permute-start(bf16[4,320,256]{2,1,0:T(8,128)(2,1)S(1)} %get-tuple-element.40), channel_id=1, source_target_pairs={{0,4},{1,5},{2,6},{3,7},{4,0},{5,1},{6,2},{7,3},{8,12},{9,13},{10,... | collective-permute-start | bytes 1966088 | tf_op jit(solution)/shard_map/ppermute | solution.py:43
  96.6 13.9 %collective-permute-start.13 = (bf16[4,320,256]{2,1,0:T(8,128)(2,1)S(1)}, bf16[4,320,256]{2,1,0:T(8,128)(2,1)S(1)}, u32[]{:S(2)}, u32[]{:S(2)}) collective-permute-start(bf16[4,320,256]{2,1,0:T(8,128)(2,1)S(1)} %get-tuple-element.42), channel_id=1, source_target_pairs={{0,12},{1,13},{2,14},{3,15},{4,8},{5,9},{6,10},{7,11},{8,4},{9,5},... | collective-permute-start | bytes 1966088 | tf_op jit(solution)/shard_map/ppermute | solution.py:43
  110.8 5.4 %collective-permute-start.14 = (bf16[320,256]{1,0:T(8,128)(2,1)S(1)}, bf16[320,256]{1,0:T(8,128)(2,1)S(1)}, u32[]{:S(2)}, u32[]{:S(2)}) collective-permute-start(bf16[320,256]{1,0:T(8,128)(2,1)S(1)} %get-tuple-element.51), channel_id=1, source_target_pairs={{0,16},{1,17},{2,18},{3,19},{4,20},{5,21},{6,22},{7,23},{8,24},{9,... | collective-permute-start | bytes 491528 | tf_op jit(solution)/shard_map/ppermute | solution.py:43
  112.5 6.9 %collective-permute-start.16 = (bf16[320,256]{1,0:T(8,128)(2,1)S(1)}, bf16[320,256]{1,0:T(8,128)(2,1)S(1)}, u32[]{:S(2)}, u32[]{:S(2)}) collective-permute-start(bf16[320,256]{1,0:T(8,128)(2,1)S(1)} %get-tuple-element.52), channel_id=1, source_target_pairs={{0,32},{1,33},{2,34},{3,35},{4,36},{5,37},{6,38},{7,39},{8,40},{9,... | collective-permute-start | bytes 491528 | tf_op jit(solution)/shard_map/ppermute | solution.py:43
  113.1 7.1 %collective-permute-start.15 = (bf16[320,256]{1,0:T(8,128)(2,1)S(1)}, bf16[320,256]{1,0:T(8,128)(2,1)S(1)}, u32[]{:S(2)}, u32[]{:S(2)}) collective-permute-start(bf16[320,256]{1,0:T(8,128)(2,1)S(1)} %get-tuple-element.53), channel_id=1, source_target_pairs={{0,48},{1,49},{2,50},{3,51},{4,52},{5,53},{6,54},{7,55},{8,56},{9,... | collective-permute-start | bytes 491528 | tf_op jit(solution)/shard_map/ppermute | solution.py:43

commit v11 on v10

--- a/solution.py
+++ b/solution.py
@@ -290,7 +290,8 @@
     r1, r3, r2 = (send(sums[k].astype(BF16), FIRST[k]) for k in (1, 3, 2))
     sums = sums[0] + (r1.astype(F32) + r3.astype(F32)) + r2.astype(F32)
     sums = jnp.concatenate([sums[:, :128], sums[:, 128:]], axis=0).reshape(8, 80, 128)
-    hidden_grad = jnp.sum(lax.all_to_all(sums, ("zl", "zh"), 0, 0), axis=0).T
+    pieces = lax.all_to_all(sums.astype(BF16), ("zl", "zh"), 0, 0)
+    hidden_grad = jnp.sum(pieces.astype(F32), axis=0).T
     return (kl_rows.reshape(128), hidden_grad, head_grad)
 
 

time: 136 us -> 133 us (0.978)
  blocking collectives: 58.1 us -> 54.2 us
    all_to_all x1, blocking collectives: 14.6 us -> 10.7 us  [per_device(): pieces = lax.all_to_all(sums.astype(BF16), ('zl', 'zh'), 0, 0)]
where the time goes in v11:
time: 133 us; the launch traced here: 132 us
  blocking collectives  54.2 us (41%)
  waiting for transfers between devices  36.1 us (27%)
  starting transfers between devices  19.8 us (15%)
  Pallas kernels  16.8 us (13%)
  other arithmetic  2.02 us (2%)
  local copies, waits for them, and re-layouts  2.02 us (2%)
    ppermute x17, waiting for transfers between devices, send(): return lax.ppermute(value, AXES, pairs)  36.1 us
    all_to_all x1, blocking collectives, per_device(): along = lax.all_to_all(copies, ('zl', 'zh'), 0, 0)  21 us
    ppermute x17, starting transfers between devices, send(): return lax.ppermute(value, AXES, pairs)  19.8 us
    all_to_all x1, blocking collectives, per_device(): stats = lax.all_to_all(stats, ('x', 'y'), 0, 0)  12.3 us
    pallas_call x7, Pallas kernels, vmem_call(): pl.pallas_call(kernel, out_shape=tuple((jax.ShapeDtypeStruct(*o) for o in...  11.2 us
    all_to_all x1, blocking collectives, per_device(): pieces = lax.all_to_all(sums.astype(BF16), ('zl', 'zh'), 0, 0)  10.7 us
    all_to_all x1, blocking collectives, per_device(): stats = lax.all_to_all(local, ('zl', 'zh'), 0, 0)  10.3 us
    pallas_call x1, Pallas kernels, head_call(): pl.pallas_call(head_kernel, out_shape=jax.ShapeDtypeStruct((ROWS, DS), BF...  5.63 us
  transfers between devices with their start and end apart: 17, of which 10 were waited for; matrix products, arithmetic and copies ran while one was open for 1% of the time, Pallas kernels for 11%

profile of v11, /device:TPU:2, one launch (start us, length us, event | category | flops | bytes accessed | tf_op | source)
XLA Modules:
  0.0 131.6 jit_solution(15851087048904677779)
XLA Ops:
  2.0 21.0 %all_to_all.20.along = bf16[8,144,128]{2,1,0:T(8,128)(2,1)S(1)} all-to-all(bf16[8,144,128]{2,1,0:T(8,128)(2,1)S(1)} %spread.1), channel_id=1, replica_groups=mesh['zl'=2,'c'=2,'x'=4,'y'=4,'zh'=4] {'zl','zh'}, dimensions={0} | all-to-all | bytes 589824 | tf_op jit(solution)/shard_map/all_to_all | solution.py:265
  23.1 1.6 %collective-permute-start.2 = (bf16[576,256]{1,0:T(8,128)(2,1)S(1)}, bf16[576,256]{1,0:T(8,128)(2,1)S(1)}, u32[]{:S(2)}, u32[]{:S(2)}) collective-permute-start(bf16[576,256]{1,0:T(8,128)(2,1)S(1)} %weave.1), channel_id=1, source_target_pairs={{0,48},{1,49},{2,50},{3,51},{4,52},{5,53},{6,54},{7,55},{8,56},{9,... | collective-permute-start | bytes 884744 | tf_op jit(solution)/shard_map/ppermute | solution.py:43
  27.2 5.8 %collective-permute-done.2 = bf16[576,256]{1,0:T(8,128)(2,1)S(1)} collective-permute-done((bf16[576,256]{1,0:T(8,128)(2,1)S(1)}, bf16[576,256]{1,0:T(8,128)(2,1)S(1)}, u32[]{:S(2)}, u32[]{:S(2)}) %collective-permute-start.2) | collective-permute-done | bytes 294944 | tf_op jit(solution)/shard_map/ppermute | solution.py:43
  33.0 2.1 %collective-permute-done = bf16[576,256]{1,0:T(8,128)(2,1)S(1)} collective-permute-done((bf16[576,256]{1,0:T(8,128)(2,1)S(1)}, bf16[576,256]{1,0:T(8,128)(2,1)S(1)}, u32[]{:S(2)}, u32[]{:S(2)}) %collective-permute-start) | collective-permute-done | bytes 294944 | tf_op jit(solution)/shard_map/ppermute | solution.py:43
  35.3 1.7 %collective-permute-start.5 = (bf16[4,576,256]{2,1,0:T(8,128)(2,1)S(1)}, bf16[4,576,256]{2,1,0:T(8,128)(2,1)S(1)}, u32[]{:S(2)}, u32[]{:S(2)}) collective-permute-start(bf16[4,576,256]{2,1,0:T(8,128)(2,1)S(1)} %pad_maximum_fusion.t0), channel_id=1, source_target_pairs={{0,4},{1,5},{2,6},{3,7},{4,0},{5,1},{6,2},{7,3},{8,12},{9,13},{10,... | collective-permute-start | bytes 3538952 | tf_op jit(solution)/shard_map/ppermute | solution.py:43
  37.0 2.2 %collective-permute-start.3 = (bf16[4,576,256]{2,1,0:T(8,128)(2,1)S(1)}, bf16[4,576,256]{2,1,0:T(8,128)(2,1)S(1)}, u32[]{:S(2)}, u32[]{:S(2)}) collective-permute-start(bf16[4,576,256]{2,1,0:T(8,128)(2,1)S(1)} %pad_maximum_fusion.t0), channel_id=1, source_target_pairs={{0,12},{1,13},{2,14},{3,15},{4,8},{5,9},{6,10},{7,11},{8,4},{9,5},... | collective-permute-start | bytes 3538952 | tf_op jit(solution)/shard_map/ppermute | solution.py:43
  39.1 12.4 %collective-permute-done.5.t1 = bf16[4,576,256]{2,1,0:T(8,128)(2,1)S(1)} collective-permute-done((bf16[4,576,256]{2,1,0:T(8,128)(2,1)S(1)}, bf16[4,576,256]{2,1,0:T(8,128)(2,1)S(1)}, u32[]{:S(2)}, u32[]{:S(2)}) %collective-permute-start.5) | collective-permute-done | bytes 1179680 | tf_op jit(solution)/shard_map/ppermute | solution.py:43
  51.6 3.1 %collective-permute-start.6 = (bf16[2,576,256]{2,1,0:T(8,128)(2,1)S(1)}, bf16[2,576,256]{2,1,0:T(8,128)(2,1)S(1)}, u32[]{:S(2)}, u32[]{:S(2)}) collective-permute-start(bf16[2,576,256]{2,1,0:T(8,128)(2,1)S(1)} %slice.38), channel_id=1, source_target_pairs={{0,12},{1,13},{2,14},{3,15},{4,8},{5,9},{6,10},{7,11},{8,4},{9,5},... | collective-permute-start | bytes 1769480 | tf_op jit(solution)/shard_map/ppermute | solution.py:43
  55.0 1.9 %copy-done.1 = bf16[384,4096]{1,0:T(8,128)(2,1)S(1)} copy-done((bf16[384,4096]{1,0:T(8,128)(2,1)S(1)}, bf16[384,4096]{1,0:T(8,128)(2,1)}, u32[]{:S(2)}) %copy-start.1) | copy-done | bytes 3145752
  56.9 4.1 %near.1 = (f32[768,256]{1,0:T(8,128)S(1)}, f32[768,256]{1,0:T(8,128)S(1)}, bf16[5120,256]{1,0:T(8,128)(2,1)S(1)}) custom-call(bf16[4,576,256]{2,1,0:T(8,128)(2,1)S(1)} %pad_maximum_fusion.t0, bf16[4,576,256]{2,1,0:T(8,128)(2,1)S(1)} %collective-permute-done.5.t1, bf16[4,576,256]{2,1,0:T(8,128)(2,1)S(1)} %collective-permute-done.3.t3, ...), custom_call_target="tpu_custom_call" | custom-call | flops 3623878656 | bytes 14000000 | tf_op jit(solution)/shard_map/near/pallas_call | solution.py:140
  61.0 1.8 %collective-permute-done.6.t2b = bf16[2,576,256]{2,1,0:T(8,128)(2,1)S(1)} collective-permute-done((bf16[2,576,256]{2,1,0:T(8,128)(2,1)S(1)}, bf16[2,576,256]{2,1,0:T(8,128)(2,1)S(1)}, u32[]{:S(2)}, u32[]{:S(2)}) %collective-permute-start.6) | collective-permute-done | bytes 589856 | tf_op jit(solution)/shard_map/ppermute | solution.py:43
  62.8 1.9 %collective-permute-done.4.t2a = bf16[2,576,256]{2,1,0:T(8,128)(2,1)S(1)} collective-permute-done((bf16[2,576,256]{2,1,0:T(8,128)(2,1)S(1)}, bf16[2,576,256]{2,1,0:T(8,128)(2,1)S(1)}, u32[]{:S(2)}, u32[]{:S(2)}) %collective-permute-start.4) | collective-permute-done | bytes 589856 | tf_op jit(solution)/shard_map/ppermute | solution.py:43
  64.7 2.1 %far.1 = (f32[768,256]{1,0:T(8,128)S(1)}, f32[768,256]{1,0:T(8,128)S(1)}, f32[8,8,256]{2,1,0:T(8,128)S(1)}, bf16[5120,256]{1,0:T(8,128)(2,1)S(1)}) custom-call(bf16[2,576,256]{2,1,0:T(8,128)(2,1)S(1)} %collective-permute-done.4.t2a, bf16[2,576,256]{2,1,0:T(8,128)(2,1)S(1)} %collective-permute-done.6.t2b, f32[768,256]{1,0:T(8,128)S(1)} %get-tuple-element.26.s_in, ...), custom_call_target="tpu_custom_call" | custom-call | flops 1207959552 | bytes 14000000 | tf_op jit(solution)/shard_map/far/pallas_call | solution.py:140
  66.9 10.3 %all_to_all.21.stats = f32[8,8,256]{2,1,0:T(8,128)S(1)} all-to-all(f32[8,8,256]{2,1,0:T(8,128)S(1)} %get-tuple-element.29.local), channel_id=1, replica_groups=mesh['zl'=2,'c'=2,'x'=4,'y'=4,'zh'=4] {'zl','zh'}, dimensions={0} | all-to-all | bytes 131072 | tf_op jit(solution)/shard_map/all_to_all | solution.py:274
  77.2 12.3 %all_to_all.22.stats = f32[16,8,256]{2,1,0:T(8,128)S(1)} all-to-all(f32[16,8,256]{2,1,0:T(8,128)S(1)} %merge.1), channel_id=1, replica_groups=mesh['zl'=2,'c'=2,'x'=4,'y'=4,'zh'=4] {'x','y'}, dimensions={0} | all-to-all | bytes 262144 | tf_op jit(solution)/shard_map/all_to_all | solution.py:276
  89.5 1.8 %opposite.1 = (f32[1,128]{1,0:T(1,128)}, bf16[384,256]{1,0:T(8,128)(2,1)S(1)}, bf16[384,256]{1,0:T(8,128)(2,1)S(1)}, bf16[4,320,256]{2,1,0:T(8,128)(2,1)S(1)}) custom-call(f32[16,8,256]{2,1,0:T(8,128)S(1)} %all_to_all.22.stats, f32[8,8,256]{2,1,0:T(8,128)S(1)} %get-tuple-element.29.local, f32[4,128]{1,0:T(4,128)S(1)} %bitcast.25, ...), custom_call_target="tpu_custom_call" | custom-call | flops 671088640 | bytes 14000000 | tf_op jit(solution)/shard_map/opposite/pallas_call | solution.py:140
  92.8 3.1 %rest.1 = (bf16[4,320,256]{2,1,0:T(8,128)(2,1)S(1)}, bf16[4,320,256]{2,1,0:T(8,128)(2,1)S(1)}, bf16[4,320,256]{2,1,0:T(8,128)(2,1)S(1)}) custom-call(bf16[384,256]{1,0:T(8,128)(2,1)S(1)} %get-tuple-element.35.g_own, bf16[384,256]{1,0:T(8,128)(2,1)S(1)} %get-tuple-element.33.g_oth, bf16[384,5120]{1,0:T(8,128)(2,1)S(1)} %copy-done, ...), custom_call_target="tpu_custom_call" | custom-call | flops 2013265920 | bytes 14000000 | tf_op jit(solution)/shard_map/rest/pallas_call | solution.py:140
  96.6 2.1 %collective-permute-start.13 = (bf16[4,320,256]{2,1,0:T(8,128)(2,1)S(1)}, bf16[4,320,256]{2,1,0:T(8,128)(2,1)S(1)}, u32[]{:S(2)}, u32[]{:S(2)}) collective-permute-start(bf16[4,320,256]{2,1,0:T(8,128)(2,1)S(1)} %get-tuple-element.42), channel_id=1, source_target_pairs={{0,12},{1,13},{2,14},{3,15},{4,8},{5,9},{6,10},{7,11},{8,4},{9,5},... | collective-permute-start | bytes 1966088 | tf_op jit(solution)/shard_map/ppermute | solution.py:43
  98.6 5.6 %head.1 = bf16[384,5120]{1,0:T(8,128)(2,1)} custom-call(bf16[384,256]{1,0:T(8,128)(2,1)S(1)} %get-tuple-element.35.g_own, bf16[384,256]{1,0:T(8,128)(2,1)S(1)} %collective-permute-done.9.g_got, bf16[5120,256]{1,0:T(8,128)(2,1)S(1)} %get-tuple-element.34.h_own, bf16[5120,256]{1,0:T(8,128)(2,1)S(1)} %collective-permute-done.10.h_got), custom_call_target="tpu_custom_call" | custom-call | flops 2013265920 | bytes 10000000 | tf_op jit(solution)/shard_map/head/pallas_call | solution.py:245
  104.3 4.6 %collective-permute-done.11 = bf16[4,320,256]{2,1,0:T(8,128)(2,1)S(1)} collective-permute-done((bf16[4,320,256]{2,1,0:T(8,128)(2,1)S(1)}, bf16[4,320,256]{2,1,0:T(8,128)(2,1)S(1)}, u32[]{:S(2)}, u32[]{:S(2)}) %collective-permute-start.11) | collective-permute-done | bytes 655392 | tf_op jit(solution)/shard_map/ppermute | solution.py:43
  110.8 1.6 %collective-permute-start.14 = (bf16[320,256]{1,0:T(8,128)(2,1)S(1)}, bf16[320,256]{1,0:T(8,128)(2,1)S(1)}, u32[]{:S(2)}, u32[]{:S(2)}) collective-permute-start(bf16[320,256]{1,0:T(8,128)(2,1)S(1)} %get-tuple-element.51), channel_id=1, source_target_pairs={{0,16},{1,17},{2,18},{3,19},{4,20},{5,21},{6,22},{7,23},{8,24},{9,... | collective-permute-start | bytes 491528 | tf_op jit(solution)/shard_map/ppermute | solution.py:43
  114.4 1.8 %collective-permute-done.14 = bf16[320,256]{1,0:T(8,128)(2,1)S(1)} collective-permute-done((bf16[320,256]{1,0:T(8,128)(2,1)S(1)}, bf16[320,256]{1,0:T(8,128)(2,1)S(1)}, u32[]{:S(2)}, u32[]{:S(2)}) %collective-permute-start.14) | collective-permute-done | bytes 163872 | tf_op jit(solution)/shard_map/ppermute | solution.py:43
  116.2 3.2 %collective-permute-done.16 = bf16[320,256]{1,0:T(8,128)(2,1)S(1)} collective-permute-done((bf16[320,256]{1,0:T(8,128)(2,1)S(1)}, bf16[320,256]{1,0:T(8,128)(2,1)S(1)}, u32[]{:S(2)}, u32[]{:S(2)}) %collective-permute-start.16) | collective-permute-done | bytes 163872 | tf_op jit(solution)/shard_map/ppermute | solution.py:43
  120.3 10.7 %all_to_all.23 = bf16[8,80,128]{2,1,0:T(8,128)(2,1)S(1)} all-to-all(bf16[8,80,128]{2,1,0:T(8,128)(2,1)S(1)} %bitcast.26), channel_id=1, replica_groups=mesh['zl'=2,'c'=2,'x'=4,'y'=4,'zh'=4] {'zl','zh'}, dimensions={0} | all-to-all | bytes 327680 | tf_op jit(solution)/shard_map/all_to_all | solution.py:293
  (38 shorter events, 12.2 us)
Async XLA Ops:
  0.6 54.4 %collective-permute-start.7 = (bf16[384,5120]{1,0:T(8,128)(2,1)}, bf16[384,5120]{1,0:T(8,128)(2,1)S(1)}, u32[]{:S(2)}, u32[]{:S(2)}) collective-permute-start(bf16[384,5120]{1,0:T(8,128)(2,1)} %ws.7), channel_id=1, source_target_pairs={{0,64},{1,65},{2,66},{3,67},{4,68},{5,69},{6,70},{7,71},{8,72},{9,... | collective-permute-start | bytes 11796488 | tf_op jit(solution)/shard_map/ppermute | solution.py:43
  0.7 54.3 %collective-permute-start.8 = (bf16[384,4096]{1,0:T(8,128)(2,1)}, bf16[384,4096]{1,0:T(8,128)(2,1)S(1)}, u32[]{:S(2)}, u32[]{:S(2)}) collective-permute-start(bf16[384,4096]{1,0:T(8,128)(2,1)} %wt.3), channel_id=1, source_target_pairs={{0,64},{1,65},{2,66},{3,67},{4,68},{5,69},{6,70},{7,71},{8,72},{9,... | collective-permute-start | bytes 9437192 | tf_op jit(solution)/shard_map/ppermute | solution.py:43
  23.1 10.0 %collective-permute-start.2 = (bf16[576,256]{1,0:T(8,128)(2,1)S(1)}, bf16[576,256]{1,0:T(8,128)(2,1)S(1)}, u32[]{:S(2)}, u32[]{:S(2)}) collective-permute-start(bf16[576,256]{1,0:T(8,128)(2,1)S(1)} %weave.1), channel_id=1, source_target_pairs={{0,48},{1,49},{2,50},{3,51},{4,52},{5,53},{6,54},{7,55},{8,56},{9,... | collective-permute-start | bytes 884744 | tf_op jit(solution)/shard_map/ppermute | solution.py:43
  24.6 8.4 %collective-permute-start.1 = (bf16[576,256]{1,0:T(8,128)(2,1)S(1)}, bf16[576,256]{1,0:T(8,128)(2,1)S(1)}, u32[]{:S(2)}, u32[]{:S(2)}) collective-permute-start(bf16[576,256]{1,0:T(8,128)(2,1)S(1)} %weave.1), channel_id=1, source_target_pairs={{0,32},{1,33},{2,34},{3,35},{4,36},{5,37},{6,38},{7,39},{8,40},{9,... | collective-permute-start | bytes 884744 | tf_op jit(solution)/shard_map/ppermute | solution.py:43
  25.7 9.4 %collective-permute-start = (bf16[576,256]{1,0:T(8,128)(2,1)S(1)}, bf16[576,256]{1,0:T(8,128)(2,1)S(1)}, u32[]{:S(2)}, u32[]{:S(2)}) collective-permute-start(bf16[576,256]{1,0:T(8,128)(2,1)S(1)} %weave.1), channel_id=1, source_target_pairs={{0,16},{1,17},{2,18},{3,19},{4,20},{5,21},{6,22},{7,23},{8,24},{9,... | collective-permute-start | bytes 884744 | tf_op jit(solution)/shard_map/ppermute | solution.py:43
  35.1 19.9 %copy-start = (bf16[384,5120]{1,0:T(8,128)(2,1)S(1)}, bf16[384,5120]{1,0:T(8,128)(2,1)}, u32[]{:S(2)}) copy-start(bf16[384,5120]{1,0:T(8,128)(2,1)} %ws.7) | copy-start | bytes 11796484
  35.3 16.3 %collective-permute-start.5 = (bf16[4,576,256]{2,1,0:T(8,128)(2,1)S(1)}, bf16[4,576,256]{2,1,0:T(8,128)(2,1)S(1)}, u32[]{:S(2)}, u32[]{:S(2)}) collective-permute-start(bf16[4,576,256]{2,1,0:T(8,128)(2,1)S(1)} %pad_maximum_fusion.t0), channel_id=1, source_target_pairs={{0,4},{1,5},{2,6},{3,7},{4,0},{5,1},{6,2},{7,3},{8,12},{9,13},{10,... | collective-permute-start | bytes 3538952 | tf_op jit(solution)/shard_map/ppermute | solution.py:43
  37.0 17.8 %collective-permute-start.3 = (bf16[4,576,256]{2,1,0:T(8,128)(2,1)S(1)}, bf16[4,576,256]{2,1,0:T(8,128)(2,1)S(1)}, u32[]{:S(2)}, u32[]{:S(2)}) collective-permute-start(bf16[4,576,256]{2,1,0:T(8,128)(2,1)S(1)} %pad_maximum_fusion.t0), channel_id=1, source_target_pairs={{0,12},{1,13},{2,14},{3,15},{4,8},{5,9},{6,10},{7,11},{8,4},{9,5},... | collective-permute-start | bytes 3538952 | tf_op jit(solution)/shard_map/ppermute | solution.py:43
  51.6 11.2 %collective-permute-start.6 = (bf16[2,576,256]{2,1,0:T(8,128)(2,1)S(1)}, bf16[2,576,256]{2,1,0:T(8,128)(2,1)S(1)}, u32[]{:S(2)}, u32[]{:S(2)}) collective-permute-start(bf16[2,576,256]{2,1,0:T(8,128)(2,1)S(1)} %slice.38), channel_id=1, source_target_pairs={{0,12},{1,13},{2,14},{3,15},{4,8},{5,9},{6,10},{7,11},{8,4},{9,5},... | collective-permute-start | bytes 1769480 | tf_op jit(solution)/shard_map/ppermute | solution.py:43
  54.8 10.0 %collective-permute-start.4 = (bf16[2,576,256]{2,1,0:T(8,128)(2,1)S(1)}, bf16[2,576,256]{2,1,0:T(8,128)(2,1)S(1)}, u32[]{:S(2)}, u32[]{:S(2)}) collective-permute-start(bf16[2,576,256]{2,1,0:T(8,128)(2,1)S(1)} %slice.37), channel_id=1, source_target_pairs={{0,4},{1,5},{2,6},{3,7},{4,0},{5,1},{6,2},{7,3},{8,12},{9,13},{10,... | collective-permute-start | bytes 1769480 | tf_op jit(solution)/shard_map/ppermute | solution.py:43
  55.0 1.9 %copy-start.1 = (bf16[384,4096]{1,0:T(8,128)(2,1)S(1)}, bf16[384,4096]{1,0:T(8,128)(2,1)}, u32[]{:S(2)}) copy-start(bf16[384,4096]{1,0:T(8,128)(2,1)} %wt.3) | copy-start | bytes 9437188
  64.7 24.8 %copy-start.2 = (f32[512]{0:T(512)S(1)}, f32[512]{0:T(512)}, u32[]{:S(2)}) copy-start(f32[512]{0:T(512)} %param.9) | copy-start | bytes 6148
  66.8 29.2 %collective-permute-start.10 = (bf16[5120,256]{1,0:T(8,128)(2,1)S(1)}, bf16[5120,256]{1,0:T(8,128)(2,1)S(1)}, u32[]{:S(2)}, u32[]{:S(2)}) collective-permute-start(bf16[5120,256]{1,0:T(8,128)(2,1)S(1)} %get-tuple-element.34.h_own), channel_id=1, source_target_pairs={{0,64},{1,65},{2,66},{3,67},{4,68},{5,69},{6,70},{7,71},{8,72},{9,... | collective-permute-start | bytes 7864328 | tf_op jit(solution)/shard_map/ppermute | solution.py:43
  91.3 4.7 %collective-permute-start.9 = (bf16[384,256]{1,0:T(8,128)(2,1)S(1)}, bf16[384,256]{1,0:T(8,128)(2,1)S(1)}, u32[]{:S(2)}, u32[]{:S(2)}) collective-permute-start(bf16[384,256]{1,0:T(8,128)(2,1)S(1)} %get-tuple-element.33.g_oth), channel_id=1, source_target_pairs={{0,64},{1,65},{2,66},{3,67},{4,68},{5,69},{6,70},{7,71},{8,72},{9,... | collective-permute-start | bytes 589832 | tf_op jit(solution)/shard_map/ppermute | solution.py:43
  91.3 13.0 %collective-permute-start.12 = (bf16[4,320,256]{2,1,0:T(8,128)(2,1)S(1)}, bf16[4,320,256]{2,1,0:T(8,128)(2,1)S(1)}, u32[]{:S(2)}, u32[]{:S(2)}) collective-permute-start(bf16[4,320,256]{2,1,0:T(8,128)(2,1)S(1)} %get-tuple-element.41), channel_id=1, source_target_pairs={{0,8},{1,9},{2,10},{3,11},{4,12},{5,13},{6,14},{7,15},{8,0},{9,1},... | collective-permute-start | bytes 1966088 | tf_op jit(solution)/shard_map/ppermute | solution.py:43
  96.0 12.9 %collective-permute-start.11 = (bf16[4,320,256]{2,1,0:T(8,128)(2,1)S(1)}, bf16[4,320,256]{2,1,0:T(8,128)(2,1)S(1)}, u32[]{:S(2)}, u32[]{:S(2)}) collective-permute-start(bf16[4,320,256]{2,1,0:T(8,128)(2,1)S(1)} %get-tuple-element.40), channel_id=1, source_target_pairs={{0,4},{1,5},{2,6},{3,7},{4,0},{5,1},{6,2},{7,3},{8,12},{9,13},{10,... | collective-permute-start | bytes 1966088 | tf_op jit(solution)/shard_map/ppermute | solution.py:43
  96.6 13.9 %collective-permute-start.13 = (bf16[4,320,256]{2,1,0:T(8,128)(2,1)S(1)}, bf16[4,320,256]{2,1,0:T(8,128)(2,1)S(1)}, u32[]{:S(2)}, u32[]{:S(2)}) collective-permute-start(bf16[4,320,256]{2,1,0:T(8,128)(2,1)S(1)} %get-tuple-element.42), channel_id=1, source_target_pairs={{0,12},{1,13},{2,14},{3,15},{4,8},{5,9},{6,10},{7,11},{8,4},{9,5},... | collective-permute-start | bytes 1966088 | tf_op jit(solution)/shard_map/ppermute | solution.py:43
  110.8 5.4 %collective-permute-start.14 = (bf16[320,256]{1,0:T(8,128)(2,1)S(1)}, bf16[320,256]{1,0:T(8,128)(2,1)S(1)}, u32[]{:S(2)}, u32[]{:S(2)}) collective-permute-start(bf16[320,256]{1,0:T(8,128)(2,1)S(1)} %get-tuple-element.51), channel_id=1, source_target_pairs={{0,16},{1,17},{2,18},{3,19},{4,20},{5,21},{6,22},{7,23},{8,24},{9,... | collective-permute-start | bytes 491528 | tf_op jit(solution)/shard_map/ppermute | solution.py:43
  112.5 6.9 %collective-permute-start.16 = (bf16[320,256]{1,0:T(8,128)(2,1)S(1)}, bf16[320,256]{1,0:T(8,128)(2,1)S(1)}, u32[]{:S(2)}, u32[]{:S(2)}) collective-permute-start(bf16[320,256]{1,0:T(8,128)(2,1)S(1)} %get-tuple-element.52), channel_id=1, source_target_pairs={{0,32},{1,33},{2,34},{3,35},{4,36},{5,37},{6,38},{7,39},{8,40},{9,... | collective-permute-start | bytes 491528 | tf_op jit(solution)/shard_map/ppermute | solution.py:43
  113.1 7.1 %collective-permute-start.15 = (bf16[320,256]{1,0:T(8,128)(2,1)S(1)}, bf16[320,256]{1,0:T(8,128)(2,1)S(1)}, u32[]{:S(2)}, u32[]{:S(2)}) collective-permute-start(bf16[320,256]{1,0:T(8,128)(2,1)S(1)} %get-tuple-element.53), channel_id=1, source_target_pairs={{0,48},{1,49},{2,50},{3,51},{4,52},{5,53},{6,54},{7,55},{8,56},{9,... | collective-permute-start | bytes 491528 | tf_op jit(solution)/shard_map/ppermute | solution.py:43
